TPU v7x, 32 devices: a whole 2x2x4 slice. The times are simulated.
32 devices in a mesh: groups: 2 (over x), blk: 8 (over z, y), sub: 2 (over core).
Axes of the slice: x: 2, y: 2, z: 4, core: 2. Of those that a mesh axis runs over, the one named last changes fastest.
Arguments:
- embeddings: bfloat16 [16384, 512], P(('groups', 'blk'), 'sub'), parts along dimension 0, may hold values from -60 to 60
- vectors: bfloat16 [32, 16384], P('sub', ('groups', 'blk')), parts along dimension 1, may hold values from -6 to 6
- boxes: int32 [4, 16384], P(None, ('groups', 'blk')), parts along dimension 1, may hold values from 0 to 1023
- spans: int32 [2, 16384], P(None, ('groups', 'blk')), parts along dimension 1, may hold values from 0 to 17999
- camera: int32 [16384], P(('groups', 'blk')), parts along dimension 0, may hold values from 0 to 7
Outputs:
- basis: float32 [32, 16384], P('sub', ('groups', 'blk')), parts along dimension 1
There are 2 independent parts, one for each index of `groups`. A program takes and returns all parts, laid end to end along the dimension named above; each array names one. Nothing has to cross between parts.
Inputs may be any that keep to these rules, and one draw needn't show every extreme that they name: `boxes`: coordinates are whole pixels and may travel packed several to a word. `spans`: frame numbers are whole and may travel packed two to a word. `camera`: camera ids may travel packed several to a word.
All inputs are finite; a program needn't handle non-finite values.
Results may differ from a plain program's by a relative error of at most 0.0005.
Values may be sent and summed in bfloat16 or wider, within the bound.
No kernel may reach another device: no remote copies, remote signals or barrier semaphores. Data moves between devices by JAX's collectives and lax.ppermute only.
A program may use at most 64 MiB of HBM per device.

v0:
```python
import jax
import jax.numpy as jnp
from jax import lax
from jax.sharding import PartitionSpec as P

SHARPNESS = 10.0
IOU_FLOOR = 0.5
HORIZON = 2000.0
MARGIN = 8.0
EPSILON = 1e-06


def inverse_norms(values, axis_number):
    squares = jnp.sum(jnp.square(values.astype(jnp.float32)), axis=axis_number)
    return lax.rsqrt(squares + EPSILON)


def track_fields(track_meta):
    left = jnp.minimum(track_meta[0], track_meta[2]).astype(jnp.float32)
    right = jnp.maximum(track_meta[0], track_meta[2]).astype(jnp.float32) + MARGIN
    bottom = jnp.minimum(track_meta[1], track_meta[3]).astype(jnp.float32)
    top = jnp.maximum(track_meta[1], track_meta[3]).astype(jnp.float32) + MARGIN
    first = jnp.minimum(track_meta[4], track_meta[5])
    last = jnp.maximum(track_meta[4], track_meta[5])
    return (left, right, bottom, top, first, last, track_meta[6], track_meta[7])


def affinity(row_emb, row_inv, row_meta, col_embt, col_inv, col_meta):
    products = jnp.dot(row_emb, col_embt, preferred_element_type=jnp.float32)
    cosine = products * row_inv[:, None] * col_inv[None, :]
    row_left, row_right, row_bottom, row_top, row_first, row_last, row_cam, row_ids = track_fields(
        row_meta
    )
    col_left, col_right, col_bottom, col_top, col_first, col_last, col_cam, col_ids = track_fields(
        col_meta
    )
    inter_width = jnp.maximum(
        jnp.minimum(row_right[:, None], col_right[None, :])
        - jnp.maximum(row_left[:, None], col_left[None, :]),
        0.0,
    )
    inter_height = jnp.maximum(
        jnp.minimum(row_top[:, None], col_top[None, :])
        - jnp.maximum(row_bottom[:, None], col_bottom[None, :]),
        0.0,
    )
    inter_area = inter_width * inter_height
    row_area = (row_right - row_left) * (row_top - row_bottom)
    col_area = (col_right - col_left) * (col_top - col_bottom)
    union_area = row_area[:, None] + col_area[None, :] - inter_area
    iou_value = inter_area / union_area
    gap_frames = jnp.maximum(
        col_first[None, :] - row_last[:, None], row_first[:, None] - col_last[None, :]
    )
    temporal = jnp.exp(-jnp.maximum(gap_frames, 0).astype(jnp.float32) / HORIZON)
    barred = (
        (row_cam[:, None] == col_cam[None, :])
        & (gap_frames < 0)
        & (row_ids[:, None] != col_ids[None, :])
    )
    weight = jnp.exp(SHARPNESS * (cosine - 1.0)) * (IOU_FLOOR + iou_value) * temporal
    return jnp.where(barred, 0.0, weight)


def cholesky_factor(share_rows, total_rows):
    local_gram = jnp.dot(
        share_rows,
        share_rows.T,
        precision=lax.Precision.HIGHEST,
        preferred_element_type=jnp.float32,
    )
    whole_gram = lax.psum(local_gram, ("blk", "sub"))
    return jnp.linalg.cholesky(whole_gram / total_rows)


def local(embeddings, vectors, boxes, spans, camera):
    row_count = embeddings.shape[0]
    sub_count = lax.axis_size("sub")
    half_rows = row_count // sub_count
    sub_index = lax.axis_index("sub")
    block_count = lax.axis_size("blk")
    block_index = lax.axis_index("blk")
    own_emb, own_vec = (
        lax.all_gather(embeddings, "sub", axis=1, tiled=True),
        lax.all_gather(vectors, "sub", axis=0, tiled=True),
    )
    track_ids = block_index * row_count + jnp.arange(row_count, dtype=jnp.int32)
    own_meta = jnp.concatenate([boxes, spans, camera[None, :], track_ids[None, :]], axis=0)
    own_inv = inverse_norms(own_emb, 1)
    half_start = sub_index * half_rows
    mine_embt = lax.dynamic_slice_in_dim(own_emb, half_start, half_rows, 0).T
    mine_vec = lax.dynamic_slice_in_dim(own_vec, half_start, half_rows, 1)
    mine_meta = lax.dynamic_slice_in_dim(own_meta, half_start, half_rows, 1)
    all_meta = lax.all_gather(mine_meta, "blk", axis=1, tiled=True)
    col_embt = lax.all_gather(mine_embt, "blk", axis=1, tiled=True)
    block_tile = affinity(
        own_emb, own_inv, own_meta, col_embt, inverse_norms(col_embt, 0), all_meta
    )
    rounded = block_tile.astype(jnp.bfloat16)
    image_sums = lax.dot_general(
        lax.all_gather(mine_vec, "blk", axis=1, tiled=True),
        rounded,
        (((1,), (1,)), ((), ())),
        preferred_element_type=jnp.float32,
    )
    totals = ((image_sums, jnp.sum(block_tile, axis=1)), rounded)[0]
    total_rows = block_count * row_count
    image_sums, degree = (
        lax.psum_scatter(totals[0], "sub", scatter_dimension=1, tiled=True),
        lax.psum_scatter(totals[1], "sub", scatter_dimension=0, tiled=True),
    )
    image = image_sums / degree[None, :]
    lower = cholesky_factor(image, total_rows)
    solved = jax.scipy.linalg.solve_triangular(lower, image, lower=True)
    return lax.all_to_all(solved, "sub", split_axis=0, concat_axis=1, tiled=True)


def solution(mesh):
    placed = (
        P(("groups", "blk"), "sub"),
        P("sub", ("groups", "blk")),
        P(None, ("groups", "blk")),
        P(None, ("groups", "blk")),
        P(("groups", "blk")),
    )
    return jax.shard_map(
        local, mesh=mesh, in_specs=placed, out_specs=P("sub", ("groups", "blk")), check_vma=False
    )
```

profile of v0, /device:TPU:0, one launch (start us, length us, event | category | flops | bytes accessed | tf_op | source)
XLA Modules:
  0.0 222.6 jit_solution(14849510265162878056)
XLA Ops:
  6.5 0.7 all-gather.3.cloned.1.call-update
  7.3 13.3 %all-gather.3.cloned.1.call-done = bf16[1024,512]{1,0:T(8,128)(2,1)} async-done(((bf16[1024,256]{1,0:T(8,128)(2,1)}), bf16[1024,512]{1,0:T(8,128)(2,1)}) %all-gather.3.cloned.1.call-update) | async-done | bytes 1048592 | tf_op jit(solution)/shard_map/all_gather | solution.py:84
  20.6 1.9 dynamic-slice_bitcast_fusion
  22.6 2.1 all_gather.15
  24.7 0.8 fusion.15
  25.5 31.6 %all_gather.17 = s32[8,4096]{1,0:T(8,128)S(1)} all-gather(s32[8,512]{1,0:T(8,128)S(1)} %fusion.15), channel_id=1, replica_groups=mesh['groups'=2,'blk'=8,'sub'=2] {'blk'}, dimensions={1}, use_global_device_ids=true | all-gather | bytes 147456 | tf_op jit(solution)/shard_map/all_gather | solution.py:94
  57.1 31.8 %all_gather.16 = bf16[32,4096]{1,0:T(8,128)(2,1)S(1)} all-gather(bf16[32,512]{1,0:T(8,128)(2,1)S(1)} %constant_dynamic-slice_fusion), channel_id=1, replica_groups=mesh['groups'=2,'blk'=8,'sub'=2] {'blk'}, dimensions={1}, use_global_device_ids=true | all-gather | bytes 294912 | tf_op jit(solution)/shard_map/all_gather | solution.py:101
  88.8 0.8 slice_maximum_fusion.1
  89.6 0.9 minimum_convert_fusion.3
  90.5 0.9 convert_add_fusion.3
  91.4 0.1 fusion.17
  91.5 0.1 subtract_multiply_fusion
  91.6 1.5 multiply_reduce_fusion.1
  93.1 8.4 %all-gather.5.cloned.1.call-done = bf16[512,4096]{0,1:T(8,128)(2,1)} async-done(((bf16[512,512]{0,1:T(8,128)(2,1)}), bf16[512,4096]{0,1:T(8,128)(2,1)}) %all-gather.5.cloned.1.call-update) | async-done | bytes 4194320 | tf_op jit(solution)/shard_map/all_gather | solution.py:95
  101.5 3.1 %multiply_reduce_fusion = f32[4096]{0:T(1024)S(1)} fusion(bf16[512,4096]{0,1:T(8,128)(2,1)} %all-gather.5.cloned.1.call-done), kind=kLoop, calls=%fused_computation.11 | loop fusion | flops 6287360 | bytes 4210688 | tf_op jit(solution)/shard_map/reduce_sum | solution.py:14
  104.6 27.1 %fusion.18 = (f32[1024]{0:T(1024)S(1)}, bf16[1024,4096]{0,1:T(8,128)(2,1)S(1)}) fusion(f32[4096]{0:T(1024)S(1)} %bitcast.40, f32[1024]{0:T(1024)S(1)} %subtract_multiply_fusion.1, f32[4096]{0:T(1024)S(1)} %bitcast.43, f32[1024]{0:T(1024)S(1)} %bitcast.49, f32[4096]{0:T(1024)S(1)} %bitcast.44, f32[1024]{0:T(1024)S(1)} %bitcast.53, f32[4096]{0:T(1024)S(1)} %bitcast.41, ...), kind=kOutput, calls=%fused_computation.54 | convolution fusion | flops 4437572608 | bytes 13840384 | tf_op jit(solution)/shard_map/dot_general | solution.py:29
  131.8 2.2 fusion.7
  134.0 0.6 dynamic-slice
  135.3 2.5 %all-reduce = f32[1024]{0:T(1024)S(1)} all-reduce(f32[1024]{0:T(1024)S(1)} %get-tuple-element.20), channel_id=3, replica_groups=mesh['groups'=2,'blk'=8,'sub'=2] {'sub'}, use_global_device_ids=true, to_apply=%region_4.5.clone | all-reduce | flops 1024 | bytes 8192
  137.7 0.1 dynamic-slice.1
  137.8 2.9 %reduce-scatter.2.cloned.1.call-done = f32[32,512]{1,0:T(8,128)} async-done(((f32[32,1024]{1,0:T(8,128)}), f32[32,512]{1,0:T(8,128)}) %reduce-scatter.2.cloned.1.call-update) | async-done | bytes 65552 | tf_op jit(solution)/shard_map/reduce_scatter | solution.py:109
  140.7 1.1 fusion.11
  141.8 61.9 %psum.7 = f32[32,32]{0,1:T(8,128)S(1)} all-reduce(f32[32,32]{0,1:T(8,128)S(1)} %fusion.11), channel_id=1, replica_groups=mesh['groups'=2,'blk'=8,'sub'=2] {'blk','sub'}, use_global_device_ids=true, to_apply=%region_5.6 | all-reduce | flops 1024 | bytes 8192 | tf_op jit(solution)/shard_map/psum | solution.py:72
  203.8 0.1 copy.14
  203.8 2.9 %cholesky.16 = f32[32,32]{1,0:T(8,128)S(1)} custom-call(f32[32,32]{1,0:T(8,128)S(1)} %fusion.16), custom_call_target="Cholesky" | custom-call | tf_op jit(solution)/shard_map/jit(cholesky)/cholesky | solution.py:73
  206.8 0.6 compare_reduce_fusion
  207.4 0.7 fusion.12
  208.1 2.4 %custom-call.7 = f32[1,32,32]{1,2,0:T(8,128)S(1)} custom-call(f32[1,32,32]{2,1,0:T(8,128)S(1)} %fusion.12), custom_call_target="InvertDiagBlocksLowerTriangular" | custom-call | tf_op jit(solution)/shard_map/jit(_solve_triangular)/triangular_solve | solution.py:114
  210.5 0.1 copy.15
  210.6 1.1 fusion.9
  211.7 3.8 %all_to_all.16 = f32[2,16,512]{2,1,0:T(8,128)S(1)} all-to-all(f32[2,16,512]{2,1,0:T(8,128)S(1)} %fusion.9), channel_id=1, replica_groups=mesh['groups'=2,'blk'=8,'sub'=2] {'sub'}, dimensions={0} | all-to-all | bytes 131072 | tf_op jit(solution)/shard_map/all_to_all | solution.py:115
  215.5 0.6 copy.18
  (18 shorter events, 0.2 us)
Async XLA Ops:
  6.5 98.1 %copy-start = (s32[1024]{0:T(1024)S(1)}, s32[1024]{0:T(1024)}, u32[]{:S(2)}) copy-start(s32[1024]{0:T(1024)} %param.9) | copy-start | bytes 12292
  6.5 14.1 %all-gather.3.cloned.1.call-start = ((), (), s32[]{:S(2)}) async-start(), calls=%async_computation.2 | async-start | bytes 1572864 | tf_op jit(solution)/shard_map/all_gather | solution.py:84
  7.3 94.3 %all-gather.5.cloned.1.call-start = ((), (), s32[]{:S(2)}) async-start(), calls=%async_computation.3 | async-start | bytes 4718592 | tf_op jit(solution)/shard_map/all_gather | solution.py:95
  22.5 118.2 %reduce-scatter.2.cloned.1.call-start = ((), (), s32[]{:S(2)}) async-start(), calls=%async_computation.4 | async-start | bytes 196608 | tf_op jit(solution)/shard_map/reduce_scatter | solution.py:109
  131.8 2.2 %copy-start.1 = (u32[32]{0:T(128)S(1)}, u32[32]{0:T(128)}, u32[]{:S(2)}) copy-start(u32[32]{0:T(128)} %constant.80) | copy-start | bytes 388
Sparse Core Ops, SparseCore 0:
  8.9 11.6 all-gather.2
  22.7 78.7 all-gather.4
  134.1 6.5 reduce-scatter.1
where the time goes:
time: 223 us
  blocking collectives  134 us (60%)
  matrix products  31.5 us (14%)
  waiting for transfers between devices  25.4 us (11%)
  other arithmetic  14.8 us (7%)
  between operations  13.9 us (6%)
  local copies, waits for them, and re-layouts  3.34 us (1%)
    psum x1, blocking collectives, cholesky_factor(): whole_gram = lax.psum(local_gram, ('blk', 'sub'))  61.9 us
    all_gather x1, blocking collectives, local(): lax.all_gather(mine_vec, 'blk', axis=1, tiled=True)  31.8 us
    all_gather x1, blocking collectives, local(): all_meta = lax.all_gather(mine_meta, 'blk', axis=1, tiled=True)  31.6 us
    dot_general x1, matrix products, affinity(): products = jnp.dot(row_emb, col_embt, preferred_element_type=jnp.float32)  27.1 us
    all_gather x1, waiting for transfers between devices, local(): lax.all_gather(embeddings, 'sub', axis=1, tiled=True)  13.3 us
    all_gather x1, waiting for transfers between devices, local(): col_embt = lax.all_gather(mine_embt, 'blk', axis=1, tiled=True)  8.42 us
    reduce_sum x2, other arithmetic, inverse_norms(): squares = jnp.sum(jnp.square(values.astype(jnp.float32)), axis=axis_number)  4.58 us
  transfers between devices with their start and end apart: 3, of which 3 were waited for; matrix products, arithmetic and copies ran while one was open for 3% of the time, Pallas kernels for 0%

commit v1 on v0

v1 whole, which is shorter than its diff:
```python
import functools
import math

import jax
import jax.numpy as jnp
from jax import lax
from jax.experimental import pallas as pl
from jax.experimental.pallas import tpu as pltpu
from jax.sharding import PartitionSpec as P

SHARPNESS = 10.0
HORIZON = 2000.0
MARGIN = 8.0
EPSILON = 1e-06

LOG2E = math.log2(math.e)
COS_SCALE = math.sqrt(SHARPNESS * LOG2E)
GAP_SCALE = LOG2E / HORIZON
BASE = SHARPNESS * LOG2E + 1.0
BARRED_BELOW = BASE - 0.5 * GAP_SCALE

FIELDS = 8
LEFT, RIGHT, BOTTOM, TOP, FIRST, LAST, CAMERA, NORM = range(FIELDS)
LANES = 128
CHUNK = 256
GROUP = 32
OUT_ROWS = 40
VMEM_LIMIT = 48 * 1024 * 1024

NT = (((1,), (1,)), ((), ()))
VMEM_SPEC = pl.BlockSpec(memory_space=pltpu.VMEM)


def params():
    return pltpu.CompilerParams(vmem_limit_bytes=VMEM_LIMIT)


def dot_nt(a, b, precision=None):
    return lax.dot_general(a, b, NT, precision=precision, preferred_element_type=jnp.float32)


def prepare_kernel(mine_ref, other_ref, vec_mine_ref, vec_other_ref, boxes_ref, spans_ref, camera_ref, out_ref):
    sub = lax.axis_index("sub")
    rows = mine_ref.shape[0]
    half_vecs = vec_mine_ref.shape[0]
    ones = jnp.ones((FIELDS, mine_ref.shape[1]), jnp.bfloat16)
    for start in range(0, rows, CHUNK):
        part = pl.ds(start, CHUNK)
        total = jnp.zeros((FIELDS, CHUNK), jnp.float32)
        for ref in (mine_ref, other_ref):
            values = ref[part, :].astype(jnp.float32)
            square = values * values
            high = square.astype(jnp.bfloat16)
            low = (square - high.astype(jnp.float32)).astype(jnp.bfloat16)
            total = total + dot_nt(ones, high) + dot_nt(ones, low)
        out_ref[NORM : NORM + 1, part] = (lax.rsqrt(total + EPSILON) * COS_SCALE)[0:1]
    corner_x, corner_y = boxes_ref[0:1, :], boxes_ref[1:2, :]
    other_x, other_y = boxes_ref[2:3, :], boxes_ref[3:4, :]
    begin, end = spans_ref[0:1, :], spans_ref[1:2, :]
    out_ref[LEFT : LEFT + 1, :] = jnp.minimum(corner_x, other_x).astype(jnp.float32)
    out_ref[RIGHT : RIGHT + 1, :] = jnp.maximum(corner_x, other_x).astype(jnp.float32) + MARGIN
    out_ref[BOTTOM : BOTTOM + 1, :] = jnp.minimum(corner_y, other_y).astype(jnp.float32)
    out_ref[TOP : TOP + 1, :] = jnp.maximum(corner_y, other_y).astype(jnp.float32) + MARGIN
    out_ref[FIRST : FIRST + 1, :] = jnp.minimum(begin, end).astype(jnp.float32) * GAP_SCALE + BASE
    out_ref[LAST : LAST + 1, :] = jnp.maximum(begin, end).astype(jnp.float32) * GAP_SCALE
    out_ref[CAMERA : CAMERA + 1, :] = camera_ref[...].astype(jnp.float32)
    own_place = pl.multiple_of(FIELDS + sub * half_vecs, 8)
    other_place = pl.multiple_of(FIELDS + (1 - sub) * half_vecs, 8)
    out_ref[pl.ds(own_place, half_vecs), :] = vec_mine_ref[...].astype(jnp.float32)
    out_ref[pl.ds(other_place, half_vecs), :] = vec_other_ref[...].astype(jnp.float32)


def prepare(mine, other, vec_mine, vec_other, boxes, spans, camera):
    rows = mine.shape[0]
    return pl.pallas_call(
        prepare_kernel,
        out_shape=jax.ShapeDtypeStruct((FIELDS + 2 * vec_mine.shape[0], rows), jnp.float32),
        in_specs=[VMEM_SPEC] * 7,
        out_specs=VMEM_SPEC,
        compiler_params=params(),
        name="prepare",
    )(mine, other, vec_mine, vec_other, boxes, spans, camera[None, :])


def weights_of(products, row, col, same):
    logit = products * row[NORM] * col[NORM]
    gap = jnp.maximum(col[FIRST] - row[LAST], row[FIRST] - col[LAST])
    width = jnp.maximum(jnp.minimum(row[RIGHT], col[RIGHT]) - jnp.maximum(row[LEFT], col[LEFT]), 0.0)
    height = jnp.maximum(jnp.minimum(row[TOP], col[TOP]) - jnp.maximum(row[BOTTOM], col[BOTTOM]), 0.0)
    inter = width * height
    both = row[FIELDS] + col[FIELDS]
    share = (both + inter) * pl.reciprocal(both - inter, approx=True)
    value = jnp.exp2(logit - jnp.maximum(gap, BASE)) * share
    barred = (row[CAMERA] == col[CAMERA]) & (gap < BARRED_BELOW)
    if same is not None:
        barred = barred & jnp.logical_not(same)
    return jnp.where(barred, 0.0, value)


def tile_kernel(blocks, own_block, receivers, *refs):
    row_mine_ref, row_other_ref, row_packet_ref = refs[:3]
    col_refs = [refs[3 + 3 * number : 6 + 3 * number] for number in range(blocks)]
    row_out_ref, col_out_ref, spread_ref, product_ref, weight_ref = refs[3 + 3 * blocks :]
    rows = row_mine_ref.shape[0]
    vecs = row_packet_ref.shape[0] - FIELDS
    row_out_ref[...] = jnp.zeros_like(row_out_ref)

    def with_ones(packet, count):
        tail = jnp.where(lax.broadcasted_iota(jnp.int32, (OUT_ROWS - vecs, count), 0) == 0, 1.0, 0.0)
        return jnp.concatenate([packet, tail], axis=0).astype(jnp.bfloat16)

    def compute():
        row_fields = row_packet_ref[0:FIELDS, :]
        turned = jnp.concatenate([row_fields] * (LANES // FIELDS), axis=0).T
        for field in range(FIELDS):
            spread_ref[field] = jnp.broadcast_to(turned[:, field : field + 1], (rows, LANES))
        spread_ref[FIELDS] = (spread_ref[RIGHT] - spread_ref[LEFT]) * (spread_ref[TOP] - spread_ref[BOTTOM])
        row_vecs = with_ones(row_packet_ref[FIELDS:, :], rows)
        sub = lax.axis_index("sub")
        done = 0
        for number, (col_mine_ref, col_other_ref, col_packet_ref) in enumerate(col_refs):
            cols = col_mine_ref.shape[0]

            def chunk(step, carry, col_mine_ref=col_mine_ref, col_other_ref=col_other_ref, col_packet_ref=col_packet_ref, number=number, done=done):
                start = pl.multiple_of(step * CHUNK, CHUNK)
                part = pl.ds(start, CHUNK)
                product_ref[...] = dot_nt(row_mine_ref[...], col_mine_ref[part, :]) + dot_nt(
                    row_other_ref[...], col_other_ref[part, :]
                )
                col = [col_packet_ref[field : field + 1, part] for field in range(FIELDS)]
                col.append((col[RIGHT] - col[LEFT]) * (col[TOP] - col[BOTTOM]))

                def group(index, inner):
                    first_row = pl.multiple_of(index * GROUP, GROUP)
                    row_part = pl.ds(first_row, GROUP)
                    row = [
                        jnp.concatenate([spread_ref[field, row_part, :]] * (CHUNK // LANES), axis=1)
                        for field in range(FIELDS + 1)
                    ]
                    same = None
                    if own_block and number == 0:
                        row_ids = lax.broadcasted_iota(jnp.int32, (GROUP, CHUNK), 0) + (sub * rows + first_row - start)
                        same = row_ids == lax.broadcasted_iota(jnp.int32, (GROUP, CHUNK), 1)
                    weight_ref[row_part, :] = weights_of(product_ref[row_part, :], row, col, same).astype(jnp.bfloat16)
                    return inner

                lax.fori_loop(0, rows // GROUP, group, 0, unroll=2)
                col_vecs = with_ones(col_packet_ref[FIELDS:, part], CHUNK)
                row_out_ref[...] += dot_nt(col_vecs, weight_ref[...])
                if col_out_ref is not None:
                    col_out_ref[:, pl.ds(pl.multiple_of(done + start, CHUNK), CHUNK)] = jnp.dot(
                        row_vecs, weight_ref[...], preferred_element_type=jnp.float32
                    )
                return carry

            lax.fori_loop(0, cols // CHUNK, chunk, 0)
            done += cols

    if receivers is None:
        compute()
        return
    pair = lax.axis_index("blk") // 2
    takes_part = functools.reduce(jnp.logical_or, [pair == one for one in receivers])

    @pl.when(takes_part)
    def _():
        compute()

    @pl.when(jnp.logical_not(takes_part))
    def _():
        col_out_ref[...] = jnp.zeros_like(col_out_ref)


def tile(row, columns, own_block=False, col_sums=True, receivers=None):
    row_mine, row_other, row_packet = row
    rows, features = row_mine.shape
    cols = sum(part[0].shape[0] for part in columns)
    shapes = [jax.ShapeDtypeStruct((OUT_ROWS, rows), jnp.float32)]
    if col_sums:
        shapes.append(jax.ShapeDtypeStruct((OUT_ROWS, cols), jnp.float32))

    def body(*refs):
        inputs = 3 + 3 * len(columns)
        refs = list(refs)
        if not col_sums:
            refs.insert(inputs + 1, None)
        tile_kernel(len(columns), own_block, receivers, *refs)

    pairs = rows * cols
    return pl.pallas_call(
        body,
        out_shape=shapes,
        in_specs=[VMEM_SPEC] * (3 + 3 * len(columns)),
        out_specs=[VMEM_SPEC] * len(shapes),
        scratch_shapes=[
            pltpu.VMEM((FIELDS + 1, rows, LANES), jnp.float32),
            pltpu.VMEM((rows, CHUNK), jnp.float32),
            pltpu.VMEM((rows, CHUNK), jnp.bfloat16),
        ],
        cost_estimate=pl.CostEstimate(
            flops=4 * pairs * features, bytes_accessed=4 * cols * features + 4 * rows * features, transcendentals=2 * pairs
        ),
        compiler_params=params(),
        name="tile",
    )(row_mine, row_other, row_packet, *[array for part in columns for array in part])


def image_kernel(*refs):
    parts, image_ref, gram_ref = refs[:-2], refs[-2], refs[-1]
    total = parts[0][...]
    for part in parts[1:]:
        total = total + part[...]
    vecs = image_ref.shape[0]
    image = total[0:vecs] / total[vecs : vecs + 1]
    image_ref[...] = image
    packed = jnp.zeros((8, LANES), jnp.float32)
    for piece in range(LANES // vecs):
        shifted = [image]
        if piece > 0:
            shifted.insert(0, jnp.zeros((piece * vecs, image.shape[1]), jnp.float32))
        if piece < LANES // vecs - 1:
            shifted.append(jnp.zeros((LANES - (piece + 1) * vecs, image.shape[1]), jnp.float32))
        packed = packed + dot_nt(image[8 * piece : 8 * piece + 8], jnp.concatenate(shifted, axis=0), lax.Precision.HIGHEST)
    gram_ref[...] = packed


def image_of(parts, vecs):
    cols = parts[0].shape[1]
    return pl.pallas_call(
        image_kernel,
        out_shape=[
            jax.ShapeDtypeStruct((vecs, cols), jnp.float32),
            jax.ShapeDtypeStruct((8, LANES), jnp.float32),
        ],
        in_specs=[VMEM_SPEC] * len(parts),
        out_specs=[VMEM_SPEC] * 2,
        compiler_params=params(),
        name="image",
    )(*parts)


def basis_kernel(total_rows, grams_ref, mine_ref, other_ref, out_ref, inverse_ref):
    vecs, half = mine_ref.shape
    sub = lax.axis_index("sub")
    packed = jnp.sum(grams_ref[...], axis=0) / total_rows
    lane = lax.broadcasted_iota(jnp.int32, (vecs, LANES), 1)
    line = lax.broadcasted_iota(jnp.int32, (vecs, LANES), 0)
    pieces = [packed] + [pltpu.roll(packed, LANES - piece * vecs, 1) for piece in range(1, LANES // vecs)]
    matrix = jnp.where(lane < vecs, jnp.concatenate(pieces, axis=0), 0.0)
    matrix = jnp.where(lane == line + vecs, 1.0, matrix)
    for step in range(vecs - 1):
        column = jnp.broadcast_to(matrix[:, step : step + 1], (vecs, LANES))
        scaled = matrix[step : step + 1, :] / column[step : step + 1, :]
        matrix = jnp.where(line > step, matrix - column * scaled, matrix)
    pivots = jnp.sum(jnp.where(lane == line, matrix, 0.0), axis=1, keepdims=True)
    inverse_ref[...] = pltpu.roll(matrix / jnp.sqrt(pivots), LANES - vecs, 1)
    share = vecs // 2
    own_rows = inverse_ref[pl.ds(pl.multiple_of(sub * share, 8), share), :][:, 0:vecs]
    for ref, place in ((mine_ref, sub), (other_ref, 1 - sub)):
        out_ref[:, pl.ds(pl.multiple_of(place * half, LANES), half)] = jnp.dot(
            own_rows, ref[...], precision=lax.Precision.HIGHEST, preferred_element_type=jnp.float32
        )


def basis_of(grams, mine, other, total_rows):
    vecs, half = mine.shape
    return pl.pallas_call(
        functools.partial(basis_kernel, total_rows),
        out_shape=jax.ShapeDtypeStruct((vecs // 2, 2 * half), jnp.float32),
        in_specs=[VMEM_SPEC] * 3,
        out_specs=VMEM_SPEC,
        scratch_shapes=[pltpu.VMEM((vecs, LANES), jnp.float32)],
        compiler_params=params(),
        name="basis",
    )(grams, mine, other)


def exchanges(pairs):
    plans = []
    for distance in range(1, pairs // 2):
        plans.append(([((p + distance) % pairs, p) for p in range(pairs)], None))
    if pairs > 1:
        half = pairs // 2
        last = [(p, p + half) if p % 2 == 0 else (p + half, p) for p in range(half)]
        plans.append((last, sorted(taker for _, taker in last)))
    return plans


def block_moves(pair_moves):
    return [(2 * source + member, 2 * target + member) for source, target in pair_moves for member in range(2)]


def back(moves):
    return [(target, source) for source, target in moves]


def local(embeddings, vectors, boxes, spans, camera):
    rows = embeddings.shape[0]
    half = rows // 2
    vecs = 2 * vectors.shape[0]
    blocks = lax.axis_size("blk")
    devices = 2 * blocks
    sub = lax.axis_index("sub")
    swap = [(0, 1), (1, 0)]
    beside = [(block, block ^ 1) for block in range(blocks)]
    plans = [(block_moves(moves), takers) for moves, takers in exchanges(blocks // 2)]

    def half_rows(array):
        return lax.dynamic_slice_in_dim(array, sub * half, half, 0)

    other = lax.ppermute(embeddings, "sub", swap)
    vec_other = lax.ppermute(vectors, "sub", swap)
    beside_mine = lax.ppermute(embeddings, "blk", beside)
    row_mine = half_rows(embeddings)
    sent_mine = [lax.ppermute(row_mine, "blk", moves) for moves, _ in plans]
    row_other = half_rows(other)
    sent_other = [lax.ppermute(row_other, "blk", moves) for moves, _ in plans]
    packet = prepare(embeddings, other, vectors, vec_other, boxes, spans, camera)
    row_packet = lax.dynamic_slice_in_dim(packet, sub * half, half, 1)
    beside_packet = lax.ppermute(packet, "blk", beside)
    sent_packet = [lax.ppermute(row_packet, "blk", moves) for moves, _ in plans]
    beside_other = lax.ppermute(beside_mine, "sub", swap)

    own_row = (row_mine, row_other, row_packet)
    own_cols = (embeddings, other, packet)
    beside_cols = (beside_mine, beside_other, beside_packet)
    parts = [
        tile(own_row, [own_cols], own_block=True, col_sums=False)[0],
        tile(own_row, [beside_cols], col_sums=False)[0],
    ]
    col_sums = None
    for (moves, takers), mine, rest, meta in zip(plans, sent_mine, sent_other, sent_packet):
        row_sums, sums = tile((mine, rest, meta), [own_cols, beside_cols], receivers=takers)
        parts.append(lax.ppermute(row_sums, "blk", back(moves)))
        col_sums = sums if col_sums is None else col_sums + sums

    def piece(place):
        return lax.dynamic_slice_in_dim(col_sums, place * half, half, 1)

    if col_sums is not None:
        crossed = [(2 * block + core, 2 * (block ^ 1) + 1 - core) for block in range(blocks) for core in range(2)]
        parts.append(piece(sub))
        parts.append(lax.ppermute(piece(1 - sub), "sub", swap))
        parts.append(lax.ppermute(piece(2 + sub), "blk", beside))
        parts.append(lax.ppermute(piece(3 - sub), ("blk", "sub"), crossed))

    image, gram = image_of(parts, vecs)
    image_other = lax.ppermute(image, "sub", swap)
    copies = jnp.broadcast_to(gram[None], (devices,) + gram.shape)
    grams = lax.all_to_all(copies, ("blk", "sub"), 0, 0, tiled=True)
    return basis_of(grams, image, image_other, blocks * rows)


def solution(mesh):
    placed = (
        P(("groups", "blk"), "sub"),
        P("sub", ("groups", "blk")),
        P(None, ("groups", "blk")),
        P(None, ("groups", "blk")),
        P(("groups", "blk")),
    )
    return jax.shard_map(
        local, mesh=mesh, in_specs=placed, out_specs=P("sub", ("groups", "blk")), check_vma=False
    )
```

time: 223 us -> 95.8 us (0.43)
  blocking collectives: 134 us -> 0 us
  starting transfers between devices: 0.08 us -> 36.3 us
  matrix products: 31.5 us -> 0 us
  Pallas kernels: 0 us -> 28.1 us
  other arithmetic: 14.8 us -> 0.04 us
  between operations: 13.9 us -> 0.22 us
    all_gather x3 -> x0, blocking collectives: 65.4 us -> none  [the longest x1 31.8 us: local(): lax.all_gather(mine_vec, 'blk', axis=1, tiled=True)]
    psum x1 -> x0, blocking collectives: 61.9 us -> none  [cholesky_factor(): whole_gram = lax.psum(local_gram, ('blk', 'sub'))]
    dot_general x3 -> x0, matrix products: 30.4 us -> none  [the longest x1 27.1 us: affinity(): products = jnp.dot(row_emb, col_embt, preferred_element_type=jnp.float32)]
    pallas_call x0 -> x7, Pallas kernels: none -> 28.1 us  [the longest x4 23.3 us: tile(): pl.pallas_call(body, out_shape=shapes, in_specs=[VMEM_SPEC] * (3 + 3 * le...]
    ppermute x0 -> x17, starting transfers between devices: none -> 23 us  [the longest x2 7.95 us: local(): sent_mine = [lax.ppermute(row_mine, 'blk', moves) for moves, _ in plans]]
    ppermute x0 -> x17, waiting for transfers between devices: none -> 21.8 us  [the longest x1 11.6 us: local(): beside_mine = lax.ppermute(embeddings, 'blk', beside)]
    all_gather x2 -> x0, waiting for transfers between devices: 21.7 us -> none  [the longest x1 13.3 us: local(): lax.all_gather(embeddings, 'sub', axis=1, tiled=True)]
    all_to_all x0 -> x1, starting transfers between devices: none -> 13.3 us  [local(): grams = lax.all_to_all(copies, ('blk', 'sub'), 0, 0, tiled=True)]
  transfers between devices with their start and end apart: 3 -> 18, of which waited for: 3 -> 6; matrix products, arithmetic and copies ran while one was open for 3% -> 1% of each run, Pallas kernels for 0% -> 25%
where the time goes in v1:
time: 95.8 us; the launch traced here: 95.4 us
  starting transfers between devices  36.3 us (38%)
  Pallas kernels  28.1 us (29%)
  waiting for transfers between devices  27.4 us (29%)
  local copies, waits for them, and re-layouts  3.37 us (4%)
    pallas_call x4, Pallas kernels, tile(): pl.pallas_call(body, out_shape=shapes, in_specs=[VMEM_SPEC] * (3 + 3 * le...  23.3 us
    all_to_all x1, starting transfers between devices, local(): grams = lax.all_to_all(copies, ('blk', 'sub'), 0, 0, tiled=True)  13.3 us
    ppermute x1, waiting for transfers between devices, local(): beside_mine = lax.ppermute(embeddings, 'blk', beside)  11.6 us
    ppermute x2, starting transfers between devices, local(): sent_mine = [lax.ppermute(row_mine, 'blk', moves) for moves, _ in plans]  7.95 us
    all_to_all x1, waiting for transfers between devices, local(): grams = lax.all_to_all(copies, ('blk', 'sub'), 0, 0, tiled=True)  5.58 us
    ppermute x2, starting transfers between devices, local(): sent_other = [lax.ppermute(row_other, 'blk', moves) for moves, _ in plans]  4.58 us
    pallas_call x1, Pallas kernels, basis_of(): pl.pallas_call(functools.partial(basis_kernel, total_rows), out_shape=jax...  3.54 us
    ppermute x2, waiting for transfers between devices, local(): sent_packet = [lax.ppermute(row_packet, 'blk', moves) for moves, _ in plans]  3.3 us
  transfers between devices with their start and end apart: 18, of which 6 were waited for; matrix products, arithmetic and copies ran while one was open for 1% of the time, Pallas kernels for 25%

profile of v1, /device:TPU:0, one launch (start us, length us, event | category | flops | bytes accessed | tf_op | source)
XLA Modules:
  0.0 95.4 jit_solution(10528506811408623901)
XLA Ops:
  0.0 3.0 %collective-permute-start.2 = (bf16[1024,256]{1,0:T(8,128)(2,1)}, bf16[1024,256]{1,0:T(8,128)(2,1)S(1)}, u32[]{:S(2)}, u32[]{:S(2)}) collective-permute-start(bf16[1024,256]{1,0:T(8,128)(2,1)} %refs_3_.5), channel_id=1, source_target_pairs={{0,2},{2,0},{4,6},{6,4},{8,10},{10,8},{12,14},{14,12},{1,3},{3,1},... | collective-permute-start | bytes 1572872 | tf_op jit(solution)/shard_map/ppermute | solution.py:313
  3.0 0.5 collective-permute-start.1
  3.5 11.6 %collective-permute-done.2.refs_3_.refs_6_ = bf16[1024,256]{1,0:T(8,128)(2,1)S(1)} collective-permute-done((bf16[1024,256]{1,0:T(8,128)(2,1)}, bf16[1024,256]{1,0:T(8,128)(2,1)S(1)}, u32[]{:S(2)}, u32[]{:S(2)}) %collective-permute-start.2) | collective-permute-done | bytes 524320 | tf_op jit(solution)/shard_map/ppermute | solution.py:313
  15.1 1.0 %constant_dynamic-slice_fusion.6.refs_0_ = bf16[512,256]{1,0:T(8,128)(2,1)S(1)} fusion(bf16[1024,256]{1,0:T(8,128)(2,1)} %refs_3_.5, s32[]{:T(128)S(6)} %select_n.17), kind=kLoop, calls=%fused_computation.6 | loop fusion | bytes 524292 | tf_op jit(solution)/shard_map/dynamic_slice | solution.py:309
  16.1 3.9 %collective-permute-start.5 = (bf16[512,256]{1,0:T(8,128)(2,1)S(1)}, bf16[512,256]{1,0:T(8,128)(2,1)S(1)}, u32[]{:S(2)}, u32[]{:S(2)}) collective-permute-start(bf16[512,256]{1,0:T(8,128)(2,1)S(1)} %constant_dynamic-slice_fusion.6.refs_0_), channel_id=1, source_target_pairs={{4,0},{6,2},{8,4},{10,6},{12,8},{14,10},{0,12},{2,14},{5,1},{7,3},... | collective-permute-start | bytes 786440 | tf_op jit(solution)/shard_map/ppermute | solution.py:315
  20.0 0.5 collective-permute-start.6
  20.5 0.1 copy-done.4
  20.7 0.7 prepare.1.refs_5_
  21.4 0.5 collective-permute-start.7
  21.9 1.5 %collective-permute-start.4 = (f32[40,1024]{1,0:T(8,128)S(1)}, f32[40,1024]{1,0:T(8,128)S(1)}, u32[]{:S(2)}, u32[]{:S(2)}) collective-permute-start(f32[40,1024]{1,0:T(8,128)S(1)} %prepare.1.refs_5_), channel_id=1, source_target_pairs={{0,2},{2,0},{4,6},{6,4},{8,10},{10,8},{12,14},{14,12},{1,3},{3,1},... | collective-permute-start | bytes 491528 | tf_op jit(solution)/shard_map/ppermute | solution.py:320
  23.4 3.2 %collective-permute-done.5.refs_0_ = bf16[512,256]{1,0:T(8,128)(2,1)S(1)} collective-permute-done((bf16[512,256]{1,0:T(8,128)(2,1)S(1)}, bf16[512,256]{1,0:T(8,128)(2,1)S(1)}, u32[]{:S(2)}, u32[]{:S(2)}) %collective-permute-start.5) | collective-permute-done | bytes 262176 | tf_op jit(solution)/shard_map/ppermute | solution.py:315
  26.6 4.1 %collective-permute-start.9 = (bf16[512,256]{1,0:T(8,128)(2,1)S(1)}, bf16[512,256]{1,0:T(8,128)(2,1)}, u32[]{:S(2)}, u32[]{:S(2)}) collective-permute-start(bf16[512,256]{1,0:T(8,128)(2,1)S(1)} %constant_dynamic-slice_fusion.6.refs_0_), channel_id=1, source_target_pairs={{0,8},{2,10},{12,4},{14,6},{1,9},{3,11},{13,5},{15,7},{16,24},{18,... | collective-permute-start | bytes 786440 | tf_op jit(solution)/shard_map/ppermute | solution.py:315
  30.7 3.3 %collective-permute-done.7.refs_2_ = f32[40,512]{1,0:T(8,128)S(1)} collective-permute-done((f32[40,512]{1,0:T(8,128)S(1)}, f32[40,512]{1,0:T(8,128)S(1)}, u32[]{:S(2)}, u32[]{:S(2)}) %collective-permute-start.7) | collective-permute-done | bytes 81952 | tf_op jit(solution)/shard_map/ppermute | solution.py:321
  34.0 0.6 copy-done.5
  34.6 4.1 %collective-permute-start.10 = (bf16[512,256]{1,0:T(8,128)(2,1)S(1)}, bf16[512,256]{1,0:T(8,128)(2,1)}, u32[]{:S(2)}, u32[]{:S(2)}) collective-permute-start(bf16[512,256]{1,0:T(8,128)(2,1)S(1)} %constant_dynamic-slice_fusion.5.refs_1_), channel_id=1, source_target_pairs={{0,8},{2,10},{12,4},{14,6},{1,9},{3,11},{13,5},{15,7},{16,24},{18,... | collective-permute-start | bytes 786440 | tf_op jit(solution)/shard_map/ppermute | solution.py:317
  38.7 1.3 %collective-permute-start.11 = (f32[40,512]{1,0:T(8,128)S(1)}, f32[40,512]{1,0:T(8,128)S(1)}, u32[]{:S(2)}, u32[]{:S(2)}) collective-permute-start(f32[40,512]{1,0:T(8,128)S(1)} %constant_dynamic-slice_fusion.4.refs_2_), channel_id=1, source_target_pairs={{0,8},{2,10},{12,4},{14,6},{1,9},{3,11},{13,5},{15,7},{16,24},{18,... | collective-permute-start | bytes 245768 | tf_op jit(solution)/shard_map/ppermute | solution.py:321
  40.0 0.9 copy-done.6
  40.9 11.0 %tile.6 = (f32[40,512]{1,0:T(8,128)S(1)}, f32[40,2048]{1,0:T(8,128)S(1)}) custom-call(bf16[512,256]{1,0:T(8,128)(2,1)S(1)} %collective-permute-done.5.refs_0_, bf16[512,256]{1,0:T(8,128)(2,1)S(1)} %collective-permute-done.6.refs_1_, f32[40,512]{1,0:T(8,128)S(1)} %copy-done.6, bf16[1024,256]{1,0:T(8,128)(2,1)S(1)} %copy-done, ...), custom_call_target="tpu_custom_call" | custom-call | flops 1073741824 | bytes 2621440 | tf_op jit(solution)/shard_map/tile/pallas_call | solution.py:190
  52.0 1.1 %tile.7 = (f32[40,512]{1,0:T(8,128)S(1)}, f32[40,2048]{1,0:T(8,128)S(1)}) custom-call(bf16[512,256]{1,0:T(8,128)(2,1)} %collective-permute-done.9.refs_0_, bf16[512,256]{1,0:T(8,128)(2,1)} %collective-permute-done.10.refs_1_, f32[40,512]{1,0:T(8,128)S(1)} %collective-permute-done.11.refs_2_, bf16[1024,256]{1,0:T(8,128)(2,1)S(1)} %copy-done, ...), custom_call_target="tpu_custom_call" | custom-call | flops 1073741824 | bytes 2621440 | tf_op jit(solution)/shard_map/tile/pallas_call | solution.py:190
  53.0 1.3 %collective-permute-start.12 = (f32[40,512]{1,0:T(8,128)S(1)}, f32[40,512]{1,0:T(8,128)S(1)}, u32[]{:S(2)}, u32[]{:S(2)}) collective-permute-start(f32[40,512]{1,0:T(8,128)S(1)} %get-tuple-element.12), channel_id=1, source_target_pairs={{8,0},{10,2},{4,12},{6,14},{9,1},{11,3},{5,13},{7,15},{24,16},{26,... | collective-permute-start | bytes 245768 | tf_op jit(solution)/shard_map/ppermute | solution.py:334
  54.5 1.6 %collective-permute-start.14 = (f32[40,512]{1,0:T(8,128)S(1)}, f32[40,512]{1,0:T(8,128)S(1)}, u32[]{:S(2)}, u32[]{:S(2)}) collective-permute-start(f32[40,512]{1,0:T(8,128)S(1)} %get-tuple-element.18), channel_id=1, source_target_pairs={{0,2},{2,0},{4,6},{6,4},{8,10},{10,8},{12,14},{14,12},{1,3},{3,1},... | collective-permute-start | bytes 245768 | tf_op jit(solution)/shard_map/ppermute | solution.py:344
  56.1 0.3 collective-permute-start.15
  56.4 5.7 %tile.4.refs_0_ = f32[40,512]{1,0:T(8,128)S(1)} custom-call(bf16[512,256]{1,0:T(8,128)(2,1)S(1)} %constant_dynamic-slice_fusion.6.refs_0_, bf16[512,256]{1,0:T(8,128)(2,1)S(1)} %constant_dynamic-slice_fusion.5.refs_1_, f32[40,512]{1,0:T(8,128)S(1)} %constant_dynamic-slice_fusion.4.refs_2_, bf16[1024,256]{1,0:T(8,128)(2,1)S(1)} %copy-done, ...), custom_call_target="tpu_custom_call" | custom-call | flops 536870912 | bytes 1572864 | tf_op jit(solution)/shard_map/tile/pallas_call | solution.py:190
  62.1 5.5 %tile.5.refs_1_ = f32[40,512]{1,0:T(8,128)S(1)} custom-call(bf16[512,256]{1,0:T(8,128)(2,1)S(1)} %constant_dynamic-slice_fusion.6.refs_0_, bf16[512,256]{1,0:T(8,128)(2,1)S(1)} %constant_dynamic-slice_fusion.5.refs_1_, f32[40,512]{1,0:T(8,128)S(1)} %constant_dynamic-slice_fusion.4.refs_2_, bf16[1024,256]{1,0:T(8,128)(2,1)S(1)} %collective-permute-done.2.refs_3_.refs_6_, ...), custom_call_target="tpu_custom_call" | custom-call | flops 536870912 | bytes 1572864 | tf_op jit(solution)/shard_map/tile/pallas_call | solution.py:190
  67.6 2.8 %collective-permute-done.12.refs_3_ = f32[40,512]{1,0:T(8,128)S(1)} collective-permute-done((f32[40,512]{1,0:T(8,128)S(1)}, f32[40,512]{1,0:T(8,128)S(1)}, u32[]{:S(2)}, u32[]{:S(2)}) %collective-permute-start.12) | collective-permute-done | bytes 81952 | tf_op jit(solution)/shard_map/ppermute | solution.py:334
  70.4 0.6 image.1
  71.0 0.7 broadcast_in_dim.10
  71.7 13.3 %all-to-all-start = ((f32[16,8,128]{2,1,0:T(8,128)}), f32[16,8,128]{2,1,0:T(8,128)S(1)}, u32[]{:S(2)}, u32[]{:S(2)}) async-start(f32[16,8,128]{2,1,0:T(8,128)} %broadcast_in_dim.10), calls=%async_computation | async-start | bytes 131072 | tf_op jit(solution)/shard_map/all_to_all | solution.py:350
  85.0 0.4 collective-permute-start.16
  85.4 0.9 collective-permute-done.16.other_ref
  86.3 5.6 %all-to-all-done.grams_ref = f32[16,8,128]{2,1,0:T(8,128)S(1)} async-done(((f32[16,8,128]{2,1,0:T(8,128)}), f32[16,8,128]{2,1,0:T(8,128)S(1)}, u32[]{:S(2)}, u32[]{:S(2)}) %all-to-all-start) | async-done | bytes 65568 | tf_op jit(solution)/shard_map/all_to_all | solution.py:350
  91.9 3.5 %basis.1 = f32[16,1024]{1,0:T(8,128)} custom-call(f32[16,8,128]{2,1,0:T(8,128)S(1)} %all-to-all-done.grams_ref, f32[32,512]{1,0:T(8,128)S(1)} %get-tuple-element.16.mine_ref, f32[32,512]{1,0:T(8,128)S(1)} %collective-permute-done.16.other_ref), custom_call_target="tpu_custom_call" | custom-call | tf_op jit(solution)/shard_map/basis/pallas_call | solution.py:267
  (31 shorter events, 0.3 us)
Async XLA Ops:
  0.0 15.1 %collective-permute-start.2 = (bf16[1024,256]{1,0:T(8,128)(2,1)}, bf16[1024,256]{1,0:T(8,128)(2,1)S(1)}, u32[]{:S(2)}, u32[]{:S(2)}) collective-permute-start(bf16[1024,256]{1,0:T(8,128)(2,1)} %refs_3_.5), channel_id=1, source_target_pairs={{0,2},{2,0},{4,6},{6,4},{8,10},{10,8},{12,14},{14,12},{1,3},{3,1},... | collective-permute-start | bytes 1572872 | tf_op jit(solution)/shard_map/ppermute | solution.py:313
  3.0 17.0 %collective-permute-start = (bf16[1024,256]{1,0:T(8,128)(2,1)}, bf16[1024,256]{1,0:T(8,128)(2,1)S(1)}, u32[]{:S(2)}, u32[]{:S(2)}) collective-permute-start(bf16[1024,256]{1,0:T(8,128)(2,1)} %refs_3_.5), channel_id=1, source_target_pairs={{0,1},{1,0},{2,3},{3,2},{4,5},{5,4},{6,7},{7,6},{8,9},{9,8},{10,11... | collective-permute-start | bytes 1572872 | tf_op jit(solution)/shard_map/ppermute | solution.py:311
  3.0 17.5 %collective-permute-start.1 = (bf16[16,1024]{1,0:T(8,128)(2,1)}, bf16[16,1024]{1,0:T(8,128)(2,1)S(1)}, u32[]{:S(2)}, u32[]{:S(2)}) collective-permute-start(bf16[16,1024]{1,0:T(8,128)(2,1)} %vec_mine_ref.1), channel_id=1, source_target_pairs={{0,1},{1,0},{2,3},{3,2},{4,5},{5,4},{6,7},{7,6},{8,9},{9,8},{10,11... | collective-permute-start | bytes 98312 | tf_op jit(solution)/shard_map/ppermute | solution.py:312
  3.5 17.0 %copy-start = (bf16[1024,256]{1,0:T(8,128)(2,1)S(1)}, bf16[1024,256]{1,0:T(8,128)(2,1)}, u32[]{:S(2)}) copy-start(bf16[1024,256]{1,0:T(8,128)(2,1)} %refs_3_.5) | copy-start | bytes 1572868
  15.1 24.9 %collective-permute-start.3 = (bf16[1024,256]{1,0:T(8,128)(2,1)S(1)}, bf16[1024,256]{1,0:T(8,128)(2,1)S(1)}, u32[]{:S(2)}, u32[]{:S(2)}) collective-permute-start(bf16[1024,256]{1,0:T(8,128)(2,1)S(1)} %collective-permute-done.2.refs_3_.refs_6_), channel_id=1, source_target_pairs={{0,1},{1,0},{2,3},{3,2},{4,5},{5,4},{6,7},{7,6},{8,9},{9,8},{10,11... | collective-permute-start | bytes 1572872 | tf_op jit(solution)/shard_map/ppermute | solution.py:322
  16.1 4.5 %copy-start.1 = (bf16[16,1024]{1,0:T(8,128)(2,1)S(1)}, bf16[16,1024]{1,0:T(8,128)(2,1)}, u32[]{:S(2)}) copy-start(bf16[16,1024]{1,0:T(8,128)(2,1)} %vec_mine_ref.1) | copy-start | bytes 98308
  16.1 4.4 %copy-start.2 = (s32[4,1024]{1,0:T(4,128)S(1)}, s32[4,1024]{1,0:T(4,128)}, u32[]{:S(2)}) copy-start(s32[4,1024]{1,0:T(4,128)} %boxes_ref.1) | copy-start | bytes 49156
  16.1 4.4 %copy-start.3 = (s32[2,1024]{1,0:T(2,128)S(1)}, s32[2,1024]{1,0:T(2,128)}, u32[]{:S(2)}) copy-start(s32[2,1024]{1,0:T(2,128)} %spans_ref.1) | copy-start | bytes 24580
  16.1 10.5 %collective-permute-start.5 = (bf16[512,256]{1,0:T(8,128)(2,1)S(1)}, bf16[512,256]{1,0:T(8,128)(2,1)S(1)}, u32[]{:S(2)}, u32[]{:S(2)}) collective-permute-start(bf16[512,256]{1,0:T(8,128)(2,1)S(1)} %constant_dynamic-slice_fusion.6.refs_0_), channel_id=1, source_target_pairs={{4,0},{6,2},{8,4},{10,6},{12,8},{14,10},{0,12},{2,14},{5,1},{7,3},... | collective-permute-start | bytes 786440 | tf_op jit(solution)/shard_map/ppermute | solution.py:315
  20.0 0.7 copy-start.4
  20.0 20.0 %collective-permute-start.6 = (bf16[512,256]{1,0:T(8,128)(2,1)S(1)}, bf16[512,256]{1,0:T(8,128)(2,1)S(1)}, u32[]{:S(2)}, u32[]{:S(2)}) collective-permute-start(bf16[512,256]{1,0:T(8,128)(2,1)S(1)} %constant_dynamic-slice_fusion.5.refs_1_), channel_id=1, source_target_pairs={{4,0},{6,2},{8,4},{10,6},{12,8},{14,10},{0,12},{2,14},{5,1},{7,3},... | collective-permute-start | bytes 786440 | tf_op jit(solution)/shard_map/ppermute | solution.py:317
  21.4 12.6 %collective-permute-start.7 = (f32[40,512]{1,0:T(8,128)S(1)}, f32[40,512]{1,0:T(8,128)S(1)}, u32[]{:S(2)}, u32[]{:S(2)}) collective-permute-start(f32[40,512]{1,0:T(8,128)S(1)} %constant_dynamic-slice_fusion.4.refs_2_), channel_id=1, source_target_pairs={{4,0},{6,2},{8,4},{10,6},{12,8},{14,10},{0,12},{2,14},{5,1},{7,3},... | collective-permute-start | bytes 245768 | tf_op jit(solution)/shard_map/ppermute | solution.py:321
  21.9 16.8 %collective-permute-start.4 = (f32[40,1024]{1,0:T(8,128)S(1)}, f32[40,1024]{1,0:T(8,128)S(1)}, u32[]{:S(2)}, u32[]{:S(2)}) collective-permute-start(f32[40,1024]{1,0:T(8,128)S(1)} %prepare.1.refs_5_), channel_id=1, source_target_pairs={{0,2},{2,0},{4,6},{6,4},{8,10},{10,8},{12,14},{14,12},{1,3},{3,1},... | collective-permute-start | bytes 491528 | tf_op jit(solution)/shard_map/ppermute | solution.py:320
  26.6 25.3 %collective-permute-start.9 = (bf16[512,256]{1,0:T(8,128)(2,1)S(1)}, bf16[512,256]{1,0:T(8,128)(2,1)}, u32[]{:S(2)}, u32[]{:S(2)}) collective-permute-start(bf16[512,256]{1,0:T(8,128)(2,1)S(1)} %constant_dynamic-slice_fusion.6.refs_0_), channel_id=1, source_target_pairs={{0,8},{2,10},{12,4},{14,6},{1,9},{3,11},{13,5},{15,7},{16,24},{18,... | collective-permute-start | bytes 786440 | tf_op jit(solution)/shard_map/ppermute | solution.py:315
  34.0 0.6 copy-start.5
  34.6 17.4 %collective-permute-start.10 = (bf16[512,256]{1,0:T(8,128)(2,1)S(1)}, bf16[512,256]{1,0:T(8,128)(2,1)}, u32[]{:S(2)}, u32[]{:S(2)}) collective-permute-start(bf16[512,256]{1,0:T(8,128)(2,1)S(1)} %constant_dynamic-slice_fusion.5.refs_1_), channel_id=1, source_target_pairs={{0,8},{2,10},{12,4},{14,6},{1,9},{3,11},{13,5},{15,7},{16,24},{18,... | collective-permute-start | bytes 786440 | tf_op jit(solution)/shard_map/ppermute | solution.py:317
  38.7 13.3 %collective-permute-start.11 = (f32[40,512]{1,0:T(8,128)S(1)}, f32[40,512]{1,0:T(8,128)S(1)}, u32[]{:S(2)}, u32[]{:S(2)}) collective-permute-start(f32[40,512]{1,0:T(8,128)S(1)} %constant_dynamic-slice_fusion.4.refs_2_), channel_id=1, source_target_pairs={{0,8},{2,10},{12,4},{14,6},{1,9},{3,11},{13,5},{15,7},{16,24},{18,... | collective-permute-start | bytes 245768 | tf_op jit(solution)/shard_map/ppermute | solution.py:321
  40.0 0.9 copy-start.6
  51.9 15.7 %collective-permute-start.8 = (f32[40,512]{1,0:T(8,128)S(1)}, f32[40,512]{1,0:T(8,128)S(1)}, u32[]{:S(2)}, u32[]{:S(2)}) collective-permute-start(f32[40,512]{1,0:T(8,128)S(1)} %get-tuple-element.11), channel_id=1, source_target_pairs={{0,4},{2,6},{4,8},{6,10},{8,12},{10,14},{12,0},{14,2},{1,5},{3,7},... | collective-permute-start | bytes 245768 | tf_op jit(solution)/shard_map/ppermute | solution.py:334
  53.0 17.4 %collective-permute-start.12 = (f32[40,512]{1,0:T(8,128)S(1)}, f32[40,512]{1,0:T(8,128)S(1)}, u32[]{:S(2)}, u32[]{:S(2)}) collective-permute-start(f32[40,512]{1,0:T(8,128)S(1)} %get-tuple-element.12), channel_id=1, source_target_pairs={{8,0},{10,2},{4,12},{6,14},{9,1},{11,3},{5,13},{7,15},{24,16},{26,... | collective-permute-start | bytes 245768 | tf_op jit(solution)/shard_map/ppermute | solution.py:334
  54.4 16.0 %collective-permute-start.13 = (f32[40,512]{1,0:T(8,128)S(1)}, f32[40,512]{1,0:T(8,128)S(1)}, u32[]{:S(2)}, u32[]{:S(2)}) collective-permute-start(f32[40,512]{1,0:T(8,128)S(1)} %get-tuple-element.19), channel_id=1, source_target_pairs={{0,1},{1,0},{2,3},{3,2},{4,5},{5,4},{6,7},{7,6},{8,9},{9,8},{10,11... | collective-permute-start | bytes 245768 | tf_op jit(solution)/shard_map/ppermute | solution.py:343
  54.5 15.9 %collective-permute-start.14 = (f32[40,512]{1,0:T(8,128)S(1)}, f32[40,512]{1,0:T(8,128)S(1)}, u32[]{:S(2)}, u32[]{:S(2)}) collective-permute-start(f32[40,512]{1,0:T(8,128)S(1)} %get-tuple-element.18), channel_id=1, source_target_pairs={{0,2},{2,0},{4,6},{6,4},{8,10},{10,8},{12,14},{14,12},{1,3},{3,1},... | collective-permute-start | bytes 245768 | tf_op jit(solution)/shard_map/ppermute | solution.py:344
  56.1 14.3 %collective-permute-start.15 = (f32[40,512]{1,0:T(8,128)S(1)}, f32[40,512]{1,0:T(8,128)S(1)}, u32[]{:S(2)}, u32[]{:S(2)}) collective-permute-start(f32[40,512]{1,0:T(8,128)S(1)} %get-tuple-element.17), channel_id=1, source_target_pairs={{0,3},{1,2},{2,1},{3,0},{4,7},{5,6},{6,5},{7,4},{8,11},{9,10},{10,... | collective-permute-start | bytes 245768 | tf_op jit(solution)/shard_map/ppermute | solution.py:345
  71.7 20.2 %all-to-all-start = ((f32[16,8,128]{2,1,0:T(8,128)}), f32[16,8,128]{2,1,0:T(8,128)S(1)}, u32[]{:S(2)}, u32[]{:S(2)}) async-start(f32[16,8,128]{2,1,0:T(8,128)} %broadcast_in_dim.10), calls=%async_computation | async-start | bytes 131072 | tf_op jit(solution)/shard_map/all_to_all | solution.py:350
  85.0 1.3 %collective-permute-start.16 = (f32[32,512]{1,0:T(8,128)S(1)}, f32[32,512]{1,0:T(8,128)S(1)}, u32[]{:S(2)}, u32[]{:S(2)}) collective-permute-start(f32[32,512]{1,0:T(8,128)S(1)} %get-tuple-element.16.mine_ref), channel_id=1, source_target_pairs={{0,1},{1,0},{2,3},{3,2},{4,5},{5,4},{6,7},{7,6},{8,9},{9,8},{10,11... | collective-permute-start | bytes 196616 | tf_op jit(solution)/shard_map/ppermute | solution.py:348

commit v2 on v1

--- a/solution.py
+++ b/solution.py
@@ -23,7 +23,6 @@
 LEFT, RIGHT, BOTTOM, TOP, FIRST, LAST, CAMERA, NORM = range(FIELDS)
 LANES = 128
 CHUNK = 256
-GROUP = 32
 OUT_ROWS = 40
 VMEM_LIMIT = 48 * 1024 * 1024
 
@@ -97,64 +96,86 @@
     return jnp.where(barred, 0.0, value)
 
 
-def tile_kernel(blocks, own_block, receivers, *refs):
+def tile_kernel(blocks, own_rows, own_block, receivers, *refs):
     row_mine_ref, row_other_ref, row_packet_ref = refs[:3]
     col_refs = [refs[3 + 3 * number : 6 + 3 * number] for number in range(blocks)]
-    row_out_ref, col_out_ref, spread_ref, product_ref, weight_ref = refs[3 + 3 * blocks :]
-    rows = row_mine_ref.shape[0]
+    row_out_ref, col_out_ref, spread_ref = refs[3 + 3 * blocks : 6 + 3 * blocks]
+    products, weights = refs[6 + 3 * blocks : 8 + 3 * blocks], refs[8 + 3 * blocks :]
+    rows = row_out_ref.shape[1]
     vecs = row_packet_ref.shape[0] - FIELDS
+    sub = lax.axis_index("sub")
+    row_part, packet_part = pl.ds(0, rows), pl.ds(0, rows)
+    if own_rows:
+        row_part = packet_part = pl.ds(pl.multiple_of(sub * rows, rows), rows)
     row_out_ref[...] = jnp.zeros_like(row_out_ref)
 
     def with_ones(packet, count):
         tail = jnp.where(lax.broadcasted_iota(jnp.int32, (OUT_ROWS - vecs, count), 0) == 0, 1.0, 0.0)
         return jnp.concatenate([packet, tail], axis=0).astype(jnp.bfloat16)
 
+    def block(number, done, row_vecs):
+        col_mine_ref, col_other_ref, col_packet_ref = col_refs[number]
+        chunks = col_mine_ref.shape[0] // CHUNK
+
+        def place(step, base=0):
+            return pl.ds(pl.multiple_of(base + step * CHUNK, CHUNK), CHUNK)
+
+        def multiply(step, product_ref):
+            part = place(step)
+            columns = jnp.concatenate([col_mine_ref[part, :], col_other_ref[part, :]], axis=1)
+            lines = jnp.concatenate([row_mine_ref[row_part, :], row_other_ref[row_part, :]], axis=1)
+            product_ref[...] = dot_nt(lines, columns)
+
+        def weigh(step, product_ref, weight_ref):
+            col = [col_packet_ref[field : field + 1, place(step)] for field in range(FIELDS)]
+            col.append((col[RIGHT] - col[LEFT]) * (col[TOP] - col[BOTTOM]))
+            col = [jnp.broadcast_to(field, (8, CHUNK)) for field in col]
+            for first_row in range(0, rows, 16):
+                both = []
+                for line in (first_row, first_row + 8):
+                    row = [
+                        jnp.concatenate([spread_ref[field, line : line + 8, :]] * (CHUNK // LANES), axis=1)
+                        for field in range(FIELDS + 1)
+                    ]
+                    same = None
+                    if own_block:
+                        row_ids = lax.broadcasted_iota(jnp.int32, (8, CHUNK), 0) + (sub * rows + line - step * CHUNK)
+                        same = row_ids == lax.broadcasted_iota(jnp.int32, (8, CHUNK), 1)
+                    both.append(weights_of(product_ref[line : line + 8, :], row, col, same))
+                weight_ref[first_row : first_row + 16, :] = jnp.concatenate(both, axis=0).astype(jnp.bfloat16)
+
+        def total(step, weight_ref):
+            col_vecs = with_ones(col_packet_ref[FIELDS:, place(step)], CHUNK)
+            row_out_ref[...] += dot_nt(col_vecs, weight_ref[...])
+            if col_out_ref is not None:
+                col_out_ref[:, place(step, done)] = jnp.dot(
+                    row_vecs, weight_ref[...], preferred_element_type=jnp.float32
+                )
+
+        def steps(index, carry):
+            for parity in range(2):
+                step = 2 * index + parity
+                multiply(lax.rem(step + 1, chunks), products[1 - parity])
+                weigh(step, products[parity], weights[parity])
+                total(lax.rem(step + chunks - 1, chunks), weights[1 - parity])
+            return carry
+
+        multiply(0, products[0])
+        weights[1][...] = jnp.zeros_like(weights[1])
+        lax.fori_loop(0, chunks // 2, steps, 0)
+        total(chunks - 1, weights[1])
+
     def compute():
-        row_fields = row_packet_ref[0:FIELDS, :]
+        row_fields = row_packet_ref[0:FIELDS, packet_part]
         turned = jnp.concatenate([row_fields] * (LANES // FIELDS), axis=0).T
         for field in range(FIELDS):
             spread_ref[field] = jnp.broadcast_to(turned[:, field : field + 1], (rows, LANES))
         spread_ref[FIELDS] = (spread_ref[RIGHT] - spread_ref[LEFT]) * (spread_ref[TOP] - spread_ref[BOTTOM])
-        row_vecs = with_ones(row_packet_ref[FIELDS:, :], rows)
-        sub = lax.axis_index("sub")
+        row_vecs = with_ones(row_packet_ref[FIELDS:, packet_part], rows)
         done = 0
-        for number, (col_mine_ref, col_other_ref, col_packet_ref) in enumerate(col_refs):
-            cols = col_mine_ref.shape[0]
-
-            def chunk(step, carry, col_mine_ref=col_mine_ref, col_other_ref=col_other_ref, col_packet_ref=col_packet_ref, number=number, done=done):
-                start = pl.multiple_of(step * CHUNK, CHUNK)
-                part = pl.ds(start, CHUNK)
-                product_ref[...] = dot_nt(row_mine_ref[...], col_mine_ref[part, :]) + dot_nt(
-                    row_other_ref[...], col_other_ref[part, :]
-                )
-                col = [col_packet_ref[field : field + 1, part] for field in range(FIELDS)]
-                col.append((col[RIGHT] - col[LEFT]) * (col[TOP] - col[BOTTOM]))
-
-                def group(index, inner):
-                    first_row = pl.multiple_of(index * GROUP, GROUP)
-                    row_part = pl.ds(first_row, GROUP)
-                    row = [
-                        jnp.concatenate([spread_ref[field, row_part, :]] * (CHUNK // LANES), axis=1)
-                        for field in range(FIELDS + 1)
-                    ]
-                    same = None
-                    if own_block and number == 0:
-                        row_ids = lax.broadcasted_iota(jnp.int32, (GROUP, CHUNK), 0) + (sub * rows + first_row - start)
-                        same = row_ids == lax.broadcasted_iota(jnp.int32, (GROUP, CHUNK), 1)
-                    weight_ref[row_part, :] = weights_of(product_ref[row_part, :], row, col, same).astype(jnp.bfloat16)
-                    return inner
-
-                lax.fori_loop(0, rows // GROUP, group, 0, unroll=2)
-                col_vecs = with_ones(col_packet_ref[FIELDS:, part], CHUNK)
-                row_out_ref[...] += dot_nt(col_vecs, weight_ref[...])
-                if col_out_ref is not None:
-                    col_out_ref[:, pl.ds(pl.multiple_of(done + start, CHUNK), CHUNK)] = jnp.dot(
-                        row_vecs, weight_ref[...], preferred_element_type=jnp.float32
-                    )
-                return carry
-
-            lax.fori_loop(0, cols // CHUNK, chunk, 0)
-            done += cols
+        for number in range(blocks):
+            block(number, done, row_vecs)
+            done += col_refs[number][0].shape[0]
 
     if receivers is None:
         compute()
@@ -171,9 +192,8 @@
         col_out_ref[...] = jnp.zeros_like(col_out_ref)
 
 
-def tile(row, columns, own_block=False, col_sums=True, receivers=None):
-    row_mine, row_other, row_packet = row
-    rows, features = row_mine.shape
+def tile(row, columns, rows, own_rows=False, own_block=False, col_sums=True, receivers=None):
+    features = 2 * row[0].shape[1]
     cols = sum(part[0].shape[0] for part in columns)
     shapes = [jax.ShapeDtypeStruct((OUT_ROWS, rows), jnp.float32)]
     if col_sums:
@@ -184,7 +204,7 @@
         refs = list(refs)
         if not col_sums:
             refs.insert(inputs + 1, None)
-        tile_kernel(len(columns), own_block, receivers, *refs)
+        tile_kernel(len(columns), own_rows, own_block, receivers, *refs)
 
     pairs = rows * cols
     return pl.pallas_call(
@@ -195,6 +215,8 @@
         scratch_shapes=[
             pltpu.VMEM((FIELDS + 1, rows, LANES), jnp.float32),
             pltpu.VMEM((rows, CHUNK), jnp.float32),
+            pltpu.VMEM((rows, CHUNK), jnp.float32),
+            pltpu.VMEM((rows, CHUNK), jnp.bfloat16),
             pltpu.VMEM((rows, CHUNK), jnp.bfloat16),
         ],
         cost_estimate=pl.CostEstimate(
@@ -202,11 +224,11 @@
         ),
         compiler_params=params(),
         name="tile",
-    )(row_mine, row_other, row_packet, *[array for part in columns for array in part])
+    )(*row, *[array for part in columns for array in part])
 
 
 def image_kernel(*refs):
-    parts, image_ref, gram_ref = refs[:-2], refs[-2], refs[-1]
+    parts, image_ref, grams_ref = refs[:-2], refs[-2], refs[-1]
     total = parts[0][...]
     for part in parts[1:]:
         total = total + part[...]
@@ -221,16 +243,17 @@
         if piece < LANES // vecs - 1:
             shifted.append(jnp.zeros((LANES - (piece + 1) * vecs, image.shape[1]), jnp.float32))
         packed = packed + dot_nt(image[8 * piece : 8 * piece + 8], jnp.concatenate(shifted, axis=0), lax.Precision.HIGHEST)
-    gram_ref[...] = packed
-
-
-def image_of(parts, vecs):
+    for copy in range(grams_ref.shape[0]):
+        grams_ref[copy] = packed
+
+
+def image_of(parts, vecs, copies):
     cols = parts[0].shape[1]
     return pl.pallas_call(
         image_kernel,
         out_shape=[
             jax.ShapeDtypeStruct((vecs, cols), jnp.float32),
-            jax.ShapeDtypeStruct((8, LANES), jnp.float32),
+            jax.ShapeDtypeStruct((copies, 8, LANES), jnp.float32),
         ],
         in_specs=[VMEM_SPEC] * len(parts),
         out_specs=[VMEM_SPEC] * 2,
@@ -305,32 +328,35 @@
     beside = [(block, block ^ 1) for block in range(blocks)]
     plans = [(block_moves(moves), takers) for moves, takers in exchanges(blocks // 2)]
 
-    def half_rows(array):
-        return lax.dynamic_slice_in_dim(array, sub * half, half, 0)
+    def half_rows(place):
+        return lax.dynamic_slice_in_dim(embeddings, place * half, half, 0)
+
+    def crossed(moves):
+        return [(2 * source + 1 - core, 2 * target + core) for source, target in moves for core in range(2)]
 
     other = lax.ppermute(embeddings, "sub", swap)
     vec_other = lax.ppermute(vectors, "sub", swap)
+    to_same, to_cross = half_rows(sub), half_rows(1 - sub)
+    sent = [
+        (lax.ppermute(to_same, "blk", moves), lax.ppermute(to_cross, ("blk", "sub"), crossed(moves)))
+        for moves, _ in plans
+    ]
     beside_mine = lax.ppermute(embeddings, "blk", beside)
-    row_mine = half_rows(embeddings)
-    sent_mine = [lax.ppermute(row_mine, "blk", moves) for moves, _ in plans]
-    row_other = half_rows(other)
-    sent_other = [lax.ppermute(row_other, "blk", moves) for moves, _ in plans]
+    beside_other = lax.ppermute(embeddings, ("blk", "sub"), crossed(beside))
     packet = prepare(embeddings, other, vectors, vec_other, boxes, spans, camera)
     row_packet = lax.dynamic_slice_in_dim(packet, sub * half, half, 1)
     beside_packet = lax.ppermute(packet, "blk", beside)
     sent_packet = [lax.ppermute(row_packet, "blk", moves) for moves, _ in plans]
-    beside_other = lax.ppermute(beside_mine, "sub", swap)
-
-    own_row = (row_mine, row_other, row_packet)
-    own_cols = (embeddings, other, packet)
-    beside_cols = (beside_mine, beside_other, beside_packet)
+
+    own = (embeddings, other, packet)
+    next_to = (beside_mine, beside_other, beside_packet)
     parts = [
-        tile(own_row, [own_cols], own_block=True, col_sums=False)[0],
-        tile(own_row, [beside_cols], col_sums=False)[0],
+        tile(own, [own], half, own_rows=True, own_block=True, col_sums=False)[0],
+        tile(own, [next_to], half, own_rows=True, col_sums=False)[0],
     ]
     col_sums = None
-    for (moves, takers), mine, rest, meta in zip(plans, sent_mine, sent_other, sent_packet):
-        row_sums, sums = tile((mine, rest, meta), [own_cols, beside_cols], receivers=takers)
+    for (moves, takers), halves, meta in zip(plans, sent, sent_packet):
+        row_sums, sums = tile((*halves, meta), [own, next_to], half, receivers=takers)
         parts.append(lax.ppermute(row_sums, "blk", back(moves)))
         col_sums = sums if col_sums is None else col_sums + sums
 
@@ -338,15 +364,13 @@
         return lax.dynamic_slice_in_dim(col_sums, place * half, half, 1)
 
     if col_sums is not None:
-        crossed = [(2 * block + core, 2 * (block ^ 1) + 1 - core) for block in range(blocks) for core in range(2)]
         parts.append(piece(sub))
         parts.append(lax.ppermute(piece(1 - sub), "sub", swap))
         parts.append(lax.ppermute(piece(2 + sub), "blk", beside))
-        parts.append(lax.ppermute(piece(3 - sub), ("blk", "sub"), crossed))
-
-    image, gram = image_of(parts, vecs)
+        parts.append(lax.ppermute(piece(3 - sub), ("blk", "sub"), crossed(beside)))
+
+    image, copies = image_of(parts, vecs, devices)
     image_other = lax.ppermute(image, "sub", swap)
-    copies = jnp.broadcast_to(gram[None], (devices,) + gram.shape)
     grams = lax.all_to_all(copies, ("blk", "sub"), 0, 0, tiled=True)
     return basis_of(grams, image, image_other, blocks * rows)
 

time: 95.8 us -> 75.5 us (0.79)
  waiting for transfers between devices: 27.4 us -> 17.8 us
  Pallas kernels: 28.1 us -> 19.4 us
  local copies, waits for them, and re-layouts: 3.37 us -> 1.19 us
    ppermute x1, waiting for transfers between devices: 11.6 us -> 0.01 us  [local(): beside_mine = lax.ppermute(embeddings, 'blk', beside)]
    pallas_call x4, Pallas kernels: 23.3 us -> 13.9 us  [tile(): pl.pallas_call(body, out_shape=shapes, in_specs=[VMEM_SPEC] * (3 + 3 * le...]
    ppermute x2, starting transfers between devices: 1.32 us -> 9.65 us  [local(): parts.append(lax.ppermute(row_sums, 'blk', back(moves)))]
    all_to_all x1, starting transfers between devices: 13.3 us -> 5.52 us  [local(): grams = lax.all_to_all(copies, ('blk', 'sub'), 0, 0, tiled=True)]
    ppermute x2, starting transfers between devices: 1.79 us -> 6.25 us  [local(): sent_packet = [lax.ppermute(row_packet, 'blk', moves) for moves, _ in plans]]
    ppermute x6, starting transfers between devices: 12.8 us -> 8.43 us  [the longest x2 5.2 us: local(): lax.ppermute(to_cross, ('blk', 'sub'), crossed(moves))]
    ppermute x6, waiting for transfers between devices: 3.22 us -> 7.04 us  [the longest x2 4.27 us: local(): lax.ppermute(to_same, 'blk', moves)]
    ppermute x2, waiting for transfers between devices: 2.78 us -> 0.23 us  [local(): parts.append(lax.ppermute(row_sums, 'blk', back(moves)))]
  transfers between devices with their start and end apart: 18 -> 18, of which waited for: 6 -> 7; matrix products, arithmetic and copies ran while one was open for 1% -> 2% of each run, Pallas kernels for 25% -> 10%
where the time goes in v2:
time: 75.5 us; the launch traced here: 75.2 us
  starting transfers between devices  36.6 us (48%)
  Pallas kernels  19.4 us (26%)
  waiting for transfers between devices  17.8 us (24%)
  local copies, waits for them, and re-layouts  1.19 us (2%)
    pallas_call x4, Pallas kernels, tile(): pl.pallas_call(body, out_shape=shapes, in_specs=[VMEM_SPEC] * (3 + 3 * le...  13.9 us
    ppermute x2, starting transfers between devices, local(): parts.append(lax.ppermute(row_sums, 'blk', back(moves)))  9.65 us
    ppermute x2, starting transfers between devices, local(): sent_packet = [lax.ppermute(row_packet, 'blk', moves) for moves, _ in plans]  6.25 us
    all_to_all x1, waiting for transfers between devices, local(): grams = lax.all_to_all(copies, ('blk', 'sub'), 0, 0, tiled=True)  5.58 us
    all_to_all x1, starting transfers between devices, local(): grams = lax.all_to_all(copies, ('blk', 'sub'), 0, 0, tiled=True)  5.52 us
    ppermute x2, starting transfers between devices, local(): lax.ppermute(to_cross, ('blk', 'sub'), crossed(moves))  5.2 us
    ppermute x2, waiting for transfers between devices, local(): lax.ppermute(to_same, 'blk', moves)  4.27 us
    ppermute x2, waiting for transfers between devices, local(): sent_packet = [lax.ppermute(row_packet, 'blk', moves) for moves, _ in plans]  4.01 us
  transfers between devices with their start and end apart: 18, of which 7 were waited for; matrix products, arithmetic and copies ran while one was open for 2% of the time, Pallas kernels for 10%

profile of v2, /device:TPU:0, one launch (start us, length us, event | category | flops | bytes accessed | tf_op | source)
XLA Modules:
  0.0 75.2 jit_solution(804153731750807716)
XLA Ops:
  0.0 0.5 collective-permute-start
  0.5 2.5 %collective-permute-start.2 = (bf16[1024,256]{1,0:T(8,128)(2,1)}, bf16[1024,256]{1,0:T(8,128)(2,1)S(1)}, u32[]{:S(2)}, u32[]{:S(2)}) collective-permute-start(bf16[1024,256]{1,0:T(8,128)(2,1)} %refs_3_.5), channel_id=1, source_target_pairs={{0,2},{2,0},{4,6},{6,4},{8,10},{10,8},{12,14},{14,12},{1,3},{3,1},... | collective-permute-start | bytes 1572872 | tf_op jit(solution)/shard_map/ppermute | solution.py:344
  3.0 0.1 collective-permute-start.3
  3.1 0.1 collective-permute-start.1
  3.2 1.1 %constant_dynamic-slice_fusion.5 = (bf16[512,256]{1,0:T(8,128)(2,1)S(1)}, bf16[512,256]{1,0:T(8,128)(2,1)S(1)}) fusion(bf16[1024,256]{1,0:T(8,128)(2,1)} %refs_3_.5, s32[]{:T(128)S(6)} %select_n.20, s32[]{:T(128)S(6)} %select_n.19), kind=kLoop, calls=%fused_computation.5 | loop fusion | bytes 1048584 | tf_op jit(solution)/shard_map/dynamic_slice | solution.py:332
  4.4 4.7 %collective-permute-start.10 = (bf16[512,256]{1,0:T(8,128)(2,1)S(1)}, bf16[512,256]{1,0:T(8,128)(2,1)S(1)}, u32[]{:S(2)}, u32[]{:S(2)}) collective-permute-start(bf16[512,256]{1,0:T(8,128)(2,1)S(1)} %get-tuple-element.17), channel_id=1, source_target_pairs={{1,8},{0,9},{3,10},{2,11},{13,4},{12,5},{15,6},{14,7},{17,24},{16,... | collective-permute-start | bytes 786440 | tf_op jit(solution)/shard_map/ppermute | solution.py:341
  9.1 1.5 %collective-permute-start.9 = (bf16[512,256]{1,0:T(8,128)(2,1)S(1)}, bf16[512,256]{1,0:T(8,128)(2,1)S(1)}, u32[]{:S(2)}, u32[]{:S(2)}) collective-permute-start(bf16[512,256]{1,0:T(8,128)(2,1)S(1)} %get-tuple-element.18), channel_id=1, source_target_pairs={{0,8},{2,10},{12,4},{14,6},{1,9},{3,11},{13,5},{15,7},{16,24},{18,... | collective-permute-start | bytes 786440 | tf_op jit(solution)/shard_map/ppermute | solution.py:341
  10.6 0.7 prepare.1.refs_2_.refs_5_
  11.3 1.6 %collective-permute-start.4 = (f32[40,1024]{1,0:T(8,128)S(1)}, f32[40,1024]{1,0:T(8,128)S(1)}, u32[]{:S(2)}, u32[]{:S(2)}) collective-permute-start(f32[40,1024]{1,0:T(8,128)S(1)} %prepare.1.refs_2_.refs_5_), channel_id=1, source_target_pairs={{0,2},{2,0},{4,6},{6,4},{8,10},{10,8},{12,14},{14,12},{1,3},{3,1},... | collective-permute-start | bytes 491528 | tf_op jit(solution)/shard_map/ppermute | solution.py:348
  12.9 2.8 %collective-permute-done.10.refs_1_ = bf16[512,256]{1,0:T(8,128)(2,1)S(1)} collective-permute-done((bf16[512,256]{1,0:T(8,128)(2,1)S(1)}, bf16[512,256]{1,0:T(8,128)(2,1)S(1)}, u32[]{:S(2)}, u32[]{:S(2)}) %collective-permute-start.10) | collective-permute-done | bytes 262176 | tf_op jit(solution)/shard_map/ppermute | solution.py:341
  15.7 1.3 %collective-permute-start.5 = (bf16[512,256]{1,0:T(8,128)(2,1)S(1)}, bf16[512,256]{1,0:T(8,128)(2,1)S(1)}, u32[]{:S(2)}, u32[]{:S(2)}) collective-permute-start(bf16[512,256]{1,0:T(8,128)(2,1)S(1)} %get-tuple-element.18), channel_id=1, source_target_pairs={{4,0},{6,2},{8,4},{10,6},{12,8},{14,10},{0,12},{2,14},{5,1},{7,3},... | collective-permute-start | bytes 786440 | tf_op jit(solution)/shard_map/ppermute | solution.py:341
  17.0 4.3 %collective-permute-done.9.refs_0_ = bf16[512,256]{1,0:T(8,128)(2,1)S(1)} collective-permute-done((bf16[512,256]{1,0:T(8,128)(2,1)S(1)}, bf16[512,256]{1,0:T(8,128)(2,1)S(1)}, u32[]{:S(2)}, u32[]{:S(2)}) %collective-permute-start.9) | collective-permute-done | bytes 262176 | tf_op jit(solution)/shard_map/ppermute | solution.py:341
  21.3 0.5 collective-permute-start.6
  21.8 4.8 %collective-permute-start.11 = (f32[40,512]{1,0:T(8,128)S(1)}, f32[40,512]{1,0:T(8,128)S(1)}, u32[]{:S(2)}, u32[]{:S(2)}) collective-permute-start(f32[40,512]{1,0:T(8,128)S(1)} %constant_dynamic-slice_fusion.4), channel_id=1, source_target_pairs={{0,8},{2,10},{12,4},{14,6},{1,9},{3,11},{13,5},{15,7},{16,24},{18,... | collective-permute-start | bytes 245768 | tf_op jit(solution)/shard_map/ppermute | solution.py:349
  26.6 3.6 %tile.4.refs_0_ = f32[40,512]{1,0:T(8,128)S(1)} custom-call(bf16[1024,256]{1,0:T(8,128)(2,1)S(1)} %copy-done, bf16[1024,256]{1,0:T(8,128)(2,1)S(1)} %collective-permute-done.other_ref.refs_1_.refs_4_, f32[40,1024]{1,0:T(8,128)S(1)} %prepare.1.refs_2_.refs_5_, bf16[1024,256]{1,0:T(8,128)(2,1)S(1)} %copy-done, ...), custom_call_target="tpu_custom_call" | custom-call | flops 1073741824 | bytes 3145728 | tf_op jit(solution)/shard_map/tile/pallas_call | solution.py:210
  30.2 1.4 %collective-permute-start.7 = (f32[40,512]{1,0:T(8,128)S(1)}, f32[40,512]{1,0:T(8,128)S(1)}, u32[]{:S(2)}, u32[]{:S(2)}) collective-permute-start(f32[40,512]{1,0:T(8,128)S(1)} %constant_dynamic-slice_fusion.4), channel_id=1, source_target_pairs={{4,0},{6,2},{8,4},{10,6},{12,8},{14,10},{0,12},{2,14},{5,1},{7,3},... | collective-permute-start | bytes 245768 | tf_op jit(solution)/shard_map/ppermute | solution.py:349
  31.6 2.6 %collective-permute-done.11.refs_2_ = f32[40,512]{1,0:T(8,128)S(1)} collective-permute-done((f32[40,512]{1,0:T(8,128)S(1)}, f32[40,512]{1,0:T(8,128)S(1)}, u32[]{:S(2)}, u32[]{:S(2)}) %collective-permute-start.11) | collective-permute-done | bytes 81952 | tf_op jit(solution)/shard_map/ppermute | solution.py:349
  34.4 1.4 %collective-permute-done.7.refs_2_ = f32[40,512]{1,0:T(8,128)S(1)} collective-permute-done((f32[40,512]{1,0:T(8,128)S(1)}, f32[40,512]{1,0:T(8,128)S(1)}, u32[]{:S(2)}, u32[]{:S(2)}) %collective-permute-start.7) | collective-permute-done | bytes 81952 | tf_op jit(solution)/shard_map/ppermute | solution.py:349
  35.7 7.0 %tile.6 = (f32[40,512]{1,0:T(8,128)S(1)}, f32[40,2048]{1,0:T(8,128)S(1)}) custom-call(bf16[512,256]{1,0:T(8,128)(2,1)S(1)} %collective-permute-done.5.refs_0_, bf16[512,256]{1,0:T(8,128)(2,1)S(1)} %collective-permute-done.6.refs_1_, f32[40,512]{1,0:T(8,128)S(1)} %collective-permute-done.7.refs_2_, bf16[1024,256]{1,0:T(8,128)(2,1)S(1)} %copy-done, ...), custom_call_target="tpu_custom_call" | custom-call | flops 2147483648 | bytes 5242880 | tf_op jit(solution)/shard_map/tile/pallas_call | solution.py:210
  42.8 0.1 collective-permute-start.13
  42.9 1.6 %collective-permute-start.14 = (f32[40,512]{1,0:T(8,128)S(1)}, f32[40,512]{1,0:T(8,128)S(1)}, u32[]{:S(2)}, u32[]{:S(2)}) collective-permute-start(f32[40,512]{1,0:T(8,128)S(1)} %get-tuple-element.20), channel_id=1, source_target_pairs={{0,2},{2,0},{4,6},{6,4},{8,10},{10,8},{12,14},{14,12},{1,3},{3,1},... | collective-permute-start | bytes 245768 | tf_op jit(solution)/shard_map/ppermute | solution.py:369
  44.4 0.3 collective-permute-start.15
  44.7 1.3 %collective-permute-start.12 = (f32[40,512]{1,0:T(8,128)S(1)}, f32[40,512]{1,0:T(8,128)S(1)}, u32[]{:S(2)}, u32[]{:S(2)}) collective-permute-start(f32[40,512]{1,0:T(8,128)S(1)} %get-tuple-element.12), channel_id=1, source_target_pairs={{8,0},{10,2},{4,12},{6,14},{9,1},{11,3},{5,13},{7,15},{24,16},{26,... | collective-permute-start | bytes 245768 | tf_op jit(solution)/shard_map/ppermute | solution.py:360
  46.0 8.4 %collective-permute-start.8 = (f32[40,512]{1,0:T(8,128)S(1)}, f32[40,512]{1,0:T(8,128)S(1)}, u32[]{:S(2)}, u32[]{:S(2)}) collective-permute-start(f32[40,512]{1,0:T(8,128)S(1)} %get-tuple-element.11), channel_id=1, source_target_pairs={{0,4},{2,6},{4,8},{6,10},{8,12},{10,14},{12,0},{14,2},{1,5},{3,7},... | collective-permute-start | bytes 245768 | tf_op jit(solution)/shard_map/ppermute | solution.py:360
  54.4 3.4 %tile.5.refs_1_ = f32[40,512]{1,0:T(8,128)S(1)} custom-call(bf16[1024,256]{1,0:T(8,128)(2,1)S(1)} %copy-done, bf16[1024,256]{1,0:T(8,128)(2,1)S(1)} %collective-permute-done.other_ref.refs_1_.refs_4_, f32[40,1024]{1,0:T(8,128)S(1)} %prepare.1.refs_2_.refs_5_, bf16[1024,256]{1,0:T(8,128)(2,1)S(1)} %collective-permute-done.2.refs_3_.refs_6_, ...), custom_call_target="tpu_custom_call" | custom-call | flops 1073741824 | bytes 3145728 | tf_op jit(solution)/shard_map/tile/pallas_call | solution.py:210
  57.8 0.2 collective-permute-done.12.refs_3_
  58.0 1.3 %image.1 = (f32[32,512]{1,0:T(8,128)S(1)}, f32[16,8,128]{2,1,0:T(8,128)}) custom-call(f32[40,512]{1,0:T(8,128)S(1)} %tile.4.refs_0_, f32[40,512]{1,0:T(8,128)S(1)} %tile.5.refs_1_, f32[40,512]{1,0:T(8,128)S(1)} %collective-permute-done.8.refs_2_, f32[40,512]{1,0:T(8,128)S(1)} %collective-permute-done.12.refs_3_, f32[40,512]{1,0:T(8,128)S(1)} %get-tuple-element.22.refs_4_, ...), custom_call_target="tpu_custom_call" | custom-call | tf_op jit(solution)/shard_map/image/pallas_call | solution.py:252
  59.3 5.5 %all-to-all-start = ((f32[16,8,128]{2,1,0:T(8,128)}), f32[16,8,128]{2,1,0:T(8,128)S(1)}, u32[]{:S(2)}, u32[]{:S(2)}) async-start(f32[16,8,128]{2,1,0:T(8,128)} %get-tuple-element.15), calls=%async_computation | async-start | bytes 131072 | tf_op jit(solution)/shard_map/all_to_all | solution.py:374
  64.8 0.4 collective-permute-start.16
  65.2 0.9 %collective-permute-done.16.other_ref = f32[32,512]{1,0:T(8,128)S(1)} collective-permute-done((f32[32,512]{1,0:T(8,128)S(1)}, f32[32,512]{1,0:T(8,128)S(1)}, u32[]{:S(2)}, u32[]{:S(2)}) %collective-permute-start.16) | collective-permute-done | bytes 65568 | tf_op jit(solution)/shard_map/ppermute | solution.py:373
  66.1 5.6 %all-to-all-done.grams_ref = f32[16,8,128]{2,1,0:T(8,128)S(1)} async-done(((f32[16,8,128]{2,1,0:T(8,128)}), f32[16,8,128]{2,1,0:T(8,128)S(1)}, u32[]{:S(2)}, u32[]{:S(2)}) %all-to-all-start) | async-done | bytes 65568 | tf_op jit(solution)/shard_map/all_to_all | solution.py:374
  71.7 3.5 %basis.1 = f32[16,1024]{1,0:T(8,128)} custom-call(f32[16,8,128]{2,1,0:T(8,128)S(1)} %all-to-all-done.grams_ref, f32[32,512]{1,0:T(8,128)S(1)} %get-tuple-element.16.mine_ref, f32[32,512]{1,0:T(8,128)S(1)} %collective-permute-done.16.other_ref), custom_call_target="tpu_custom_call" | custom-call | tf_op jit(solution)/shard_map/basis/pallas_call | solution.py:290
  (25 shorter events, 0.2 us)
Async XLA Ops:
  0.0 10.6 %collective-permute-start = (bf16[1024,256]{1,0:T(8,128)(2,1)}, bf16[1024,256]{1,0:T(8,128)(2,1)S(1)}, u32[]{:S(2)}, u32[]{:S(2)}) collective-permute-start(bf16[1024,256]{1,0:T(8,128)(2,1)} %refs_3_.5), channel_id=1, source_target_pairs={{0,1},{1,0},{2,3},{3,2},{4,5},{5,4},{6,7},{7,6},{8,9},{9,8},{10,11... | collective-permute-start | bytes 1572872 | tf_op jit(solution)/shard_map/ppermute | solution.py:337
  0.5 21.3 %collective-permute-start.2 = (bf16[1024,256]{1,0:T(8,128)(2,1)}, bf16[1024,256]{1,0:T(8,128)(2,1)S(1)}, u32[]{:S(2)}, u32[]{:S(2)}) collective-permute-start(bf16[1024,256]{1,0:T(8,128)(2,1)} %refs_3_.5), channel_id=1, source_target_pairs={{0,2},{2,0},{4,6},{6,4},{8,10},{10,8},{12,14},{14,12},{1,3},{3,1},... | collective-permute-start | bytes 1572872 | tf_op jit(solution)/shard_map/ppermute | solution.py:344
  3.0 27.2 %collective-permute-start.3 = (bf16[1024,256]{1,0:T(8,128)(2,1)}, bf16[1024,256]{1,0:T(8,128)(2,1)S(1)}, u32[]{:S(2)}, u32[]{:S(2)}) collective-permute-start(bf16[1024,256]{1,0:T(8,128)(2,1)} %refs_3_.5), channel_id=1, source_target_pairs={{1,2},{0,3},{3,0},{2,1},{5,6},{4,7},{7,4},{6,5},{9,10},{8,11},{11,... | collective-permute-start | bytes 1572872 | tf_op jit(solution)/shard_map/ppermute | solution.py:345
  3.1 6.0 %collective-permute-start.1 = (bf16[16,1024]{1,0:T(8,128)(2,1)}, bf16[16,1024]{1,0:T(8,128)(2,1)S(1)}, u32[]{:S(2)}, u32[]{:S(2)}) collective-permute-start(bf16[16,1024]{1,0:T(8,128)(2,1)} %vec_mine_ref.1), channel_id=1, source_target_pairs={{0,1},{1,0},{2,3},{3,2},{4,5},{5,4},{6,7},{7,6},{8,9},{9,8},{10,11... | collective-permute-start | bytes 98312 | tf_op jit(solution)/shard_map/ppermute | solution.py:338
  3.2 7.4 %copy-start = (bf16[1024,256]{1,0:T(8,128)(2,1)S(1)}, bf16[1024,256]{1,0:T(8,128)(2,1)}, u32[]{:S(2)}) copy-start(bf16[1024,256]{1,0:T(8,128)(2,1)} %refs_3_.5) | copy-start | bytes 1572868
  3.2 7.4 %copy-start.2 = (s32[4,1024]{1,0:T(4,128)S(1)}, s32[4,1024]{1,0:T(4,128)}, u32[]{:S(2)}) copy-start(s32[4,1024]{1,0:T(4,128)} %boxes_ref.1) | copy-start | bytes 49156
  3.2 7.4 %copy-start.3 = (s32[2,1024]{1,0:T(2,128)S(1)}, s32[2,1024]{1,0:T(2,128)}, u32[]{:S(2)}) copy-start(s32[2,1024]{1,0:T(2,128)} %spans_ref.1) | copy-start | bytes 24580
  3.2 7.4 %copy-start.4 = (s32[1024]{0:T(1024)S(1)}, s32[1024]{0:T(1024)}, u32[]{:S(2)}) copy-start(s32[1024]{0:T(1024)} %param.9) | copy-start | bytes 12292
  4.3 6.3 %copy-start.1 = (bf16[16,1024]{1,0:T(8,128)(2,1)S(1)}, bf16[16,1024]{1,0:T(8,128)(2,1)}, u32[]{:S(2)}) copy-start(bf16[16,1024]{1,0:T(8,128)(2,1)} %vec_mine_ref.1) | copy-start | bytes 98308
  4.4 11.3 %collective-permute-start.10 = (bf16[512,256]{1,0:T(8,128)(2,1)S(1)}, bf16[512,256]{1,0:T(8,128)(2,1)S(1)}, u32[]{:S(2)}, u32[]{:S(2)}) collective-permute-start(bf16[512,256]{1,0:T(8,128)(2,1)S(1)} %get-tuple-element.17), channel_id=1, source_target_pairs={{1,8},{0,9},{3,10},{2,11},{13,4},{12,5},{15,6},{14,7},{17,24},{16,... | collective-permute-start | bytes 786440 | tf_op jit(solution)/shard_map/ppermute | solution.py:341
  9.1 12.2 %collective-permute-start.9 = (bf16[512,256]{1,0:T(8,128)(2,1)S(1)}, bf16[512,256]{1,0:T(8,128)(2,1)S(1)}, u32[]{:S(2)}, u32[]{:S(2)}) collective-permute-start(bf16[512,256]{1,0:T(8,128)(2,1)S(1)} %get-tuple-element.18), channel_id=1, source_target_pairs={{0,8},{2,10},{12,4},{14,6},{1,9},{3,11},{13,5},{15,7},{16,24},{18,... | collective-permute-start | bytes 786440 | tf_op jit(solution)/shard_map/ppermute | solution.py:341
  11.3 23.0 %collective-permute-start.4 = (f32[40,1024]{1,0:T(8,128)S(1)}, f32[40,1024]{1,0:T(8,128)S(1)}, u32[]{:S(2)}, u32[]{:S(2)}) collective-permute-start(f32[40,1024]{1,0:T(8,128)S(1)} %prepare.1.refs_2_.refs_5_), channel_id=1, source_target_pairs={{0,2},{2,0},{4,6},{6,4},{8,10},{10,8},{12,14},{14,12},{1,3},{3,1},... | collective-permute-start | bytes 491528 | tf_op jit(solution)/shard_map/ppermute | solution.py:348
  15.7 18.7 %collective-permute-start.5 = (bf16[512,256]{1,0:T(8,128)(2,1)S(1)}, bf16[512,256]{1,0:T(8,128)(2,1)S(1)}, u32[]{:S(2)}, u32[]{:S(2)}) collective-permute-start(bf16[512,256]{1,0:T(8,128)(2,1)S(1)} %get-tuple-element.18), channel_id=1, source_target_pairs={{4,0},{6,2},{8,4},{10,6},{12,8},{14,10},{0,12},{2,14},{5,1},{7,3},... | collective-permute-start | bytes 786440 | tf_op jit(solution)/shard_map/ppermute | solution.py:341
  21.3 13.1 %collective-permute-start.6 = (bf16[512,256]{1,0:T(8,128)(2,1)S(1)}, bf16[512,256]{1,0:T(8,128)(2,1)S(1)}, u32[]{:S(2)}, u32[]{:S(2)}) collective-permute-start(bf16[512,256]{1,0:T(8,128)(2,1)S(1)} %get-tuple-element.17), channel_id=1, source_target_pairs={{5,0},{4,1},{7,2},{6,3},{9,4},{8,5},{11,6},{10,7},{13,8},{12,9},{1... | collective-permute-start | bytes 786440 | tf_op jit(solution)/shard_map/ppermute | solution.py:341
  21.8 12.5 %collective-permute-start.11 = (f32[40,512]{1,0:T(8,128)S(1)}, f32[40,512]{1,0:T(8,128)S(1)}, u32[]{:S(2)}, u32[]{:S(2)}) collective-permute-start(f32[40,512]{1,0:T(8,128)S(1)} %constant_dynamic-slice_fusion.4), channel_id=1, source_target_pairs={{0,8},{2,10},{12,4},{14,6},{1,9},{3,11},{13,5},{15,7},{16,24},{18,... | collective-permute-start | bytes 245768 | tf_op jit(solution)/shard_map/ppermute | solution.py:349
  30.2 5.5 %collective-permute-start.7 = (f32[40,512]{1,0:T(8,128)S(1)}, f32[40,512]{1,0:T(8,128)S(1)}, u32[]{:S(2)}, u32[]{:S(2)}) collective-permute-start(f32[40,512]{1,0:T(8,128)S(1)} %constant_dynamic-slice_fusion.4), channel_id=1, source_target_pairs={{4,0},{6,2},{8,4},{10,6},{12,8},{14,10},{0,12},{2,14},{5,1},{7,3},... | collective-permute-start | bytes 245768 | tf_op jit(solution)/shard_map/ppermute | solution.py:349
  42.8 15.0 %collective-permute-start.13 = (f32[40,512]{1,0:T(8,128)S(1)}, f32[40,512]{1,0:T(8,128)S(1)}, u32[]{:S(2)}, u32[]{:S(2)}) collective-permute-start(f32[40,512]{1,0:T(8,128)S(1)} %get-tuple-element.21), channel_id=1, source_target_pairs={{0,1},{1,0},{2,3},{3,2},{4,5},{5,4},{6,7},{7,6},{8,9},{9,8},{10,11... | collective-permute-start | bytes 245768 | tf_op jit(solution)/shard_map/ppermute | solution.py:368
  42.9 14.9 %collective-permute-start.14 = (f32[40,512]{1,0:T(8,128)S(1)}, f32[40,512]{1,0:T(8,128)S(1)}, u32[]{:S(2)}, u32[]{:S(2)}) collective-permute-start(f32[40,512]{1,0:T(8,128)S(1)} %get-tuple-element.20), channel_id=1, source_target_pairs={{0,2},{2,0},{4,6},{6,4},{8,10},{10,8},{12,14},{14,12},{1,3},{3,1},... | collective-permute-start | bytes 245768 | tf_op jit(solution)/shard_map/ppermute | solution.py:369
  44.4 13.3 %collective-permute-start.15 = (f32[40,512]{1,0:T(8,128)S(1)}, f32[40,512]{1,0:T(8,128)S(1)}, u32[]{:S(2)}, u32[]{:S(2)}) collective-permute-start(f32[40,512]{1,0:T(8,128)S(1)} %get-tuple-element.19), channel_id=1, source_target_pairs={{1,2},{0,3},{3,0},{2,1},{5,6},{4,7},{7,4},{6,5},{9,10},{8,11},{11,... | collective-permute-start | bytes 245768 | tf_op jit(solution)/shard_map/ppermute | solution.py:370
  44.7 13.3 %collective-permute-start.12 = (f32[40,512]{1,0:T(8,128)S(1)}, f32[40,512]{1,0:T(8,128)S(1)}, u32[]{:S(2)}, u32[]{:S(2)}) collective-permute-start(f32[40,512]{1,0:T(8,128)S(1)} %get-tuple-element.12), channel_id=1, source_target_pairs={{8,0},{10,2},{4,12},{6,14},{9,1},{11,3},{5,13},{7,15},{24,16},{26,... | collective-permute-start | bytes 245768 | tf_op jit(solution)/shard_map/ppermute | solution.py:360
  46.0 12.0 %collective-permute-start.8 = (f32[40,512]{1,0:T(8,128)S(1)}, f32[40,512]{1,0:T(8,128)S(1)}, u32[]{:S(2)}, u32[]{:S(2)}) collective-permute-start(f32[40,512]{1,0:T(8,128)S(1)} %get-tuple-element.11), channel_id=1, source_target_pairs={{0,4},{2,6},{4,8},{6,10},{8,12},{10,14},{12,0},{14,2},{1,5},{3,7},... | collective-permute-start | bytes 245768 | tf_op jit(solution)/shard_map/ppermute | solution.py:360
  59.3 12.4 %all-to-all-start = ((f32[16,8,128]{2,1,0:T(8,128)}), f32[16,8,128]{2,1,0:T(8,128)S(1)}, u32[]{:S(2)}, u32[]{:S(2)}) async-start(f32[16,8,128]{2,1,0:T(8,128)} %get-tuple-element.15), calls=%async_computation | async-start | bytes 131072 | tf_op jit(solution)/shard_map/all_to_all | solution.py:374
  64.8 1.3 %collective-permute-start.16 = (f32[32,512]{1,0:T(8,128)S(1)}, f32[32,512]{1,0:T(8,128)S(1)}, u32[]{:S(2)}, u32[]{:S(2)}) collective-permute-start(f32[32,512]{1,0:T(8,128)S(1)} %get-tuple-element.16.mine_ref), channel_id=1, source_target_pairs={{0,1},{1,0},{2,3},{3,2},{4,5},{5,4},{6,7},{7,6},{8,9},{9,8},{10,11... | collective-permute-start | bytes 196616 | tf_op jit(solution)/shard_map/ppermute | solution.py:373

commit v3 on v2

--- a/solution.py
+++ b/solution.py
@@ -19,8 +19,9 @@
 BASE = SHARPNESS * LOG2E + 1.0
 BARRED_BELOW = BASE - 0.5 * GAP_SCALE
 
-FIELDS = 8
-LEFT, RIGHT, BOTTOM, TOP, FIRST, LAST, CAMERA, NORM = range(FIELDS)
+FIELDS = 9
+LEFT, RIGHT, BOTTOM, TOP, FIRST, LAST, CAMERA, NORM, AREA = range(FIELDS)
+CODE_ROWS = 16
 LANES = 128
 CHUNK = 256
 OUT_ROWS = 40
@@ -38,47 +39,100 @@
     return lax.dot_general(a, b, NT, precision=precision, preferred_element_type=jnp.float32)
 
 
-def prepare_kernel(mine_ref, other_ref, vec_mine_ref, vec_other_ref, boxes_ref, spans_ref, camera_ref, out_ref):
+def pack_rows(rows, half_vecs):
+    return rows + rows // CHUNK * (half_vecs + CODE_ROWS)
+
+
+def vec_place(total, half_vecs, chunk):
+    return pl.ds(pl.multiple_of(total + chunk * half_vecs, 16), half_vecs)
+
+
+def code_place(total, half_vecs, chunk):
+    return pl.ds(pl.multiple_of(total + total // CHUNK * half_vecs + chunk * CODE_ROWS, 16), CODE_ROWS)
+
+
+def pack_kernel(emb_ref, vec_ref, boxes_ref, spans_ref, camera_ref, full_ref, same_ref, cross_ref):
     sub = lax.axis_index("sub")
-    rows = mine_ref.shape[0]
-    half_vecs = vec_mine_ref.shape[0]
-    ones = jnp.ones((FIELDS, mine_ref.shape[1]), jnp.bfloat16)
-    for start in range(0, rows, CHUNK):
-        part = pl.ds(start, CHUNK)
-        total = jnp.zeros((FIELDS, CHUNK), jnp.float32)
-        for ref in (mine_ref, other_ref):
-            values = ref[part, :].astype(jnp.float32)
-            square = values * values
-            high = square.astype(jnp.bfloat16)
-            low = (square - high.astype(jnp.float32)).astype(jnp.bfloat16)
-            total = total + dot_nt(ones, high) + dot_nt(ones, low)
-        out_ref[NORM : NORM + 1, part] = (lax.rsqrt(total + EPSILON) * COS_SCALE)[0:1]
-    corner_x, corner_y = boxes_ref[0:1, :], boxes_ref[1:2, :]
-    other_x, other_y = boxes_ref[2:3, :], boxes_ref[3:4, :]
-    begin, end = spans_ref[0:1, :], spans_ref[1:2, :]
-    out_ref[LEFT : LEFT + 1, :] = jnp.minimum(corner_x, other_x).astype(jnp.float32)
-    out_ref[RIGHT : RIGHT + 1, :] = jnp.maximum(corner_x, other_x).astype(jnp.float32) + MARGIN
-    out_ref[BOTTOM : BOTTOM + 1, :] = jnp.minimum(corner_y, other_y).astype(jnp.float32)
-    out_ref[TOP : TOP + 1, :] = jnp.maximum(corner_y, other_y).astype(jnp.float32) + MARGIN
-    out_ref[FIRST : FIRST + 1, :] = jnp.minimum(begin, end).astype(jnp.float32) * GAP_SCALE + BASE
-    out_ref[LAST : LAST + 1, :] = jnp.maximum(begin, end).astype(jnp.float32) * GAP_SCALE
-    out_ref[CAMERA : CAMERA + 1, :] = camera_ref[...].astype(jnp.float32)
-    own_place = pl.multiple_of(FIELDS + sub * half_vecs, 8)
-    other_place = pl.multiple_of(FIELDS + (1 - sub) * half_vecs, 8)
-    out_ref[pl.ds(own_place, half_vecs), :] = vec_mine_ref[...].astype(jnp.float32)
-    out_ref[pl.ds(other_place, half_vecs), :] = vec_other_ref[...].astype(jnp.float32)
-
-
-def prepare(mine, other, vec_mine, vec_other, boxes, spans, camera):
-    rows = mine.shape[0]
+    rows = emb_ref.shape[0]
+    half = same_ref.shape[0] * rows // full_ref.shape[0]
+    half_vecs = vec_ref.shape[0]
+    full_ref[0:rows, :] = emb_ref[...]
+    same_ref[0:half, :] = emb_ref[pl.ds(pl.multiple_of(sub * half, half), half), :]
+    cross_ref[0:half, :] = emb_ref[pl.ds(pl.multiple_of((1 - sub) * half, half), half), :]
+    ones = jnp.ones((8, CHUNK), jnp.bfloat16)
+    for chunk in range(rows // CHUNK):
+        part = pl.ds(chunk * CHUNK, CHUNK)
+        codes = []
+
+        def whole(number, low_bits):
+            codes.append((number >> low_bits) << low_bits)
+            codes.append(number & ((1 << low_bits) - 1))
+
+        boxes, spans = boxes_ref[:, part], spans_ref[:, part]
+        for axis in range(2):
+            whole(jnp.minimum(boxes[axis : axis + 1], boxes[axis + 2 : axis + 3]), 5)
+            whole(jnp.maximum(boxes[axis : axis + 1], boxes[axis + 2 : axis + 3]), 5)
+        whole(jnp.minimum(spans[0:1], spans[1:2]), 7)
+        whole(jnp.maximum(spans[0:1], spans[1:2]), 7)
+        codes.append(camera_ref[:, part])
+        codes = [code.astype(jnp.float32) for code in codes]
+        values = emb_ref[part, :].astype(jnp.float32)
+        square = values * values
+        high = square.astype(jnp.bfloat16)
+        low = (square - high.astype(jnp.float32)).astype(jnp.bfloat16)
+        rest = (dot_nt(ones, high) + dot_nt(ones, low))[0:1]
+        for _ in range(3):
+            piece = rest.astype(jnp.bfloat16).astype(jnp.float32)
+            codes.append(piece)
+            rest = rest - piece
+        coded = jnp.concatenate(codes, axis=0).astype(jnp.bfloat16)
+        vecs = vec_ref[:, part]
+        full_ref[vec_place(rows, half_vecs, chunk), :] = vecs
+        full_ref[code_place(rows, half_vecs, chunk), :] = coded
+        in_half = chunk % (half // CHUNK)
+        first_half = chunk < half // CHUNK
+
+        def put(ref):
+            ref[vec_place(half, half_vecs, in_half), :] = vecs
+            ref[code_place(half, half_vecs, in_half), :] = coded
+
+        pl.when((sub == 0) == first_half)(functools.partial(put, same_ref))
+        pl.when((sub == 0) != first_half)(functools.partial(put, cross_ref))
+
+
+def packs_of(embeddings, vectors, boxes, spans, camera):
+    rows, width = embeddings.shape
+    half_vecs = vectors.shape[0]
+    sizes = [pack_rows(rows, half_vecs)] + [pack_rows(rows // 2, half_vecs)] * 2
     return pl.pallas_call(
-        prepare_kernel,
-        out_shape=jax.ShapeDtypeStruct((FIELDS + 2 * vec_mine.shape[0], rows), jnp.float32),
-        in_specs=[VMEM_SPEC] * 7,
-        out_specs=VMEM_SPEC,
+        pack_kernel,
+        out_shape=[jax.ShapeDtypeStruct((size, width), jnp.bfloat16) for size in sizes],
+        in_specs=[VMEM_SPEC] * 5,
+        out_specs=[VMEM_SPEC] * 3,
         compiler_params=params(),
-        name="prepare",
-    )(mine, other, vec_mine, vec_other, boxes, spans, camera[None, :])
+        name="pack",
+    )(embeddings, vectors, boxes, spans, camera[None, :])
+
+
+def decode(mine_ref, other_ref, place):
+    mine, other = mine_ref[place, :].astype(jnp.float32), other_ref[place, :].astype(jnp.float32)
+    numbers = [mine[2 * index : 2 * index + 1] + mine[2 * index + 1 : 2 * index + 2] for index in range(6)]
+    left, right, bottom, top, first, last = numbers
+    right, top = right + MARGIN, top + MARGIN
+    square = jnp.zeros_like(left)
+    for index in (15, 14, 13):
+        square = square + (mine[index : index + 1] + other[index : index + 1])
+    norm = lax.rsqrt(square + EPSILON) * COS_SCALE
+    area = (right - left) * (top - bottom)
+    return [left, right, bottom, top, first * GAP_SCALE + BASE, last * GAP_SCALE, mine[12:13], norm, area]
+
+
+def vectors_of(mine_ref, other_ref, place):
+    mine, other = mine_ref[place, :].astype(jnp.float32), other_ref[place, :].astype(jnp.float32)
+    swapped = lax.axis_index("sub") != 0
+    tail = jnp.where(lax.broadcasted_iota(jnp.int32, mine.shape, 0) == 0, 1.0, 0.0)
+    ordered = [jnp.where(swapped, other, mine), jnp.where(swapped, mine, other), tail]
+    return jnp.concatenate(ordered, axis=0).astype(jnp.bfloat16)
 
 
 def weights_of(products, row, col, same):
@@ -87,7 +141,7 @@
     width = jnp.maximum(jnp.minimum(row[RIGHT], col[RIGHT]) - jnp.maximum(row[LEFT], col[LEFT]), 0.0)
     height = jnp.maximum(jnp.minimum(row[TOP], col[TOP]) - jnp.maximum(row[BOTTOM], col[BOTTOM]), 0.0)
     inter = width * height
-    both = row[FIELDS] + col[FIELDS]
+    both = row[AREA] + col[AREA]
     share = (both + inter) * pl.reciprocal(both - inter, approx=True)
     value = jnp.exp2(logit - jnp.maximum(gap, BASE)) * share
     barred = (row[CAMERA] == col[CAMERA]) & (gap < BARRED_BELOW)
@@ -96,26 +150,24 @@
     return jnp.where(barred, 0.0, value)
 
 
-def tile_kernel(blocks, own_rows, own_block, receivers, *refs):
-    row_mine_ref, row_other_ref, row_packet_ref = refs[:3]
-    col_refs = [refs[3 + 3 * number : 6 + 3 * number] for number in range(blocks)]
-    row_out_ref, col_out_ref, spread_ref = refs[3 + 3 * blocks : 6 + 3 * blocks]
-    products, weights = refs[6 + 3 * blocks : 8 + 3 * blocks], refs[8 + 3 * blocks :]
+def tile_kernel(blocks, own_rows, own_block, receivers, half_vecs, *refs):
+    row_mine_ref, row_other_ref = refs[:2]
+    col_refs = [refs[2 + 2 * number : 4 + 2 * number] for number in range(blocks)]
+    row_out_ref, col_out_ref, field_ref, spread_ref = refs[2 + 2 * blocks : 6 + 2 * blocks]
+    products, weights = refs[6 + 2 * blocks : 8 + 2 * blocks], refs[8 + 2 * blocks :]
     rows = row_out_ref.shape[1]
-    vecs = row_packet_ref.shape[0] - FIELDS
     sub = lax.axis_index("sub")
-    row_part, packet_part = pl.ds(0, rows), pl.ds(0, rows)
+    row_total, first_chunk = rows, 0
+    row_part = pl.ds(0, rows)
     if own_rows:
-        row_part = packet_part = pl.ds(pl.multiple_of(sub * rows, rows), rows)
+        row_total, first_chunk = 2 * rows, sub * (rows // CHUNK)
+        row_part = pl.ds(pl.multiple_of(sub * rows, rows), rows)
     row_out_ref[...] = jnp.zeros_like(row_out_ref)
 
-    def with_ones(packet, count):
-        tail = jnp.where(lax.broadcasted_iota(jnp.int32, (OUT_ROWS - vecs, count), 0) == 0, 1.0, 0.0)
-        return jnp.concatenate([packet, tail], axis=0).astype(jnp.bfloat16)
-
     def block(number, done, row_vecs):
-        col_mine_ref, col_other_ref, col_packet_ref = col_refs[number]
-        chunks = col_mine_ref.shape[0] // CHUNK
+        col_mine_ref, col_other_ref = col_refs[number]
+        cols = 2 * rows
+        chunks = cols // CHUNK
 
         def place(step, base=0):
             return pl.ds(pl.multiple_of(base + step * CHUNK, CHUNK), CHUNK)
@@ -127,15 +179,14 @@
             product_ref[...] = dot_nt(lines, columns)
 
         def weigh(step, product_ref, weight_ref):
-            col = [col_packet_ref[field : field + 1, place(step)] for field in range(FIELDS)]
-            col.append((col[RIGHT] - col[LEFT]) * (col[TOP] - col[BOTTOM]))
+            col = decode(col_mine_ref, col_other_ref, code_place(cols, half_vecs, step))
             col = [jnp.broadcast_to(field, (8, CHUNK)) for field in col]
             for first_row in range(0, rows, 16):
                 both = []
                 for line in (first_row, first_row + 8):
                     row = [
                         jnp.concatenate([spread_ref[field, line : line + 8, :]] * (CHUNK // LANES), axis=1)
-                        for field in range(FIELDS + 1)
+                        for field in range(FIELDS)
                     ]
                     same = None
                     if own_block:
@@ -145,12 +196,12 @@
                 weight_ref[first_row : first_row + 16, :] = jnp.concatenate(both, axis=0).astype(jnp.bfloat16)
 
         def total(step, weight_ref):
-            col_vecs = with_ones(col_packet_ref[FIELDS:, place(step)], CHUNK)
-            row_out_ref[...] += dot_nt(col_vecs, weight_ref[...])
+            col_vecs = vectors_of(col_mine_ref, col_other_ref, vec_place(cols, half_vecs, step))
+            row_out_ref[...] += dot_nt(col_vecs, weight_ref[...])[0:OUT_ROWS]
             if col_out_ref is not None:
                 col_out_ref[:, place(step, done)] = jnp.dot(
                     row_vecs, weight_ref[...], preferred_element_type=jnp.float32
-                )
+                )[0:OUT_ROWS]
 
         def steps(index, carry):
             for parity in range(2):
@@ -166,16 +217,18 @@
         total(chunks - 1, weights[1])
 
     def compute():
-        row_fields = row_packet_ref[0:FIELDS, packet_part]
-        turned = jnp.concatenate([row_fields] * (LANES // FIELDS), axis=0).T
+        row_vecs = []
+        for chunk in range(rows // CHUNK):
+            codes = code_place(row_total, half_vecs, first_chunk + chunk)
+            for field, values in enumerate(decode(row_mine_ref, row_other_ref, codes)):
+                field_ref[field : field + 1, chunk * CHUNK : (chunk + 1) * CHUNK] = values
+            row_vecs.append(vectors_of(row_mine_ref, row_other_ref, vec_place(row_total, half_vecs, first_chunk + chunk)))
+        row_vecs = jnp.concatenate(row_vecs, axis=1)
+        turned = field_ref[...].T
         for field in range(FIELDS):
             spread_ref[field] = jnp.broadcast_to(turned[:, field : field + 1], (rows, LANES))
-        spread_ref[FIELDS] = (spread_ref[RIGHT] - spread_ref[LEFT]) * (spread_ref[TOP] - spread_ref[BOTTOM])
-        row_vecs = with_ones(row_packet_ref[FIELDS:, packet_part], rows)
-        done = 0
         for number in range(blocks):
-            block(number, done, row_vecs)
-            done += col_refs[number][0].shape[0]
+            block(number, number * 2 * rows, row_vecs)
 
     if receivers is None:
         compute()
@@ -192,28 +245,29 @@
         col_out_ref[...] = jnp.zeros_like(col_out_ref)
 
 
-def tile(row, columns, rows, own_rows=False, own_block=False, col_sums=True, receivers=None):
+def tile(row, columns, rows, half_vecs, own_rows=False, own_block=False, col_sums=True, receivers=None):
     features = 2 * row[0].shape[1]
-    cols = sum(part[0].shape[0] for part in columns)
+    cols = 2 * rows * len(columns)
     shapes = [jax.ShapeDtypeStruct((OUT_ROWS, rows), jnp.float32)]
     if col_sums:
         shapes.append(jax.ShapeDtypeStruct((OUT_ROWS, cols), jnp.float32))
 
     def body(*refs):
-        inputs = 3 + 3 * len(columns)
+        inputs = 2 + 2 * len(columns)
         refs = list(refs)
         if not col_sums:
             refs.insert(inputs + 1, None)
-        tile_kernel(len(columns), own_rows, own_block, receivers, *refs)
+        tile_kernel(len(columns), own_rows, own_block, receivers, half_vecs, *refs)
 
     pairs = rows * cols
     return pl.pallas_call(
         body,
         out_shape=shapes,
-        in_specs=[VMEM_SPEC] * (3 + 3 * len(columns)),
+        in_specs=[VMEM_SPEC] * (2 + 2 * len(columns)),
         out_specs=[VMEM_SPEC] * len(shapes),
         scratch_shapes=[
-            pltpu.VMEM((FIELDS + 1, rows, LANES), jnp.float32),
+            pltpu.VMEM((LANES, rows), jnp.float32),
+            pltpu.VMEM((FIELDS, rows, LANES), jnp.float32),
             pltpu.VMEM((rows, CHUNK), jnp.float32),
             pltpu.VMEM((rows, CHUNK), jnp.float32),
             pltpu.VMEM((rows, CHUNK), jnp.bfloat16),
@@ -328,35 +382,24 @@
     beside = [(block, block ^ 1) for block in range(blocks)]
     plans = [(block_moves(moves), takers) for moves, takers in exchanges(blocks // 2)]
 
-    def half_rows(place):
-        return lax.dynamic_slice_in_dim(embeddings, place * half, half, 0)
-
     def crossed(moves):
         return [(2 * source + 1 - core, 2 * target + core) for source, target in moves for core in range(2)]
 
-    other = lax.ppermute(embeddings, "sub", swap)
-    vec_other = lax.ppermute(vectors, "sub", swap)
-    to_same, to_cross = half_rows(sub), half_rows(1 - sub)
+    full, to_same, to_cross = packs_of(embeddings, vectors, boxes, spans, camera)
     sent = [
         (lax.ppermute(to_same, "blk", moves), lax.ppermute(to_cross, ("blk", "sub"), crossed(moves)))
         for moves, _ in plans
     ]
-    beside_mine = lax.ppermute(embeddings, "blk", beside)
-    beside_other = lax.ppermute(embeddings, ("blk", "sub"), crossed(beside))
-    packet = prepare(embeddings, other, vectors, vec_other, boxes, spans, camera)
-    row_packet = lax.dynamic_slice_in_dim(packet, sub * half, half, 1)
-    beside_packet = lax.ppermute(packet, "blk", beside)
-    sent_packet = [lax.ppermute(row_packet, "blk", moves) for moves, _ in plans]
-
-    own = (embeddings, other, packet)
-    next_to = (beside_mine, beside_other, beside_packet)
+    own = (full, lax.ppermute(full, "sub", swap))
+    next_to = (lax.ppermute(full, "blk", beside), lax.ppermute(full, ("blk", "sub"), crossed(beside)))
+    weigh = functools.partial(tile, rows=half, half_vecs=vecs // 2)
     parts = [
-        tile(own, [own], half, own_rows=True, own_block=True, col_sums=False)[0],
-        tile(own, [next_to], half, own_rows=True, col_sums=False)[0],
+        weigh(own, [own], own_rows=True, own_block=True, col_sums=False)[0],
+        weigh(own, [next_to], own_rows=True, col_sums=False)[0],
     ]
     col_sums = None
-    for (moves, takers), halves, meta in zip(plans, sent, sent_packet):
-        row_sums, sums = tile((*halves, meta), [own, next_to], half, receivers=takers)
+    for (moves, takers), halves in zip(plans, sent):
+        row_sums, sums = weigh(halves, [own, next_to], receivers=takers)
         parts.append(lax.ppermute(row_sums, "blk", back(moves)))
         col_sums = sums if col_sums is None else col_sums + sums
 

time: 75.5 us -> 79.2 us (1.049)
  starting transfers between devices: 36.6 us -> 24 us
  waiting for transfers between devices: 17.8 us -> 27.8 us
  local copies, waits for them, and re-layouts: 1.19 us -> 5.62 us
  Pallas kernels: 19.4 us -> 21 us
    ppermute x7 -> x3, starting transfers between devices: 11 us -> 3.18 us  [the longest x1 2.6 us: local(): lax.ppermute(full, 'blk', beside)]
    unnamed x10 -> x14, local copies, waits for them, and re-layouts: 0.02 us -> 5.58 us
    ppermute x2, waiting for transfers between devices: 2.76 us -> 8.15 us  [local(): lax.ppermute(to_cross, ('blk', 'sub'), crossed(moves))]
    ppermute x2, starting transfers between devices: 5.2 us -> 1.31 us  [local(): lax.ppermute(to_cross, ('blk', 'sub'), crossed(moves))]
    ppermute x2, starting transfers between devices: 2.81 us -> 6.05 us  [local(): lax.ppermute(to_same, 'blk', moves)]
    ppermute x7 -> x3, waiting for transfers between devices: 4.03 us -> 7.15 us  [the longest x1 7.15 us: local(): lax.ppermute(full, ('blk', 'sub'), crossed(beside))]
    ppermute x2, starting transfers between devices: 9.65 us -> 6.95 us  [local(): parts.append(lax.ppermute(row_sums, 'blk', back(moves)))]
    ppermute x2, waiting for transfers between devices: 4.27 us -> 5.99 us  [local(): lax.ppermute(to_same, 'blk', moves)]
  transfers between devices with their start and end apart: 18 -> 14, of which waited for: 7 -> 6; matrix products, arithmetic and copies ran while one was open for 2% -> 0% of each run, Pallas kernels for 10% -> 9%
where the time goes in v3:
time: 79.2 us; the launch traced here: 78.6 us
  waiting for transfers between devices  27.8 us (35%)
  starting transfers between devices  24 us (30%)
  Pallas kernels  21 us (27%)
  local copies, waits for them, and re-layouts  5.62 us (7%)
    pallas_call x4, Pallas kernels, tile(): pl.pallas_call(body, out_shape=shapes, in_specs=[VMEM_SPEC] * (2 + 2 * le...  15.1 us
    ppermute x2, waiting for transfers between devices, local(): lax.ppermute(to_cross, ('blk', 'sub'), crossed(moves))  8.15 us
    ppermute x1, waiting for transfers between devices, local(): lax.ppermute(full, ('blk', 'sub'), crossed(beside))  7.15 us
    ppermute x2, starting transfers between devices, local(): parts.append(lax.ppermute(row_sums, 'blk', back(moves)))  6.95 us
    ppermute x2, starting transfers between devices, local(): lax.ppermute(to_same, 'blk', moves)  6.05 us
    ppermute x2, waiting for transfers between devices, local(): lax.ppermute(to_same, 'blk', moves)  5.99 us
    unnamed x14, local copies, waits for them, and re-layouts  5.58 us
    all_to_all x1, waiting for transfers between devices, local(): grams = lax.all_to_all(copies, ('blk', 'sub'), 0, 0, tiled=True)  5.58 us
  transfers between devices with their start and end apart: 14, of which 6 were waited for; matrix products, arithmetic and copies ran while one was open for 0% of the time, Pallas kernels for 9%

profile of v3, /device:TPU:0, one launch (start us, length us, event | category | flops | bytes accessed | tf_op | source)
XLA Modules:
  0.0 78.6 jit_solution(11534146143789269756)
XLA Ops:
  0.0 1.0 %copy-done = bf16[1024,256]{1,0:T(8,128)(2,1)S(1)} copy-done((bf16[1024,256]{1,0:T(8,128)(2,1)S(1)}, bf16[1024,256]{1,0:T(8,128)(2,1)}, u32[]{:S(2)}) %copy-start) | copy-done | bytes 524312
  1.0 0.8 copy-done.1
  1.8 0.7 copy-done.2
  2.5 0.7 copy-done.3
  3.2 0.7 copy-done.4
  3.9 1.1 %pack.1 = (bf16[1152,256]{1,0:T(8,128)(2,1)S(1)}, bf16[576,256]{1,0:T(8,128)(2,1)S(1)}, bf16[576,256]{1,0:T(8,128)(2,1)S(1)}) custom-call(bf16[1024,256]{1,0:T(8,128)(2,1)S(1)} %copy-done, bf16[16,1024]{1,0:T(8,128)(2,1)S(1)} %copy-done.1, s32[4,1024]{1,0:T(4,128)S(1)} %copy-done.2, s32[2,1024]{1,0:T(2,128)S(1)} %copy-done.3, s32[1,1024]{1,0:T(1,128)S(1)} %bitcast.1), custom_call_target="tpu_custom_call" | custom-call | tf_op jit(solution)/shard_map/pack/pallas_call | solution.py:107
  5.0 0.5 collective-permute-start
  5.5 2.6 %collective-permute-start.1 = (bf16[1152,256]{1,0:T(8,128)(2,1)S(1)}, bf16[1152,256]{1,0:T(8,128)(2,1)S(1)}, u32[]{:S(2)}, u32[]{:S(2)}) collective-permute-start(bf16[1152,256]{1,0:T(8,128)(2,1)S(1)} %get-tuple-element.14.refs_0_.refs_2_), channel_id=1, source_target_pairs={{0,2},{2,0},{4,6},{6,4},{8,10},{10,8},{12,14},{14,12},{1,3},{3,1},... | collective-permute-start | bytes 1769480 | tf_op jit(solution)/shard_map/ppermute | solution.py:394
  8.1 0.1 collective-permute-start.2
  8.2 4.7 %collective-permute-start.6 = (bf16[576,256]{1,0:T(8,128)(2,1)S(1)}, bf16[576,256]{1,0:T(8,128)(2,1)S(1)}, u32[]{:S(2)}, u32[]{:S(2)}) collective-permute-start(bf16[576,256]{1,0:T(8,128)(2,1)S(1)} %get-tuple-element.15), channel_id=1, source_target_pairs={{0,8},{2,10},{12,4},{14,6},{1,9},{3,11},{13,5},{15,7},{16,24},{18,... | collective-permute-start | bytes 884744 | tf_op jit(solution)/shard_map/ppermute | solution.py:390
  12.9 1.3 %collective-permute-start.7 = (bf16[576,256]{1,0:T(8,128)(2,1)S(1)}, bf16[576,256]{1,0:T(8,128)(2,1)S(1)}, u32[]{:S(2)}, u32[]{:S(2)}) collective-permute-start(bf16[576,256]{1,0:T(8,128)(2,1)S(1)} %get-tuple-element.16), channel_id=1, source_target_pairs={{1,8},{0,9},{3,10},{2,11},{13,4},{12,5},{15,6},{14,7},{17,24},{16,... | collective-permute-start | bytes 884744 | tf_op jit(solution)/shard_map/ppermute | solution.py:390
  14.2 6.0 %collective-permute-done.6.refs_0_ = bf16[576,256]{1,0:T(8,128)(2,1)S(1)} collective-permute-done((bf16[576,256]{1,0:T(8,128)(2,1)S(1)}, bf16[576,256]{1,0:T(8,128)(2,1)S(1)}, u32[]{:S(2)}, u32[]{:S(2)}) %collective-permute-start.6) | collective-permute-done | bytes 294944 | tf_op jit(solution)/shard_map/ppermute | solution.py:390
  20.2 1.3 %collective-permute-start.3 = (bf16[576,256]{1,0:T(8,128)(2,1)S(1)}, bf16[576,256]{1,0:T(8,128)(2,1)S(1)}, u32[]{:S(2)}, u32[]{:S(2)}) collective-permute-start(bf16[576,256]{1,0:T(8,128)(2,1)S(1)} %get-tuple-element.15), channel_id=1, source_target_pairs={{4,0},{6,2},{8,4},{10,6},{12,8},{14,10},{0,12},{2,14},{5,1},{7,3},... | collective-permute-start | bytes 884744 | tf_op jit(solution)/shard_map/ppermute | solution.py:390
  21.5 5.0 %collective-permute-done.7.refs_1_ = bf16[576,256]{1,0:T(8,128)(2,1)S(1)} collective-permute-done((bf16[576,256]{1,0:T(8,128)(2,1)S(1)}, bf16[576,256]{1,0:T(8,128)(2,1)S(1)}, u32[]{:S(2)}, u32[]{:S(2)}) %collective-permute-start.7) | collective-permute-done | bytes 294944 | tf_op jit(solution)/shard_map/ppermute | solution.py:390
  26.5 0.7 copy-done.5
  27.2 7.1 %collective-permute-done.2.refs_3_.refs_5_ = bf16[1152,256]{1,0:T(8,128)(2,1)S(1)} collective-permute-done((bf16[1152,256]{1,0:T(8,128)(2,1)S(1)}, bf16[1152,256]{1,0:T(8,128)(2,1)S(1)}, u32[]{:S(2)}, u32[]{:S(2)}) %collective-permute-start.2) | collective-permute-done | bytes 589856 | tf_op jit(solution)/shard_map/ppermute | solution.py:394
  34.4 1.0 %copy-done.6 = bf16[576,256]{1,0:T(8,128)(2,1)S(1)} copy-done((bf16[576,256]{1,0:T(8,128)(2,1)S(1)}, bf16[576,256]{1,0:T(8,128)(2,1)}, u32[]{:S(2)}) %copy-start.6) | copy-done | bytes 294936
  35.4 3.2 %collective-permute-done.4.refs_1_ = bf16[576,256]{1,0:T(8,128)(2,1)} collective-permute-done((bf16[576,256]{1,0:T(8,128)(2,1)S(1)}, bf16[576,256]{1,0:T(8,128)(2,1)}, u32[]{:S(2)}, u32[]{:S(2)}) %collective-permute-start.4) | collective-permute-done | bytes 294944 | tf_op jit(solution)/shard_map/ppermute | solution.py:390
  38.6 8.0 %tile.6 = (f32[40,512]{1,0:T(8,128)S(1)}, f32[40,2048]{1,0:T(8,128)S(1)}) custom-call(bf16[576,256]{1,0:T(8,128)(2,1)S(1)} %collective-permute-done.3.refs_0_, bf16[576,256]{1,0:T(8,128)(2,1)} %collective-permute-done.4.refs_1_, bf16[1152,256]{1,0:T(8,128)(2,1)S(1)} %get-tuple-element.14.refs_0_.refs_2_, ...), custom_call_target="tpu_custom_call" | custom-call | flops 2147483648 | bytes 5242880 | tf_op jit(solution)/shard_map/tile/pallas_call | solution.py:263
  46.6 1.6 %collective-permute-start.10 = (f32[40,512]{1,0:T(8,128)S(1)}, f32[40,512]{1,0:T(8,128)S(1)}, u32[]{:S(2)}, u32[]{:S(2)}) collective-permute-start(f32[40,512]{1,0:T(8,128)S(1)} %get-tuple-element.24), channel_id=1, source_target_pairs={{0,2},{2,0},{4,6},{6,4},{8,10},{10,8},{12,14},{14,12},{1,3},{3,1},... | collective-permute-start | bytes 245768 | tf_op jit(solution)/shard_map/ppermute | solution.py:412
  48.2 0.6 collective-permute-start.9
  48.8 1.3 %collective-permute-start.8 = (f32[40,512]{1,0:T(8,128)S(1)}, f32[40,512]{1,0:T(8,128)S(1)}, u32[]{:S(2)}, u32[]{:S(2)}) collective-permute-start(f32[40,512]{1,0:T(8,128)S(1)} %get-tuple-element.18), channel_id=1, source_target_pairs={{8,0},{10,2},{4,12},{6,14},{9,1},{11,3},{5,13},{7,15},{24,16},{26,... | collective-permute-start | bytes 245768 | tf_op jit(solution)/shard_map/ppermute | solution.py:403
  50.1 5.7 %collective-permute-start.5 = (f32[40,512]{1,0:T(8,128)S(1)}, f32[40,512]{1,0:T(8,128)S(1)}, u32[]{:S(2)}, u32[]{:S(2)}) collective-permute-start(f32[40,512]{1,0:T(8,128)S(1)} %get-tuple-element.17), channel_id=1, source_target_pairs={{0,4},{2,6},{4,8},{6,10},{8,12},{10,14},{12,0},{14,2},{1,5},{3,7},... | collective-permute-start | bytes 245768 | tf_op jit(solution)/shard_map/ppermute | solution.py:403
  55.8 3.4 %tile.5.refs_1_ = f32[40,512]{1,0:T(8,128)S(1)} custom-call(bf16[1152,256]{1,0:T(8,128)(2,1)S(1)} %get-tuple-element.14.refs_0_.refs_2_, bf16[1152,256]{1,0:T(8,128)(2,1)S(1)} %collective-permute-done.refs_1_.refs_3_, bf16[1152,256]{1,0:T(8,128)(2,1)S(1)} %collective-permute-done.1.refs_2_.refs_4_, bf16[1152,256]{1,0:T(8,128)(2,1)S(1)} %collective-permute-done.2.refs_3_.refs_5_), custom_call_target="tpu_custom_call" | custom-call | flops 1073741824 | bytes 3145728 | tf_op jit(solution)/shard_map/tile/pallas_call | solution.py:263
  59.2 3.7 %tile.4.refs_0_ = f32[40,512]{1,0:T(8,128)S(1)} custom-call(bf16[1152,256]{1,0:T(8,128)(2,1)S(1)} %get-tuple-element.14.refs_0_.refs_2_, bf16[1152,256]{1,0:T(8,128)(2,1)S(1)} %collective-permute-done.refs_1_.refs_3_, bf16[1152,256]{1,0:T(8,128)(2,1)S(1)} %get-tuple-element.14.refs_0_.refs_2_, bf16[1152,256]{1,0:T(8,128)(2,1)S(1)} %collective-permute-done.refs_1_.refs_3_), custom_call_target="tpu_custom_call" | custom-call | flops 1073741824 | bytes 3145728 | tf_op jit(solution)/shard_map/tile/pallas_call | solution.py:263
  62.9 0.0 collective-permute-done.10.refs_6_
  63.0 1.3 %image.1 = (f32[32,512]{1,0:T(8,128)S(1)}, f32[16,8,128]{2,1,0:T(8,128)}) custom-call(f32[40,512]{1,0:T(8,128)S(1)} %tile.4.refs_0_, f32[40,512]{1,0:T(8,128)S(1)} %tile.5.refs_1_, f32[40,512]{1,0:T(8,128)S(1)} %collective-permute-done.5.refs_2_, f32[40,512]{1,0:T(8,128)S(1)} %collective-permute-done.8.refs_3_, f32[40,512]{1,0:T(8,128)S(1)} %get-tuple-element.26.refs_4_, ...), custom_call_target="tpu_custom_call" | custom-call | tf_op jit(solution)/shard_map/image/pallas_call | solution.py:306
  64.3 3.9 %all-to-all-start = ((f32[16,8,128]{2,1,0:T(8,128)}), f32[16,8,128]{2,1,0:T(8,128)S(1)}, u32[]{:S(2)}, u32[]{:S(2)}) async-start(f32[16,8,128]{2,1,0:T(8,128)} %get-tuple-element.21), calls=%async_computation | async-start | bytes 131072 | tf_op jit(solution)/shard_map/all_to_all | solution.py:417
  68.2 0.4 collective-permute-start.12
  68.6 0.9 %collective-permute-done.12.other_ref = f32[32,512]{1,0:T(8,128)S(1)} collective-permute-done((f32[32,512]{1,0:T(8,128)S(1)}, f32[32,512]{1,0:T(8,128)S(1)}, u32[]{:S(2)}, u32[]{:S(2)}) %collective-permute-start.12) | collective-permute-done | bytes 65568 | tf_op jit(solution)/shard_map/ppermute | solution.py:416
  69.5 5.6 %all-to-all-done.grams_ref = f32[16,8,128]{2,1,0:T(8,128)S(1)} async-done(((f32[16,8,128]{2,1,0:T(8,128)}), f32[16,8,128]{2,1,0:T(8,128)S(1)}, u32[]{:S(2)}, u32[]{:S(2)}) %all-to-all-start) | async-done | bytes 65568 | tf_op jit(solution)/shard_map/all_to_all | solution.py:417
  75.1 3.5 %basis.1 = f32[16,1024]{1,0:T(8,128)} custom-call(f32[16,8,128]{2,1,0:T(8,128)S(1)} %all-to-all-done.grams_ref, f32[32,512]{1,0:T(8,128)S(1)} %get-tuple-element.22.mine_ref, f32[32,512]{1,0:T(8,128)S(1)} %collective-permute-done.12.other_ref), custom_call_target="tpu_custom_call" | custom-call | tf_op jit(solution)/shard_map/basis/pallas_call | solution.py:344
  (19 shorter events, 0.1 us)
Async XLA Ops:
  0.0 1.0 %copy-start = (bf16[1024,256]{1,0:T(8,128)(2,1)S(1)}, bf16[1024,256]{1,0:T(8,128)(2,1)}, u32[]{:S(2)}) copy-start(bf16[1024,256]{1,0:T(8,128)(2,1)} %emb_ref.1) | copy-start | bytes 1572868
  1.0 0.8 copy-start.1
  1.8 0.7 copy-start.2
  2.5 0.7 copy-start.3
  3.2 0.7 copy-start.4
  5.0 22.3 %collective-permute-start = (bf16[1152,256]{1,0:T(8,128)(2,1)S(1)}, bf16[1152,256]{1,0:T(8,128)(2,1)S(1)}, u32[]{:S(2)}, u32[]{:S(2)}) collective-permute-start(bf16[1152,256]{1,0:T(8,128)(2,1)S(1)} %get-tuple-element.14.refs_0_.refs_2_), channel_id=1, source_target_pairs={{0,1},{1,0},{2,3},{3,2},{4,5},{5,4},{6,7},{7,6},{8,9},{9,8},{10,11... | collective-permute-start | bytes 1769480 | tf_op jit(solution)/shard_map/ppermute | solution.py:393
  5.5 21.7 %collective-permute-start.1 = (bf16[1152,256]{1,0:T(8,128)(2,1)S(1)}, bf16[1152,256]{1,0:T(8,128)(2,1)S(1)}, u32[]{:S(2)}, u32[]{:S(2)}) collective-permute-start(bf16[1152,256]{1,0:T(8,128)(2,1)S(1)} %get-tuple-element.14.refs_0_.refs_2_), channel_id=1, source_target_pairs={{0,2},{2,0},{4,6},{6,4},{8,10},{10,8},{12,14},{14,12},{1,3},{3,1},... | collective-permute-start | bytes 1769480 | tf_op jit(solution)/shard_map/ppermute | solution.py:394
  8.1 26.3 %collective-permute-start.2 = (bf16[1152,256]{1,0:T(8,128)(2,1)S(1)}, bf16[1152,256]{1,0:T(8,128)(2,1)S(1)}, u32[]{:S(2)}, u32[]{:S(2)}) collective-permute-start(bf16[1152,256]{1,0:T(8,128)(2,1)S(1)} %get-tuple-element.14.refs_0_.refs_2_), channel_id=1, source_target_pairs={{1,2},{0,3},{3,0},{2,1},{5,6},{4,7},{7,4},{6,5},{9,10},{8,11},{11,... | collective-permute-start | bytes 1769480 | tf_op jit(solution)/shard_map/ppermute | solution.py:394
  8.2 12.0 %collective-permute-start.6 = (bf16[576,256]{1,0:T(8,128)(2,1)S(1)}, bf16[576,256]{1,0:T(8,128)(2,1)S(1)}, u32[]{:S(2)}, u32[]{:S(2)}) collective-permute-start(bf16[576,256]{1,0:T(8,128)(2,1)S(1)} %get-tuple-element.15), channel_id=1, source_target_pairs={{0,8},{2,10},{12,4},{14,6},{1,9},{3,11},{13,5},{15,7},{16,24},{18,... | collective-permute-start | bytes 884744 | tf_op jit(solution)/shard_map/ppermute | solution.py:390
  12.9 13.6 %collective-permute-start.7 = (bf16[576,256]{1,0:T(8,128)(2,1)S(1)}, bf16[576,256]{1,0:T(8,128)(2,1)S(1)}, u32[]{:S(2)}, u32[]{:S(2)}) collective-permute-start(bf16[576,256]{1,0:T(8,128)(2,1)S(1)} %get-tuple-element.16), channel_id=1, source_target_pairs={{1,8},{0,9},{3,10},{2,11},{13,4},{12,5},{15,6},{14,7},{17,24},{16,... | collective-permute-start | bytes 884744 | tf_op jit(solution)/shard_map/ppermute | solution.py:390
  20.2 15.2 %collective-permute-start.3 = (bf16[576,256]{1,0:T(8,128)(2,1)S(1)}, bf16[576,256]{1,0:T(8,128)(2,1)S(1)}, u32[]{:S(2)}, u32[]{:S(2)}) collective-permute-start(bf16[576,256]{1,0:T(8,128)(2,1)S(1)} %get-tuple-element.15), channel_id=1, source_target_pairs={{4,0},{6,2},{8,4},{10,6},{12,8},{14,10},{0,12},{2,14},{5,1},{7,3},... | collective-permute-start | bytes 884744 | tf_op jit(solution)/shard_map/ppermute | solution.py:390
  26.5 0.7 copy-start.5
  27.2 11.3 %collective-permute-start.4 = (bf16[576,256]{1,0:T(8,128)(2,1)S(1)}, bf16[576,256]{1,0:T(8,128)(2,1)}, u32[]{:S(2)}, u32[]{:S(2)}) collective-permute-start(bf16[576,256]{1,0:T(8,128)(2,1)S(1)} %get-tuple-element.16), channel_id=1, source_target_pairs={{5,0},{4,1},{7,2},{6,3},{9,4},{8,5},{11,6},{10,7},{13,8},{12,9},{1... | collective-permute-start | bytes 884744 | tf_op jit(solution)/shard_map/ppermute | solution.py:390
  34.4 1.0 %copy-start.6 = (bf16[576,256]{1,0:T(8,128)(2,1)S(1)}, bf16[576,256]{1,0:T(8,128)(2,1)}, u32[]{:S(2)}) copy-start(bf16[576,256]{1,0:T(8,128)(2,1)} %copy-done.5) | copy-start | bytes 884740
  46.6 16.3 %collective-permute-start.10 = (f32[40,512]{1,0:T(8,128)S(1)}, f32[40,512]{1,0:T(8,128)S(1)}, u32[]{:S(2)}, u32[]{:S(2)}) collective-permute-start(f32[40,512]{1,0:T(8,128)S(1)} %get-tuple-element.24), channel_id=1, source_target_pairs={{0,2},{2,0},{4,6},{6,4},{8,10},{10,8},{12,14},{14,12},{1,3},{3,1},... | collective-permute-start | bytes 245768 | tf_op jit(solution)/shard_map/ppermute | solution.py:412
  48.2 14.7 %collective-permute-start.11 = (f32[40,512]{1,0:T(8,128)S(1)}, f32[40,512]{1,0:T(8,128)S(1)}, u32[]{:S(2)}, u32[]{:S(2)}) collective-permute-start(f32[40,512]{1,0:T(8,128)S(1)} %get-tuple-element.23), channel_id=1, source_target_pairs={{1,2},{0,3},{3,0},{2,1},{5,6},{4,7},{7,4},{6,5},{9,10},{8,11},{11,... | collective-permute-start | bytes 245768 | tf_op jit(solution)/shard_map/ppermute | solution.py:413
  48.2 14.7 %collective-permute-start.9 = (f32[40,512]{1,0:T(8,128)S(1)}, f32[40,512]{1,0:T(8,128)S(1)}, u32[]{:S(2)}, u32[]{:S(2)}) collective-permute-start(f32[40,512]{1,0:T(8,128)S(1)} %get-tuple-element.25), channel_id=1, source_target_pairs={{0,1},{1,0},{2,3},{3,2},{4,5},{5,4},{6,7},{7,6},{8,9},{9,8},{10,11... | collective-permute-start | bytes 245768 | tf_op jit(solution)/shard_map/ppermute | solution.py:411
  48.8 14.1 %collective-permute-start.8 = (f32[40,512]{1,0:T(8,128)S(1)}, f32[40,512]{1,0:T(8,128)S(1)}, u32[]{:S(2)}, u32[]{:S(2)}) collective-permute-start(f32[40,512]{1,0:T(8,128)S(1)} %get-tuple-element.18), channel_id=1, source_target_pairs={{8,0},{10,2},{4,12},{6,14},{9,1},{11,3},{5,13},{7,15},{24,16},{26,... | collective-permute-start | bytes 245768 | tf_op jit(solution)/shard_map/ppermute | solution.py:403
  50.1 12.9 %collective-permute-start.5 = (f32[40,512]{1,0:T(8,128)S(1)}, f32[40,512]{1,0:T(8,128)S(1)}, u32[]{:S(2)}, u32[]{:S(2)}) collective-permute-start(f32[40,512]{1,0:T(8,128)S(1)} %get-tuple-element.17), channel_id=1, source_target_pairs={{0,4},{2,6},{4,8},{6,10},{8,12},{10,14},{12,0},{14,2},{1,5},{3,7},... | collective-permute-start | bytes 245768 | tf_op jit(solution)/shard_map/ppermute | solution.py:403
  64.3 10.8 %all-to-all-start = ((f32[16,8,128]{2,1,0:T(8,128)}), f32[16,8,128]{2,1,0:T(8,128)S(1)}, u32[]{:S(2)}, u32[]{:S(2)}) async-start(f32[16,8,128]{2,1,0:T(8,128)} %get-tuple-element.21), calls=%async_computation | async-start | bytes 131072 | tf_op jit(solution)/shard_map/all_to_all | solution.py:417
  68.2 1.3 %collective-permute-start.12 = (f32[32,512]{1,0:T(8,128)S(1)}, f32[32,512]{1,0:T(8,128)S(1)}, u32[]{:S(2)}, u32[]{:S(2)}) collective-permute-start(f32[32,512]{1,0:T(8,128)S(1)} %get-tuple-element.22.mine_ref), channel_id=1, source_target_pairs={{0,1},{1,0},{2,3},{3,2},{4,5},{5,4},{6,7},{7,6},{8,9},{9,8},{10,11... | collective-permute-start | bytes 196616 | tf_op jit(solution)/shard_map/ppermute | solution.py:416

commit v4 on v3

--- a/solution.py
+++ b/solution.py
@@ -25,7 +25,9 @@
 LANES = 128
 CHUNK = 256
 OUT_ROWS = 40
+COST = 1
 VMEM_LIMIT = 48 * 1024 * 1024
+PACK_VMEM_LIMIT = 63 * 1024 * 1024
 
 NT = (((1,), (1,)), ((), ()))
 VMEM_SPEC = pl.BlockSpec(memory_space=pltpu.VMEM)
@@ -51,14 +53,26 @@
     return pl.ds(pl.multiple_of(total + total // CHUNK * half_vecs + chunk * CODE_ROWS, 16), CODE_ROWS)
 
 
-def pack_kernel(emb_ref, vec_ref, boxes_ref, spans_ref, camera_ref, full_ref, same_ref, cross_ref):
+def pack_kernel(*refs):
+    sources, (full_ref, same_ref, cross_ref), loaded, side_ref, sems = refs[:5], refs[5:8], refs[8:13], refs[13], refs[14]
+    emb_ref, vec_ref, boxes_ref, spans_ref, camera_ref = loaded
     sub = lax.axis_index("sub")
     rows = emb_ref.shape[0]
-    half = same_ref.shape[0] * rows // full_ref.shape[0]
+    half = rows // 2
     half_vecs = vec_ref.shape[0]
-    full_ref[0:rows, :] = emb_ref[...]
-    same_ref[0:half, :] = emb_ref[pl.ds(pl.multiple_of(sub * half, half), half), :]
-    cross_ref[0:half, :] = emb_ref[pl.ds(pl.multiple_of((1 - sub) * half, half), half), :]
+    halves = ((same_ref, sub), (cross_ref, 1 - sub))
+    number = iter(range(sems.shape[0]))
+
+    def start(source, target):
+        copy = pltpu.make_async_copy(source, target, sems.at[next(number)])
+        copy.start()
+        return copy
+
+    loads = [start(source, target) for source, target in zip(sources, loaded)]
+    moves = [start(sources[0].at[pl.ds(pl.multiple_of(place * half, half), half)], ref.at[pl.ds(0, half)]) for ref, place in halves]
+    moves.append(start(sources[0], full_ref.at[pl.ds(0, rows)]))
+    for load in loads:
+        load.wait()
     ones = jnp.ones((8, CHUNK), jnp.bfloat16)
     for chunk in range(rows // CHUNK):
         part = pl.ds(chunk * CHUNK, CHUNK)
@@ -86,32 +100,36 @@
             codes.append(piece)
             rest = rest - piece
         coded = jnp.concatenate(codes, axis=0).astype(jnp.bfloat16)
-        vecs = vec_ref[:, part]
-        full_ref[vec_place(rows, half_vecs, chunk), :] = vecs
-        full_ref[code_place(rows, half_vecs, chunk), :] = coded
-        in_half = chunk % (half // CHUNK)
-        first_half = chunk < half // CHUNK
-
-        def put(ref):
-            ref[vec_place(half, half_vecs, in_half), :] = vecs
-            ref[code_place(half, half_vecs, in_half), :] = coded
-
-        pl.when((sub == 0) == first_half)(functools.partial(put, same_ref))
-        pl.when((sub == 0) != first_half)(functools.partial(put, cross_ref))
+        side_ref[vec_place(0, half_vecs, chunk), :] = vec_ref[:, part]
+        first_code = rows // CHUNK * half_vecs + chunk * CODE_ROWS
+        side_ref[first_code : first_code + CODE_ROWS, :] = coded
+    side_rows = side_ref.shape[0]
+    moves.append(start(side_ref, full_ref.at[pl.ds(rows, side_rows)]))
+    vec_rows, code_rows = half // CHUNK * half_vecs, half // CHUNK * CODE_ROWS
+    for ref, place in halves:
+        vec_start = pl.multiple_of(place * vec_rows, 16)
+        code_start = pl.multiple_of(2 * vec_rows + place * code_rows, 16)
+        moves.append(start(side_ref.at[pl.ds(vec_start, vec_rows)], ref.at[pl.ds(half, vec_rows)]))
+        moves.append(start(side_ref.at[pl.ds(code_start, code_rows)], ref.at[pl.ds(half + vec_rows, code_rows)]))
+    for move in moves:
+        move.wait()
 
 
 def packs_of(embeddings, vectors, boxes, spans, camera):
     rows, width = embeddings.shape
     half_vecs = vectors.shape[0]
     sizes = [pack_rows(rows, half_vecs)] + [pack_rows(rows // 2, half_vecs)] * 2
+    inputs = (embeddings, vectors, boxes, spans, camera[None, :])
     return pl.pallas_call(
         pack_kernel,
         out_shape=[jax.ShapeDtypeStruct((size, width), jnp.bfloat16) for size in sizes],
-        in_specs=[VMEM_SPEC] * 5,
-        out_specs=[VMEM_SPEC] * 3,
-        compiler_params=params(),
+        in_specs=[pl.BlockSpec(memory_space=pltpu.HBM)] * 5,
+        out_specs=[pl.BlockSpec(memory_space=pltpu.HBM)] * 3,
+        scratch_shapes=[pltpu.VMEM(array.shape, array.dtype) for array in inputs]
+        + [pltpu.VMEM((sizes[0] - rows, width), jnp.bfloat16), pltpu.SemaphoreType.DMA((13,))],
+        compiler_params=pltpu.CompilerParams(vmem_limit_bytes=PACK_VMEM_LIMIT),
         name="pack",
-    )(embeddings, vectors, boxes, spans, camera[None, :])
+    )(*inputs)
 
 
 def decode(mine_ref, other_ref, place):
@@ -274,7 +292,7 @@
             pltpu.VMEM((rows, CHUNK), jnp.bfloat16),
         ],
         cost_estimate=pl.CostEstimate(
-            flops=4 * pairs * features, bytes_accessed=4 * cols * features + 4 * rows * features, transcendentals=2 * pairs
+            flops=COST, bytes_accessed=COST, transcendentals=0
         ),
         compiler_params=params(),
         name="tile",
@@ -391,14 +409,16 @@
         for moves, _ in plans
     ]
     own = (full, lax.ppermute(full, "sub", swap))
-    next_to = (lax.ppermute(full, "blk", beside), lax.ppermute(full, ("blk", "sub"), crossed(beside)))
     weigh = functools.partial(tile, rows=half, half_vecs=vecs // 2)
-    parts = [
-        weigh(own, [own], own_rows=True, own_block=True, col_sums=False)[0],
-        weigh(own, [next_to], own_rows=True, col_sums=False)[0],
-    ]
+    own_sums = weigh(own, [own], own_rows=True, own_block=True, col_sums=False)[0]
+    beside_mine = lax.ppermute(full, "blk", beside)
+    own_sums, beside_mine, sent[:1] = lax.optimization_barrier((own_sums, beside_mine, sent[:1]))
+    next_to = (beside_mine, lax.ppermute(beside_mine, "sub", swap))
+    parts = [own_sums, weigh(own, [next_to], own_rows=True, col_sums=False)[0]]
     col_sums = None
     for (moves, takers), halves in zip(plans, sent):
+        if col_sums is not None:
+            halves, col_sums = lax.optimization_barrier((halves, col_sums))
         row_sums, sums = weigh(halves, [own, next_to], receivers=takers)
         parts.append(lax.ppermute(row_sums, "blk", back(moves)))
         col_sums = sums if col_sums is None else col_sums + sums

time: 79.2 us -> 103 us (1.30)
  Pallas kernels: 21 us -> 52.9 us
  waiting for transfers between devices: 27.8 us -> 19 us
  starting transfers between devices: 24 us -> 30 us
  local copies, waits for them, and re-layouts: 5.62 us -> 1.1 us
    pallas_call x1, Pallas kernels: 1.07 us -> 33 us  [packs_of(): pl.pallas_call(pack_kernel, out_shape=[jax.ShapeDtypeStruct((size, width)...]
    ppermute x2, waiting for transfers between devices: 7.15 us -> 0.01 us  [the longest x1 0.01 us: local(): next_to = (beside_mine, lax.ppermute(beside_mine, 'sub', swap))]
    unnamed x14 -> x4, local copies, waits for them, and re-layouts: 5.58 us -> 1.07 us
    ppermute x2, starting transfers between devices: 6.95 us -> 11.3 us  [local(): parts.append(lax.ppermute(row_sums, 'blk', back(moves)))]
    ppermute x2, waiting for transfers between devices: 5.99 us -> 2.92 us  [local(): lax.ppermute(to_same, 'blk', moves)]
    ppermute x2, waiting for transfers between devices: 8.15 us -> 9.55 us  [local(): lax.ppermute(to_cross, ('blk', 'sub'), crossed(moves))]
  transfers between devices with their start and end apart: 14 -> 14, of which waited for: 6 -> 5; matrix products, arithmetic and copies ran while one was open for 0% -> 0% of each run, Pallas kernels for 9% -> 14%
where the time goes in v4:
time: 103 us
  Pallas kernels  52.9 us (51%)
  starting transfers between devices  30 us (29%)
  waiting for transfers between devices  19 us (18%)
  local copies, waits for them, and re-layouts  1.1 us (1%)
    pallas_call x1, Pallas kernels, packs_of(): pl.pallas_call(pack_kernel, out_shape=[jax.ShapeDtypeStruct((size, width)...  33 us
    pallas_call x4, Pallas kernels, tile(): pl.pallas_call(body, out_shape=shapes, in_specs=[VMEM_SPEC] * (2 + 2 * le...  15.1 us
    ppermute x2, starting transfers between devices, local(): parts.append(lax.ppermute(row_sums, 'blk', back(moves)))  11.3 us
    ppermute x2, waiting for transfers between devices, local(): lax.ppermute(to_cross, ('blk', 'sub'), crossed(moves))  9.55 us
    ppermute x2, starting transfers between devices, local(): lax.ppermute(to_same, 'blk', moves)  6.69 us
    all_to_all x1, waiting for transfers between devices, local(): grams = lax.all_to_all(copies, ('blk', 'sub'), 0, 0, tiled=True)  5.58 us
    all_to_all x1, starting transfers between devices, local(): grams = lax.all_to_all(copies, ('blk', 'sub'), 0, 0, tiled=True)  4.18 us
    pallas_call x1, Pallas kernels, basis_of(): pl.pallas_call(functools.partial(basis_kernel, total_rows), out_shape=jax...  3.54 us
  transfers between devices with their start and end apart: 14, of which 5 were waited for; matrix products, arithmetic and copies ran while one was open for 0% of the time, Pallas kernels for 14%

profile of v4, /device:TPU:0, one launch (start us, length us, event | category | flops | bytes accessed | tf_op | source)
XLA Modules:
  0.0 103.1 jit_solution(16523328070520106308)
XLA Ops:
  0.0 33.0 %pack.1 = (bf16[1152,256]{1,0:T(8,128)(2,1)}, bf16[576,256]{1,0:T(8,128)(2,1)}, bf16[576,256]{1,0:T(8,128)(2,1)}) custom-call(bf16[1024,256]{1,0:T(8,128)(2,1)} %refs_0_.1, bf16[16,1024]{1,0:T(8,128)(2,1)} %refs_1_.1, s32[4,1024]{1,0:T(4,128)} %refs_2_.1, s32[2,1024]{1,0:T(2,128)} %refs_3_.1, s32[1,1024]{1,0:T(1,128)} %bitcast.1), custom_call_target="tpu_custom_call" | custom-call | tf_op jit(solution)/shard_map/pack/pallas_call | solution.py:123
  33.0 0.5 collective-permute-start
  33.5 2.6 %collective-permute-start.1 = (bf16[1152,256]{1,0:T(8,128)(2,1)}, bf16[1152,256]{1,0:T(8,128)(2,1)S(1)}, u32[]{:S(2)}, u32[]{:S(2)}) collective-permute-start(bf16[1152,256]{1,0:T(8,128)(2,1)} %get-tuple-element.21.refs_0_.refs_2_), channel_id=1, source_target_pairs={{0,2},{2,0},{4,6},{6,4},{8,10},{10,8},{12,14},{14,12},{1,3},{3,1},... | collective-permute-start | bytes 1769480 | tf_op jit(solution)/shard_map/ppermute | solution.py:414
  36.1 3.6 %collective-permute-start.2 = (bf16[576,256]{1,0:T(8,128)(2,1)}, bf16[576,256]{1,0:T(8,128)(2,1)S(1)}, u32[]{:S(2)}, u32[]{:S(2)}) collective-permute-start(bf16[576,256]{1,0:T(8,128)(2,1)} %get-tuple-element.22), channel_id=1, source_target_pairs={{4,0},{6,2},{8,4},{10,6},{12,8},{14,10},{0,12},{2,14},{5,1},{7,3},... | collective-permute-start | bytes 884744 | tf_op jit(solution)/shard_map/ppermute | solution.py:408
  39.7 0.0 collective-permute-start.3
  39.7 0.0 collective-permute-done.refs_1_.refs_3_
  39.7 1.1 %copy-done = bf16[1152,256]{1,0:T(8,128)(2,1)S(1)} copy-done((bf16[1152,256]{1,0:T(8,128)(2,1)S(1)}, bf16[1152,256]{1,0:T(8,128)(2,1)}, u32[]{:S(2)}) %copy-start) | copy-done | bytes 589848
  40.8 3.7 %tile.4.refs_0_ = f32[40,512]{1,0:T(8,128)S(1)} custom-call(bf16[1152,256]{1,0:T(8,128)(2,1)S(1)} %copy-done, bf16[1152,256]{1,0:T(8,128)(2,1)S(1)} %collective-permute-done.refs_1_.refs_3_, bf16[1152,256]{1,0:T(8,128)(2,1)S(1)} %copy-done, bf16[1152,256]{1,0:T(8,128)(2,1)S(1)} %collective-permute-done.refs_1_.refs_3_), custom_call_target="tpu_custom_call" | custom-call | flops 1 | bytes 1 | tf_op jit(solution)/shard_map/tile/pallas_call | solution.py:281
  44.5 2.9 %collective-permute-done.2.refs_0_ = bf16[576,256]{1,0:T(8,128)(2,1)S(1)} collective-permute-done((bf16[576,256]{1,0:T(8,128)(2,1)}, bf16[576,256]{1,0:T(8,128)(2,1)S(1)}, u32[]{:S(2)}, u32[]{:S(2)}) %collective-permute-start.2) | collective-permute-done | bytes 294944 | tf_op jit(solution)/shard_map/ppermute | solution.py:408
  47.4 5.5 %collective-permute-done.3.refs_1_ = bf16[576,256]{1,0:T(8,128)(2,1)S(1)} collective-permute-done((bf16[576,256]{1,0:T(8,128)(2,1)}, bf16[576,256]{1,0:T(8,128)(2,1)S(1)}, u32[]{:S(2)}, u32[]{:S(2)}) %collective-permute-start.3) | collective-permute-done | bytes 294944 | tf_op jit(solution)/shard_map/ppermute | solution.py:408
  52.9 0.0 collective-permute-done.1.refs_2_.refs_4_
  52.9 0.0 collective-permute-start.4
  53.0 3.1 %collective-permute-start.6 = (bf16[576,256]{1,0:T(8,128)(2,1)}, bf16[576,256]{1,0:T(8,128)(2,1)S(1)}, u32[]{:S(2)}, u32[]{:S(2)}) collective-permute-start(bf16[576,256]{1,0:T(8,128)(2,1)} %get-tuple-element.22), channel_id=1, source_target_pairs={{0,8},{2,10},{12,4},{14,6},{1,9},{3,11},{13,5},{15,7},{16,24},{18,... | collective-permute-start | bytes 884744 | tf_op jit(solution)/shard_map/ppermute | solution.py:408
  56.1 2.0 %collective-permute-start.7 = (bf16[576,256]{1,0:T(8,128)(2,1)}, bf16[576,256]{1,0:T(8,128)(2,1)}, u32[]{:S(2)}, u32[]{:S(2)}) collective-permute-start(bf16[576,256]{1,0:T(8,128)(2,1)} %get-tuple-element.23), channel_id=1, source_target_pairs={{1,8},{0,9},{3,10},{2,11},{13,4},{12,5},{15,6},{14,7},{17,24},{16,... | collective-permute-start | bytes 884744 | tf_op jit(solution)/shard_map/ppermute | solution.py:408
  58.1 0.0 collective-permute-done.4.refs_3_.refs_5_
  58.1 7.0 %tile.6 = (f32[40,512]{1,0:T(8,128)S(1)}, f32[40,2048]{1,0:T(8,128)S(1)}) custom-call(bf16[576,256]{1,0:T(8,128)(2,1)S(1)} %collective-permute-done.2.refs_0_, bf16[576,256]{1,0:T(8,128)(2,1)S(1)} %collective-permute-done.3.refs_1_, bf16[1152,256]{1,0:T(8,128)(2,1)S(1)} %copy-done.1, bf16[1152,256]{1,0:T(8,128)(2,1)S(1)} %collective-permute-done.refs_1_.refs_3_, ...), custom_call_target="tpu_custom_call" | custom-call | flops 1 | bytes 1 | tf_op jit(solution)/shard_map/tile/pallas_call | solution.py:281
  65.1 0.0 collective-permute-done.6.refs_0_
  65.1 4.0 %collective-permute-done.7.refs_1_ = bf16[576,256]{1,0:T(8,128)(2,1)} collective-permute-done((bf16[576,256]{1,0:T(8,128)(2,1)}, bf16[576,256]{1,0:T(8,128)(2,1)}, u32[]{:S(2)}, u32[]{:S(2)}) %collective-permute-start.7) | collective-permute-done | bytes 294944 | tf_op jit(solution)/shard_map/ppermute | solution.py:408
  69.1 1.0 tile.7
  70.2 1.0 collective-permute-start.10
  71.2 0.0 collective-permute-start.11
  71.2 1.2 %collective-permute-start.9 = (f32[40,512]{1,0:T(8,128)S(1)}, f32[40,512]{1,0:T(8,128)S(1)}, u32[]{:S(2)}, u32[]{:S(2)}) collective-permute-start(f32[40,512]{1,0:T(8,128)S(1)} %get-tuple-element.39), channel_id=1, source_target_pairs={{0,1},{1,0},{2,3},{3,2},{4,5},{5,4},{6,7},{7,6},{8,9},{9,8},{10,11... | collective-permute-start | bytes 245768 | tf_op jit(solution)/shard_map/ppermute | solution.py:431
  72.4 1.3 %collective-permute-start.8 = (f32[40,512]{1,0:T(8,128)S(1)}, f32[40,512]{1,0:T(8,128)S(1)}, u32[]{:S(2)}, u32[]{:S(2)}) collective-permute-start(f32[40,512]{1,0:T(8,128)S(1)} %get-tuple-element.32), channel_id=1, source_target_pairs={{8,0},{10,2},{4,12},{6,14},{9,1},{11,3},{5,13},{7,15},{24,16},{26,... | collective-permute-start | bytes 245768 | tf_op jit(solution)/shard_map/ppermute | solution.py:423
  73.7 10.1 %collective-permute-start.5 = (f32[40,512]{1,0:T(8,128)S(1)}, f32[40,512]{1,0:T(8,128)S(1)}, u32[]{:S(2)}, u32[]{:S(2)}) collective-permute-start(f32[40,512]{1,0:T(8,128)S(1)} %get-tuple-element.28), channel_id=1, source_target_pairs={{0,4},{2,6},{4,8},{6,10},{8,12},{10,14},{12,0},{14,2},{1,5},{3,7},... | collective-permute-start | bytes 245768 | tf_op jit(solution)/shard_map/ppermute | solution.py:423
  83.7 3.4 %tile.5.refs_1_ = f32[40,512]{1,0:T(8,128)S(1)} custom-call(bf16[1152,256]{1,0:T(8,128)(2,1)S(1)} %copy-done.1, bf16[1152,256]{1,0:T(8,128)(2,1)S(1)} %collective-permute-done.refs_1_.refs_3_, bf16[1152,256]{1,0:T(8,128)(2,1)S(1)} %collective-permute-done.1.refs_2_.refs_4_, bf16[1152,256]{1,0:T(8,128)(2,1)S(1)} %collective-permute-done.4.refs_3_.refs_5_), custom_call_target="tpu_custom_call" | custom-call | flops 1 | bytes 1 | tf_op jit(solution)/shard_map/tile/pallas_call | solution.py:281
  87.2 0.0 collective-permute-done.9.refs_5_
  87.2 1.3 %image.1 = (f32[32,512]{1,0:T(8,128)S(1)}, f32[16,8,128]{2,1,0:T(8,128)}) custom-call(f32[40,512]{1,0:T(8,128)S(1)} %tile.4.refs_0_, f32[40,512]{1,0:T(8,128)S(1)} %tile.5.refs_1_, f32[40,512]{1,0:T(8,128)S(1)} %collective-permute-done.5.refs_2_, f32[40,512]{1,0:T(8,128)S(1)} %collective-permute-done.8.refs_3_, f32[40,512]{1,0:T(8,128)S(1)} %get-tuple-element.40.refs_4_, ...), custom_call_target="tpu_custom_call" | custom-call | tf_op jit(solution)/shard_map/image/pallas_call | solution.py:324
  88.5 4.2 %all-to-all-start = ((f32[16,8,128]{2,1,0:T(8,128)}), f32[16,8,128]{2,1,0:T(8,128)S(1)}, u32[]{:S(2)}, u32[]{:S(2)}) async-start(f32[16,8,128]{2,1,0:T(8,128)} %get-tuple-element.35), calls=%async_computation | async-start | bytes 131072 | tf_op jit(solution)/shard_map/all_to_all | solution.py:437
  92.7 0.4 collective-permute-start.12
  93.1 0.9 collective-permute-done.12.other_ref
  94.0 5.6 %all-to-all-done.grams_ref = f32[16,8,128]{2,1,0:T(8,128)S(1)} async-done(((f32[16,8,128]{2,1,0:T(8,128)}), f32[16,8,128]{2,1,0:T(8,128)S(1)}, u32[]{:S(2)}, u32[]{:S(2)}) %all-to-all-start) | async-done | bytes 65568 | tf_op jit(solution)/shard_map/all_to_all | solution.py:437
  99.6 3.5 %basis.1 = f32[16,1024]{1,0:T(8,128)} custom-call(f32[16,8,128]{2,1,0:T(8,128)S(1)} %all-to-all-done.grams_ref, f32[32,512]{1,0:T(8,128)S(1)} %get-tuple-element.36.mine_ref, f32[32,512]{1,0:T(8,128)S(1)} %collective-permute-done.12.other_ref), custom_call_target="tpu_custom_call" | custom-call | tf_op jit(solution)/shard_map/basis/pallas_call | solution.py:362
  (9 shorter events, 0.1 us)
Async XLA Ops:
  33.0 6.7 %collective-permute-start = (bf16[1152,256]{1,0:T(8,128)(2,1)}, bf16[1152,256]{1,0:T(8,128)(2,1)S(1)}, u32[]{:S(2)}, u32[]{:S(2)}) collective-permute-start(bf16[1152,256]{1,0:T(8,128)(2,1)} %get-tuple-element.21.refs_0_.refs_2_), channel_id=1, source_target_pairs={{0,1},{1,0},{2,3},{3,2},{4,5},{5,4},{6,7},{7,6},{8,9},{9,8},{10,11... | collective-permute-start | bytes 1769480 | tf_op jit(solution)/shard_map/ppermute | solution.py:411
  33.5 19.4 %collective-permute-start.1 = (bf16[1152,256]{1,0:T(8,128)(2,1)}, bf16[1152,256]{1,0:T(8,128)(2,1)S(1)}, u32[]{:S(2)}, u32[]{:S(2)}) collective-permute-start(bf16[1152,256]{1,0:T(8,128)(2,1)} %get-tuple-element.21.refs_0_.refs_2_), channel_id=1, source_target_pairs={{0,2},{2,0},{4,6},{6,4},{8,10},{10,8},{12,14},{14,12},{1,3},{3,1},... | collective-permute-start | bytes 1769480 | tf_op jit(solution)/shard_map/ppermute | solution.py:414
  36.1 11.3 %collective-permute-start.2 = (bf16[576,256]{1,0:T(8,128)(2,1)}, bf16[576,256]{1,0:T(8,128)(2,1)S(1)}, u32[]{:S(2)}, u32[]{:S(2)}) collective-permute-start(bf16[576,256]{1,0:T(8,128)(2,1)} %get-tuple-element.22), channel_id=1, source_target_pairs={{4,0},{6,2},{8,4},{10,6},{12,8},{14,10},{0,12},{2,14},{5,1},{7,3},... | collective-permute-start | bytes 884744 | tf_op jit(solution)/shard_map/ppermute | solution.py:408
  39.7 13.2 %collective-permute-start.3 = (bf16[576,256]{1,0:T(8,128)(2,1)}, bf16[576,256]{1,0:T(8,128)(2,1)S(1)}, u32[]{:S(2)}, u32[]{:S(2)}) collective-permute-start(bf16[576,256]{1,0:T(8,128)(2,1)} %get-tuple-element.23), channel_id=1, source_target_pairs={{5,0},{4,1},{7,2},{6,3},{9,4},{8,5},{11,6},{10,7},{13,8},{12,9},{1... | collective-permute-start | bytes 884744 | tf_op jit(solution)/shard_map/ppermute | solution.py:408
  39.7 1.1 %copy-start = (bf16[1152,256]{1,0:T(8,128)(2,1)S(1)}, bf16[1152,256]{1,0:T(8,128)(2,1)}, u32[]{:S(2)}) copy-start(bf16[1152,256]{1,0:T(8,128)(2,1)} %get-tuple-element.21.refs_0_.refs_2_) | copy-start | bytes 1769476
  40.8 17.3 %copy-start.1 = (bf16[1152,256]{1,0:T(8,128)(2,1)S(1)}, bf16[1152,256]{1,0:T(8,128)(2,1)}, u32[]{:S(2)}) copy-start(bf16[1152,256]{1,0:T(8,128)(2,1)} %get-tuple-element.21.refs_0_.refs_2_) | copy-start | bytes 1769476
  52.9 5.1 %collective-permute-start.4 = (bf16[1152,256]{1,0:T(8,128)(2,1)S(1)}, bf16[1152,256]{1,0:T(8,128)(2,1)S(1)}, u32[]{:S(2)}, u32[]{:S(2)}) collective-permute-start(bf16[1152,256]{1,0:T(8,128)(2,1)S(1)} %collective-permute-done.1.refs_2_.refs_4_), channel_id=1, source_target_pairs={{0,1},{1,0},{2,3},{3,2},{4,5},{5,4},{6,7},{7,6},{8,9},{9,8},{10,11... | collective-permute-start | bytes 1769480 | tf_op jit(solution)/shard_map/ppermute | solution.py:416
  53.0 12.1 %collective-permute-start.6 = (bf16[576,256]{1,0:T(8,128)(2,1)}, bf16[576,256]{1,0:T(8,128)(2,1)S(1)}, u32[]{:S(2)}, u32[]{:S(2)}) collective-permute-start(bf16[576,256]{1,0:T(8,128)(2,1)} %get-tuple-element.22), channel_id=1, source_target_pairs={{0,8},{2,10},{12,4},{14,6},{1,9},{3,11},{13,5},{15,7},{16,24},{18,... | collective-permute-start | bytes 884744 | tf_op jit(solution)/shard_map/ppermute | solution.py:408
  56.1 13.0 %collective-permute-start.7 = (bf16[576,256]{1,0:T(8,128)(2,1)}, bf16[576,256]{1,0:T(8,128)(2,1)}, u32[]{:S(2)}, u32[]{:S(2)}) collective-permute-start(bf16[576,256]{1,0:T(8,128)(2,1)} %get-tuple-element.23), channel_id=1, source_target_pairs={{1,8},{0,9},{3,10},{2,11},{13,4},{12,5},{15,6},{14,7},{17,24},{16,... | collective-permute-start | bytes 884744 | tf_op jit(solution)/shard_map/ppermute | solution.py:408
  70.2 17.0 %collective-permute-start.10 = (f32[40,512]{1,0:T(8,128)S(1)}, f32[40,512]{1,0:T(8,128)S(1)}, u32[]{:S(2)}, u32[]{:S(2)}) collective-permute-start(f32[40,512]{1,0:T(8,128)S(1)} %get-tuple-element.38), channel_id=1, source_target_pairs={{0,2},{2,0},{4,6},{6,4},{8,10},{10,8},{12,14},{14,12},{1,3},{3,1},... | collective-permute-start | bytes 245768 | tf_op jit(solution)/shard_map/ppermute | solution.py:432
  71.2 16.0 %collective-permute-start.11 = (f32[40,512]{1,0:T(8,128)S(1)}, f32[40,512]{1,0:T(8,128)S(1)}, u32[]{:S(2)}, u32[]{:S(2)}) collective-permute-start(f32[40,512]{1,0:T(8,128)S(1)} %get-tuple-element.37), channel_id=1, source_target_pairs={{1,2},{0,3},{3,0},{2,1},{5,6},{4,7},{7,4},{6,5},{9,10},{8,11},{11,... | collective-permute-start | bytes 245768 | tf_op jit(solution)/shard_map/ppermute | solution.py:433
  71.2 16.0 %collective-permute-start.9 = (f32[40,512]{1,0:T(8,128)S(1)}, f32[40,512]{1,0:T(8,128)S(1)}, u32[]{:S(2)}, u32[]{:S(2)}) collective-permute-start(f32[40,512]{1,0:T(8,128)S(1)} %get-tuple-element.39), channel_id=1, source_target_pairs={{0,1},{1,0},{2,3},{3,2},{4,5},{5,4},{6,7},{7,6},{8,9},{9,8},{10,11... | collective-permute-start | bytes 245768 | tf_op jit(solution)/shard_map/ppermute | solution.py:431
  72.4 14.8 %collective-permute-start.8 = (f32[40,512]{1,0:T(8,128)S(1)}, f32[40,512]{1,0:T(8,128)S(1)}, u32[]{:S(2)}, u32[]{:S(2)}) collective-permute-start(f32[40,512]{1,0:T(8,128)S(1)} %get-tuple-element.32), channel_id=1, source_target_pairs={{8,0},{10,2},{4,12},{6,14},{9,1},{11,3},{5,13},{7,15},{24,16},{26,... | collective-permute-start | bytes 245768 | tf_op jit(solution)/shard_map/ppermute | solution.py:423
  73.7 13.5 %collective-permute-start.5 = (f32[40,512]{1,0:T(8,128)S(1)}, f32[40,512]{1,0:T(8,128)S(1)}, u32[]{:S(2)}, u32[]{:S(2)}) collective-permute-start(f32[40,512]{1,0:T(8,128)S(1)} %get-tuple-element.28), channel_id=1, source_target_pairs={{0,4},{2,6},{4,8},{6,10},{8,12},{10,14},{12,0},{14,2},{1,5},{3,7},... | collective-permute-start | bytes 245768 | tf_op jit(solution)/shard_map/ppermute | solution.py:423
  88.5 11.1 %all-to-all-start = ((f32[16,8,128]{2,1,0:T(8,128)}), f32[16,8,128]{2,1,0:T(8,128)S(1)}, u32[]{:S(2)}, u32[]{:S(2)}) async-start(f32[16,8,128]{2,1,0:T(8,128)} %get-tuple-element.35), calls=%async_computation | async-start | bytes 131072 | tf_op jit(solution)/shard_map/all_to_all | solution.py:437
  92.7 1.3 %collective-permute-start.12 = (f32[32,512]{1,0:T(8,128)S(1)}, f32[32,512]{1,0:T(8,128)S(1)}, u32[]{:S(2)}, u32[]{:S(2)}) collective-permute-start(f32[32,512]{1,0:T(8,128)S(1)} %get-tuple-element.36.mine_ref), channel_id=1, source_target_pairs={{0,1},{1,0},{2,3},{3,2},{4,5},{5,4},{6,7},{7,6},{8,9},{9,8},{10,11... | collective-permute-start | bytes 196616 | tf_op jit(solution)/shard_map/ppermute | solution.py:436

commit v5 on v3

v5 whole, which is shorter than its diff:
```python
import functools
import math

import jax
import jax.numpy as jnp
from jax import lax
from jax.experimental import pallas as pl
from jax.experimental.pallas import tpu as pltpu
from jax.sharding import PartitionSpec as P

SHARPNESS = 10.0
HORIZON = 2000.0
MARGIN = 8.0
EPSILON = 1e-06

LOG2E = math.log2(math.e)
COS_SCALE = math.sqrt(SHARPNESS * LOG2E)
GAP_SCALE = LOG2E / HORIZON
BASE = SHARPNESS * LOG2E + 1.0
BARRED_BELOW = BASE - 0.5 * GAP_SCALE

FIELDS = 9
LEFT, RIGHT, BOTTOM, TOP, FIRST, LAST, CAMERA, NORM, AREA = range(FIELDS)
CODE_ROWS = 16
LANES = 128
CHUNK = 256
OUT_ROWS = 40
COST = 1
SWAPS = 2
VMEM_LIMIT = 48 * 1024 * 1024

NT = (((1,), (1,)), ((), ()))
VMEM_SPEC = pl.BlockSpec(memory_space=pltpu.VMEM)


def params():
    return pltpu.CompilerParams(vmem_limit_bytes=VMEM_LIMIT)


def dot_nt(a, b, precision=None):
    return lax.dot_general(a, b, NT, precision=precision, preferred_element_type=jnp.float32)


def pack_rows(half, vecs):
    return half + vecs + CODE_ROWS


def pack_kernel(emb_ref, emb_other_ref, vec_ref, vec_other_ref, meta_ref, own_ref, mine_ref, code_ref):
    sub = lax.axis_index("sub")
    rows, width = emb_ref.shape
    half = rows // 2
    half_vecs = vec_ref.shape[0]
    ones = jnp.ones((8, width), jnp.bfloat16)
    for start in range(0, rows, CHUNK):
        part = pl.ds(start, CHUNK)
        codes = []

        def whole(number, low_bits):
            codes.append((number >> low_bits) << low_bits)
            codes.append(number & ((1 << low_bits) - 1))

        boxes, spans = meta_ref[0:4, part], meta_ref[4:6, part]
        for axis in range(2):
            whole(jnp.minimum(boxes[axis : axis + 1], boxes[axis + 2 : axis + 3]), 5)
            whole(jnp.maximum(boxes[axis : axis + 1], boxes[axis + 2 : axis + 3]), 5)
        whole(jnp.minimum(spans[0:1], spans[1:2]), 7)
        whole(jnp.maximum(spans[0:1], spans[1:2]), 7)
        codes.append(meta_ref[6:7, part])
        codes = [code.astype(jnp.float32) for code in codes]
        rest = jnp.zeros((8, CHUNK), jnp.float32)
        for ref in (emb_ref, emb_other_ref):
            values = ref[part, :].astype(jnp.float32)
            square = values * values
            high = square.astype(jnp.bfloat16)
            low = (square - high.astype(jnp.float32)).astype(jnp.bfloat16)
            rest = rest + (dot_nt(ones, high) + dot_nt(ones, low))
        rest = rest[0:1]
        for _ in range(3):
            piece = rest.astype(jnp.bfloat16).astype(jnp.float32)
            codes.append(piece)
            rest = rest - piece
        code_ref[:, part] = jnp.concatenate(codes, axis=0).astype(jnp.bfloat16)
    size = mine_ref.shape[0]
    targets = [(own_ref, 0, sub), (own_ref, size, 1 - sub), (mine_ref, 0, sub)]
    for ref, base, place in targets:
        source = pl.ds(pl.multiple_of(place * half, half), half)
        sides = ((emb_ref, vec_ref, sub), (emb_other_ref, vec_other_ref, 1 - sub))
        for values_ref, vectors_ref, side in sides:
            ref[base : base + half, pl.ds(pl.multiple_of(side * width, width), width)] = values_ref[source, :]
            first_vec = pl.multiple_of(base + half + side * half_vecs, 16)
            ref[pl.ds(first_vec, half_vecs), :] = vectors_ref[:, source]
        first_code = base + half + 2 * half_vecs
        ref[first_code : first_code + CODE_ROWS, :] = code_ref[:, source]


def packs_of(embeddings, emb_other, vectors, vec_other, meta):
    rows, width = embeddings.shape
    half, features = rows // 2, 2 * width
    assert half == features
    size = pack_rows(half, 2 * vectors.shape[0])
    return pl.pallas_call(
        pack_kernel,
        out_shape=[jax.ShapeDtypeStruct((count * size, features), jnp.bfloat16) for count in (2, 1)],
        in_specs=[VMEM_SPEC] * 5,
        out_specs=[VMEM_SPEC] * 2,
        scratch_shapes=[pltpu.VMEM((CODE_ROWS, rows), jnp.bfloat16)],
        compiler_params=params(),
        name="pack",
    )(embeddings, emb_other, vectors, vec_other, meta)


def decode(codes):
    codes = codes.astype(jnp.float32)
    numbers = [codes[2 * index : 2 * index + 1] + codes[2 * index + 1 : 2 * index + 2] for index in range(6)]
    left, right, bottom, top, first, last = numbers
    right, top = right + MARGIN, top + MARGIN
    square = codes[15:16] + codes[14:15] + codes[13:14]
    norm = lax.rsqrt(square + EPSILON) * COS_SCALE
    area = (right - left) * (top - bottom)
    return [left, right, bottom, top, first * GAP_SCALE + BASE, last * GAP_SCALE, codes[12:13], norm, area]


def with_ones(vectors):
    shape = (CODE_ROWS, vectors.shape[1])
    tail = jnp.where(lax.broadcasted_iota(jnp.int32, shape, 0) == 0, 1.0, 0.0)
    return jnp.concatenate([vectors, tail.astype(jnp.bfloat16)], axis=0)


def weights_of(products, row, col, same):
    logit = products * row[NORM] * col[NORM]
    gap = jnp.maximum(col[FIRST] - row[LAST], row[FIRST] - col[LAST])
    width = jnp.maximum(jnp.minimum(row[RIGHT], col[RIGHT]) - jnp.maximum(row[LEFT], col[LEFT]), 0.0)
    height = jnp.maximum(jnp.minimum(row[TOP], col[TOP]) - jnp.maximum(row[BOTTOM], col[BOTTOM]), 0.0)
    inter = width * height
    both = row[AREA] + col[AREA]
    share = (both + inter) * pl.reciprocal(both - inter, approx=True)
    value = jnp.exp2(logit - jnp.maximum(gap, BASE)) * share
    barred = (row[CAMERA] == col[CAMERA]) & (gap < BARRED_BELOW)
    if same is not None:
        barred = barred & jnp.logical_not(same)
    return jnp.where(barred, 0.0, value)


def tile_kernel(blocks, own_block, receivers, vecs, *refs):
    row_ref, col_refs = refs[0], refs[1 : 1 + blocks]
    row_out_ref, col_out_ref, field_ref, spread_ref = refs[1 + blocks : 5 + blocks]
    products, weights = refs[5 + blocks : 7 + blocks], refs[7 + blocks :]
    rows = row_out_ref.shape[1]
    size = row_ref.shape[0]
    per_pack = rows // CHUNK
    row_out_ref[...] = jnp.zeros_like(row_out_ref)

    def block(col_ref, done, row_vecs):
        chunks = col_ref.shape[0] // size * per_pack

        def within(step):
            pack, chunk = step // per_pack, lax.rem(step, per_pack)
            return pack * size, pl.multiple_of(chunk * CHUNK, CHUNK)

        def multiply(step, product_ref):
            base, start = within(step)
            columns = col_ref[pl.ds(pl.multiple_of(base + start, 16), CHUNK), :]
            product_ref[...] = dot_nt(row_ref[0:rows, :], columns)

        def weigh(step, product_ref, weight_ref):
            base, start = within(step)
            code_part = pl.ds(pl.multiple_of(base + rows + vecs, 16), CODE_ROWS)
            col = decode(col_ref[code_part, pl.ds(start, CHUNK)])
            col = [jnp.broadcast_to(field, (8, CHUNK)) for field in col]
            for first_row in range(0, rows, 16):
                both = []
                for line in (first_row, first_row + 8):
                    row = [
                        jnp.concatenate([spread_ref[field, line : line + 8, :]] * (CHUNK // LANES), axis=1)
                        for field in range(FIELDS)
                    ]
                    same = None
                    if own_block:
                        row_ids = lax.broadcasted_iota(jnp.int32, (8, CHUNK), 0) + (line - step * CHUNK)
                        same = row_ids == lax.broadcasted_iota(jnp.int32, (8, CHUNK), 1)
                    both.append(weights_of(product_ref[line : line + 8, :], row, col, same))
                weight_ref[first_row : first_row + 16, :] = jnp.concatenate(both, axis=0).astype(jnp.bfloat16)

        def total(step, weight_ref):
            base, start = within(step)
            vec_part = pl.ds(pl.multiple_of(base + rows, 16), vecs)
            col_vecs = with_ones(col_ref[vec_part, pl.ds(start, CHUNK)])
            row_out_ref[...] += dot_nt(col_vecs, weight_ref[...])[0:OUT_ROWS]
            if col_out_ref is not None:
                col_out_ref[:, pl.ds(pl.multiple_of(done + step * CHUNK, CHUNK), CHUNK)] = jnp.dot(
                    row_vecs, weight_ref[...], preferred_element_type=jnp.float32
                )[0:OUT_ROWS]

        def steps(index, carry):
            for parity in range(2):
                step = 2 * index + parity
                multiply(lax.rem(step + 1, chunks), products[1 - parity])
                weigh(step, products[parity], weights[parity])
                total(lax.rem(step + chunks - 1, chunks), weights[1 - parity])
            return carry

        multiply(0, products[0])
        weights[1][...] = jnp.zeros_like(weights[1])
        lax.fori_loop(0, chunks // 2, steps, 0)
        total(chunks - 1, weights[1])

    def compute():
        for field, values in enumerate(decode(row_ref[rows + vecs : rows + vecs + CODE_ROWS, :])):
            field_ref[field : field + 1, :] = values
        turned = field_ref[...].T
        for field in range(FIELDS):
            spread_ref[field] = jnp.broadcast_to(turned[:, field : field + 1], (rows, LANES))
        row_vecs = with_ones(row_ref[rows : rows + vecs, :])
        done = 0
        for col_ref in col_refs:
            block(col_ref, done, row_vecs)
            done += col_ref.shape[0] // size * rows

    if receivers is None:
        compute()
        return
    pair = lax.axis_index("blk") // 2
    takes_part = functools.reduce(jnp.logical_or, [pair == one for one in receivers])

    @pl.when(takes_part)
    def _():
        compute()

    @pl.when(jnp.logical_not(takes_part))
    def _():
        col_out_ref[...] = jnp.zeros_like(col_out_ref)


def tile(row, columns, vecs, own_block=False, col_sums=True, receivers=None):
    size, rows = row.shape
    cols = sum(part.shape[0] // size for part in columns) * rows
    shapes = [jax.ShapeDtypeStruct((OUT_ROWS, rows), jnp.float32)]
    if col_sums:
        shapes.append(jax.ShapeDtypeStruct((OUT_ROWS, cols), jnp.float32))

    def body(*refs):
        refs = list(refs)
        if not col_sums:
            refs.insert(2 + len(columns), None)
        tile_kernel(len(columns), own_block, receivers, vecs, *refs)

    return pl.pallas_call(
        body,
        out_shape=shapes,
        in_specs=[VMEM_SPEC] * (1 + len(columns)),
        out_specs=[VMEM_SPEC] * len(shapes),
        scratch_shapes=[
            pltpu.VMEM((LANES, rows), jnp.float32),
            pltpu.VMEM((FIELDS, rows, LANES), jnp.float32),
            pltpu.VMEM((rows, CHUNK), jnp.float32),
            pltpu.VMEM((rows, CHUNK), jnp.float32),
            pltpu.VMEM((rows, CHUNK), jnp.bfloat16),
            pltpu.VMEM((rows, CHUNK), jnp.bfloat16),
        ],
        cost_estimate=pl.CostEstimate(flops=COST, bytes_accessed=COST, transcendentals=0),
        compiler_params=params(),
        name="tile",
    )(row, *columns)


def image_kernel(*refs):
    parts, image_ref, grams_ref = refs[:-2], refs[-2], refs[-1]
    total = parts[0][...]
    for part in parts[1:]:
        total = total + part[...]
    vecs = image_ref.shape[0]
    image = total[0:vecs] / total[vecs : vecs + 1]
    image_ref[...] = image
    packed = jnp.zeros((8, LANES), jnp.float32)
    for piece in range(LANES // vecs):
        shifted = [image]
        if piece > 0:
            shifted.insert(0, jnp.zeros((piece * vecs, image.shape[1]), jnp.float32))
        if piece < LANES // vecs - 1:
            shifted.append(jnp.zeros((LANES - (piece + 1) * vecs, image.shape[1]), jnp.float32))
        packed = packed + dot_nt(image[8 * piece : 8 * piece + 8], jnp.concatenate(shifted, axis=0), lax.Precision.HIGHEST)
    for copy in range(grams_ref.shape[0]):
        grams_ref[copy] = packed


def image_of(parts, vecs, copies):
    cols = parts[0].shape[1]
    return pl.pallas_call(
        image_kernel,
        out_shape=[
            jax.ShapeDtypeStruct((vecs, cols), jnp.float32),
            jax.ShapeDtypeStruct((copies, 8, LANES), jnp.float32),
        ],
        in_specs=[VMEM_SPEC] * len(parts),
        out_specs=[VMEM_SPEC] * 2,
        compiler_params=params(),
        name="image",
    )(*parts)


def basis_kernel(total_rows, grams_ref, mine_ref, other_ref, out_ref, inverse_ref):
    vecs, half = mine_ref.shape
    sub = lax.axis_index("sub")
    packed = jnp.sum(grams_ref[...], axis=0) / total_rows
    lane = lax.broadcasted_iota(jnp.int32, (vecs, LANES), 1)
    line = lax.broadcasted_iota(jnp.int32, (vecs, LANES), 0)
    pieces = [packed] + [pltpu.roll(packed, LANES - piece * vecs, 1) for piece in range(1, LANES // vecs)]
    matrix = jnp.where(lane < vecs, jnp.concatenate(pieces, axis=0), 0.0)
    matrix = jnp.where(lane == line + vecs, 1.0, matrix)
    for step in range(vecs - 1):
        column = jnp.broadcast_to(matrix[:, step : step + 1], (vecs, LANES))
        scaled = matrix[step : step + 1, :] / column[step : step + 1, :]
        matrix = jnp.where(line > step, matrix - column * scaled, matrix)
    pivots = jnp.sum(jnp.where(lane == line, matrix, 0.0), axis=1, keepdims=True)
    inverse_ref[...] = pltpu.roll(matrix / jnp.sqrt(pivots), LANES - vecs, 1)
    share = vecs // 2
    own_rows = inverse_ref[pl.ds(pl.multiple_of(sub * share, 8), share), :][:, 0:vecs]
    for ref, place in ((mine_ref, sub), (other_ref, 1 - sub)):
        out_ref[:, pl.ds(pl.multiple_of(place * half, LANES), half)] = jnp.dot(
            own_rows, ref[...], precision=lax.Precision.HIGHEST, preferred_element_type=jnp.float32
        )


def basis_of(grams, mine, other, total_rows):
    vecs, half = mine.shape
    return pl.pallas_call(
        functools.partial(basis_kernel, total_rows),
        out_shape=jax.ShapeDtypeStruct((vecs // 2, 2 * half), jnp.float32),
        in_specs=[VMEM_SPEC] * 3,
        out_specs=VMEM_SPEC,
        scratch_shapes=[pltpu.VMEM((vecs, LANES), jnp.float32)],
        compiler_params=params(),
        name="basis",
    )(grams, mine, other)


def exchanges(pairs):
    plans = []
    for distance in range(1, pairs // 2):
        plans.append(([((p + distance) % pairs, p) for p in range(pairs)], None))
    if pairs > 1:
        half = pairs // 2
        last = [(p, p + half) if p % 2 == 0 else (p + half, p) for p in range(half)]
        plans.append((last, sorted(taker for _, taker in last)))
    return plans


def block_moves(pair_moves):
    return [(2 * source + member, 2 * target + member) for source, target in pair_moves for member in range(2)]


def back(moves):
    return [(target, source) for source, target in moves]


def local(embeddings, vectors, boxes, spans, camera):
    rows = embeddings.shape[0]
    half = rows // 2
    vecs = 2 * vectors.shape[0]
    blocks = lax.axis_size("blk")
    devices = 2 * blocks
    swap = [(0, 1), (1, 0)]
    beside = [(block, block ^ 1) for block in range(blocks)]
    plans = [(block_moves(moves), takers) for moves, takers in exchanges(blocks // 2)]

    def crossed(moves):
        return [(2 * source + 1 - core, 2 * target + core) for source, target in moves for core in range(2)]

    emb_other = lax.ppermute(embeddings, "sub", swap)
    vec_other = lax.ppermute(vectors, "sub", swap)
    meta = jnp.concatenate([boxes, spans, camera[None, :]], axis=0)
    own, mine = packs_of(embeddings, emb_other, vectors, vec_other, meta)
    sent = [lax.ppermute(mine, "blk", moves) for moves, _ in plans]
    beside_mine = lax.ppermute(mine, "blk", beside)
    weigh = functools.partial(tile, vecs=vecs)
    own_sums = weigh(mine, [own], own_block=True, col_sums=False)[0]
    own_sums, beside_mine, sent[:1] = lax.optimization_barrier((own_sums, beside_mine, sent[:1]))
    cut = beside_mine.shape[0] // SWAPS // 16 * 16
    shares = [beside_mine[at * cut : (at + 1) * cut if at < SWAPS - 1 else None] for at in range(SWAPS)]
    next_to = jnp.concatenate([beside_mine] + [lax.ppermute(share, "sub", swap) for share in shares], axis=0)
    parts = [own_sums, weigh(mine, [next_to], col_sums=False)[0]]
    col_sums = None
    for (moves, takers), pack in zip(plans, sent):
        if col_sums is not None:
            pack, col_sums = lax.optimization_barrier((pack, col_sums))
        row_sums, sums = weigh(pack, [own, next_to], receivers=takers)
        parts.append(lax.ppermute(row_sums, "blk", back(moves)))
        col_sums = sums if col_sums is None else col_sums + sums
    if col_sums is not None:
        pieces = [col_sums[:, place * half : (place + 1) * half] for place in range(4)]
        parts.append(pieces[0])
        parts.append(lax.ppermute(pieces[1], "sub", swap))
        parts.append(lax.ppermute(pieces[2], "blk", beside))
        parts.append(lax.ppermute(pieces[3], ("blk", "sub"), crossed(beside)))

    image, copies = image_of(parts, vecs, devices)
    image_other = lax.ppermute(image, "sub", swap)
    grams = lax.all_to_all(copies, ("blk", "sub"), 0, 0, tiled=True)
    return basis_of(grams, image, image_other, blocks * rows)


def solution(mesh):
    placed = (
        P(("groups", "blk"), "sub"),
        P("sub", ("groups", "blk")),
        P(None, ("groups", "blk")),
        P(None, ("groups", "blk")),
        P(("groups", "blk")),
    )
    return jax.shard_map(
        local, mesh=mesh, in_specs=placed, out_specs=P("sub", ("groups", "blk")), check_vma=False
    )
```

time: 79.2 us -> 68.1 us (0.86)
  waiting for transfers between devices: 27.8 us -> 20.1 us
  local copies, waits for them, and re-layouts: 5.62 us -> 1.94 us
  Pallas kernels: 21 us -> 19.6 us
  starting transfers between devices: 24 us -> 25.2 us
    ppermute x10, waiting for transfers between devices: 21.3 us -> 12.8 us  [the longest x2 5.82 us: local(): sent = [lax.ppermute(mine, 'blk', moves) for moves, _ in plans]]
    unnamed x14 -> x6, local copies, waits for them, and re-layouts: 5.58 us -> 1.86 us
    ppermute x2, starting transfers between devices: 6.95 us -> 9.92 us  [local(): parts.append(lax.ppermute(row_sums, 'blk', back(moves)))]
    ppermute x10, starting transfers between devices: 12.8 us -> 11.3 us  [the longest x2 4.97 us: local(): sent = [lax.ppermute(mine, 'blk', moves) for moves, _ in plans]]
    pallas_call x5, Pallas kernels: 16.2 us -> 14.8 us  [the longest x4 14 us: tile(): pl.pallas_call(body, out_shape=shapes, in_specs=[VMEM_SPEC] * (1 + len(co...]
    ppermute x2, waiting for transfers between devices: 0.01 us -> 0.81 us  [local(): parts.append(lax.ppermute(row_sums, 'blk', back(moves)))]
  transfers between devices with their start and end apart: 14 -> 14, of which waited for: 6 -> 9; matrix products, arithmetic and copies ran while one was open for 0% -> 1% of each run, Pallas kernels for 9% -> 21%
where the time goes in v5:
time: 68.1 us; the launch traced here: 67.7 us
  starting transfers between devices  25.2 us (37%)
  waiting for transfers between devices  20.1 us (30%)
  Pallas kernels  19.6 us (29%)
  local copies, waits for them, and re-layouts  1.94 us (3%)
  other arithmetic  0.8 us (1%)
    pallas_call x4, Pallas kernels, tile(): pl.pallas_call(body, out_shape=shapes, in_specs=[VMEM_SPEC] * (1 + len(co...  14 us
    ppermute x2, starting transfers between devices, local(): parts.append(lax.ppermute(row_sums, 'blk', back(moves)))  9.92 us
    ppermute x2, waiting for transfers between devices, local(): sent = [lax.ppermute(mine, 'blk', moves) for moves, _ in plans]  5.82 us
    all_to_all x1, waiting for transfers between devices, local(): grams = lax.all_to_all(copies, ('blk', 'sub'), 0, 0, tiled=True)  5.58 us
    ppermute x2, starting transfers between devices, local(): sent = [lax.ppermute(mine, 'blk', moves) for moves, _ in plans]  4.97 us
    ppermute x1, waiting for transfers between devices, local(): beside_mine = lax.ppermute(mine, 'blk', beside)  4.65 us
    all_to_all x1, starting transfers between devices, local(): grams = lax.all_to_all(copies, ('blk', 'sub'), 0, 0, tiled=True)  3.59 us
    pallas_call x1, Pallas kernels, basis_of(): pl.pallas_call(functools.partial(basis_kernel, total_rows), out_shape=jax...  3.54 us
  transfers between devices with their start and end apart: 14, of which 9 were waited for; matrix products, arithmetic and copies ran while one was open for 1% of the time, Pallas kernels for 21%

profile of v5, /device:TPU:0, one launch (start us, length us, event | category | flops | bytes accessed | tf_op | source)
XLA Modules:
  0.0 67.7 jit_solution(15679727822978859039)
XLA Ops:
  0.0 0.5 collective-permute-start
  0.5 0.1 collective-permute-start.1
  0.5 0.8 %pad_add_fusion.meta_ref = s32[7,1024]{1,0:T(8,128)S(1)} fusion(s32[1,1024]{1,0:T(1,128)} %bitcast.1, s32[2,1024]{1,0:T(2,128)} %param.8, s32[4,1024]{1,0:T(4,128)} %param.7), kind=kLoop, calls=%fused_computation | loop fusion | flops 14336 | bytes 57344 | tf_op jit(solution)/shard_map/concatenate | solution.py:371
  1.3 1.0 %collective-permute-done.1.vec_other_ref = bf16[16,1024]{1,0:T(8,128)(2,1)S(1)} collective-permute-done((bf16[16,1024]{1,0:T(8,128)(2,1)}, bf16[16,1024]{1,0:T(8,128)(2,1)S(1)}, u32[]{:S(2)}, u32[]{:S(2)}) %collective-permute-start.1) | collective-permute-done | bytes 32800 | tf_op jit(solution)/shard_map/ppermute | solution.py:370
  2.3 1.0 %copy-done = bf16[1024,256]{1,0:T(8,128)(2,1)S(1)} copy-done((bf16[1024,256]{1,0:T(8,128)(2,1)S(1)}, bf16[1024,256]{1,0:T(8,128)(2,1)}, u32[]{:S(2)}) %copy-start) | copy-done | bytes 524312
  3.3 0.8 %copy-done.1 = bf16[16,1024]{1,0:T(8,128)(2,1)S(1)} copy-done((bf16[16,1024]{1,0:T(8,128)(2,1)S(1)}, bf16[16,1024]{1,0:T(8,128)(2,1)}, u32[]{:S(2)}) %copy-start.1) | copy-done | bytes 32792
  4.1 0.8 %pack.1 = (bf16[1120,512]{1,0:T(8,128)(2,1)S(1)}, bf16[560,512]{1,0:T(8,128)(2,1)S(1)}) custom-call(bf16[1024,256]{1,0:T(8,128)(2,1)S(1)} %copy-done, bf16[1024,256]{1,0:T(8,128)(2,1)S(1)} %collective-permute-done.emb_other_ref, bf16[16,1024]{1,0:T(8,128)(2,1)S(1)} %copy-done.1, bf16[16,1024]{1,0:T(8,128)(2,1)S(1)} %collective-permute-done.1.vec_other_ref, ...), custom_call_target="tpu_custom_call" | custom-call | tf_op jit(solution)/shard_map/pack/pallas_call | solution.py:101
  4.8 3.0 %collective-permute-start.2 = (bf16[560,512]{1,0:T(8,128)(2,1)S(1)}, bf16[560,512]{1,0:T(8,128)(2,1)S(1)}, u32[]{:S(2)}, u32[]{:S(2)}) collective-permute-start(bf16[560,512]{1,0:T(8,128)(2,1)S(1)} %get-tuple-element.18.refs_0_), channel_id=1, source_target_pairs={{0,2},{2,0},{4,6},{6,4},{8,10},{10,8},{12,14},{14,12},{1,3},{3,1},... | collective-permute-start | bytes 1720328 | tf_op jit(solution)/shard_map/ppermute | solution.py:374
  7.8 3.6 %collective-permute-start.3 = (bf16[560,512]{1,0:T(8,128)(2,1)S(1)}, bf16[560,512]{1,0:T(8,128)(2,1)S(1)}, u32[]{:S(2)}, u32[]{:S(2)}) collective-permute-start(bf16[560,512]{1,0:T(8,128)(2,1)S(1)} %get-tuple-element.18.refs_0_), channel_id=1, source_target_pairs={{4,0},{6,2},{8,4},{10,6},{12,8},{14,10},{0,12},{2,14},{5,1},{7,3},... | collective-permute-start | bytes 1720328 | tf_op jit(solution)/shard_map/ppermute | solution.py:373
  11.4 1.4 %collective-permute-start.7 = (bf16[560,512]{1,0:T(8,128)(2,1)S(1)}, bf16[560,512]{1,0:T(8,128)(2,1)S(1)}, u32[]{:S(2)}, u32[]{:S(2)}) collective-permute-start(bf16[560,512]{1,0:T(8,128)(2,1)S(1)} %get-tuple-element.18.refs_0_), channel_id=1, source_target_pairs={{0,8},{2,10},{12,4},{14,6},{1,9},{3,11},{13,5},{15,7},{16,24},{18,... | collective-permute-start | bytes 1720328 | tf_op jit(solution)/shard_map/ppermute | solution.py:373
  12.7 3.6 %tile.4.refs_0_ = f32[40,512]{1,0:T(8,128)S(1)} custom-call(bf16[560,512]{1,0:T(8,128)(2,1)S(1)} %get-tuple-element.18.refs_0_, bf16[1120,512]{1,0:T(8,128)(2,1)S(1)} %get-tuple-element.19.refs_1_), custom_call_target="tpu_custom_call" | custom-call | flops 1 | bytes 1 | tf_op jit(solution)/shard_map/tile/pallas_call | solution.py:247
  16.4 4.6 %collective-permute-done.2 = bf16[560,512]{1,0:T(8,128)(2,1)S(1)} collective-permute-done((bf16[560,512]{1,0:T(8,128)(2,1)S(1)}, bf16[560,512]{1,0:T(8,128)(2,1)S(1)}, u32[]{:S(2)}, u32[]{:S(2)}) %collective-permute-start.2) | collective-permute-done | bytes 573472 | tf_op jit(solution)/shard_map/ppermute | solution.py:374
  21.1 3.7 %collective-permute-done.3.refs_0_ = bf16[560,512]{1,0:T(8,128)(2,1)S(1)} collective-permute-done((bf16[560,512]{1,0:T(8,128)(2,1)S(1)}, bf16[560,512]{1,0:T(8,128)(2,1)S(1)}, u32[]{:S(2)}, u32[]{:S(2)}) %collective-permute-start.3) | collective-permute-done | bytes 573472 | tf_op jit(solution)/shard_map/ppermute | solution.py:373
  24.8 0.1 collective-permute-start.4
  24.9 0.6 collective-permute-start.5
  25.5 0.9 %collective-permute-done.4 = bf16[272,512]{1,0:T(8,128)(2,1)S(1)} collective-permute-done((bf16[272,512]{1,0:T(8,128)(2,1)S(1)}, bf16[272,512]{1,0:T(8,128)(2,1)S(1)}, u32[]{:S(2)}, u32[]{:S(2)}) %collective-permute-start.4) | collective-permute-done | bytes 278560 | tf_op jit(solution)/shard_map/ppermute | solution.py:380
  26.4 0.4 collective-permute-done.5
  26.8 6.9 %tile.6 = (f32[40,512]{1,0:T(8,128)S(1)}, f32[40,2048]{1,0:T(8,128)S(1)}) custom-call(bf16[560,512]{1,0:T(8,128)(2,1)S(1)} %collective-permute-done.3.refs_0_, bf16[1120,512]{1,0:T(8,128)(2,1)S(1)} %get-tuple-element.19.refs_1_, bf16[1120,512]{1,0:T(8,128)(2,1)S(1)} %constant_dynamic-update-slice_fusion.refs_1_.refs_2_), custom_call_target="tpu_custom_call" | custom-call | flops 1 | bytes 1 | tf_op jit(solution)/shard_map/tile/pallas_call | solution.py:247
  33.8 2.1 %collective-permute-done.7.refs_0_ = bf16[560,512]{1,0:T(8,128)(2,1)S(1)} collective-permute-done((bf16[560,512]{1,0:T(8,128)(2,1)S(1)}, bf16[560,512]{1,0:T(8,128)(2,1)S(1)}, u32[]{:S(2)}, u32[]{:S(2)}) %collective-permute-start.7) | collective-permute-done | bytes 573472 | tf_op jit(solution)/shard_map/ppermute | solution.py:373
  36.0 0.6 collective-permute-start.10
  36.6 1.6 %collective-permute-start.9 = (f32[40,512]{1,0:T(8,128)S(1)}, f32[40,512]{1,0:T(8,128)S(1)}, u32[]{:S(2)}, u32[]{:S(2)}) collective-permute-start(f32[40,512]{1,0:T(8,128)S(1)} %get-tuple-element.33), channel_id=1, source_target_pairs={{0,1},{1,0},{2,3},{3,2},{4,5},{5,4},{6,7},{7,6},{8,9},{9,8},{10,11... | collective-permute-start | bytes 245768 | tf_op jit(solution)/shard_map/ppermute | solution.py:392
  38.2 1.3 %collective-permute-start.8 = (f32[40,512]{1,0:T(8,128)S(1)}, f32[40,512]{1,0:T(8,128)S(1)}, u32[]{:S(2)}, u32[]{:S(2)}) collective-permute-start(f32[40,512]{1,0:T(8,128)S(1)} %get-tuple-element.26), channel_id=1, source_target_pairs={{8,0},{10,2},{4,12},{6,14},{9,1},{11,3},{5,13},{7,15},{24,16},{26,... | collective-permute-start | bytes 245768 | tf_op jit(solution)/shard_map/ppermute | solution.py:387
  39.5 8.6 %collective-permute-start.6 = (f32[40,512]{1,0:T(8,128)S(1)}, f32[40,512]{1,0:T(8,128)S(1)}, u32[]{:S(2)}, u32[]{:S(2)}) collective-permute-start(f32[40,512]{1,0:T(8,128)S(1)} %get-tuple-element.23), channel_id=1, source_target_pairs={{0,4},{2,6},{4,8},{6,10},{8,12},{10,14},{12,0},{14,2},{1,5},{3,7},... | collective-permute-start | bytes 245768 | tf_op jit(solution)/shard_map/ppermute | solution.py:387
  48.2 3.4 %tile.5.refs_1_ = f32[40,512]{1,0:T(8,128)S(1)} custom-call(bf16[560,512]{1,0:T(8,128)(2,1)S(1)} %get-tuple-element.18.refs_0_, bf16[1120,512]{1,0:T(8,128)(2,1)S(1)} %constant_dynamic-update-slice_fusion.refs_1_.refs_2_), custom_call_target="tpu_custom_call" | custom-call | flops 1 | bytes 1 | tf_op jit(solution)/shard_map/tile/pallas_call | solution.py:247
  51.6 0.0 collective-permute-done.11.refs_7_
  51.6 0.8 %collective-permute-done.8.refs_3_ = f32[40,512]{1,0:T(8,128)S(1)} collective-permute-done((f32[40,512]{1,0:T(8,128)S(1)}, f32[40,512]{1,0:T(8,128)S(1)}, u32[]{:S(2)}, u32[]{:S(2)}) %collective-permute-start.8) | collective-permute-done | bytes 81952 | tf_op jit(solution)/shard_map/ppermute | solution.py:387
  52.4 1.3 %image.1 = (f32[32,512]{1,0:T(8,128)S(1)}, f32[16,8,128]{2,1,0:T(8,128)}) custom-call(f32[40,512]{1,0:T(8,128)S(1)} %tile.4.refs_0_, f32[40,512]{1,0:T(8,128)S(1)} %tile.5.refs_1_, f32[40,512]{1,0:T(8,128)S(1)} %collective-permute-done.6.refs_2_, f32[40,512]{1,0:T(8,128)S(1)} %collective-permute-done.8.refs_3_, f32[40,512]{1,0:T(8,128)S(1)} %get-tuple-element.34.refs_4_, ...), custom_call_target="tpu_custom_call" | custom-call | tf_op jit(solution)/shard_map/image/pallas_call | solution.py:288
  53.7 3.6 %all-to-all-start = ((f32[16,8,128]{2,1,0:T(8,128)}), f32[16,8,128]{2,1,0:T(8,128)S(1)}, u32[]{:S(2)}, u32[]{:S(2)}) async-start(f32[16,8,128]{2,1,0:T(8,128)} %get-tuple-element.29), calls=%async_computation | async-start | bytes 131072 | tf_op jit(solution)/shard_map/all_to_all | solution.py:398
  57.3 0.4 collective-permute-start.12
  57.7 0.9 %collective-permute-done.12.other_ref = f32[32,512]{1,0:T(8,128)S(1)} collective-permute-done((f32[32,512]{1,0:T(8,128)S(1)}, f32[32,512]{1,0:T(8,128)S(1)}, u32[]{:S(2)}, u32[]{:S(2)}) %collective-permute-start.12) | collective-permute-done | bytes 65568 | tf_op jit(solution)/shard_map/ppermute | solution.py:397
  58.6 5.6 %all-to-all-done.grams_ref = f32[16,8,128]{2,1,0:T(8,128)S(1)} async-done(((f32[16,8,128]{2,1,0:T(8,128)}), f32[16,8,128]{2,1,0:T(8,128)S(1)}, u32[]{:S(2)}, u32[]{:S(2)}) %all-to-all-start) | async-done | bytes 65568 | tf_op jit(solution)/shard_map/all_to_all | solution.py:398
  64.2 3.5 %basis.1 = f32[16,1024]{1,0:T(8,128)} custom-call(f32[16,8,128]{2,1,0:T(8,128)S(1)} %all-to-all-done.grams_ref, f32[32,512]{1,0:T(8,128)S(1)} %get-tuple-element.30.mine_ref, f32[32,512]{1,0:T(8,128)S(1)} %collective-permute-done.12.other_ref), custom_call_target="tpu_custom_call" | custom-call | tf_op jit(solution)/shard_map/basis/pallas_call | solution.py:326
  (15 shorter events, 0.2 us)
Async XLA Ops:
  0.0 2.3 %collective-permute-start = (bf16[1024,256]{1,0:T(8,128)(2,1)}, bf16[1024,256]{1,0:T(8,128)(2,1)S(1)}, u32[]{:S(2)}, u32[]{:S(2)}) collective-permute-start(bf16[1024,256]{1,0:T(8,128)(2,1)} %emb_ref.1), channel_id=1, source_target_pairs={{0,1},{1,0},{2,3},{3,2},{4,5},{5,4},{6,7},{7,6},{8,9},{9,8},{10,11... | collective-permute-start | bytes 1572872 | tf_op jit(solution)/shard_map/ppermute | solution.py:369
  0.5 1.8 %collective-permute-start.1 = (bf16[16,1024]{1,0:T(8,128)(2,1)}, bf16[16,1024]{1,0:T(8,128)(2,1)S(1)}, u32[]{:S(2)}, u32[]{:S(2)}) collective-permute-start(bf16[16,1024]{1,0:T(8,128)(2,1)} %vec_ref.1), channel_id=1, source_target_pairs={{0,1},{1,0},{2,3},{3,2},{4,5},{5,4},{6,7},{7,6},{8,9},{9,8},{10,11... | collective-permute-start | bytes 98312 | tf_op jit(solution)/shard_map/ppermute | solution.py:370
  2.3 1.0 %copy-start = (bf16[1024,256]{1,0:T(8,128)(2,1)S(1)}, bf16[1024,256]{1,0:T(8,128)(2,1)}, u32[]{:S(2)}) copy-start(bf16[1024,256]{1,0:T(8,128)(2,1)} %emb_ref.1) | copy-start | bytes 1572868
  3.3 0.8 %copy-start.1 = (bf16[16,1024]{1,0:T(8,128)(2,1)S(1)}, bf16[16,1024]{1,0:T(8,128)(2,1)}, u32[]{:S(2)}) copy-start(bf16[16,1024]{1,0:T(8,128)(2,1)} %vec_ref.1) | copy-start | bytes 98308
  4.8 16.2 %collective-permute-start.2 = (bf16[560,512]{1,0:T(8,128)(2,1)S(1)}, bf16[560,512]{1,0:T(8,128)(2,1)S(1)}, u32[]{:S(2)}, u32[]{:S(2)}) collective-permute-start(bf16[560,512]{1,0:T(8,128)(2,1)S(1)} %get-tuple-element.18.refs_0_), channel_id=1, source_target_pairs={{0,2},{2,0},{4,6},{6,4},{8,10},{10,8},{12,14},{14,12},{1,3},{3,1},... | collective-permute-start | bytes 1720328 | tf_op jit(solution)/shard_map/ppermute | solution.py:374
  7.8 17.0 %collective-permute-start.3 = (bf16[560,512]{1,0:T(8,128)(2,1)S(1)}, bf16[560,512]{1,0:T(8,128)(2,1)S(1)}, u32[]{:S(2)}, u32[]{:S(2)}) collective-permute-start(bf16[560,512]{1,0:T(8,128)(2,1)S(1)} %get-tuple-element.18.refs_0_), channel_id=1, source_target_pairs={{4,0},{6,2},{8,4},{10,6},{12,8},{14,10},{0,12},{2,14},{5,1},{7,3},... | collective-permute-start | bytes 1720328 | tf_op jit(solution)/shard_map/ppermute | solution.py:373
  11.4 24.5 %collective-permute-start.7 = (bf16[560,512]{1,0:T(8,128)(2,1)S(1)}, bf16[560,512]{1,0:T(8,128)(2,1)S(1)}, u32[]{:S(2)}, u32[]{:S(2)}) collective-permute-start(bf16[560,512]{1,0:T(8,128)(2,1)S(1)} %get-tuple-element.18.refs_0_), channel_id=1, source_target_pairs={{0,8},{2,10},{12,4},{14,6},{1,9},{3,11},{13,5},{15,7},{16,24},{18,... | collective-permute-start | bytes 1720328 | tf_op jit(solution)/shard_map/ppermute | solution.py:373
  24.8 1.6 %collective-permute-start.4 = (bf16[272,512]{1,0:T(8,128)(2,1)S(1)}, bf16[272,512]{1,0:T(8,128)(2,1)S(1)}, u32[]{:S(2)}, u32[]{:S(2)}) collective-permute-start(bf16[272,512]{1,0:T(8,128)(2,1)S(1)} %slice.18), channel_id=1, source_target_pairs={{0,1},{1,0},{2,3},{3,2},{4,5},{5,4},{6,7},{7,6},{8,9},{9,8},{10,11... | collective-permute-start | bytes 835592 | tf_op jit(solution)/shard_map/ppermute | solution.py:380
  24.9 1.9 %collective-permute-start.5 = (bf16[288,512]{1,0:T(8,128)(2,1)S(1)}, bf16[288,512]{1,0:T(8,128)(2,1)S(1)}, u32[]{:S(2)}, u32[]{:S(2)}) collective-permute-start(bf16[288,512]{1,0:T(8,128)(2,1)S(1)} %slice.19), channel_id=1, source_target_pairs={{0,1},{1,0},{2,3},{3,2},{4,5},{5,4},{6,7},{7,6},{8,9},{9,8},{10,11... | collective-permute-start | bytes 884744 | tf_op jit(solution)/shard_map/ppermute | solution.py:380
  36.0 15.6 %collective-permute-start.10 = (f32[40,512]{1,0:T(8,128)S(1)}, f32[40,512]{1,0:T(8,128)S(1)}, u32[]{:S(2)}, u32[]{:S(2)}) collective-permute-start(f32[40,512]{1,0:T(8,128)S(1)} %get-tuple-element.32), channel_id=1, source_target_pairs={{0,2},{2,0},{4,6},{6,4},{8,10},{10,8},{12,14},{14,12},{1,3},{3,1},... | collective-permute-start | bytes 245768 | tf_op jit(solution)/shard_map/ppermute | solution.py:393
  36.6 15.0 %collective-permute-start.11 = (f32[40,512]{1,0:T(8,128)S(1)}, f32[40,512]{1,0:T(8,128)S(1)}, u32[]{:S(2)}, u32[]{:S(2)}) collective-permute-start(f32[40,512]{1,0:T(8,128)S(1)} %get-tuple-element.31), channel_id=1, source_target_pairs={{1,2},{0,3},{3,0},{2,1},{5,6},{4,7},{7,4},{6,5},{9,10},{8,11},{11,... | collective-permute-start | bytes 245768 | tf_op jit(solution)/shard_map/ppermute | solution.py:394
  36.6 15.0 %collective-permute-start.9 = (f32[40,512]{1,0:T(8,128)S(1)}, f32[40,512]{1,0:T(8,128)S(1)}, u32[]{:S(2)}, u32[]{:S(2)}) collective-permute-start(f32[40,512]{1,0:T(8,128)S(1)} %get-tuple-element.33), channel_id=1, source_target_pairs={{0,1},{1,0},{2,3},{3,2},{4,5},{5,4},{6,7},{7,6},{8,9},{9,8},{10,11... | collective-permute-start | bytes 245768 | tf_op jit(solution)/shard_map/ppermute | solution.py:392
  38.2 14.2 %collective-permute-start.8 = (f32[40,512]{1,0:T(8,128)S(1)}, f32[40,512]{1,0:T(8,128)S(1)}, u32[]{:S(2)}, u32[]{:S(2)}) collective-permute-start(f32[40,512]{1,0:T(8,128)S(1)} %get-tuple-element.26), channel_id=1, source_target_pairs={{8,0},{10,2},{4,12},{6,14},{9,1},{11,3},{5,13},{7,15},{24,16},{26,... | collective-permute-start | bytes 245768 | tf_op jit(solution)/shard_map/ppermute | solution.py:387
  39.5 12.9 %collective-permute-start.6 = (f32[40,512]{1,0:T(8,128)S(1)}, f32[40,512]{1,0:T(8,128)S(1)}, u32[]{:S(2)}, u32[]{:S(2)}) collective-permute-start(f32[40,512]{1,0:T(8,128)S(1)} %get-tuple-element.23), channel_id=1, source_target_pairs={{0,4},{2,6},{4,8},{6,10},{8,12},{10,14},{12,0},{14,2},{1,5},{3,7},... | collective-permute-start | bytes 245768 | tf_op jit(solution)/shard_map/ppermute | solution.py:387
  53.7 10.5 %all-to-all-start = ((f32[16,8,128]{2,1,0:T(8,128)}), f32[16,8,128]{2,1,0:T(8,128)S(1)}, u32[]{:S(2)}, u32[]{:S(2)}) async-start(f32[16,8,128]{2,1,0:T(8,128)} %get-tuple-element.29), calls=%async_computation | async-start | bytes 131072 | tf_op jit(solution)/shard_map/all_to_all | solution.py:398
  57.3 1.3 %collective-permute-start.12 = (f32[32,512]{1,0:T(8,128)S(1)}, f32[32,512]{1,0:T(8,128)S(1)}, u32[]{:S(2)}, u32[]{:S(2)}) collective-permute-start(f32[32,512]{1,0:T(8,128)S(1)} %get-tuple-element.30.mine_ref), channel_id=1, source_target_pairs={{0,1},{1,0},{2,3},{3,2},{4,5},{5,4},{6,7},{7,6},{8,9},{9,8},{10,11... | collective-permute-start | bytes 196616 | tf_op jit(solution)/shard_map/ppermute | solution.py:397

commit v6 on v5

--- a/solution.py
+++ b/solution.py
@@ -45,68 +45,71 @@
     return half + vecs + CODE_ROWS
 
 
-def pack_kernel(emb_ref, emb_other_ref, vec_ref, vec_other_ref, meta_ref, own_ref, mine_ref, code_ref):
+def pack_kernel(emb_mine_ref, emb_rest_ref, emb_other_ref, vec_other_ref, meta_ref, own_ref, mine_ref, code_ref):
     sub = lax.axis_index("sub")
-    rows, width = emb_ref.shape
-    half = rows // 2
-    half_vecs = vec_ref.shape[0]
+    half, width = emb_mine_ref.shape
+    half_vecs = vec_other_ref.shape[0]
+    size = mine_ref.shape[0]
     ones = jnp.ones((8, width), jnp.bfloat16)
-    for start in range(0, rows, CHUNK):
-        part = pl.ds(start, CHUNK)
-        codes = []
-
-        def whole(number, low_bits):
-            codes.append((number >> low_bits) << low_bits)
-            codes.append(number & ((1 << low_bits) - 1))
-
-        boxes, spans = meta_ref[0:4, part], meta_ref[4:6, part]
-        for axis in range(2):
-            whole(jnp.minimum(boxes[axis : axis + 1], boxes[axis + 2 : axis + 3]), 5)
-            whole(jnp.maximum(boxes[axis : axis + 1], boxes[axis + 2 : axis + 3]), 5)
-        whole(jnp.minimum(spans[0:1], spans[1:2]), 7)
-        whole(jnp.maximum(spans[0:1], spans[1:2]), 7)
-        codes.append(meta_ref[6:7, part])
-        codes = [code.astype(jnp.float32) for code in codes]
-        rest = jnp.zeros((8, CHUNK), jnp.float32)
-        for ref in (emb_ref, emb_other_ref):
-            values = ref[part, :].astype(jnp.float32)
-            square = values * values
-            high = square.astype(jnp.bfloat16)
-            low = (square - high.astype(jnp.float32)).astype(jnp.bfloat16)
-            rest = rest + (dot_nt(ones, high) + dot_nt(ones, low))
-        rest = rest[0:1]
-        for _ in range(3):
-            piece = rest.astype(jnp.bfloat16).astype(jnp.float32)
-            codes.append(piece)
-            rest = rest - piece
-        code_ref[:, part] = jnp.concatenate(codes, axis=0).astype(jnp.bfloat16)
-    size = mine_ref.shape[0]
-    targets = [(own_ref, 0, sub), (own_ref, size, 1 - sub), (mine_ref, 0, sub)]
-    for ref, base, place in targets:
-        source = pl.ds(pl.multiple_of(place * half, half), half)
-        sides = ((emb_ref, vec_ref, sub), (emb_other_ref, vec_other_ref, 1 - sub))
-        for values_ref, vectors_ref, side in sides:
-            ref[base : base + half, pl.ds(pl.multiple_of(side * width, width), width)] = values_ref[source, :]
-            first_vec = pl.multiple_of(base + half + side * half_vecs, 16)
-            ref[pl.ds(first_vec, half_vecs), :] = vectors_ref[:, source]
-        first_code = base + half + 2 * half_vecs
-        ref[first_code : first_code + CODE_ROWS, :] = code_ref[:, source]
-
-
-def packs_of(embeddings, emb_other, vectors, vec_other, meta):
-    rows, width = embeddings.shape
-    half, features = rows // 2, 2 * width
+    for base, emb_ref, place in ((0, emb_mine_ref, sub), (size, emb_rest_ref, 1 - sub)):
+        first = pl.multiple_of(place * half, half)
+        for start in range(0, half, CHUNK):
+            part = pl.ds(first + start, CHUNK)
+            codes = []
+
+            def whole(number, unit):
+                high = jnp.floor(number * (1.0 / unit)) * unit
+                codes.append(high)
+                codes.append(number - high)
+
+            meta = meta_ref[half_vecs:, part]
+            for axis in range(2):
+                whole(jnp.minimum(meta[axis : axis + 1], meta[axis + 2 : axis + 3]), 32.0)
+                whole(jnp.maximum(meta[axis : axis + 1], meta[axis + 2 : axis + 3]), 32.0)
+            whole(jnp.minimum(meta[4:5], meta[5:6]), 128.0)
+            whole(jnp.maximum(meta[4:5], meta[5:6]), 128.0)
+            codes.append(meta[6:7])
+            rest = jnp.zeros((8, CHUNK), jnp.float32)
+            for values in (emb_ref[start : start + CHUNK, :], emb_other_ref[part, :]):
+                values = values.astype(jnp.float32)
+                square = values * values
+                high = square.astype(jnp.bfloat16)
+                low = (square - high.astype(jnp.float32)).astype(jnp.bfloat16)
+                rest = rest + (dot_nt(ones, high) + dot_nt(ones, low))
+            rest = rest[0:1]
+            for _ in range(3):
+                piece = rest.astype(jnp.bfloat16).astype(jnp.float32)
+                codes.append(piece)
+                rest = rest - piece
+            code_ref[:, start : start + CHUNK] = jnp.concatenate(codes, axis=0).astype(jnp.bfloat16)
+        source = pl.ds(first, half)
+        refs = [(own_ref, base)] + ([(mine_ref, 0)] if base == 0 else [])
+        sides = (
+            (emb_ref[...], meta_ref[0:half_vecs, source].astype(jnp.bfloat16), sub),
+            (emb_other_ref[source, :], vec_other_ref[:, source], 1 - sub),
+        )
+        for ref, top in refs:
+            for values, vectors, side in sides:
+                ref[top : top + half, pl.ds(pl.multiple_of(side * width, width), width)] = values
+                ref[pl.ds(pl.multiple_of(top + half + side * half_vecs, 16), half_vecs), :] = vectors
+            first_code = top + half + 2 * half_vecs
+            ref[first_code : first_code + CODE_ROWS, :] = code_ref[...]
+
+
+def packs_of(emb_mine, emb_rest, emb_other, vec_other, meta):
+    half, width = emb_mine.shape
+    features = 2 * width
     assert half == features
-    size = pack_rows(half, 2 * vectors.shape[0])
+    size = pack_rows(half, 2 * vec_other.shape[0])
     return pl.pallas_call(
         pack_kernel,
         out_shape=[jax.ShapeDtypeStruct((count * size, features), jnp.bfloat16) for count in (2, 1)],
         in_specs=[VMEM_SPEC] * 5,
         out_specs=[VMEM_SPEC] * 2,
-        scratch_shapes=[pltpu.VMEM((CODE_ROWS, rows), jnp.bfloat16)],
+        scratch_shapes=[pltpu.VMEM((CODE_ROWS, half), jnp.bfloat16)],
         compiler_params=params(),
         name="pack",
-    )(embeddings, emb_other, vectors, vec_other, meta)
+    )(emb_mine, emb_rest, emb_other, vec_other, meta)
 
 
 def decode(codes):
@@ -264,38 +267,54 @@
 
 
 def image_kernel(*refs):
-    parts, image_ref, grams_ref = refs[:-2], refs[-2], refs[-1]
+    parts, image_ref = refs[:-1], refs[-1]
     total = parts[0][...]
     for part in parts[1:]:
         total = total + part[...]
     vecs = image_ref.shape[0]
-    image = total[0:vecs] / total[vecs : vecs + 1]
-    image_ref[...] = image
-    packed = jnp.zeros((8, LANES), jnp.float32)
-    for piece in range(LANES // vecs):
-        shifted = [image]
-        if piece > 0:
-            shifted.insert(0, jnp.zeros((piece * vecs, image.shape[1]), jnp.float32))
-        if piece < LANES // vecs - 1:
-            shifted.append(jnp.zeros((LANES - (piece + 1) * vecs, image.shape[1]), jnp.float32))
-        packed = packed + dot_nt(image[8 * piece : 8 * piece + 8], jnp.concatenate(shifted, axis=0), lax.Precision.HIGHEST)
-    for copy in range(grams_ref.shape[0]):
-        grams_ref[copy] = packed
-
-
-def image_of(parts, vecs, copies):
-    cols = parts[0].shape[1]
+    image_ref[...] = total[0:vecs] / total[vecs : vecs + 1]
+
+
+def image_of(parts, vecs):
     return pl.pallas_call(
         image_kernel,
-        out_shape=[
-            jax.ShapeDtypeStruct((vecs, cols), jnp.float32),
-            jax.ShapeDtypeStruct((copies, 8, LANES), jnp.float32),
-        ],
+        out_shape=jax.ShapeDtypeStruct((vecs, parts[0].shape[1]), jnp.float32),
         in_specs=[VMEM_SPEC] * len(parts),
-        out_specs=[VMEM_SPEC] * 2,
+        out_specs=VMEM_SPEC,
         compiler_params=params(),
         name="image",
     )(*parts)
+
+
+def gram_kernel(mine_ref, other_ref, grams_ref):
+    vecs, cols = mine_ref.shape
+    packed = []
+    for ref in (mine_ref, other_ref):
+        image = ref[...]
+        total = jnp.zeros((8, LANES), jnp.float32)
+        for piece in range(LANES // vecs):
+            shifted = [image]
+            if piece > 0:
+                shifted.insert(0, jnp.zeros((piece * vecs, cols), jnp.float32))
+            if piece < LANES // vecs - 1:
+                shifted.append(jnp.zeros((LANES - (piece + 1) * vecs, cols), jnp.float32))
+            lines = image[8 * piece : 8 * piece + 8]
+            total = total + dot_nt(lines, jnp.concatenate(shifted, axis=0), lax.Precision.HIGHEST)
+        packed.append(total)
+    both = packed[0] + packed[1]
+    for copy in range(grams_ref.shape[0]):
+        grams_ref[copy] = both
+
+
+def grams_of(mine, other, copies):
+    return pl.pallas_call(
+        gram_kernel,
+        out_shape=jax.ShapeDtypeStruct((copies, 8, LANES), jnp.float32),
+        in_specs=[VMEM_SPEC] * 2,
+        out_specs=VMEM_SPEC,
+        compiler_params=params(),
+        name="gram",
+    )(mine, other)
 
 
 def basis_kernel(total_rows, grams_ref, mine_ref, other_ref, out_ref, inverse_ref):
@@ -358,7 +377,6 @@
     half = rows // 2
     vecs = 2 * vectors.shape[0]
     blocks = lax.axis_size("blk")
-    devices = 2 * blocks
     swap = [(0, 1), (1, 0)]
     beside = [(block, block ^ 1) for block in range(blocks)]
     plans = [(block_moves(moves), takers) for moves, takers in exchanges(blocks // 2)]
@@ -368,8 +386,10 @@
 
     emb_other = lax.ppermute(embeddings, "sub", swap)
     vec_other = lax.ppermute(vectors, "sub", swap)
-    meta = jnp.concatenate([boxes, spans, camera[None, :]], axis=0)
-    own, mine = packs_of(embeddings, emb_other, vectors, vec_other, meta)
+    meta = jnp.concatenate([array.astype(jnp.float32) for array in (vectors, boxes, spans, camera[None, :])], axis=0)
+    sub = lax.axis_index("sub")
+    halves = [lax.dynamic_slice_in_dim(embeddings, place * half, half, 0) for place in (sub, 1 - sub)]
+    own, mine = packs_of(*halves, emb_other, vec_other, meta)
     sent = [lax.ppermute(mine, "blk", moves) for moves, _ in plans]
     beside_mine = lax.ppermute(mine, "blk", beside)
     weigh = functools.partial(tile, vecs=vecs)
@@ -382,7 +402,7 @@
     col_sums = None
     for (moves, takers), pack in zip(plans, sent):
         if col_sums is not None:
-            pack, col_sums = lax.optimization_barrier((pack, col_sums))
+            pack, col_sums, parts[1:2] = lax.optimization_barrier((pack, col_sums, parts[1:2]))
         row_sums, sums = weigh(pack, [own, next_to], receivers=takers)
         parts.append(lax.ppermute(row_sums, "blk", back(moves)))
         col_sums = sums if col_sums is None else col_sums + sums
@@ -393,9 +413,9 @@
         parts.append(lax.ppermute(pieces[2], "blk", beside))
         parts.append(lax.ppermute(pieces[3], ("blk", "sub"), crossed(beside)))
 
-    image, copies = image_of(parts, vecs, devices)
+    image = image_of(parts, vecs)
     image_other = lax.ppermute(image, "sub", swap)
-    grams = lax.all_to_all(copies, ("blk", "sub"), 0, 0, tiled=True)
+    grams = lax.all_to_all(grams_of(image, image_other, blocks), "blk", 0, 0, tiled=True)
     return basis_of(grams, image, image_other, blocks * rows)
 
 

time: 68.1 us -> 69.1 us (1.015)
  blocking collectives: 0 us -> 9.97 us
  starting transfers between devices: 25.2 us -> 19.5 us
  waiting for transfers between devices: 20.1 us -> 15.4 us
  other arithmetic: 0.8 us -> 2.93 us
  local copies, waits for them, and re-layouts: 1.94 us -> 1.2 us
    all_to_all x0 -> x1, blocking collectives: none -> 9.97 us  [local(): lax.all_to_all(grams_of(image, image_other, blocks), 'blk', 0, 0, tiled=T...]
    all_to_all x1 -> x0, waiting for transfers between devices: 5.58 us -> none  [local(): grams = lax.all_to_all(copies, ('blk', 'sub'), 0, 0, tiled=True)]
    ppermute x2, waiting for transfers between devices: 0.81 us -> 4.44 us  [local(): parts.append(lax.ppermute(row_sums, 'blk', back(moves)))]
    all_to_all x1 -> x0, starting transfers between devices: 3.59 us -> none  [local(): grams = lax.all_to_all(copies, ('blk', 'sub'), 0, 0, tiled=True)]
    convert_element_type x0 -> x4, other arithmetic: none -> 2.87 us  [local(): array.astype(jnp.float32)]
    ppermute x2, waiting for transfers between devices: 5.82 us -> 3.86 us  [local(): sent = [lax.ppermute(mine, 'blk', moves) for moves, _ in plans]]
    ppermute x2, starting transfers between devices: 9.92 us -> 8.08 us  [local(): parts.append(lax.ppermute(row_sums, 'blk', back(moves)))]
    unnamed x6 -> x2, local copies, waits for them, and re-layouts: 1.86 us -> 0.06 us
  transfers between devices with their start and end apart: 14 -> 13, of which waited for: 9 -> 6; matrix products, arithmetic and copies ran while one was open for 1% -> 6% of each run, Pallas kernels for 21% -> 20%
where the time goes in v6:
time: 69.1 us; the launch traced here: 68.7 us
  Pallas kernels  19.6 us (28%)
  starting transfers between devices  19.5 us (28%)
  waiting for transfers between devices  15.4 us (22%)
  blocking collectives  9.97 us (14%)
  other arithmetic  2.93 us (4%)
  local copies, waits for them, and re-layouts  1.2 us (2%)
    pallas_call x4, Pallas kernels, tile(): pl.pallas_call(body, out_shape=shapes, in_specs=[VMEM_SPEC] * (1 + len(co...  14.2 us
    all_to_all x1, blocking collectives, local(): lax.all_to_all(grams_of(image, image_other, blocks), 'blk', 0, 0, tiled=T...  9.97 us
    ppermute x2, starting transfers between devices, local(): parts.append(lax.ppermute(row_sums, 'blk', back(moves)))  8.08 us
    ppermute x2, starting transfers between devices, local(): sent = [lax.ppermute(mine, 'blk', moves) for moves, _ in plans]  4.97 us
    ppermute x1, waiting for transfers between devices, local(): beside_mine = lax.ppermute(mine, 'blk', beside)  4.52 us
    ppermute x2, waiting for transfers between devices, local(): parts.append(lax.ppermute(row_sums, 'blk', back(moves)))  4.44 us
    ppermute x2, waiting for transfers between devices, local(): sent = [lax.ppermute(mine, 'blk', moves) for moves, _ in plans]  3.86 us
    pallas_call x1, Pallas kernels, basis_of(): pl.pallas_call(functools.partial(basis_kernel, total_rows), out_shape=jax...  3.52 us
  transfers between devices with their start and end apart: 13, of which 6 were waited for; matrix products, arithmetic and copies ran while one was open for 6% of the time, Pallas kernels for 20%

profile of v6, /device:TPU:0, one launch (start us, length us, event | category | flops | bytes accessed | tf_op | source)
XLA Modules:
  0.0 68.7 jit_solution(16348947689203961782)
XLA Ops:
  0.0 0.5 collective-permute-start
  0.5 0.1 collective-permute-start.1
  0.5 0.8 %convert_element_type.15 = f32[16,1024]{1,0:T(8,128)S(1)} convert(bf16[16,1024]{1,0:T(8,128)(2,1)} %param.6) | non-fusion elementwise | flops 16384 | bytes 98304 | tf_op jit(solution)/shard_map/convert_element_type | solution.py:389
  1.3 0.7 %convert_element_type.16 = f32[4,1024]{1,0:T(4,128)S(1)} convert(s32[4,1024]{1,0:T(4,128)} %param.7) | non-fusion elementwise | flops 4096 | bytes 32768 | tf_op jit(solution)/shard_map/convert_element_type | solution.py:389
  2.0 0.7 %convert_element_type.17 = f32[2,1024]{1,0:T(2,128)S(1)} convert(s32[2,1024]{1,0:T(2,128)} %param.8) | non-fusion elementwise | flops 2048 | bytes 16384 | tf_op jit(solution)/shard_map/convert_element_type | solution.py:389
  2.7 0.7 %convert_element_type.18 = f32[1024]{0:T(1024)S(1)} convert(s32[1024]{0:T(1024)} %param.9) | non-fusion elementwise | flops 1024 | bytes 8192 | tf_op jit(solution)/shard_map/convert_element_type | solution.py:389
  3.4 1.1 %constant_dynamic-slice_fusion = (bf16[512,256]{1,0:T(8,128)(2,1)S(1)}, bf16[512,256]{1,0:T(8,128)(2,1)S(1)}) fusion(bf16[1024,256]{1,0:T(8,128)(2,1)} %param.5, s32[]{:T(128)S(6)} %select_n.7, s32[]{:T(128)S(6)} %select_n.6), kind=kLoop, calls=%fused_computation.4 | loop fusion | bytes 1048584 | tf_op jit(solution)/shard_map/dynamic_slice | solution.py:391
  4.5 0.7 %pack.1 = (bf16[1120,512]{1,0:T(8,128)(2,1)S(1)}, bf16[560,512]{1,0:T(8,128)(2,1)S(1)}) custom-call(bf16[512,256]{1,0:T(8,128)(2,1)S(1)} %get-tuple-element.30.emb_mine_ref, bf16[512,256]{1,0:T(8,128)(2,1)S(1)} %get-tuple-element.29.emb_rest_ref, bf16[1024,256]{1,0:T(8,128)(2,1)S(1)} %collective-permute-done.emb_other_ref, ...), custom_call_target="tpu_custom_call" | custom-call | tf_op jit(solution)/shard_map/pack/pallas_call | solution.py:104
  5.2 3.0 %collective-permute-start.2 = (bf16[560,512]{1,0:T(8,128)(2,1)S(1)}, bf16[560,512]{1,0:T(8,128)(2,1)S(1)}, u32[]{:S(2)}, u32[]{:S(2)}) collective-permute-start(bf16[560,512]{1,0:T(8,128)(2,1)S(1)} %get-tuple-element.17.refs_0_), channel_id=1, source_target_pairs={{0,2},{2,0},{4,6},{6,4},{8,10},{10,8},{12,14},{14,12},{1,3},{3,1},... | collective-permute-start | bytes 1720328 | tf_op jit(solution)/shard_map/ppermute | solution.py:394
  8.2 3.6 %collective-permute-start.3 = (bf16[560,512]{1,0:T(8,128)(2,1)S(1)}, bf16[560,512]{1,0:T(8,128)(2,1)S(1)}, u32[]{:S(2)}, u32[]{:S(2)}) collective-permute-start(bf16[560,512]{1,0:T(8,128)(2,1)S(1)} %get-tuple-element.17.refs_0_), channel_id=1, source_target_pairs={{4,0},{6,2},{8,4},{10,6},{12,8},{14,10},{0,12},{2,14},{5,1},{7,3},... | collective-permute-start | bytes 1720328 | tf_op jit(solution)/shard_map/ppermute | solution.py:393
  11.9 1.4 %collective-permute-start.4 = (bf16[560,512]{1,0:T(8,128)(2,1)S(1)}, bf16[560,512]{1,0:T(8,128)(2,1)S(1)}, u32[]{:S(2)}, u32[]{:S(2)}) collective-permute-start(bf16[560,512]{1,0:T(8,128)(2,1)S(1)} %get-tuple-element.17.refs_0_), channel_id=1, source_target_pairs={{0,8},{2,10},{12,4},{14,6},{1,9},{3,11},{13,5},{15,7},{16,24},{18,... | collective-permute-start | bytes 1720328 | tf_op jit(solution)/shard_map/ppermute | solution.py:393
  13.2 3.6 %tile.4.refs_0_ = f32[40,512]{1,0:T(8,128)S(1)} custom-call(bf16[560,512]{1,0:T(8,128)(2,1)S(1)} %get-tuple-element.17.refs_0_, bf16[1120,512]{1,0:T(8,128)(2,1)S(1)} %get-tuple-element.18.refs_1_), custom_call_target="tpu_custom_call" | custom-call | flops 1 | bytes 1 | tf_op jit(solution)/shard_map/tile/pallas_call | solution.py:250
  16.9 4.5 %collective-permute-done.2 = bf16[560,512]{1,0:T(8,128)(2,1)S(1)} collective-permute-done((bf16[560,512]{1,0:T(8,128)(2,1)S(1)}, bf16[560,512]{1,0:T(8,128)(2,1)S(1)}, u32[]{:S(2)}, u32[]{:S(2)}) %collective-permute-start.2) | collective-permute-done | bytes 573472 | tf_op jit(solution)/shard_map/ppermute | solution.py:394
  21.4 3.9 %collective-permute-done.3.refs_0_ = bf16[560,512]{1,0:T(8,128)(2,1)S(1)} collective-permute-done((bf16[560,512]{1,0:T(8,128)(2,1)S(1)}, bf16[560,512]{1,0:T(8,128)(2,1)S(1)}, u32[]{:S(2)}, u32[]{:S(2)}) %collective-permute-start.3) | collective-permute-done | bytes 573472 | tf_op jit(solution)/shard_map/ppermute | solution.py:393
  25.3 0.1 collective-permute-start.5
  25.4 0.6 collective-permute-start.6
  26.0 0.9 %collective-permute-done.5 = bf16[272,512]{1,0:T(8,128)(2,1)S(1)} collective-permute-done((bf16[272,512]{1,0:T(8,128)(2,1)S(1)}, bf16[272,512]{1,0:T(8,128)(2,1)S(1)}, u32[]{:S(2)}, u32[]{:S(2)}) %collective-permute-start.5) | collective-permute-done | bytes 278560 | tf_op jit(solution)/shard_map/ppermute | solution.py:400
  26.9 0.4 collective-permute-done.6
  27.3 3.4 %tile.6.refs_1_ = f32[40,512]{1,0:T(8,128)S(1)} custom-call(bf16[560,512]{1,0:T(8,128)(2,1)S(1)} %get-tuple-element.17.refs_0_, bf16[1120,512]{1,0:T(8,128)(2,1)S(1)} %constant_dynamic-update-slice_fusion.refs_2_.refs_1_), custom_call_target="tpu_custom_call" | custom-call | flops 1 | bytes 1 | tf_op jit(solution)/shard_map/tile/pallas_call | solution.py:250
  30.8 6.9 %tile.5 = (f32[40,512]{1,0:T(8,128)S(1)}, f32[40,2048]{1,0:T(8,128)S(1)}) custom-call(bf16[560,512]{1,0:T(8,128)(2,1)S(1)} %collective-permute-done.3.refs_0_, bf16[1120,512]{1,0:T(8,128)(2,1)S(1)} %get-tuple-element.18.refs_1_, bf16[1120,512]{1,0:T(8,128)(2,1)S(1)} %constant_dynamic-update-slice_fusion.refs_2_.refs_1_), custom_call_target="tpu_custom_call" | custom-call | flops 1 | bytes 1 | tf_op jit(solution)/shard_map/tile/pallas_call | solution.py:250
  37.7 0.2 tile.7
  38.0 0.6 collective-permute-start.10
  38.6 1.0 %collective-permute-start.11 = (f32[40,512]{1,0:T(8,128)S(1)}, f32[40,512]{1,0:T(8,128)S(1)}, u32[]{:S(2)}, u32[]{:S(2)}) collective-permute-start(f32[40,512]{1,0:T(8,128)S(1)} %get-tuple-element.31), channel_id=1, source_target_pairs={{1,2},{0,3},{3,0},{2,1},{5,6},{4,7},{7,4},{6,5},{9,10},{8,11},{11,... | collective-permute-start | bytes 245768 | tf_op jit(solution)/shard_map/ppermute | solution.py:414
  39.6 0.6 collective-permute-start.9
  40.2 1.3 %collective-permute-start.8 = (f32[40,512]{1,0:T(8,128)S(1)}, f32[40,512]{1,0:T(8,128)S(1)}, u32[]{:S(2)}, u32[]{:S(2)}) collective-permute-start(f32[40,512]{1,0:T(8,128)S(1)} %get-tuple-element.26), channel_id=1, source_target_pairs={{8,0},{10,2},{4,12},{6,14},{9,1},{11,3},{5,13},{7,15},{24,16},{26,... | collective-permute-start | bytes 245768 | tf_op jit(solution)/shard_map/ppermute | solution.py:407
  41.5 6.8 %collective-permute-start.7 = (f32[40,512]{1,0:T(8,128)S(1)}, f32[40,512]{1,0:T(8,128)S(1)}, u32[]{:S(2)}, u32[]{:S(2)}) collective-permute-start(f32[40,512]{1,0:T(8,128)S(1)} %get-tuple-element.24), channel_id=1, source_target_pairs={{0,4},{2,6},{4,8},{6,10},{8,12},{10,14},{12,0},{14,2},{1,5},{3,7},... | collective-permute-start | bytes 245768 | tf_op jit(solution)/shard_map/ppermute | solution.py:407
  48.3 4.4 %collective-permute-done.8.refs_3_ = f32[40,512]{1,0:T(8,128)S(1)} collective-permute-done((f32[40,512]{1,0:T(8,128)S(1)}, f32[40,512]{1,0:T(8,128)S(1)}, u32[]{:S(2)}, u32[]{:S(2)}) %collective-permute-start.8) | collective-permute-done | bytes 81952 | tf_op jit(solution)/shard_map/ppermute | solution.py:407
  52.8 0.1 collective-permute-start.12
  52.9 1.2 %collective-permute-done.12.other_ref = f32[32,512]{1,0:T(8,128)S(1)} collective-permute-done((f32[32,512]{1,0:T(8,128)S(1)}, f32[32,512]{1,0:T(8,128)S(1)}, u32[]{:S(2)}, u32[]{:S(2)}) %collective-permute-start.12) | collective-permute-done | bytes 65568 | tf_op jit(solution)/shard_map/ppermute | solution.py:417
  54.1 1.1 %gram.1 = f32[8,8,128]{2,1,0:T(8,128)S(1)} custom-call(f32[32,512]{1,0:T(8,128)S(1)} %image.1.mine_ref, f32[32,512]{1,0:T(8,128)S(1)} %collective-permute-done.12.other_ref), custom_call_target="tpu_custom_call" | custom-call | tf_op jit(solution)/shard_map/gram/pallas_call | solution.py:310
  55.2 10.0 %all_to_all.5.grams_ref = f32[8,8,128]{2,1,0:T(8,128)S(1)} all-to-all(f32[8,8,128]{2,1,0:T(8,128)S(1)} %gram.1), channel_id=1, replica_groups=mesh['groups'=2,'blk'=8,'sub'=2] {'blk'}, dimensions={0} | all-to-all | bytes 65536 | tf_op jit(solution)/shard_map/all_to_all | solution.py:418
  65.2 3.5 %basis.1 = f32[16,1024]{1,0:T(8,128)} custom-call(f32[8,8,128]{2,1,0:T(8,128)S(1)} %all_to_all.5.grams_ref, f32[32,512]{1,0:T(8,128)S(1)} %image.1.mine_ref, f32[32,512]{1,0:T(8,128)S(1)} %collective-permute-done.12.other_ref), custom_call_target="tpu_custom_call" | custom-call | tf_op jit(solution)/shard_map/basis/pallas_call | solution.py:345
  (16 shorter events, 0.3 us)
Async XLA Ops:
  0.0 4.5 %collective-permute-start = (bf16[1024,256]{1,0:T(8,128)(2,1)}, bf16[1024,256]{1,0:T(8,128)(2,1)S(1)}, u32[]{:S(2)}, u32[]{:S(2)}) collective-permute-start(bf16[1024,256]{1,0:T(8,128)(2,1)} %param.5), channel_id=1, source_target_pairs={{0,1},{1,0},{2,3},{3,2},{4,5},{5,4},{6,7},{7,6},{8,9},{9,8},{10,11... | collective-permute-start | bytes 1572872 | tf_op jit(solution)/shard_map/ppermute | solution.py:387
  0.5 4.0 %collective-permute-start.1 = (bf16[16,1024]{1,0:T(8,128)(2,1)}, bf16[16,1024]{1,0:T(8,128)(2,1)S(1)}, u32[]{:S(2)}, u32[]{:S(2)}) collective-permute-start(bf16[16,1024]{1,0:T(8,128)(2,1)} %param.6), channel_id=1, source_target_pairs={{0,1},{1,0},{2,3},{3,2},{4,5},{5,4},{6,7},{7,6},{8,9},{9,8},{10,11... | collective-permute-start | bytes 98312 | tf_op jit(solution)/shard_map/ppermute | solution.py:388
  5.2 16.2 %collective-permute-start.2 = (bf16[560,512]{1,0:T(8,128)(2,1)S(1)}, bf16[560,512]{1,0:T(8,128)(2,1)S(1)}, u32[]{:S(2)}, u32[]{:S(2)}) collective-permute-start(bf16[560,512]{1,0:T(8,128)(2,1)S(1)} %get-tuple-element.17.refs_0_), channel_id=1, source_target_pairs={{0,2},{2,0},{4,6},{6,4},{8,10},{10,8},{12,14},{14,12},{1,3},{3,1},... | collective-permute-start | bytes 1720328 | tf_op jit(solution)/shard_map/ppermute | solution.py:394
  8.2 17.0 %collective-permute-start.3 = (bf16[560,512]{1,0:T(8,128)(2,1)S(1)}, bf16[560,512]{1,0:T(8,128)(2,1)S(1)}, u32[]{:S(2)}, u32[]{:S(2)}) collective-permute-start(bf16[560,512]{1,0:T(8,128)(2,1)S(1)} %get-tuple-element.17.refs_0_), channel_id=1, source_target_pairs={{4,0},{6,2},{8,4},{10,6},{12,8},{14,10},{0,12},{2,14},{5,1},{7,3},... | collective-permute-start | bytes 1720328 | tf_op jit(solution)/shard_map/ppermute | solution.py:393
  11.9 25.9 %collective-permute-start.4 = (bf16[560,512]{1,0:T(8,128)(2,1)S(1)}, bf16[560,512]{1,0:T(8,128)(2,1)S(1)}, u32[]{:S(2)}, u32[]{:S(2)}) collective-permute-start(bf16[560,512]{1,0:T(8,128)(2,1)S(1)} %get-tuple-element.17.refs_0_), channel_id=1, source_target_pairs={{0,8},{2,10},{12,4},{14,6},{1,9},{3,11},{13,5},{15,7},{16,24},{18,... | collective-permute-start | bytes 1720328 | tf_op jit(solution)/shard_map/ppermute | solution.py:393
  25.3 1.6 %collective-permute-start.5 = (bf16[272,512]{1,0:T(8,128)(2,1)S(1)}, bf16[272,512]{1,0:T(8,128)(2,1)S(1)}, u32[]{:S(2)}, u32[]{:S(2)}) collective-permute-start(bf16[272,512]{1,0:T(8,128)(2,1)S(1)} %slice.18), channel_id=1, source_target_pairs={{0,1},{1,0},{2,3},{3,2},{4,5},{5,4},{6,7},{7,6},{8,9},{9,8},{10,11... | collective-permute-start | bytes 835592 | tf_op jit(solution)/shard_map/ppermute | solution.py:400
  25.4 1.9 %collective-permute-start.6 = (bf16[288,512]{1,0:T(8,128)(2,1)S(1)}, bf16[288,512]{1,0:T(8,128)(2,1)S(1)}, u32[]{:S(2)}, u32[]{:S(2)}) collective-permute-start(bf16[288,512]{1,0:T(8,128)(2,1)S(1)} %slice.19), channel_id=1, source_target_pairs={{0,1},{1,0},{2,3},{3,2},{4,5},{5,4},{6,7},{7,6},{8,9},{9,8},{10,11... | collective-permute-start | bytes 884744 | tf_op jit(solution)/shard_map/ppermute | solution.py:400
  38.0 10.3 %collective-permute-start.10 = (f32[40,512]{1,0:T(8,128)S(1)}, f32[40,512]{1,0:T(8,128)S(1)}, u32[]{:S(2)}, u32[]{:S(2)}) collective-permute-start(f32[40,512]{1,0:T(8,128)S(1)} %get-tuple-element.32), channel_id=1, source_target_pairs={{0,2},{2,0},{4,6},{6,4},{8,10},{10,8},{12,14},{14,12},{1,3},{3,1},... | collective-permute-start | bytes 245768 | tf_op jit(solution)/shard_map/ppermute | solution.py:413
  38.6 9.7 %collective-permute-start.11 = (f32[40,512]{1,0:T(8,128)S(1)}, f32[40,512]{1,0:T(8,128)S(1)}, u32[]{:S(2)}, u32[]{:S(2)}) collective-permute-start(f32[40,512]{1,0:T(8,128)S(1)} %get-tuple-element.31), channel_id=1, source_target_pairs={{1,2},{0,3},{3,0},{2,1},{5,6},{4,7},{7,4},{6,5},{9,10},{8,11},{11,... | collective-permute-start | bytes 245768 | tf_op jit(solution)/shard_map/ppermute | solution.py:414
  39.6 8.7 %collective-permute-start.9 = (f32[40,512]{1,0:T(8,128)S(1)}, f32[40,512]{1,0:T(8,128)S(1)}, u32[]{:S(2)}, u32[]{:S(2)}) collective-permute-start(f32[40,512]{1,0:T(8,128)S(1)} %get-tuple-element.33), channel_id=1, source_target_pairs={{0,1},{1,0},{2,3},{3,2},{4,5},{5,4},{6,7},{7,6},{8,9},{9,8},{10,11... | collective-permute-start | bytes 245768 | tf_op jit(solution)/shard_map/ppermute | solution.py:412
  40.2 12.5 %collective-permute-start.8 = (f32[40,512]{1,0:T(8,128)S(1)}, f32[40,512]{1,0:T(8,128)S(1)}, u32[]{:S(2)}, u32[]{:S(2)}) collective-permute-start(f32[40,512]{1,0:T(8,128)S(1)} %get-tuple-element.26), channel_id=1, source_target_pairs={{8,0},{10,2},{4,12},{6,14},{9,1},{11,3},{5,13},{7,15},{24,16},{26,... | collective-permute-start | bytes 245768 | tf_op jit(solution)/shard_map/ppermute | solution.py:407
  41.5 11.3 %collective-permute-start.7 = (f32[40,512]{1,0:T(8,128)S(1)}, f32[40,512]{1,0:T(8,128)S(1)}, u32[]{:S(2)}, u32[]{:S(2)}) collective-permute-start(f32[40,512]{1,0:T(8,128)S(1)} %get-tuple-element.24), channel_id=1, source_target_pairs={{0,4},{2,6},{4,8},{6,10},{8,12},{10,14},{12,0},{14,2},{1,5},{3,7},... | collective-permute-start | bytes 245768 | tf_op jit(solution)/shard_map/ppermute | solution.py:407
  52.8 1.3 %collective-permute-start.12 = (f32[32,512]{1,0:T(8,128)S(1)}, f32[32,512]{1,0:T(8,128)S(1)}, u32[]{:S(2)}, u32[]{:S(2)}) collective-permute-start(f32[32,512]{1,0:T(8,128)S(1)} %image.1.mine_ref), channel_id=1, source_target_pairs={{0,1},{1,0},{2,3},{3,2},{4,5},{5,4},{6,7},{7,6},{8,9},{9,8},{10,11... | collective-permute-start | bytes 196616 | tf_op jit(solution)/shard_map/ppermute | solution.py:417

commit v7 on v6

--- a/solution.py
+++ b/solution.py
@@ -45,7 +45,7 @@
     return half + vecs + CODE_ROWS
 
 
-def pack_kernel(emb_mine_ref, emb_rest_ref, emb_other_ref, vec_other_ref, meta_ref, own_ref, mine_ref, code_ref):
+def pack_kernel(emb_mine_ref, emb_rest_ref, emb_other_ref, vec_ref, vec_other_ref, meta_ref, own_ref, mine_ref, code_ref):
     sub = lax.axis_index("sub")
     half, width = emb_mine_ref.shape
     half_vecs = vec_other_ref.shape[0]
@@ -57,18 +57,18 @@
             part = pl.ds(first + start, CHUNK)
             codes = []
 
-            def whole(number, unit):
-                high = jnp.floor(number * (1.0 / unit)) * unit
-                codes.append(high)
-                codes.append(number - high)
-
-            meta = meta_ref[half_vecs:, part]
+            def whole(number, low_bits):
+                codes.append((number >> low_bits) << low_bits)
+                codes.append(number & ((1 << low_bits) - 1))
+
+            meta = meta_ref[:, part]
             for axis in range(2):
-                whole(jnp.minimum(meta[axis : axis + 1], meta[axis + 2 : axis + 3]), 32.0)
-                whole(jnp.maximum(meta[axis : axis + 1], meta[axis + 2 : axis + 3]), 32.0)
-            whole(jnp.minimum(meta[4:5], meta[5:6]), 128.0)
-            whole(jnp.maximum(meta[4:5], meta[5:6]), 128.0)
+                whole(jnp.minimum(meta[axis : axis + 1], meta[axis + 2 : axis + 3]), 5)
+                whole(jnp.maximum(meta[axis : axis + 1], meta[axis + 2 : axis + 3]), 5)
+            whole(jnp.minimum(meta[4:5], meta[5:6]), 7)
+            whole(jnp.maximum(meta[4:5], meta[5:6]), 7)
             codes.append(meta[6:7])
+            codes = [code.astype(jnp.float32) for code in codes]
             rest = jnp.zeros((8, CHUNK), jnp.float32)
             for values in (emb_ref[start : start + CHUNK, :], emb_other_ref[part, :]):
                 values = values.astype(jnp.float32)
@@ -85,7 +85,7 @@
         source = pl.ds(first, half)
         refs = [(own_ref, base)] + ([(mine_ref, 0)] if base == 0 else [])
         sides = (
-            (emb_ref[...], meta_ref[0:half_vecs, source].astype(jnp.bfloat16), sub),
+            (emb_ref[...], vec_ref[:, source], sub),
             (emb_other_ref[source, :], vec_other_ref[:, source], 1 - sub),
         )
         for ref, top in refs:
@@ -96,7 +96,7 @@
             ref[first_code : first_code + CODE_ROWS, :] = code_ref[...]
 
 
-def packs_of(emb_mine, emb_rest, emb_other, vec_other, meta):
+def packs_of(emb_mine, emb_rest, emb_other, vec, vec_other, meta):
     half, width = emb_mine.shape
     features = 2 * width
     assert half == features
@@ -104,12 +104,12 @@
     return pl.pallas_call(
         pack_kernel,
         out_shape=[jax.ShapeDtypeStruct((count * size, features), jnp.bfloat16) for count in (2, 1)],
-        in_specs=[VMEM_SPEC] * 5,
+        in_specs=[VMEM_SPEC] * 6,
         out_specs=[VMEM_SPEC] * 2,
         scratch_shapes=[pltpu.VMEM((CODE_ROWS, half), jnp.bfloat16)],
         compiler_params=params(),
         name="pack",
-    )(emb_mine, emb_rest, emb_other, vec_other, meta)
+    )(emb_mine, emb_rest, emb_other, vec, vec_other, meta)
 
 
 def decode(codes):
@@ -286,30 +286,24 @@
     )(*parts)
 
 
-def gram_kernel(mine_ref, other_ref, grams_ref):
+def gram_kernel(mine_ref, other_ref, gram_ref):
     vecs, cols = mine_ref.shape
-    packed = []
+    totals = []
     for ref in (mine_ref, other_ref):
         image = ref[...]
-        total = jnp.zeros((8, LANES), jnp.float32)
-        for piece in range(LANES // vecs):
-            shifted = [image]
-            if piece > 0:
-                shifted.insert(0, jnp.zeros((piece * vecs, cols), jnp.float32))
-            if piece < LANES // vecs - 1:
-                shifted.append(jnp.zeros((LANES - (piece + 1) * vecs, cols), jnp.float32))
-            lines = image[8 * piece : 8 * piece + 8]
-            total = total + dot_nt(lines, jnp.concatenate(shifted, axis=0), lax.Precision.HIGHEST)
-        packed.append(total)
-    both = packed[0] + packed[1]
-    for copy in range(grams_ref.shape[0]):
-        grams_ref[copy] = both
-
-
-def grams_of(mine, other, copies):
+        padded = jnp.concatenate([image, jnp.zeros((LANES - vecs, cols), jnp.float32)], axis=0)
+        totals.append(dot_nt(image, padded, lax.Precision.HIGHEST))
+    gram = totals[0] + totals[1]
+    packed = gram[0:8]
+    for piece in range(1, vecs // 8):
+        packed = packed + pltpu.roll(gram[8 * piece : 8 * piece + 8], piece * vecs, 1)
+    gram_ref[...] = packed
+
+
+def gram_of(mine, other):
     return pl.pallas_call(
         gram_kernel,
-        out_shape=jax.ShapeDtypeStruct((copies, 8, LANES), jnp.float32),
+        out_shape=jax.ShapeDtypeStruct((8, LANES), jnp.float32),
         in_specs=[VMEM_SPEC] * 2,
         out_specs=VMEM_SPEC,
         compiler_params=params(),
@@ -317,19 +311,34 @@
     )(mine, other)
 
 
-def basis_kernel(total_rows, grams_ref, mine_ref, other_ref, out_ref, inverse_ref):
+def inverse_of(number):
+    guess = pl.reciprocal(number, approx=True)
+    guess = guess * (2.0 - number * guess)
+    return guess * (2.0 - number * guess)
+
+
+def basis_kernel(total_rows, gram_ref, mine_ref, other_ref, out_ref, inverse_ref):
     vecs, half = mine_ref.shape
     sub = lax.axis_index("sub")
-    packed = jnp.sum(grams_ref[...], axis=0) / total_rows
+    packed = gram_ref[...] / total_rows
     lane = lax.broadcasted_iota(jnp.int32, (vecs, LANES), 1)
     line = lax.broadcasted_iota(jnp.int32, (vecs, LANES), 0)
     pieces = [packed] + [pltpu.roll(packed, LANES - piece * vecs, 1) for piece in range(1, LANES // vecs)]
     matrix = jnp.where(lane < vecs, jnp.concatenate(pieces, axis=0), 0.0)
     matrix = jnp.where(lane == line + vecs, 1.0, matrix)
-    for step in range(vecs - 1):
-        column = jnp.broadcast_to(matrix[:, step : step + 1], (vecs, LANES))
-        scaled = matrix[step : step + 1, :] / column[step : step + 1, :]
-        matrix = jnp.where(line > step, matrix - column * scaled, matrix)
+    for step in range(0, vecs, 2):
+        left = jnp.broadcast_to(matrix[:, step : step + 1], (vecs, LANES))
+        right = jnp.broadcast_to(matrix[:, step + 1 : step + 2], (vecs, LANES))
+        upper, lower = matrix[step : step + 1, :], matrix[step + 1 : step + 2, :]
+        across = right[step : step + 1, :]
+        inverse = inverse_of(left[step : step + 1, :])
+        factor = left[step + 1 : step + 2, :] * inverse
+        lower = lower - factor * upper
+        inverse_next = inverse_of(right[step + 1 : step + 2, :] - factor * across)
+        first = left * inverse
+        second = (right - first * across) * inverse_next
+        reduced = matrix - first * upper - second * lower
+        matrix = jnp.where(line > step + 1, reduced, jnp.where(line == step + 1, lower, matrix))
     pivots = jnp.sum(jnp.where(lane == line, matrix, 0.0), axis=1, keepdims=True)
     inverse_ref[...] = pltpu.roll(matrix / jnp.sqrt(pivots), LANES - vecs, 1)
     share = vecs // 2
@@ -340,7 +349,7 @@
         )
 
 
-def basis_of(grams, mine, other, total_rows):
+def basis_of(gram, mine, other, total_rows):
     vecs, half = mine.shape
     return pl.pallas_call(
         functools.partial(basis_kernel, total_rows),
@@ -350,7 +359,7 @@
         scratch_shapes=[pltpu.VMEM((vecs, LANES), jnp.float32)],
         compiler_params=params(),
         name="basis",
-    )(grams, mine, other)
+    )(gram, mine, other)
 
 
 def exchanges(pairs):
@@ -368,6 +377,16 @@
     return [(2 * source + member, 2 * target + member) for source, target in pair_moves for member in range(2)]
 
 
+def rounds(blocks):
+    bits = blocks.bit_length() - 1
+    assert blocks == 1 << bits
+    plan, first = ([(1,)], 1) if bits > 0 else ([], 0)
+    while first < bits:
+        plan.append(tuple(part << first for part in range(1, min(4, 1 << (bits - first)))))
+        first += 2
+    return plan
+
+
 def back(moves):
     return [(target, source) for source, target in moves]
 
@@ -381,15 +400,12 @@
     beside = [(block, block ^ 1) for block in range(blocks)]
     plans = [(block_moves(moves), takers) for moves, takers in exchanges(blocks // 2)]
 
-    def crossed(moves):
-        return [(2 * source + 1 - core, 2 * target + core) for source, target in moves for core in range(2)]
-
     emb_other = lax.ppermute(embeddings, "sub", swap)
     vec_other = lax.ppermute(vectors, "sub", swap)
-    meta = jnp.concatenate([array.astype(jnp.float32) for array in (vectors, boxes, spans, camera[None, :])], axis=0)
+    meta = jnp.concatenate([boxes, spans, camera[None, :]], axis=0)
     sub = lax.axis_index("sub")
     halves = [lax.dynamic_slice_in_dim(embeddings, place * half, half, 0) for place in (sub, 1 - sub)]
-    own, mine = packs_of(*halves, emb_other, vec_other, meta)
+    own, mine = packs_of(*halves, emb_other, vectors, vec_other, meta)
     sent = [lax.ppermute(mine, "blk", moves) for moves, _ in plans]
     beside_mine = lax.ppermute(mine, "blk", beside)
     weigh = functools.partial(tile, vecs=vecs)
@@ -407,16 +423,18 @@
         parts.append(lax.ppermute(row_sums, "blk", back(moves)))
         col_sums = sums if col_sums is None else col_sums + sums
     if col_sums is not None:
-        pieces = [col_sums[:, place * half : (place + 1) * half] for place in range(4)]
-        parts.append(pieces[0])
-        parts.append(lax.ppermute(pieces[1], "sub", swap))
-        parts.append(lax.ppermute(pieces[2], "blk", beside))
-        parts.append(lax.ppermute(pieces[3], ("blk", "sub"), crossed(beside)))
-
+        own_mine, own_rest, next_mine, next_rest = [col_sums[:, place * half : (place + 1) * half] for place in range(4)]
+        sides = lax.ppermute(jnp.concatenate([own_rest, next_rest], axis=1), "sub", swap)
+        parts.append(own_mine)
+        parts.append(sides[:, :half])
+        parts.append(lax.ppermute(next_mine + sides[:, half:], "blk", beside))
     image = image_of(parts, vecs)
     image_other = lax.ppermute(image, "sub", swap)
-    grams = lax.all_to_all(grams_of(image, image_other, blocks), "blk", 0, 0, tiled=True)
-    return basis_of(grams, image, image_other, blocks * rows)
+    gram = gram_of(image, image_other)
+    for offsets in rounds(blocks):
+        shares = [lax.ppermute(gram, "blk", [(block, block ^ offset) for block in range(blocks)]) for offset in offsets]
+        gram = sum(shares, gram)
+    return basis_of(gram, image, image_other, blocks * rows)
 
 
 def solution(mesh):

time: 69.1 us -> 65.7 us (0.951)
  blocking collectives: 9.97 us -> 0 us
  waiting for transfers between devices: 15.4 us -> 22 us
  starting transfers between devices: 19.5 us -> 23.1 us
  other arithmetic: 2.93 us -> 0.85 us
  Pallas kernels: 19.6 us -> 18.1 us
    all_to_all x1 -> x0, blocking collectives: 9.97 us -> none  [local(): lax.all_to_all(grams_of(image, image_other, blocks), 'blk', 0, 0, tiled=T...]
    ppermute x3 -> x6, waiting for transfers between devices: 0.01 us -> 6.71 us  [the longest x4 6.71 us: local(): lax.ppermute(gram, 'blk', [(block, block ^ offset) for block in range(blo...]
    ppermute x3 -> x6, starting transfers between devices: 2.21 us -> 5.92 us  [the longest x4 5.08 us: local(): lax.ppermute(gram, 'blk', [(block, block ^ offset) for block in range(blo...]
    convert_element_type x4 -> x0, other arithmetic: 2.87 us -> none  [local(): array.astype(jnp.float32)]
    pallas_call x1, Pallas kernels: 1.1 us -> 0.31 us  [gram_of(): pl.pallas_call(gram_kernel, out_shape=jax.ShapeDtypeStruct((8, LANES), jn...]
    concatenate x1 -> x2, other arithmetic: 0.02 us -> 0.78 us  [the longest x1 0.77 us: local(): meta = jnp.concatenate([boxes, spans, camera[None, :]], axis=0)]
  transfers between devices with their start and end apart: 13 -> 16, of which waited for: 6 -> 9; matrix products, arithmetic and copies ran while one was open for 6% -> 3% of each run, Pallas kernels for 20% -> 21%
where the time goes in v7:
time: 65.7 us; the launch traced here: 65.4 us
  starting transfers between devices  23.1 us (35%)
  waiting for transfers between devices  22 us (33%)
  Pallas kernels  18.1 us (28%)
  local copies, waits for them, and re-layouts  1.2 us (2%)
  other arithmetic  0.85 us (1%)
    pallas_call x4, Pallas kernels, tile(): pl.pallas_call(body, out_shape=shapes, in_specs=[VMEM_SPEC] * (1 + len(co...  14.2 us
    ppermute x2, starting transfers between devices, local(): parts.append(lax.ppermute(row_sums, 'blk', back(moves)))  7.97 us
    ppermute x4, waiting for transfers between devices, local(): lax.ppermute(gram, 'blk', [(block, block ^ offset) for block in range(blo...  6.71 us
    ppermute x4, starting transfers between devices, local(): lax.ppermute(gram, 'blk', [(block, block ^ offset) for block in range(blo...  5.08 us
    ppermute x2, starting transfers between devices, local(): sent = [lax.ppermute(mine, 'blk', moves) for moves, _ in plans]  4.97 us
    ppermute x1, waiting for transfers between devices, local(): beside_mine = lax.ppermute(mine, 'blk', beside)  4.57 us
    ppermute x2, waiting for transfers between devices, local(): parts.append(lax.ppermute(row_sums, 'blk', back(moves)))  4.33 us
    ppermute x2, waiting for transfers between devices, local(): sent = [lax.ppermute(mine, 'blk', moves) for moves, _ in plans]  3.79 us
  transfers between devices with their start and end apart: 16, of which 9 were waited for; matrix products, arithmetic and copies ran while one was open for 3% of the time, Pallas kernels for 21%

profile of v7, /device:TPU:0, one launch (start us, length us, event | category | flops | bytes accessed | tf_op | source)
XLA Modules:
  0.0 65.4 jit_solution(12193693086986483321)
XLA Ops:
  0.0 0.5 collective-permute-start
  0.5 1.1 %constant_dynamic-slice_fusion = (bf16[512,256]{1,0:T(8,128)(2,1)S(1)}, bf16[512,256]{1,0:T(8,128)(2,1)S(1)}) fusion(bf16[1024,256]{1,0:T(8,128)(2,1)} %param.5, s32[]{:T(128)S(6)} %select_n.7, s32[]{:T(128)S(6)} %select_n.6), kind=kLoop, calls=%fused_computation.7 | loop fusion | bytes 1048584 | tf_op jit(solution)/shard_map/dynamic_slice | solution.py:407
  1.6 0.8 %pad_add_fusion.meta_ref = s32[7,1024]{1,0:T(8,128)S(1)} fusion(s32[1,1024]{1,0:T(1,128)} %bitcast.1, s32[2,1024]{1,0:T(2,128)} %param.8, s32[4,1024]{1,0:T(4,128)} %param.7), kind=kLoop, calls=%fused_computation.2 | loop fusion | flops 14336 | bytes 57344 | tf_op jit(solution)/shard_map/concatenate | solution.py:405
  2.4 0.7 %pack.1 = (bf16[1120,512]{1,0:T(8,128)(2,1)S(1)}, bf16[560,512]{1,0:T(8,128)(2,1)S(1)}) custom-call(bf16[512,256]{1,0:T(8,128)(2,1)S(1)} %get-tuple-element.30.emb_mine_ref, bf16[512,256]{1,0:T(8,128)(2,1)S(1)} %get-tuple-element.29.emb_rest_ref, bf16[1024,256]{1,0:T(8,128)(2,1)S(1)} %collective-permute-done.emb_other_ref, bf16[16,1024]{1,0:T(8,128)(2,1)S(1)} %copy-done, ...), custom_call_target="tpu_custom_call" | custom-call | tf_op jit(solution)/shard_map/pack/pallas_call | solution.py:104
  3.1 3.0 %collective-permute-start.2 = (bf16[560,512]{1,0:T(8,128)(2,1)S(1)}, bf16[560,512]{1,0:T(8,128)(2,1)S(1)}, u32[]{:S(2)}, u32[]{:S(2)}) collective-permute-start(bf16[560,512]{1,0:T(8,128)(2,1)S(1)} %get-tuple-element.17.refs_0_), channel_id=1, source_target_pairs={{0,2},{2,0},{4,6},{6,4},{8,10},{10,8},{12,14},{14,12},{1,3},{3,1},... | collective-permute-start | bytes 1720328 | tf_op jit(solution)/shard_map/ppermute | solution.py:410
  6.1 3.6 %collective-permute-start.3 = (bf16[560,512]{1,0:T(8,128)(2,1)S(1)}, bf16[560,512]{1,0:T(8,128)(2,1)S(1)}, u32[]{:S(2)}, u32[]{:S(2)}) collective-permute-start(bf16[560,512]{1,0:T(8,128)(2,1)S(1)} %get-tuple-element.17.refs_0_), channel_id=1, source_target_pairs={{4,0},{6,2},{8,4},{10,6},{12,8},{14,10},{0,12},{2,14},{5,1},{7,3},... | collective-permute-start | bytes 1720328 | tf_op jit(solution)/shard_map/ppermute | solution.py:409
  9.7 1.4 %collective-permute-start.4 = (bf16[560,512]{1,0:T(8,128)(2,1)S(1)}, bf16[560,512]{1,0:T(8,128)(2,1)S(1)}, u32[]{:S(2)}, u32[]{:S(2)}) collective-permute-start(bf16[560,512]{1,0:T(8,128)(2,1)S(1)} %get-tuple-element.17.refs_0_), channel_id=1, source_target_pairs={{0,8},{2,10},{12,4},{14,6},{1,9},{3,11},{13,5},{15,7},{16,24},{18,... | collective-permute-start | bytes 1720328 | tf_op jit(solution)/shard_map/ppermute | solution.py:409
  11.1 3.6 %tile.4.refs_0_ = f32[40,512]{1,0:T(8,128)S(1)} custom-call(bf16[560,512]{1,0:T(8,128)(2,1)S(1)} %get-tuple-element.17.refs_0_, bf16[1120,512]{1,0:T(8,128)(2,1)S(1)} %get-tuple-element.18.refs_1_), custom_call_target="tpu_custom_call" | custom-call | flops 1 | bytes 1 | tf_op jit(solution)/shard_map/tile/pallas_call | solution.py:250
  14.8 4.6 %collective-permute-done.2 = bf16[560,512]{1,0:T(8,128)(2,1)S(1)} collective-permute-done((bf16[560,512]{1,0:T(8,128)(2,1)S(1)}, bf16[560,512]{1,0:T(8,128)(2,1)S(1)}, u32[]{:S(2)}, u32[]{:S(2)}) %collective-permute-start.2) | collective-permute-done | bytes 573472 | tf_op jit(solution)/shard_map/ppermute | solution.py:410
  19.3 3.8 %collective-permute-done.3.refs_0_ = bf16[560,512]{1,0:T(8,128)(2,1)S(1)} collective-permute-done((bf16[560,512]{1,0:T(8,128)(2,1)S(1)}, bf16[560,512]{1,0:T(8,128)(2,1)S(1)}, u32[]{:S(2)}, u32[]{:S(2)}) %collective-permute-start.3) | collective-permute-done | bytes 573472 | tf_op jit(solution)/shard_map/ppermute | solution.py:409
  23.3 0.6 collective-permute-start.6
  23.9 0.9 %collective-permute-done.5 = bf16[272,512]{1,0:T(8,128)(2,1)S(1)} collective-permute-done((bf16[272,512]{1,0:T(8,128)(2,1)S(1)}, bf16[272,512]{1,0:T(8,128)(2,1)S(1)}, u32[]{:S(2)}, u32[]{:S(2)}) %collective-permute-start.5) | collective-permute-done | bytes 278560 | tf_op jit(solution)/shard_map/ppermute | solution.py:416
  24.8 0.4 collective-permute-done.6
  25.2 3.4 %tile.6.refs_1_ = f32[40,512]{1,0:T(8,128)S(1)} custom-call(bf16[560,512]{1,0:T(8,128)(2,1)S(1)} %get-tuple-element.17.refs_0_, bf16[1120,512]{1,0:T(8,128)(2,1)S(1)} %constant_dynamic-update-slice_fusion.refs_2_.refs_1_), custom_call_target="tpu_custom_call" | custom-call | flops 1 | bytes 1 | tf_op jit(solution)/shard_map/tile/pallas_call | solution.py:250
  28.6 6.9 %tile.5 = (f32[40,512]{1,0:T(8,128)S(1)}, f32[40,2048]{1,0:T(8,128)S(1)}) custom-call(bf16[560,512]{1,0:T(8,128)(2,1)S(1)} %collective-permute-done.3.refs_0_, bf16[1120,512]{1,0:T(8,128)(2,1)S(1)} %get-tuple-element.18.refs_1_, bf16[1120,512]{1,0:T(8,128)(2,1)S(1)} %constant_dynamic-update-slice_fusion.refs_2_.refs_1_), custom_call_target="tpu_custom_call" | custom-call | flops 1 | bytes 1 | tf_op jit(solution)/shard_map/tile/pallas_call | solution.py:250
  35.6 0.2 tile.7
  35.9 0.3 collective-permute-start.9
  36.2 1.3 %collective-permute-start.8 = (f32[40,512]{1,0:T(8,128)S(1)}, f32[40,512]{1,0:T(8,128)S(1)}, u32[]{:S(2)}, u32[]{:S(2)}) collective-permute-start(f32[40,512]{1,0:T(8,128)S(1)} %get-tuple-element.26), channel_id=1, source_target_pairs={{8,0},{10,2},{4,12},{6,14},{9,1},{11,3},{5,13},{7,15},{24,16},{26,... | collective-permute-start | bytes 245768 | tf_op jit(solution)/shard_map/ppermute | solution.py:423
  37.5 6.7 %collective-permute-start.7 = (f32[40,512]{1,0:T(8,128)S(1)}, f32[40,512]{1,0:T(8,128)S(1)}, u32[]{:S(2)}, u32[]{:S(2)}) collective-permute-start(f32[40,512]{1,0:T(8,128)S(1)} %get-tuple-element.24), channel_id=1, source_target_pairs={{0,4},{2,6},{4,8},{6,10},{8,12},{10,14},{12,0},{14,2},{1,5},{3,7},... | collective-permute-start | bytes 245768 | tf_op jit(solution)/shard_map/ppermute | solution.py:423
  44.2 0.6 collective-permute-start.10
  44.8 4.3 %collective-permute-done.8.refs_3_ = f32[40,512]{1,0:T(8,128)S(1)} collective-permute-done((f32[40,512]{1,0:T(8,128)S(1)}, f32[40,512]{1,0:T(8,128)S(1)}, u32[]{:S(2)}, u32[]{:S(2)}) %collective-permute-start.8) | collective-permute-done | bytes 81952 | tf_op jit(solution)/shard_map/ppermute | solution.py:423
  49.1 0.1 collective-permute-start.11
  49.2 1.2 %collective-permute-done.11.other_ref = f32[32,512]{1,0:T(8,128)S(1)} collective-permute-done((f32[32,512]{1,0:T(8,128)S(1)}, f32[32,512]{1,0:T(8,128)S(1)}, u32[]{:S(2)}, u32[]{:S(2)}) %collective-permute-start.11) | collective-permute-done | bytes 65568 | tf_op jit(solution)/shard_map/ppermute | solution.py:432
  50.5 0.3 gram.1
  50.8 0.5 collective-permute-start.12
  51.3 3.1 %collective-permute-done.12 = f32[8,128]{1,0:T(8,128)S(1)} collective-permute-done((f32[8,128]{1,0:T(8,128)S(1)}, f32[8,128]{1,0:T(8,128)S(1)}, u32[]{:S(2)}, u32[]{:S(2)}) %collective-permute-start.12) | collective-permute-done | bytes 4128 | tf_op jit(solution)/shard_map/ppermute | solution.py:435
  54.4 2.2 %collective-permute-start.13 = (f32[8,128]{1,0:T(8,128)S(1)}, f32[8,128]{1,0:T(8,128)S(1)}, u32[]{:S(2)}, u32[]{:S(2)}) collective-permute-start(f32[8,128]{1,0:T(8,128)S(1)} %add.28), channel_id=1, source_target_pairs={{0,4},{2,6},{4,0},{6,2},{8,12},{10,14},{12,8},{14,10},{1,5},{3,7},... | collective-permute-start | bytes 12296 | tf_op jit(solution)/shard_map/ppermute | solution.py:435
  56.6 0.6 collective-permute-start.14
  57.1 1.8 %collective-permute-start.15 = (f32[8,128]{1,0:T(8,128)S(1)}, f32[8,128]{1,0:T(8,128)S(1)}, u32[]{:S(2)}, u32[]{:S(2)}) collective-permute-start(f32[8,128]{1,0:T(8,128)S(1)} %add.28), channel_id=1, source_target_pairs={{0,12},{2,14},{4,8},{6,10},{8,4},{10,6},{12,0},{14,2},{1,13},{3,15... | collective-permute-start | bytes 12296 | tf_op jit(solution)/shard_map/ppermute | solution.py:435
  58.9 2.1 %collective-permute-done.14 = f32[8,128]{1,0:T(8,128)S(1)} collective-permute-done((f32[8,128]{1,0:T(8,128)S(1)}, f32[8,128]{1,0:T(8,128)S(1)}, u32[]{:S(2)}, u32[]{:S(2)}) %collective-permute-start.14) | collective-permute-done | bytes 4128 | tf_op jit(solution)/shard_map/ppermute | solution.py:435
  61.1 1.5 %collective-permute-done.15 = f32[8,128]{1,0:T(8,128)S(1)} collective-permute-done((f32[8,128]{1,0:T(8,128)S(1)}, f32[8,128]{1,0:T(8,128)S(1)}, u32[]{:S(2)}, u32[]{:S(2)}) %collective-permute-start.15) | collective-permute-done | bytes 4128 | tf_op jit(solution)/shard_map/ppermute | solution.py:435
  62.6 2.9 %basis.1 = f32[16,1024]{1,0:T(8,128)} custom-call(f32[8,128]{1,0:T(8,128)S(1)} %add_add_fusion.gram_ref, f32[32,512]{1,0:T(8,128)S(1)} %image.1.mine_ref, f32[32,512]{1,0:T(8,128)S(1)} %collective-permute-done.11.other_ref), custom_call_target="tpu_custom_call" | custom-call | tf_op jit(solution)/shard_map/basis/pallas_call | solution.py:354
  (23 shorter events, 0.4 us)
Async XLA Ops:
  0.0 2.4 %copy-start = (bf16[16,1024]{1,0:T(8,128)(2,1)S(1)}, bf16[16,1024]{1,0:T(8,128)(2,1)}, u32[]{:S(2)}) copy-start(bf16[16,1024]{1,0:T(8,128)(2,1)} %vec_ref.1) | copy-start | bytes 98308
  0.0 2.4 %collective-permute-start = (bf16[1024,256]{1,0:T(8,128)(2,1)}, bf16[1024,256]{1,0:T(8,128)(2,1)S(1)}, u32[]{:S(2)}, u32[]{:S(2)}) collective-permute-start(bf16[1024,256]{1,0:T(8,128)(2,1)} %param.5), channel_id=1, source_target_pairs={{0,1},{1,0},{2,3},{3,2},{4,5},{5,4},{6,7},{7,6},{8,9},{9,8},{10,11... | collective-permute-start | bytes 1572872 | tf_op jit(solution)/shard_map/ppermute | solution.py:403
  0.5 1.9 %collective-permute-start.1 = (bf16[16,1024]{1,0:T(8,128)(2,1)}, bf16[16,1024]{1,0:T(8,128)(2,1)S(1)}, u32[]{:S(2)}, u32[]{:S(2)}) collective-permute-start(bf16[16,1024]{1,0:T(8,128)(2,1)} %vec_ref.1), channel_id=1, source_target_pairs={{0,1},{1,0},{2,3},{3,2},{4,5},{5,4},{6,7},{7,6},{8,9},{9,8},{10,11... | collective-permute-start | bytes 98312 | tf_op jit(solution)/shard_map/ppermute | solution.py:404
  3.1 16.2 %collective-permute-start.2 = (bf16[560,512]{1,0:T(8,128)(2,1)S(1)}, bf16[560,512]{1,0:T(8,128)(2,1)S(1)}, u32[]{:S(2)}, u32[]{:S(2)}) collective-permute-start(bf16[560,512]{1,0:T(8,128)(2,1)S(1)} %get-tuple-element.17.refs_0_), channel_id=1, source_target_pairs={{0,2},{2,0},{4,6},{6,4},{8,10},{10,8},{12,14},{14,12},{1,3},{3,1},... | collective-permute-start | bytes 1720328 | tf_op jit(solution)/shard_map/ppermute | solution.py:410
  6.1 17.0 %collective-permute-start.3 = (bf16[560,512]{1,0:T(8,128)(2,1)S(1)}, bf16[560,512]{1,0:T(8,128)(2,1)S(1)}, u32[]{:S(2)}, u32[]{:S(2)}) collective-permute-start(bf16[560,512]{1,0:T(8,128)(2,1)S(1)} %get-tuple-element.17.refs_0_), channel_id=1, source_target_pairs={{4,0},{6,2},{8,4},{10,6},{12,8},{14,10},{0,12},{2,14},{5,1},{7,3},... | collective-permute-start | bytes 1720328 | tf_op jit(solution)/shard_map/ppermute | solution.py:409
  9.7 25.9 %collective-permute-start.4 = (bf16[560,512]{1,0:T(8,128)(2,1)S(1)}, bf16[560,512]{1,0:T(8,128)(2,1)S(1)}, u32[]{:S(2)}, u32[]{:S(2)}) collective-permute-start(bf16[560,512]{1,0:T(8,128)(2,1)S(1)} %get-tuple-element.17.refs_0_), channel_id=1, source_target_pairs={{0,8},{2,10},{12,4},{14,6},{1,9},{3,11},{13,5},{15,7},{16,24},{18,... | collective-permute-start | bytes 1720328 | tf_op jit(solution)/shard_map/ppermute | solution.py:409
  23.1 1.6 %collective-permute-start.5 = (bf16[272,512]{1,0:T(8,128)(2,1)S(1)}, bf16[272,512]{1,0:T(8,128)(2,1)S(1)}, u32[]{:S(2)}, u32[]{:S(2)}) collective-permute-start(bf16[272,512]{1,0:T(8,128)(2,1)S(1)} %slice.24), channel_id=1, source_target_pairs={{0,1},{1,0},{2,3},{3,2},{4,5},{5,4},{6,7},{7,6},{8,9},{9,8},{10,11... | collective-permute-start | bytes 835592 | tf_op jit(solution)/shard_map/ppermute | solution.py:416
  23.3 1.9 %collective-permute-start.6 = (bf16[288,512]{1,0:T(8,128)(2,1)S(1)}, bf16[288,512]{1,0:T(8,128)(2,1)S(1)}, u32[]{:S(2)}, u32[]{:S(2)}) collective-permute-start(bf16[288,512]{1,0:T(8,128)(2,1)S(1)} %slice.25), channel_id=1, source_target_pairs={{0,1},{1,0},{2,3},{3,2},{4,5},{5,4},{6,7},{7,6},{8,9},{9,8},{10,11... | collective-permute-start | bytes 884744 | tf_op jit(solution)/shard_map/ppermute | solution.py:416
  35.9 8.3 %collective-permute-start.9 = (f32[40,1024]{1,0:T(8,128)S(1)}, f32[40,1024]{1,0:T(8,128)S(1)}, u32[]{:S(2)}, u32[]{:S(2)}) collective-permute-start(f32[40,1024]{1,0:T(8,128)S(1)} %pad_maximum_fusion), channel_id=1, source_target_pairs={{0,1},{1,0},{2,3},{3,2},{4,5},{5,4},{6,7},{7,6},{8,9},{9,8},{10,11... | collective-permute-start | bytes 491528 | tf_op jit(solution)/shard_map/ppermute | solution.py:427
  36.2 12.9 %collective-permute-start.8 = (f32[40,512]{1,0:T(8,128)S(1)}, f32[40,512]{1,0:T(8,128)S(1)}, u32[]{:S(2)}, u32[]{:S(2)}) collective-permute-start(f32[40,512]{1,0:T(8,128)S(1)} %get-tuple-element.26), channel_id=1, source_target_pairs={{8,0},{10,2},{4,12},{6,14},{9,1},{11,3},{5,13},{7,15},{24,16},{26,... | collective-permute-start | bytes 245768 | tf_op jit(solution)/shard_map/ppermute | solution.py:423
  37.5 11.6 %collective-permute-start.7 = (f32[40,512]{1,0:T(8,128)S(1)}, f32[40,512]{1,0:T(8,128)S(1)}, u32[]{:S(2)}, u32[]{:S(2)}) collective-permute-start(f32[40,512]{1,0:T(8,128)S(1)} %get-tuple-element.24), channel_id=1, source_target_pairs={{0,4},{2,6},{4,8},{6,10},{8,12},{10,14},{12,0},{14,2},{1,5},{3,7},... | collective-permute-start | bytes 245768 | tf_op jit(solution)/shard_map/ppermute | solution.py:423
  44.2 4.9 %collective-permute-start.10 = (f32[40,512]{1,0:T(8,128)S(1)}, f32[40,512]{1,0:T(8,128)S(1)}, u32[]{:S(2)}, u32[]{:S(2)}) collective-permute-start(f32[40,512]{1,0:T(8,128)S(1)} %get-tuple-element.31), channel_id=1, source_target_pairs={{0,2},{2,0},{4,6},{6,4},{8,10},{10,8},{12,14},{14,12},{1,3},{3,1},... | collective-permute-start | bytes 245768 | tf_op jit(solution)/shard_map/ppermute | solution.py:430
  49.1 1.3 %collective-permute-start.11 = (f32[32,512]{1,0:T(8,128)S(1)}, f32[32,512]{1,0:T(8,128)S(1)}, u32[]{:S(2)}, u32[]{:S(2)}) collective-permute-start(f32[32,512]{1,0:T(8,128)S(1)} %image.1.mine_ref), channel_id=1, source_target_pairs={{0,1},{1,0},{2,3},{3,2},{4,5},{5,4},{6,7},{7,6},{8,9},{9,8},{10,11... | collective-permute-start | bytes 196616 | tf_op jit(solution)/shard_map/ppermute | solution.py:432
  50.8 3.6 %collective-permute-start.12 = (f32[8,128]{1,0:T(8,128)S(1)}, f32[8,128]{1,0:T(8,128)S(1)}, u32[]{:S(2)}, u32[]{:S(2)}) collective-permute-start(f32[8,128]{1,0:T(8,128)S(1)} %gram.1), channel_id=1, source_target_pairs={{0,2},{2,0},{4,6},{6,4},{8,10},{10,8},{12,14},{14,12},{1,3},{3,1},... | collective-permute-start | bytes 12296 | tf_op jit(solution)/shard_map/ppermute | solution.py:435
  54.4 4.6 %collective-permute-start.13 = (f32[8,128]{1,0:T(8,128)S(1)}, f32[8,128]{1,0:T(8,128)S(1)}, u32[]{:S(2)}, u32[]{:S(2)}) collective-permute-start(f32[8,128]{1,0:T(8,128)S(1)} %add.28), channel_id=1, source_target_pairs={{0,4},{2,6},{4,0},{6,2},{8,12},{10,14},{12,8},{14,10},{1,5},{3,7},... | collective-permute-start | bytes 12296 | tf_op jit(solution)/shard_map/ppermute | solution.py:435
  56.6 4.5 %collective-permute-start.14 = (f32[8,128]{1,0:T(8,128)S(1)}, f32[8,128]{1,0:T(8,128)S(1)}, u32[]{:S(2)}, u32[]{:S(2)}) collective-permute-start(f32[8,128]{1,0:T(8,128)S(1)} %add.28), channel_id=1, source_target_pairs={{0,8},{2,10},{4,12},{6,14},{8,0},{10,2},{12,4},{14,6},{1,9},{3,11}... | collective-permute-start | bytes 12296 | tf_op jit(solution)/shard_map/ppermute | solution.py:435
  57.1 5.4 %collective-permute-start.15 = (f32[8,128]{1,0:T(8,128)S(1)}, f32[8,128]{1,0:T(8,128)S(1)}, u32[]{:S(2)}, u32[]{:S(2)}) collective-permute-start(f32[8,128]{1,0:T(8,128)S(1)} %add.28), channel_id=1, source_target_pairs={{0,12},{2,14},{4,8},{6,10},{8,4},{10,6},{12,0},{14,2},{1,13},{3,15... | collective-permute-start | bytes 12296 | tf_op jit(solution)/shard_map/ppermute | solution.py:435

commit v8 on v7

--- a/solution.py
+++ b/solution.py
@@ -45,13 +45,12 @@
     return half + vecs + CODE_ROWS
 
 
-def pack_kernel(emb_mine_ref, emb_rest_ref, emb_other_ref, vec_ref, vec_other_ref, meta_ref, own_ref, mine_ref, code_ref):
+def pack_kernel(emb_mine_ref, emb_rest_ref, emb_other_ref, vec_ref, vec_other_ref, meta_ref, mine_ref, rest_ref, code_ref):
     sub = lax.axis_index("sub")
     half, width = emb_mine_ref.shape
     half_vecs = vec_other_ref.shape[0]
-    size = mine_ref.shape[0]
     ones = jnp.ones((8, width), jnp.bfloat16)
-    for base, emb_ref, place in ((0, emb_mine_ref, sub), (size, emb_rest_ref, 1 - sub)):
+    for ref, emb_ref, place in ((mine_ref, emb_mine_ref, sub), (rest_ref, emb_rest_ref, 1 - sub)):
         first = pl.multiple_of(place * half, half)
         for start in range(0, half, CHUNK):
             part = pl.ds(first + start, CHUNK)
@@ -83,17 +82,15 @@
                 rest = rest - piece
             code_ref[:, start : start + CHUNK] = jnp.concatenate(codes, axis=0).astype(jnp.bfloat16)
         source = pl.ds(first, half)
-        refs = [(own_ref, base)] + ([(mine_ref, 0)] if base == 0 else [])
         sides = (
             (emb_ref[...], vec_ref[:, source], sub),
             (emb_other_ref[source, :], vec_other_ref[:, source], 1 - sub),
         )
-        for ref, top in refs:
-            for values, vectors, side in sides:
-                ref[top : top + half, pl.ds(pl.multiple_of(side * width, width), width)] = values
-                ref[pl.ds(pl.multiple_of(top + half + side * half_vecs, 16), half_vecs), :] = vectors
-            first_code = top + half + 2 * half_vecs
-            ref[first_code : first_code + CODE_ROWS, :] = code_ref[...]
+        for values, vectors, side in sides:
+            ref[0:half, pl.ds(pl.multiple_of(side * width, width), width)] = values
+            ref[pl.ds(pl.multiple_of(half + side * half_vecs, 16), half_vecs), :] = vectors
+        first_code = half + 2 * half_vecs
+        ref[first_code : first_code + CODE_ROWS, :] = code_ref[...]
 
 
 def packs_of(emb_mine, emb_rest, emb_other, vec, vec_other, meta):
@@ -103,7 +100,7 @@
     size = pack_rows(half, 2 * vec_other.shape[0])
     return pl.pallas_call(
         pack_kernel,
-        out_shape=[jax.ShapeDtypeStruct((count * size, features), jnp.bfloat16) for count in (2, 1)],
+        out_shape=[jax.ShapeDtypeStruct((size, features), jnp.bfloat16)] * 2,
         in_specs=[VMEM_SPEC] * 6,
         out_specs=[VMEM_SPEC] * 2,
         scratch_shapes=[pltpu.VMEM((CODE_ROWS, half), jnp.bfloat16)],
@@ -144,32 +141,28 @@
     return jnp.where(barred, 0.0, value)
 
 
-def tile_kernel(blocks, own_block, receivers, vecs, *refs):
+def tile_kernel(blocks, turns, own_block, receivers, vecs, *refs):
     row_ref, col_refs = refs[0], refs[1 : 1 + blocks]
-    row_out_ref, col_out_ref, field_ref, spread_ref = refs[1 + blocks : 5 + blocks]
-    products, weights = refs[5 + blocks : 7 + blocks], refs[7 + blocks :]
-    rows = row_out_ref.shape[1]
-    size = row_ref.shape[0]
-    per_pack = rows // CHUNK
-    row_out_ref[...] = jnp.zeros_like(row_out_ref)
+    row_out_ref, col_out_ref, field_ref, spread_ref, sum_ref = refs[1 + blocks : 6 + blocks]
+    products, weights = refs[6 + blocks : 8 + blocks], refs[8 + blocks :]
+    size, rows = row_ref.shape
+    features = size - vecs - CODE_ROWS
+    vec_rows, code_rows = slice(features, features + vecs), slice(features + vecs, size)
+    sum_ref[...] = jnp.zeros_like(sum_ref)
 
     def block(col_ref, done, row_vecs):
-        chunks = col_ref.shape[0] // size * per_pack
-
-        def within(step):
-            pack, chunk = step // per_pack, lax.rem(step, per_pack)
-            return pack * size, pl.multiple_of(chunk * CHUNK, CHUNK)
+        chunks = col_ref.shape[1] // CHUNK
+
+        def place(step, base=0):
+            return pl.ds(pl.multiple_of(base + step * CHUNK, CHUNK), CHUNK)
 
         def multiply(step, product_ref):
-            base, start = within(step)
-            columns = col_ref[pl.ds(pl.multiple_of(base + start, 16), CHUNK), :]
-            product_ref[...] = dot_nt(row_ref[0:rows, :], columns)
+            product_ref[...] = jnp.dot(
+                row_ref[0:rows, :], col_ref[0:features, place(step)], preferred_element_type=jnp.float32
+            )
 
         def weigh(step, product_ref, weight_ref):
-            base, start = within(step)
-            code_part = pl.ds(pl.multiple_of(base + rows + vecs, 16), CODE_ROWS)
-            col = decode(col_ref[code_part, pl.ds(start, CHUNK)])
-            col = [jnp.broadcast_to(field, (8, CHUNK)) for field in col]
+            col = [jnp.broadcast_to(field, (8, CHUNK)) for field in decode(col_ref[code_rows, place(step)])]
             for first_row in range(0, rows, 16):
                 both = []
                 for line in (first_row, first_row + 8):
@@ -185,12 +178,9 @@
                 weight_ref[first_row : first_row + 16, :] = jnp.concatenate(both, axis=0).astype(jnp.bfloat16)
 
         def total(step, weight_ref):
-            base, start = within(step)
-            vec_part = pl.ds(pl.multiple_of(base + rows, 16), vecs)
-            col_vecs = with_ones(col_ref[vec_part, pl.ds(start, CHUNK)])
-            row_out_ref[...] += dot_nt(col_vecs, weight_ref[...])[0:OUT_ROWS]
-            if col_out_ref is not None:
-                col_out_ref[:, pl.ds(pl.multiple_of(done + step * CHUNK, CHUNK), CHUNK)] = jnp.dot(
+            sum_ref[:, 0 : vecs + CODE_ROWS] += dot_nt(weight_ref[...], with_ones(col_ref[vec_rows, place(step)]))
+            if not turns:
+                col_out_ref[:, place(step, done)] = jnp.dot(
                     row_vecs, weight_ref[...], preferred_element_type=jnp.float32
                 )[0:OUT_ROWS]
 
@@ -208,19 +198,30 @@
         total(chunks - 1, weights[1])
 
     def compute():
-        for field, values in enumerate(decode(row_ref[rows + vecs : rows + vecs + CODE_ROWS, :])):
+        for field, values in enumerate(decode(row_ref[code_rows, :])):
             field_ref[field : field + 1, :] = values
         turned = field_ref[...].T
         for field in range(FIELDS):
             spread_ref[field] = jnp.broadcast_to(turned[:, field : field + 1], (rows, LANES))
-        row_vecs = with_ones(row_ref[rows : rows + vecs, :])
-        done = 0
-        for col_ref in col_refs:
-            block(col_ref, done, row_vecs)
-            done += col_ref.shape[0] // size * rows
+        row_vecs = with_ones(row_ref[vec_rows, :])
+        if turns:
+            for number, pack_ref in enumerate(col_refs):
+                part = pl.ds(number * rows, rows)
+                col_out_ref[0:features, part] = pack_ref[0:rows, :].T
+                col_out_ref[features:size, part] = pack_ref[features:size, :]
+            block(col_out_ref, 0, row_vecs)
+        else:
+            done = 0
+            for col_ref in col_refs:
+                block(col_ref, done, row_vecs)
+                done += col_ref.shape[1]
+
+    def finish():
+        row_out_ref[...] = sum_ref[...].T[0:OUT_ROWS]
 
     if receivers is None:
         compute()
+        finish()
         return
     pair = lax.axis_index("blk") // 2
     takes_part = functools.reduce(jnp.logical_or, [pair == one for one in receivers])
@@ -228,33 +229,29 @@
     @pl.when(takes_part)
     def _():
         compute()
+        finish()
 
     @pl.when(jnp.logical_not(takes_part))
     def _():
+        row_out_ref[...] = jnp.zeros_like(row_out_ref)
         col_out_ref[...] = jnp.zeros_like(col_out_ref)
 
 
-def tile(row, columns, vecs, own_block=False, col_sums=True, receivers=None):
+def tile(row, columns, vecs, turns=False, own_block=False, receivers=None):
     size, rows = row.shape
-    cols = sum(part.shape[0] // size for part in columns) * rows
-    shapes = [jax.ShapeDtypeStruct((OUT_ROWS, rows), jnp.float32)]
-    if col_sums:
-        shapes.append(jax.ShapeDtypeStruct((OUT_ROWS, cols), jnp.float32))
-
-    def body(*refs):
-        refs = list(refs)
-        if not col_sums:
-            refs.insert(2 + len(columns), None)
-        tile_kernel(len(columns), own_block, receivers, vecs, *refs)
-
+    cols = len(columns) * rows if turns else sum(part.shape[1] for part in columns)
+    second = jax.ShapeDtypeStruct((size, cols), jnp.bfloat16)
+    if not turns:
+        second = jax.ShapeDtypeStruct((OUT_ROWS, cols), jnp.float32)
     return pl.pallas_call(
-        body,
-        out_shape=shapes,
+        functools.partial(tile_kernel, len(columns), turns, own_block, receivers, vecs),
+        out_shape=[jax.ShapeDtypeStruct((OUT_ROWS, rows), jnp.float32), second],
         in_specs=[VMEM_SPEC] * (1 + len(columns)),
-        out_specs=[VMEM_SPEC] * len(shapes),
+        out_specs=[VMEM_SPEC] * 2,
         scratch_shapes=[
             pltpu.VMEM((LANES, rows), jnp.float32),
             pltpu.VMEM((FIELDS, rows, LANES), jnp.float32),
+            pltpu.VMEM((rows, LANES), jnp.float32),
             pltpu.VMEM((rows, CHUNK), jnp.float32),
             pltpu.VMEM((rows, CHUNK), jnp.float32),
             pltpu.VMEM((rows, CHUNK), jnp.bfloat16),
@@ -286,29 +283,27 @@
     )(*parts)
 
 
-def gram_kernel(mine_ref, other_ref, gram_ref):
-    vecs, cols = mine_ref.shape
-    totals = []
-    for ref in (mine_ref, other_ref):
-        image = ref[...]
-        padded = jnp.concatenate([image, jnp.zeros((LANES - vecs, cols), jnp.float32)], axis=0)
-        totals.append(dot_nt(image, padded, lax.Precision.HIGHEST))
-    gram = totals[0] + totals[1]
+def gram_kernel(image_ref, grams_ref):
+    vecs, cols = image_ref.shape
+    image = image_ref[...]
+    padded = jnp.concatenate([image, jnp.zeros((LANES - vecs, cols), jnp.float32)], axis=0)
+    gram = dot_nt(image, padded, lax.Precision.HIGHEST)
     packed = gram[0:8]
     for piece in range(1, vecs // 8):
         packed = packed + pltpu.roll(gram[8 * piece : 8 * piece + 8], piece * vecs, 1)
-    gram_ref[...] = packed
-
-
-def gram_of(mine, other):
+    for copy in range(grams_ref.shape[0]):
+        grams_ref[copy] = packed
+
+
+def grams_of(image, copies):
     return pl.pallas_call(
         gram_kernel,
-        out_shape=jax.ShapeDtypeStruct((8, LANES), jnp.float32),
-        in_specs=[VMEM_SPEC] * 2,
+        out_shape=jax.ShapeDtypeStruct((copies, 8, LANES), jnp.float32),
+        in_specs=[VMEM_SPEC],
         out_specs=VMEM_SPEC,
         compiler_params=params(),
         name="gram",
-    )(mine, other)
+    )(image)
 
 
 def inverse_of(number):
@@ -317,10 +312,10 @@
     return guess * (2.0 - number * guess)
 
 
-def basis_kernel(total_rows, gram_ref, mine_ref, other_ref, out_ref, inverse_ref):
+def basis_kernel(total_rows, grams_ref, mine_ref, other_ref, out_ref, inverse_ref):
     vecs, half = mine_ref.shape
     sub = lax.axis_index("sub")
-    packed = gram_ref[...] / total_rows
+    packed = jnp.sum(grams_ref[...], axis=0) / total_rows
     lane = lax.broadcasted_iota(jnp.int32, (vecs, LANES), 1)
     line = lax.broadcasted_iota(jnp.int32, (vecs, LANES), 0)
     pieces = [packed] + [pltpu.roll(packed, LANES - piece * vecs, 1) for piece in range(1, LANES // vecs)]
@@ -349,7 +344,7 @@
         )
 
 
-def basis_of(gram, mine, other, total_rows):
+def basis_of(grams, mine, other, total_rows):
     vecs, half = mine.shape
     return pl.pallas_call(
         functools.partial(basis_kernel, total_rows),
@@ -359,7 +354,7 @@
         scratch_shapes=[pltpu.VMEM((vecs, LANES), jnp.float32)],
         compiler_params=params(),
         name="basis",
-    )(gram, mine, other)
+    )(grams, mine, other)
 
 
 def exchanges(pairs):
@@ -377,16 +372,6 @@
     return [(2 * source + member, 2 * target + member) for source, target in pair_moves for member in range(2)]
 
 
-def rounds(blocks):
-    bits = blocks.bit_length() - 1
-    assert blocks == 1 << bits
-    plan, first = ([(1,)], 1) if bits > 0 else ([], 0)
-    while first < bits:
-        plan.append(tuple(part << first for part in range(1, min(4, 1 << (bits - first)))))
-        first += 2
-    return plan
-
-
 def back(moves):
     return [(target, source) for source, target in moves]
 
@@ -405,36 +390,41 @@
     meta = jnp.concatenate([boxes, spans, camera[None, :]], axis=0)
     sub = lax.axis_index("sub")
     halves = [lax.dynamic_slice_in_dim(embeddings, place * half, half, 0) for place in (sub, 1 - sub)]
-    own, mine = packs_of(*halves, emb_other, vectors, vec_other, meta)
+    mine, rest = packs_of(*halves, emb_other, vectors, vec_other, meta)
     sent = [lax.ppermute(mine, "blk", moves) for moves, _ in plans]
     beside_mine = lax.ppermute(mine, "blk", beside)
     weigh = functools.partial(tile, vecs=vecs)
-    own_sums = weigh(mine, [own], own_block=True, col_sums=False)[0]
-    own_sums, beside_mine, sent[:1] = lax.optimization_barrier((own_sums, beside_mine, sent[:1]))
+    own_sums, own = weigh(mine, [mine, rest], turns=True, own_block=True)
+    own_sums, own, beside_mine, sent[:1] = lax.optimization_barrier((own_sums, own, beside_mine, sent[:1]))
     cut = beside_mine.shape[0] // SWAPS // 16 * 16
     shares = [beside_mine[at * cut : (at + 1) * cut if at < SWAPS - 1 else None] for at in range(SWAPS)]
-    next_to = jnp.concatenate([beside_mine] + [lax.ppermute(share, "sub", swap) for share in shares], axis=0)
-    parts = [own_sums, weigh(mine, [next_to], col_sums=False)[0]]
+    beside_rest = jnp.concatenate([lax.ppermute(share, "sub", swap) for share in shares], axis=0)
+    beside_sums, next_to = weigh(mine, [beside_mine, beside_rest], turns=True)
+    parts = [own_sums, beside_sums]
     col_sums = None
+    returns = []
     for (moves, takers), pack in zip(plans, sent):
         if col_sums is not None:
-            pack, col_sums, parts[1:2] = lax.optimization_barrier((pack, col_sums, parts[1:2]))
+            pack, col_sums = lax.optimization_barrier((pack, col_sums))
         row_sums, sums = weigh(pack, [own, next_to], receivers=takers)
-        parts.append(lax.ppermute(row_sums, "blk", back(moves)))
+        returns.append((row_sums, back(moves)))
         col_sums = sums if col_sums is None else col_sums + sums
     if col_sums is not None:
         own_mine, own_rest, next_mine, next_rest = [col_sums[:, place * half : (place + 1) * half] for place in range(4)]
         sides = lax.ppermute(jnp.concatenate([own_rest, next_rest], axis=1), "sub", swap)
+        last_sums, last_moves = returns.pop()
+        parts.append(lax.ppermute(last_sums, "blk", last_moves))
+        crossing = next_mine + sides[:, half:]
         parts.append(own_mine)
         parts.append(sides[:, :half])
-        parts.append(lax.ppermute(next_mine + sides[:, half:], "blk", beside))
+        parts.append(lax.ppermute(crossing, "blk", beside))
+        for row_sums, moves in returns:
+            row_sums, _ = lax.optimization_barrier((row_sums, crossing))
+            parts.append(lax.ppermute(row_sums, "blk", moves))
     image = image_of(parts, vecs)
     image_other = lax.ppermute(image, "sub", swap)
-    gram = gram_of(image, image_other)
-    for offsets in rounds(blocks):
-        shares = [lax.ppermute(gram, "blk", [(block, block ^ offset) for block in range(blocks)]) for offset in offsets]
-        gram = sum(shares, gram)
-    return basis_of(gram, image, image_other, blocks * rows)
+    grams = lax.all_to_all(grams_of(image, 2 * blocks), ("blk", "sub"), 0, 0, tiled=True)
+    return basis_of(grams, image, image_other, blocks * rows)
 
 
 def solution(mesh):

time: 65.7 us -> 64.1 us (0.976)
  waiting for transfers between devices: 22 us -> 20 us
  Pallas kernels: 18.1 us -> 20 us
  starting transfers between devices: 23.1 us -> 21.6 us
    ppermute x7 -> x3, waiting for transfers between devices: 11 us -> 4.36 us  [the longest x1 4.35 us: local(): parts.append(lax.ppermute(last_sums, 'blk', last_moves))]
    all_to_all x0 -> x1, waiting for transfers between devices: none -> 5.58 us  [local(): lax.all_to_all(grams_of(image, 2 * blocks), ('blk', 'sub'), 0, 0, tiled=T...]
    ppermute x7 -> x3, starting transfers between devices: 13.6 us -> 8.27 us  [the longest x1 6.5 us: local(): parts.append(lax.ppermute(row_sums, 'blk', moves))]
    all_to_all x0 -> x1, starting transfers between devices: none -> 3.56 us  [local(): lax.all_to_all(grams_of(image, 2 * blocks), ('blk', 'sub'), 0, 0, tiled=T...]
    pallas_call x6, Pallas kernels: 15.2 us -> 17.1 us  [the longest x4 15.5 us: tile(): pl.pallas_call(functools.partial(tile_kernel, len(columns), turns, own_bl...]
  transfers between devices with their start and end apart: 16 -> 13, of which waited for: 9 -> 6; matrix products, arithmetic and copies ran while one was open for 3% -> 3% of each run, Pallas kernels for 21% -> 24%
where the time goes in v8:
time: 64.1 us; the launch traced here: 63.8 us
  starting transfers between devices  21.6 us (34%)
  waiting for transfers between devices  20 us (31%)
  Pallas kernels  20 us (31%)
  local copies, waits for them, and re-layouts  1.12 us (2%)
  other arithmetic  0.88 us (1%)
    pallas_call x4, Pallas kernels, tile(): pl.pallas_call(functools.partial(tile_kernel, len(columns), turns, own_bl...  15.5 us
    ppermute x1, starting transfers between devices, local(): parts.append(lax.ppermute(row_sums, 'blk', moves))  6.5 us
    all_to_all x1, waiting for transfers between devices, local(): lax.all_to_all(grams_of(image, 2 * blocks), ('blk', 'sub'), 0, 0, tiled=T...  5.58 us
    ppermute x2, starting transfers between devices, local(): sent = [lax.ppermute(mine, 'blk', moves) for moves, _ in plans]  4.97 us
    ppermute x1, waiting for transfers between devices, local(): parts.append(lax.ppermute(last_sums, 'blk', last_moves))  4.35 us
    ppermute x1, waiting for transfers between devices, local(): beside_mine = lax.ppermute(mine, 'blk', beside)  3.99 us
    ppermute x2, waiting for transfers between devices, local(): sent = [lax.ppermute(mine, 'blk', moves) for moves, _ in plans]  3.79 us
    all_to_all x1, starting transfers between devices, local(): lax.all_to_all(grams_of(image, 2 * blocks), ('blk', 'sub'), 0, 0, tiled=T...  3.56 us
  transfers between devices with their start and end apart: 13, of which 6 were waited for; matrix products, arithmetic and copies ran while one was open for 3% of the time, Pallas kernels for 24%

profile of v8, /device:TPU:0, one launch (start us, length us, event | category | flops | bytes accessed | tf_op | source)
XLA Modules:
  0.0 63.8 jit_solution(2578858672483649775)
XLA Ops:
  0.0 0.5 collective-permute-start
  0.5 0.1 collective-permute-start.1
  0.5 1.1 %constant_dynamic-slice_fusion = (bf16[512,256]{1,0:T(8,128)(2,1)S(1)}, bf16[512,256]{1,0:T(8,128)(2,1)S(1)}) fusion(bf16[1024,256]{1,0:T(8,128)(2,1)} %param.5, s32[]{:T(128)S(6)} %select_n.7, s32[]{:T(128)S(6)} %select_n.6), kind=kLoop, calls=%fused_computation.4 | loop fusion | bytes 1048584 | tf_op jit(solution)/shard_map/dynamic_slice | solution.py:392
  1.6 0.8 %pad_add_fusion.meta_ref = s32[7,1024]{1,0:T(8,128)S(1)} fusion(s32[1,1024]{1,0:T(1,128)} %bitcast.1, s32[2,1024]{1,0:T(2,128)} %param.8, s32[4,1024]{1,0:T(4,128)} %param.7), kind=kLoop, calls=%fused_computation.3 | loop fusion | flops 14336 | bytes 57344 | tf_op jit(solution)/shard_map/concatenate | solution.py:390
  2.4 0.0 collective-permute-done.emb_other_ref
  2.4 0.7 %pack.1 = (bf16[560,512]{1,0:T(8,128)(2,1)S(1)}, bf16[560,512]{1,0:T(8,128)(2,1)S(1)}) custom-call(bf16[512,256]{1,0:T(8,128)(2,1)S(1)} %get-tuple-element.40.emb_mine_ref, bf16[512,256]{1,0:T(8,128)(2,1)S(1)} %get-tuple-element.39.emb_rest_ref, bf16[1024,256]{1,0:T(8,128)(2,1)S(1)} %collective-permute-done.emb_other_ref, bf16[16,1024]{1,0:T(8,128)(2,1)S(1)} %copy-done, ...), custom_call_target="tpu_custom_call" | custom-call | tf_op jit(solution)/shard_map/pack/pallas_call | solution.py:101
  3.1 3.0 %collective-permute-start.2 = (bf16[560,512]{1,0:T(8,128)(2,1)S(1)}, bf16[560,512]{1,0:T(8,128)(2,1)S(1)}, u32[]{:S(2)}, u32[]{:S(2)}) collective-permute-start(bf16[560,512]{1,0:T(8,128)(2,1)S(1)} %get-tuple-element.22.refs_0_.refs_1_), channel_id=1, source_target_pairs={{0,2},{2,0},{4,6},{6,4},{8,10},{10,8},{12,14},{14,12},{1,3},{3,1},... | collective-permute-start | bytes 1720328 | tf_op jit(solution)/shard_map/ppermute | solution.py:395
  6.1 3.6 %collective-permute-start.3 = (bf16[560,512]{1,0:T(8,128)(2,1)S(1)}, bf16[560,512]{1,0:T(8,128)(2,1)S(1)}, u32[]{:S(2)}, u32[]{:S(2)}) collective-permute-start(bf16[560,512]{1,0:T(8,128)(2,1)S(1)} %get-tuple-element.22.refs_0_.refs_1_), channel_id=1, source_target_pairs={{4,0},{6,2},{8,4},{10,6},{12,8},{14,10},{0,12},{2,14},{5,1},{7,3},... | collective-permute-start | bytes 1720328 | tf_op jit(solution)/shard_map/ppermute | solution.py:394
  9.7 1.4 %collective-permute-start.6 = (bf16[560,512]{1,0:T(8,128)(2,1)S(1)}, bf16[560,512]{1,0:T(8,128)(2,1)S(1)}, u32[]{:S(2)}, u32[]{:S(2)}) collective-permute-start(bf16[560,512]{1,0:T(8,128)(2,1)S(1)} %get-tuple-element.22.refs_0_.refs_1_), channel_id=1, source_target_pairs={{0,8},{2,10},{12,4},{14,6},{1,9},{3,11},{13,5},{15,7},{16,24},{18,... | collective-permute-start | bytes 1720328 | tf_op jit(solution)/shard_map/ppermute | solution.py:394
  11.1 4.2 %tile.4 = (f32[40,512]{1,0:T(8,128)S(1)}, bf16[560,1024]{1,0:T(8,128)(2,1)S(1)}) custom-call(bf16[560,512]{1,0:T(8,128)(2,1)S(1)} %get-tuple-element.22.refs_0_.refs_1_, bf16[560,512]{1,0:T(8,128)(2,1)S(1)} %get-tuple-element.22.refs_0_.refs_1_, bf16[560,512]{1,0:T(8,128)(2,1)S(1)} %get-tuple-element.23.refs_2_), custom_call_target="tpu_custom_call" | custom-call | flops 1 | bytes 1 | tf_op jit(solution)/shard_map/tile/pallas_call | solution.py:246
  15.3 4.0 %collective-permute-done.2.refs_1_ = bf16[560,512]{1,0:T(8,128)(2,1)S(1)} collective-permute-done((bf16[560,512]{1,0:T(8,128)(2,1)S(1)}, bf16[560,512]{1,0:T(8,128)(2,1)S(1)}, u32[]{:S(2)}, u32[]{:S(2)}) %collective-permute-start.2) | collective-permute-done | bytes 573472 | tf_op jit(solution)/shard_map/ppermute | solution.py:395
  19.3 3.8 %collective-permute-done.3.refs_0_ = bf16[560,512]{1,0:T(8,128)(2,1)S(1)} collective-permute-done((bf16[560,512]{1,0:T(8,128)(2,1)S(1)}, bf16[560,512]{1,0:T(8,128)(2,1)S(1)}, u32[]{:S(2)}, u32[]{:S(2)}) %collective-permute-start.3) | collective-permute-done | bytes 573472 | tf_op jit(solution)/shard_map/ppermute | solution.py:394
  23.1 0.1 collective-permute-start.5
  23.2 0.6 collective-permute-start.4
  23.8 1.4 %collective-permute-done.4 = bf16[272,512]{1,0:T(8,128)(2,1)S(1)} collective-permute-done((bf16[272,512]{1,0:T(8,128)(2,1)S(1)}, bf16[272,512]{1,0:T(8,128)(2,1)S(1)}, u32[]{:S(2)}, u32[]{:S(2)}) %collective-permute-start.4) | collective-permute-done | bytes 278560 | tf_op jit(solution)/shard_map/ppermute | solution.py:401
  25.2 0.0 collective-permute-done.5
  25.2 4.0 %tile.5 = (f32[40,512]{1,0:T(8,128)S(1)}, bf16[560,1024]{1,0:T(8,128)(2,1)S(1)}) custom-call(bf16[560,512]{1,0:T(8,128)(2,1)S(1)} %get-tuple-element.22.refs_0_.refs_1_, bf16[560,512]{1,0:T(8,128)(2,1)S(1)} %collective-permute-done.2.refs_1_, bf16[560,512]{1,0:T(8,128)(2,1)S(1)} %pad_maximum_fusion.refs_2_), custom_call_target="tpu_custom_call" | custom-call | flops 1 | bytes 1 | tf_op jit(solution)/shard_map/tile/pallas_call | solution.py:246
  29.2 7.1 %tile.6 = (f32[40,512]{1,0:T(8,128)S(1)}, f32[40,2048]{1,0:T(8,128)S(1)}) custom-call(bf16[560,512]{1,0:T(8,128)(2,1)S(1)} %collective-permute-done.3.refs_0_, bf16[560,1024]{1,0:T(8,128)(2,1)S(1)} %get-tuple-element.30.refs_1_, bf16[560,1024]{1,0:T(8,128)(2,1)S(1)} %get-tuple-element.31.refs_2_), custom_call_target="tpu_custom_call" | custom-call | flops 1 | bytes 1 | tf_op jit(solution)/shard_map/tile/pallas_call | solution.py:246
  36.3 0.0 collective-permute-done.6.refs_0_
  36.3 0.2 tile.7
  36.6 0.2 collective-permute-start.8
  36.9 1.3 %collective-permute-start.7 = (f32[40,512]{1,0:T(8,128)S(1)}, f32[40,512]{1,0:T(8,128)S(1)}, u32[]{:S(2)}, u32[]{:S(2)}) collective-permute-start(f32[40,512]{1,0:T(8,128)S(1)} %get-tuple-element.34), channel_id=1, source_target_pairs={{8,0},{10,2},{4,12},{6,14},{9,1},{11,3},{5,13},{7,15},{24,16},{26,... | collective-permute-start | bytes 245768 | tf_op jit(solution)/shard_map/ppermute | solution.py:416
  38.2 6.5 %collective-permute-start.10 = (f32[40,512]{1,0:T(8,128)S(1)}, f32[40,512]{1,0:T(8,128)S(1)}, u32[]{:S(2)}, u32[]{:S(2)}) collective-permute-start(f32[40,512]{1,0:T(8,128)S(1)} %get-tuple-element.38), channel_id=1, source_target_pairs={{0,4},{2,6},{4,8},{6,10},{8,12},{10,14},{12,0},{14,2},{1,5},{3,7},... | collective-permute-start | bytes 245768 | tf_op jit(solution)/shard_map/ppermute | solution.py:423
  44.7 0.5 collective-permute-start.9
  45.2 4.4 %collective-permute-done.7.refs_2_ = f32[40,512]{1,0:T(8,128)S(1)} collective-permute-done((f32[40,512]{1,0:T(8,128)S(1)}, f32[40,512]{1,0:T(8,128)S(1)}, u32[]{:S(2)}, u32[]{:S(2)}) %collective-permute-start.7) | collective-permute-done | bytes 81952 | tf_op jit(solution)/shard_map/ppermute | solution.py:416
  49.5 0.0 collective-permute-done.10.refs_6_
  49.6 0.9 %gram.1 = f32[16,8,128]{2,1,0:T(8,128)} custom-call(f32[32,512]{1,0:T(8,128)S(1)} %image.1.image_ref.mine_ref), custom_call_target="tpu_custom_call" | custom-call | tf_op jit(solution)/shard_map/gram/pallas_call | solution.py:299
  50.5 3.6 %all-to-all-start = ((f32[16,8,128]{2,1,0:T(8,128)}), f32[16,8,128]{2,1,0:T(8,128)S(1)}, u32[]{:S(2)}, u32[]{:S(2)}) async-start(f32[16,8,128]{2,1,0:T(8,128)} %gram.1), calls=%async_computation | async-start | bytes 131072 | tf_op jit(solution)/shard_map/all_to_all | solution.py:426
  54.0 0.4 collective-permute-start.11
  54.4 0.9 %collective-permute-done.11.other_ref = f32[32,512]{1,0:T(8,128)S(1)} collective-permute-done((f32[32,512]{1,0:T(8,128)S(1)}, f32[32,512]{1,0:T(8,128)S(1)}, u32[]{:S(2)}, u32[]{:S(2)}) %collective-permute-start.11) | collective-permute-done | bytes 65568 | tf_op jit(solution)/shard_map/ppermute | solution.py:425
  55.4 5.6 %all-to-all-done.grams_ref = f32[16,8,128]{2,1,0:T(8,128)S(1)} async-done(((f32[16,8,128]{2,1,0:T(8,128)}), f32[16,8,128]{2,1,0:T(8,128)S(1)}, u32[]{:S(2)}, u32[]{:S(2)}) %all-to-all-start) | async-done | bytes 65568 | tf_op jit(solution)/shard_map/all_to_all | solution.py:426
  60.9 2.9 %basis.1 = f32[16,1024]{1,0:T(8,128)} custom-call(f32[16,8,128]{2,1,0:T(8,128)S(1)} %all-to-all-done.grams_ref, f32[32,512]{1,0:T(8,128)S(1)} %image.1.image_ref.mine_ref, f32[32,512]{1,0:T(8,128)S(1)} %collective-permute-done.11.other_ref), custom_call_target="tpu_custom_call" | custom-call | tf_op jit(solution)/shard_map/basis/pallas_call | solution.py:349
  (13 shorter events, 0.2 us)
Async XLA Ops:
  0.0 2.4 %copy-start = (bf16[16,1024]{1,0:T(8,128)(2,1)S(1)}, bf16[16,1024]{1,0:T(8,128)(2,1)}, u32[]{:S(2)}) copy-start(bf16[16,1024]{1,0:T(8,128)(2,1)} %vec_ref.1) | copy-start | bytes 98308
  0.0 2.4 %collective-permute-start = (bf16[1024,256]{1,0:T(8,128)(2,1)}, bf16[1024,256]{1,0:T(8,128)(2,1)S(1)}, u32[]{:S(2)}, u32[]{:S(2)}) collective-permute-start(bf16[1024,256]{1,0:T(8,128)(2,1)} %param.5), channel_id=1, source_target_pairs={{0,1},{1,0},{2,3},{3,2},{4,5},{5,4},{6,7},{7,6},{8,9},{9,8},{10,11... | collective-permute-start | bytes 1572872 | tf_op jit(solution)/shard_map/ppermute | solution.py:388
  0.5 1.9 %collective-permute-start.1 = (bf16[16,1024]{1,0:T(8,128)(2,1)}, bf16[16,1024]{1,0:T(8,128)(2,1)S(1)}, u32[]{:S(2)}, u32[]{:S(2)}) collective-permute-start(bf16[16,1024]{1,0:T(8,128)(2,1)} %vec_ref.1), channel_id=1, source_target_pairs={{0,1},{1,0},{2,3},{3,2},{4,5},{5,4},{6,7},{7,6},{8,9},{9,8},{10,11... | collective-permute-start | bytes 98312 | tf_op jit(solution)/shard_map/ppermute | solution.py:389
  3.1 16.2 %collective-permute-start.2 = (bf16[560,512]{1,0:T(8,128)(2,1)S(1)}, bf16[560,512]{1,0:T(8,128)(2,1)S(1)}, u32[]{:S(2)}, u32[]{:S(2)}) collective-permute-start(bf16[560,512]{1,0:T(8,128)(2,1)S(1)} %get-tuple-element.22.refs_0_.refs_1_), channel_id=1, source_target_pairs={{0,2},{2,0},{4,6},{6,4},{8,10},{10,8},{12,14},{14,12},{1,3},{3,1},... | collective-permute-start | bytes 1720328 | tf_op jit(solution)/shard_map/ppermute | solution.py:395
  6.1 17.0 %collective-permute-start.3 = (bf16[560,512]{1,0:T(8,128)(2,1)S(1)}, bf16[560,512]{1,0:T(8,128)(2,1)S(1)}, u32[]{:S(2)}, u32[]{:S(2)}) collective-permute-start(bf16[560,512]{1,0:T(8,128)(2,1)S(1)} %get-tuple-element.22.refs_0_.refs_1_), channel_id=1, source_target_pairs={{4,0},{6,2},{8,4},{10,6},{12,8},{14,10},{0,12},{2,14},{5,1},{7,3},... | collective-permute-start | bytes 1720328 | tf_op jit(solution)/shard_map/ppermute | solution.py:394
  9.7 26.6 %collective-permute-start.6 = (bf16[560,512]{1,0:T(8,128)(2,1)S(1)}, bf16[560,512]{1,0:T(8,128)(2,1)S(1)}, u32[]{:S(2)}, u32[]{:S(2)}) collective-permute-start(bf16[560,512]{1,0:T(8,128)(2,1)S(1)} %get-tuple-element.22.refs_0_.refs_1_), channel_id=1, source_target_pairs={{0,8},{2,10},{12,4},{14,6},{1,9},{3,11},{13,5},{15,7},{16,24},{18,... | collective-permute-start | bytes 1720328 | tf_op jit(solution)/shard_map/ppermute | solution.py:394
  23.1 2.0 %collective-permute-start.5 = (bf16[288,512]{1,0:T(8,128)(2,1)S(1)}, bf16[288,512]{1,0:T(8,128)(2,1)S(1)}, u32[]{:S(2)}, u32[]{:S(2)}) collective-permute-start(bf16[288,512]{1,0:T(8,128)(2,1)S(1)} %slice.25), channel_id=1, source_target_pairs={{0,1},{1,0},{2,3},{3,2},{4,5},{5,4},{6,7},{7,6},{8,9},{9,8},{10,11... | collective-permute-start | bytes 884744 | tf_op jit(solution)/shard_map/ppermute | solution.py:401
  23.2 1.9 %collective-permute-start.4 = (bf16[272,512]{1,0:T(8,128)(2,1)S(1)}, bf16[272,512]{1,0:T(8,128)(2,1)S(1)}, u32[]{:S(2)}, u32[]{:S(2)}) collective-permute-start(bf16[272,512]{1,0:T(8,128)(2,1)S(1)} %slice.24), channel_id=1, source_target_pairs={{0,1},{1,0},{2,3},{3,2},{4,5},{5,4},{6,7},{7,6},{8,9},{9,8},{10,11... | collective-permute-start | bytes 835592 | tf_op jit(solution)/shard_map/ppermute | solution.py:401
  36.6 1.5 %collective-permute-start.8 = (f32[40,1024]{1,0:T(8,128)S(1)}, f32[40,1024]{1,0:T(8,128)S(1)}, u32[]{:S(2)}, u32[]{:S(2)}) collective-permute-start(f32[40,1024]{1,0:T(8,128)S(1)} %pad_maximum_fusion.1), channel_id=1, source_target_pairs={{0,1},{1,0},{2,3},{3,2},{4,5},{5,4},{6,7},{7,6},{8,9},{9,8},{10,11... | collective-permute-start | bytes 491528 | tf_op jit(solution)/shard_map/ppermute | solution.py:414
  36.9 12.7 %collective-permute-start.7 = (f32[40,512]{1,0:T(8,128)S(1)}, f32[40,512]{1,0:T(8,128)S(1)}, u32[]{:S(2)}, u32[]{:S(2)}) collective-permute-start(f32[40,512]{1,0:T(8,128)S(1)} %get-tuple-element.34), channel_id=1, source_target_pairs={{8,0},{10,2},{4,12},{6,14},{9,1},{11,3},{5,13},{7,15},{24,16},{26,... | collective-permute-start | bytes 245768 | tf_op jit(solution)/shard_map/ppermute | solution.py:416
  38.2 11.3 %collective-permute-start.10 = (f32[40,512]{1,0:T(8,128)S(1)}, f32[40,512]{1,0:T(8,128)S(1)}, u32[]{:S(2)}, u32[]{:S(2)}) collective-permute-start(f32[40,512]{1,0:T(8,128)S(1)} %get-tuple-element.38), channel_id=1, source_target_pairs={{0,4},{2,6},{4,8},{6,10},{8,12},{10,14},{12,0},{14,2},{1,5},{3,7},... | collective-permute-start | bytes 245768 | tf_op jit(solution)/shard_map/ppermute | solution.py:423
  44.7 4.9 %collective-permute-start.9 = (f32[40,512]{1,0:T(8,128)S(1)}, f32[40,512]{1,0:T(8,128)S(1)}, u32[]{:S(2)}, u32[]{:S(2)}) collective-permute-start(f32[40,512]{1,0:T(8,128)S(1)} %get-tuple-element.41), channel_id=1, source_target_pairs={{0,2},{2,0},{4,6},{6,4},{8,10},{10,8},{12,14},{14,12},{1,3},{3,1},... | collective-permute-start | bytes 245768 | tf_op jit(solution)/shard_map/ppermute | solution.py:420
  50.5 10.5 %all-to-all-start = ((f32[16,8,128]{2,1,0:T(8,128)}), f32[16,8,128]{2,1,0:T(8,128)S(1)}, u32[]{:S(2)}, u32[]{:S(2)}) async-start(f32[16,8,128]{2,1,0:T(8,128)} %gram.1), calls=%async_computation | async-start | bytes 131072 | tf_op jit(solution)/shard_map/all_to_all | solution.py:426
  54.0 1.3 %collective-permute-start.11 = (f32[32,512]{1,0:T(8,128)S(1)}, f32[32,512]{1,0:T(8,128)S(1)}, u32[]{:S(2)}, u32[]{:S(2)}) collective-permute-start(f32[32,512]{1,0:T(8,128)S(1)} %image.1.image_ref.mine_ref), channel_id=1, source_target_pairs={{0,1},{1,0},{2,3},{3,2},{4,5},{5,4},{6,7},{7,6},{8,9},{9,8},{10,11... | collective-permute-start | bytes 196616 | tf_op jit(solution)/shard_map/ppermute | solution.py:425

commit v9 on v8

--- a/solution.py
+++ b/solution.py
@@ -26,6 +26,7 @@
 CHUNK = 256
 OUT_ROWS = 40
 COST = 1
+GROUP = 32
 SWAPS = 2
 VMEM_LIMIT = 48 * 1024 * 1024
 
@@ -127,15 +128,15 @@
 
 
 def weights_of(products, row, col, same):
-    logit = products * row[NORM] * col[NORM]
-    gap = jnp.maximum(col[FIRST] - row[LAST], row[FIRST] - col[LAST])
-    width = jnp.maximum(jnp.minimum(row[RIGHT], col[RIGHT]) - jnp.maximum(row[LEFT], col[LEFT]), 0.0)
-    height = jnp.maximum(jnp.minimum(row[TOP], col[TOP]) - jnp.maximum(row[BOTTOM], col[BOTTOM]), 0.0)
+    width = jnp.maximum(jnp.minimum(row(RIGHT), col(RIGHT)) - jnp.maximum(row(LEFT), col(LEFT)), 0.0)
+    height = jnp.maximum(jnp.minimum(row(TOP), col(TOP)) - jnp.maximum(row(BOTTOM), col(BOTTOM)), 0.0)
     inter = width * height
-    both = row[AREA] + col[AREA]
+    both = row(AREA) + col(AREA)
     share = (both + inter) * pl.reciprocal(both - inter, approx=True)
+    gap = jnp.maximum(col(FIRST) - row(LAST), row(FIRST) - col(LAST))
+    logit = products * row(NORM) * col(NORM)
     value = jnp.exp2(logit - jnp.maximum(gap, BASE)) * share
-    barred = (row[CAMERA] == col[CAMERA]) & (gap < BARRED_BELOW)
+    barred = (row(CAMERA) == col(CAMERA)) & (gap < BARRED_BELOW)
     if same is not None:
         barred = barred & jnp.logical_not(same)
     return jnp.where(barred, 0.0, value)
@@ -144,7 +145,7 @@
 def tile_kernel(blocks, turns, own_block, receivers, vecs, *refs):
     row_ref, col_refs = refs[0], refs[1 : 1 + blocks]
     row_out_ref, col_out_ref, field_ref, spread_ref, sum_ref = refs[1 + blocks : 6 + blocks]
-    products, weights = refs[6 + blocks : 8 + blocks], refs[8 + blocks :]
+    products, weights, col_spreads = [refs[at : at + 2] for at in range(6 + blocks, 12 + blocks, 2)]
     size, rows = row_ref.shape
     features = size - vecs - CODE_ROWS
     vec_rows, code_rows = slice(features, features + vecs), slice(features + vecs, size)
@@ -161,21 +162,23 @@
                 row_ref[0:rows, :], col_ref[0:features, place(step)], preferred_element_type=jnp.float32
             )
 
-        def weigh(step, product_ref, weight_ref):
-            col = [jnp.broadcast_to(field, (8, CHUNK)) for field in decode(col_ref[code_rows, place(step)])]
-            for first_row in range(0, rows, 16):
-                both = []
-                for line in (first_row, first_row + 8):
-                    row = [
-                        jnp.concatenate([spread_ref[field, line : line + 8, :]] * (CHUNK // LANES), axis=1)
-                        for field in range(FIELDS)
-                    ]
-                    same = None
-                    if own_block:
-                        row_ids = lax.broadcasted_iota(jnp.int32, (8, CHUNK), 0) + (line - step * CHUNK)
-                        same = row_ids == lax.broadcasted_iota(jnp.int32, (8, CHUNK), 1)
-                    both.append(weights_of(product_ref[line : line + 8, :], row, col, same))
-                weight_ref[first_row : first_row + 16, :] = jnp.concatenate(both, axis=0).astype(jnp.bfloat16)
+        def weigh(step, product_ref, weight_ref, col_spread_ref):
+            for field, values in enumerate(decode(col_ref[code_rows, place(step)])):
+                col_spread_ref[field] = jnp.broadcast_to(values, (8, CHUNK))
+            for first_row in range(0, rows, GROUP):
+                row_part = slice(first_row, first_row + GROUP)
+
+                def row(field):
+                    return jnp.concatenate([spread_ref[field, row_part, :]] * (CHUNK // LANES), axis=1)
+
+                def col(field):
+                    return jnp.concatenate([col_spread_ref[field]] * (GROUP // 8), axis=0)
+
+                same = None
+                if own_block:
+                    row_ids = lax.broadcasted_iota(jnp.int32, (GROUP, CHUNK), 0) + (first_row - step * CHUNK)
+                    same = row_ids == lax.broadcasted_iota(jnp.int32, (GROUP, CHUNK), 1)
+                weight_ref[row_part, :] = weights_of(product_ref[row_part, :], row, col, same).astype(jnp.bfloat16)
 
         def total(step, weight_ref):
             sum_ref[:, 0 : vecs + CODE_ROWS] += dot_nt(weight_ref[...], with_ones(col_ref[vec_rows, place(step)]))
@@ -188,7 +191,7 @@
             for parity in range(2):
                 step = 2 * index + parity
                 multiply(lax.rem(step + 1, chunks), products[1 - parity])
-                weigh(step, products[parity], weights[parity])
+                weigh(step, products[parity], weights[parity], col_spreads[parity])
                 total(lax.rem(step + chunks - 1, chunks), weights[1 - parity])
             return carry
 
@@ -256,6 +259,8 @@
             pltpu.VMEM((rows, CHUNK), jnp.float32),
             pltpu.VMEM((rows, CHUNK), jnp.bfloat16),
             pltpu.VMEM((rows, CHUNK), jnp.bfloat16),
+            pltpu.VMEM((FIELDS, 8, CHUNK), jnp.float32),
+            pltpu.VMEM((FIELDS, 8, CHUNK), jnp.float32),
         ],
         cost_estimate=pl.CostEstimate(flops=COST, bytes_accessed=COST, transcendentals=0),
         compiler_params=params(),
@@ -417,10 +422,10 @@
         crossing = next_mine + sides[:, half:]
         parts.append(own_mine)
         parts.append(sides[:, :half])
-        parts.append(lax.ppermute(crossing, "blk", beside))
         for row_sums, moves in returns:
             row_sums, _ = lax.optimization_barrier((row_sums, crossing))
             parts.append(lax.ppermute(row_sums, "blk", moves))
+        parts.append(lax.ppermute(crossing, "blk", beside))
     image = image_of(parts, vecs)
     image_other = lax.ppermute(image, "sub", swap)
     grams = lax.all_to_all(grams_of(image, 2 * blocks), ("blk", "sub"), 0, 0, tiled=True)

time: 64.1 us -> 64.3 us (level)
  no operation moved by 1% of the time
where the time goes in v9:
time: 64.3 us; the launch traced here: 64 us
  starting transfers between devices  21.7 us (34%)
  Pallas kernels  20.1 us (31%)
  waiting for transfers between devices  20 us (31%)
  local copies, waits for them, and re-layouts  1.12 us (2%)
  other arithmetic  0.88 us (1%)
    pallas_call x4, Pallas kernels, tile(): pl.pallas_call(functools.partial(tile_kernel, len(columns), turns, own_bl...  15.6 us
    ppermute x1, starting transfers between devices, local(): parts.append(lax.ppermute(row_sums, 'blk', moves))  6.59 us
    all_to_all x1, waiting for transfers between devices, local(): lax.all_to_all(grams_of(image, 2 * blocks), ('blk', 'sub'), 0, 0, tiled=T...  5.58 us
    ppermute x2, starting transfers between devices, local(): sent = [lax.ppermute(mine, 'blk', moves) for moves, _ in plans]  4.97 us
    ppermute x1, waiting for transfers between devices, local(): parts.append(lax.ppermute(last_sums, 'blk', last_moves))  4.34 us
    ppermute x1, waiting for transfers between devices, local(): beside_mine = lax.ppermute(mine, 'blk', beside)  4 us
    ppermute x2, waiting for transfers between devices, local(): sent = [lax.ppermute(mine, 'blk', moves) for moves, _ in plans]  3.79 us
    all_to_all x1, starting transfers between devices, local(): lax.all_to_all(grams_of(image, 2 * blocks), ('blk', 'sub'), 0, 0, tiled=T...  3.55 us
  transfers between devices with their start and end apart: 13, of which 6 were waited for; matrix products, arithmetic and copies ran while one was open for 3% of the time, Pallas kernels for 24%

profile of v9, /device:TPU:0, one launch (start us, length us, event | category | flops | bytes accessed | tf_op | source)
XLA Modules:
  0.0 64.0 jit_solution(13653291007403697641)
XLA Ops:
  0.0 0.5 collective-permute-start
  0.5 0.1 collective-permute-start.1
  0.5 1.1 %constant_dynamic-slice_fusion = (bf16[512,256]{1,0:T(8,128)(2,1)S(1)}, bf16[512,256]{1,0:T(8,128)(2,1)S(1)}) fusion(bf16[1024,256]{1,0:T(8,128)(2,1)} %param.5, s32[]{:T(128)S(6)} %select_n.7, s32[]{:T(128)S(6)} %select_n.6), kind=kLoop, calls=%fused_computation.4 | loop fusion | bytes 1048584 | tf_op jit(solution)/shard_map/dynamic_slice | solution.py:397
  1.6 0.8 %pad_add_fusion.meta_ref = s32[7,1024]{1,0:T(8,128)S(1)} fusion(s32[1,1024]{1,0:T(1,128)} %bitcast.1, s32[2,1024]{1,0:T(2,128)} %param.8, s32[4,1024]{1,0:T(4,128)} %param.7), kind=kLoop, calls=%fused_computation.3 | loop fusion | flops 14336 | bytes 57344 | tf_op jit(solution)/shard_map/concatenate | solution.py:395
  2.4 0.0 collective-permute-done.emb_other_ref
  2.4 0.7 %pack.1 = (bf16[560,512]{1,0:T(8,128)(2,1)S(1)}, bf16[560,512]{1,0:T(8,128)(2,1)S(1)}) custom-call(bf16[512,256]{1,0:T(8,128)(2,1)S(1)} %get-tuple-element.40.emb_mine_ref, bf16[512,256]{1,0:T(8,128)(2,1)S(1)} %get-tuple-element.39.emb_rest_ref, bf16[1024,256]{1,0:T(8,128)(2,1)S(1)} %collective-permute-done.emb_other_ref, bf16[16,1024]{1,0:T(8,128)(2,1)S(1)} %copy-done, ...), custom_call_target="tpu_custom_call" | custom-call | tf_op jit(solution)/shard_map/pack/pallas_call | solution.py:102
  3.1 3.0 %collective-permute-start.2 = (bf16[560,512]{1,0:T(8,128)(2,1)S(1)}, bf16[560,512]{1,0:T(8,128)(2,1)S(1)}, u32[]{:S(2)}, u32[]{:S(2)}) collective-permute-start(bf16[560,512]{1,0:T(8,128)(2,1)S(1)} %get-tuple-element.22.refs_0_.refs_1_), channel_id=1, source_target_pairs={{0,2},{2,0},{4,6},{6,4},{8,10},{10,8},{12,14},{14,12},{1,3},{3,1},... | collective-permute-start | bytes 1720328 | tf_op jit(solution)/shard_map/ppermute | solution.py:400
  6.1 3.6 %collective-permute-start.3 = (bf16[560,512]{1,0:T(8,128)(2,1)S(1)}, bf16[560,512]{1,0:T(8,128)(2,1)S(1)}, u32[]{:S(2)}, u32[]{:S(2)}) collective-permute-start(bf16[560,512]{1,0:T(8,128)(2,1)S(1)} %get-tuple-element.22.refs_0_.refs_1_), channel_id=1, source_target_pairs={{4,0},{6,2},{8,4},{10,6},{12,8},{14,10},{0,12},{2,14},{5,1},{7,3},... | collective-permute-start | bytes 1720328 | tf_op jit(solution)/shard_map/ppermute | solution.py:399
  9.7 1.4 %collective-permute-start.6 = (bf16[560,512]{1,0:T(8,128)(2,1)S(1)}, bf16[560,512]{1,0:T(8,128)(2,1)S(1)}, u32[]{:S(2)}, u32[]{:S(2)}) collective-permute-start(bf16[560,512]{1,0:T(8,128)(2,1)S(1)} %get-tuple-element.22.refs_0_.refs_1_), channel_id=1, source_target_pairs={{0,8},{2,10},{12,4},{14,6},{1,9},{3,11},{13,5},{15,7},{16,24},{18,... | collective-permute-start | bytes 1720328 | tf_op jit(solution)/shard_map/ppermute | solution.py:399
  11.1 4.2 %tile.4 = (f32[40,512]{1,0:T(8,128)S(1)}, bf16[560,1024]{1,0:T(8,128)(2,1)S(1)}) custom-call(bf16[560,512]{1,0:T(8,128)(2,1)S(1)} %get-tuple-element.22.refs_0_.refs_1_, bf16[560,512]{1,0:T(8,128)(2,1)S(1)} %get-tuple-element.22.refs_0_.refs_1_, bf16[560,512]{1,0:T(8,128)(2,1)S(1)} %get-tuple-element.23.refs_2_), custom_call_target="tpu_custom_call" | custom-call | flops 1 | bytes 1 | tf_op jit(solution)/shard_map/tile/pallas_call | solution.py:249
  15.3 4.0 %collective-permute-done.2.refs_1_ = bf16[560,512]{1,0:T(8,128)(2,1)S(1)} collective-permute-done((bf16[560,512]{1,0:T(8,128)(2,1)S(1)}, bf16[560,512]{1,0:T(8,128)(2,1)S(1)}, u32[]{:S(2)}, u32[]{:S(2)}) %collective-permute-start.2) | collective-permute-done | bytes 573472 | tf_op jit(solution)/shard_map/ppermute | solution.py:400
  19.3 3.8 %collective-permute-done.3.refs_0_ = bf16[560,512]{1,0:T(8,128)(2,1)S(1)} collective-permute-done((bf16[560,512]{1,0:T(8,128)(2,1)S(1)}, bf16[560,512]{1,0:T(8,128)(2,1)S(1)}, u32[]{:S(2)}, u32[]{:S(2)}) %collective-permute-start.3) | collective-permute-done | bytes 573472 | tf_op jit(solution)/shard_map/ppermute | solution.py:399
  23.1 0.1 collective-permute-start.5
  23.2 0.6 collective-permute-start.4
  23.8 1.4 %collective-permute-done.4 = bf16[272,512]{1,0:T(8,128)(2,1)S(1)} collective-permute-done((bf16[272,512]{1,0:T(8,128)(2,1)S(1)}, bf16[272,512]{1,0:T(8,128)(2,1)S(1)}, u32[]{:S(2)}, u32[]{:S(2)}) %collective-permute-start.4) | collective-permute-done | bytes 278560 | tf_op jit(solution)/shard_map/ppermute | solution.py:406
  25.2 0.0 collective-permute-done.5
  25.2 4.0 %tile.5 = (f32[40,512]{1,0:T(8,128)S(1)}, bf16[560,1024]{1,0:T(8,128)(2,1)S(1)}) custom-call(bf16[560,512]{1,0:T(8,128)(2,1)S(1)} %get-tuple-element.22.refs_0_.refs_1_, bf16[560,512]{1,0:T(8,128)(2,1)S(1)} %collective-permute-done.2.refs_1_, bf16[560,512]{1,0:T(8,128)(2,1)S(1)} %pad_maximum_fusion.refs_2_), custom_call_target="tpu_custom_call" | custom-call | flops 1 | bytes 1 | tf_op jit(solution)/shard_map/tile/pallas_call | solution.py:249
  29.2 7.2 %tile.6 = (f32[40,512]{1,0:T(8,128)S(1)}, f32[40,2048]{1,0:T(8,128)S(1)}) custom-call(bf16[560,512]{1,0:T(8,128)(2,1)S(1)} %collective-permute-done.3.refs_0_, bf16[560,1024]{1,0:T(8,128)(2,1)S(1)} %get-tuple-element.30.refs_1_, bf16[560,1024]{1,0:T(8,128)(2,1)S(1)} %get-tuple-element.31.refs_2_), custom_call_target="tpu_custom_call" | custom-call | flops 1 | bytes 1 | tf_op jit(solution)/shard_map/tile/pallas_call | solution.py:249
  36.4 0.0 collective-permute-done.6.refs_0_
  36.4 0.2 tile.7
  36.7 0.2 collective-permute-start.8
  36.9 1.3 %collective-permute-start.7 = (f32[40,512]{1,0:T(8,128)S(1)}, f32[40,512]{1,0:T(8,128)S(1)}, u32[]{:S(2)}, u32[]{:S(2)}) collective-permute-start(f32[40,512]{1,0:T(8,128)S(1)} %get-tuple-element.34), channel_id=1, source_target_pairs={{8,0},{10,2},{4,12},{6,14},{9,1},{11,3},{5,13},{7,15},{24,16},{26,... | collective-permute-start | bytes 245768 | tf_op jit(solution)/shard_map/ppermute | solution.py:421
  38.3 6.6 %collective-permute-start.9 = (f32[40,512]{1,0:T(8,128)S(1)}, f32[40,512]{1,0:T(8,128)S(1)}, u32[]{:S(2)}, u32[]{:S(2)}) collective-permute-start(f32[40,512]{1,0:T(8,128)S(1)} %get-tuple-element.38), channel_id=1, source_target_pairs={{0,4},{2,6},{4,8},{6,10},{8,12},{10,14},{12,0},{14,2},{1,5},{3,7},... | collective-permute-start | bytes 245768 | tf_op jit(solution)/shard_map/ppermute | solution.py:427
  44.9 0.5 collective-permute-start.10
  45.4 4.3 %collective-permute-done.7.refs_2_ = f32[40,512]{1,0:T(8,128)S(1)} collective-permute-done((f32[40,512]{1,0:T(8,128)S(1)}, f32[40,512]{1,0:T(8,128)S(1)}, u32[]{:S(2)}, u32[]{:S(2)}) %collective-permute-start.7) | collective-permute-done | bytes 81952 | tf_op jit(solution)/shard_map/ppermute | solution.py:421
  49.7 0.0 collective-permute-done.9.refs_5_
  49.8 0.9 %gram.1 = f32[16,8,128]{2,1,0:T(8,128)} custom-call(f32[32,512]{1,0:T(8,128)S(1)} %image.1.image_ref.mine_ref), custom_call_target="tpu_custom_call" | custom-call | tf_op jit(solution)/shard_map/gram/pallas_call | solution.py:304
  50.6 3.5 %all-to-all-start = ((f32[16,8,128]{2,1,0:T(8,128)}), f32[16,8,128]{2,1,0:T(8,128)S(1)}, u32[]{:S(2)}, u32[]{:S(2)}) async-start(f32[16,8,128]{2,1,0:T(8,128)} %gram.1), calls=%async_computation | async-start | bytes 131072 | tf_op jit(solution)/shard_map/all_to_all | solution.py:431
  54.2 0.4 collective-permute-start.11
  54.6 0.9 %collective-permute-done.11.other_ref = f32[32,512]{1,0:T(8,128)S(1)} collective-permute-done((f32[32,512]{1,0:T(8,128)S(1)}, f32[32,512]{1,0:T(8,128)S(1)}, u32[]{:S(2)}, u32[]{:S(2)}) %collective-permute-start.11) | collective-permute-done | bytes 65568 | tf_op jit(solution)/shard_map/ppermute | solution.py:430
  55.5 5.6 %all-to-all-done.grams_ref = f32[16,8,128]{2,1,0:T(8,128)S(1)} async-done(((f32[16,8,128]{2,1,0:T(8,128)}), f32[16,8,128]{2,1,0:T(8,128)S(1)}, u32[]{:S(2)}, u32[]{:S(2)}) %all-to-all-start) | async-done | bytes 65568 | tf_op jit(solution)/shard_map/all_to_all | solution.py:431
  61.1 2.9 %basis.1 = f32[16,1024]{1,0:T(8,128)} custom-call(f32[16,8,128]{2,1,0:T(8,128)S(1)} %all-to-all-done.grams_ref, f32[32,512]{1,0:T(8,128)S(1)} %image.1.image_ref.mine_ref, f32[32,512]{1,0:T(8,128)S(1)} %collective-permute-done.11.other_ref), custom_call_target="tpu_custom_call" | custom-call | tf_op jit(solution)/shard_map/basis/pallas_call | solution.py:354
  (13 shorter events, 0.2 us)
Async XLA Ops:
  0.0 2.4 %copy-start = (bf16[16,1024]{1,0:T(8,128)(2,1)S(1)}, bf16[16,1024]{1,0:T(8,128)(2,1)}, u32[]{:S(2)}) copy-start(bf16[16,1024]{1,0:T(8,128)(2,1)} %vec_ref.1) | copy-start | bytes 98308
  0.0 2.4 %collective-permute-start = (bf16[1024,256]{1,0:T(8,128)(2,1)}, bf16[1024,256]{1,0:T(8,128)(2,1)S(1)}, u32[]{:S(2)}, u32[]{:S(2)}) collective-permute-start(bf16[1024,256]{1,0:T(8,128)(2,1)} %param.5), channel_id=1, source_target_pairs={{0,1},{1,0},{2,3},{3,2},{4,5},{5,4},{6,7},{7,6},{8,9},{9,8},{10,11... | collective-permute-start | bytes 1572872 | tf_op jit(solution)/shard_map/ppermute | solution.py:393
  0.5 1.9 %collective-permute-start.1 = (bf16[16,1024]{1,0:T(8,128)(2,1)}, bf16[16,1024]{1,0:T(8,128)(2,1)S(1)}, u32[]{:S(2)}, u32[]{:S(2)}) collective-permute-start(bf16[16,1024]{1,0:T(8,128)(2,1)} %vec_ref.1), channel_id=1, source_target_pairs={{0,1},{1,0},{2,3},{3,2},{4,5},{5,4},{6,7},{7,6},{8,9},{9,8},{10,11... | collective-permute-start | bytes 98312 | tf_op jit(solution)/shard_map/ppermute | solution.py:394
  3.1 16.2 %collective-permute-start.2 = (bf16[560,512]{1,0:T(8,128)(2,1)S(1)}, bf16[560,512]{1,0:T(8,128)(2,1)S(1)}, u32[]{:S(2)}, u32[]{:S(2)}) collective-permute-start(bf16[560,512]{1,0:T(8,128)(2,1)S(1)} %get-tuple-element.22.refs_0_.refs_1_), channel_id=1, source_target_pairs={{0,2},{2,0},{4,6},{6,4},{8,10},{10,8},{12,14},{14,12},{1,3},{3,1},... | collective-permute-start | bytes 1720328 | tf_op jit(solution)/shard_map/ppermute | solution.py:400
  6.1 17.0 %collective-permute-start.3 = (bf16[560,512]{1,0:T(8,128)(2,1)S(1)}, bf16[560,512]{1,0:T(8,128)(2,1)S(1)}, u32[]{:S(2)}, u32[]{:S(2)}) collective-permute-start(bf16[560,512]{1,0:T(8,128)(2,1)S(1)} %get-tuple-element.22.refs_0_.refs_1_), channel_id=1, source_target_pairs={{4,0},{6,2},{8,4},{10,6},{12,8},{14,10},{0,12},{2,14},{5,1},{7,3},... | collective-permute-start | bytes 1720328 | tf_op jit(solution)/shard_map/ppermute | solution.py:399
  9.7 26.6 %collective-permute-start.6 = (bf16[560,512]{1,0:T(8,128)(2,1)S(1)}, bf16[560,512]{1,0:T(8,128)(2,1)S(1)}, u32[]{:S(2)}, u32[]{:S(2)}) collective-permute-start(bf16[560,512]{1,0:T(8,128)(2,1)S(1)} %get-tuple-element.22.refs_0_.refs_1_), channel_id=1, source_target_pairs={{0,8},{2,10},{12,4},{14,6},{1,9},{3,11},{13,5},{15,7},{16,24},{18,... | collective-permute-start | bytes 1720328 | tf_op jit(solution)/shard_map/ppermute | solution.py:399
  23.1 2.0 %collective-permute-start.5 = (bf16[288,512]{1,0:T(8,128)(2,1)S(1)}, bf16[288,512]{1,0:T(8,128)(2,1)S(1)}, u32[]{:S(2)}, u32[]{:S(2)}) collective-permute-start(bf16[288,512]{1,0:T(8,128)(2,1)S(1)} %slice.25), channel_id=1, source_target_pairs={{0,1},{1,0},{2,3},{3,2},{4,5},{5,4},{6,7},{7,6},{8,9},{9,8},{10,11... | collective-permute-start | bytes 884744 | tf_op jit(solution)/shard_map/ppermute | solution.py:406
  23.2 1.9 %collective-permute-start.4 = (bf16[272,512]{1,0:T(8,128)(2,1)S(1)}, bf16[272,512]{1,0:T(8,128)(2,1)S(1)}, u32[]{:S(2)}, u32[]{:S(2)}) collective-permute-start(bf16[272,512]{1,0:T(8,128)(2,1)S(1)} %slice.24), channel_id=1, source_target_pairs={{0,1},{1,0},{2,3},{3,2},{4,5},{5,4},{6,7},{7,6},{8,9},{9,8},{10,11... | collective-permute-start | bytes 835592 | tf_op jit(solution)/shard_map/ppermute | solution.py:406
  36.7 1.5 %collective-permute-start.8 = (f32[40,1024]{1,0:T(8,128)S(1)}, f32[40,1024]{1,0:T(8,128)S(1)}, u32[]{:S(2)}, u32[]{:S(2)}) collective-permute-start(f32[40,1024]{1,0:T(8,128)S(1)} %pad_maximum_fusion.1), channel_id=1, source_target_pairs={{0,1},{1,0},{2,3},{3,2},{4,5},{5,4},{6,7},{7,6},{8,9},{9,8},{10,11... | collective-permute-start | bytes 491528 | tf_op jit(solution)/shard_map/ppermute | solution.py:419
  36.9 12.8 %collective-permute-start.7 = (f32[40,512]{1,0:T(8,128)S(1)}, f32[40,512]{1,0:T(8,128)S(1)}, u32[]{:S(2)}, u32[]{:S(2)}) collective-permute-start(f32[40,512]{1,0:T(8,128)S(1)} %get-tuple-element.34), channel_id=1, source_target_pairs={{8,0},{10,2},{4,12},{6,14},{9,1},{11,3},{5,13},{7,15},{24,16},{26,... | collective-permute-start | bytes 245768 | tf_op jit(solution)/shard_map/ppermute | solution.py:421
  38.3 11.4 %collective-permute-start.9 = (f32[40,512]{1,0:T(8,128)S(1)}, f32[40,512]{1,0:T(8,128)S(1)}, u32[]{:S(2)}, u32[]{:S(2)}) collective-permute-start(f32[40,512]{1,0:T(8,128)S(1)} %get-tuple-element.38), channel_id=1, source_target_pairs={{0,4},{2,6},{4,8},{6,10},{8,12},{10,14},{12,0},{14,2},{1,5},{3,7},... | collective-permute-start | bytes 245768 | tf_op jit(solution)/shard_map/ppermute | solution.py:427
  44.9 4.9 %collective-permute-start.10 = (f32[40,512]{1,0:T(8,128)S(1)}, f32[40,512]{1,0:T(8,128)S(1)}, u32[]{:S(2)}, u32[]{:S(2)}) collective-permute-start(f32[40,512]{1,0:T(8,128)S(1)} %get-tuple-element.41), channel_id=1, source_target_pairs={{0,2},{2,0},{4,6},{6,4},{8,10},{10,8},{12,14},{14,12},{1,3},{3,1},... | collective-permute-start | bytes 245768 | tf_op jit(solution)/shard_map/ppermute | solution.py:428
  50.6 10.5 %all-to-all-start = ((f32[16,8,128]{2,1,0:T(8,128)}), f32[16,8,128]{2,1,0:T(8,128)S(1)}, u32[]{:S(2)}, u32[]{:S(2)}) async-start(f32[16,8,128]{2,1,0:T(8,128)} %gram.1), calls=%async_computation | async-start | bytes 131072 | tf_op jit(solution)/shard_map/all_to_all | solution.py:431
  54.2 1.3 %collective-permute-start.11 = (f32[32,512]{1,0:T(8,128)S(1)}, f32[32,512]{1,0:T(8,128)S(1)}, u32[]{:S(2)}, u32[]{:S(2)}) collective-permute-start(f32[32,512]{1,0:T(8,128)S(1)} %image.1.image_ref.mine_ref), channel_id=1, source_target_pairs={{0,1},{1,0},{2,3},{3,2},{4,5},{5,4},{6,7},{7,6},{8,9},{9,8},{10,11... | collective-permute-start | bytes 196616 | tf_op jit(solution)/shard_map/ppermute | solution.py:430

commit v10 on v9

--- a/solution.py
+++ b/solution.py
@@ -132,7 +132,7 @@
     height = jnp.maximum(jnp.minimum(row(TOP), col(TOP)) - jnp.maximum(row(BOTTOM), col(BOTTOM)), 0.0)
     inter = width * height
     both = row(AREA) + col(AREA)
-    share = (both + inter) * pl.reciprocal(both - inter, approx=True)
+    share = (both + inter) * pltpu.reciprocal(both - inter, approx=True, full_range=False)
     gap = jnp.maximum(col(FIRST) - row(LAST), row(FIRST) - col(LAST))
     logit = products * row(NORM) * col(NORM)
     value = jnp.exp2(logit - jnp.maximum(gap, BASE)) * share
@@ -312,7 +312,7 @@
 
 
 def inverse_of(number):
-    guess = pl.reciprocal(number, approx=True)
+    guess = pltpu.reciprocal(number, approx=True)
     guess = guess * (2.0 - number * guess)
     return guess * (2.0 - number * guess)
 
@@ -407,25 +407,18 @@
     beside_sums, next_to = weigh(mine, [beside_mine, beside_rest], turns=True)
     parts = [own_sums, beside_sums]
     col_sums = None
-    returns = []
     for (moves, takers), pack in zip(plans, sent):
         if col_sums is not None:
-            pack, col_sums = lax.optimization_barrier((pack, col_sums))
+            pack, col_sums, parts[-1] = lax.optimization_barrier((pack, col_sums, parts[-1]))
         row_sums, sums = weigh(pack, [own, next_to], receivers=takers)
-        returns.append((row_sums, back(moves)))
+        parts.append(lax.ppermute(row_sums, "blk", back(moves)))
         col_sums = sums if col_sums is None else col_sums + sums
     if col_sums is not None:
         own_mine, own_rest, next_mine, next_rest = [col_sums[:, place * half : (place + 1) * half] for place in range(4)]
         sides = lax.ppermute(jnp.concatenate([own_rest, next_rest], axis=1), "sub", swap)
-        last_sums, last_moves = returns.pop()
-        parts.append(lax.ppermute(last_sums, "blk", last_moves))
-        crossing = next_mine + sides[:, half:]
         parts.append(own_mine)
         parts.append(sides[:, :half])
-        for row_sums, moves in returns:
-            row_sums, _ = lax.optimization_barrier((row_sums, crossing))
-            parts.append(lax.ppermute(row_sums, "blk", moves))
-        parts.append(lax.ppermute(crossing, "blk", beside))
+        parts.append(lax.ppermute(next_mine + sides[:, half:], "blk", beside))
     image = image_of(parts, vecs)
     image_other = lax.ppermute(image, "sub", swap)
     grams = lax.all_to_all(grams_of(image, 2 * blocks), ("blk", "sub"), 0, 0, tiled=True)

time: 64.3 us -> 69.7 us (1.084)
  waiting for transfers between devices: 20 us -> 32.2 us
  starting transfers between devices: 21.7 us -> 14.9 us
    ppermute x3, waiting for transfers between devices: 4.34 us -> 16.3 us  [the longest x2 16.3 us: local(): parts.append(lax.ppermute(row_sums, 'blk', back(moves)))]
    ppermute x3, starting transfers between devices: 8.38 us -> 1.91 us  [the longest x2 1.33 us: local(): parts.append(lax.ppermute(row_sums, 'blk', back(moves)))]
  transfers between devices with their start and end apart: 13 -> 13, of which waited for: 6 -> 8; matrix products, arithmetic and copies ran while one was open for 3% -> 3% of each run, Pallas kernels for 24% -> 22%
where the time goes in v10:
time: 69.7 us; the launch traced here: 69.3 us
  waiting for transfers between devices  32.2 us (46%)
  Pallas kernels  20.1 us (29%)
  starting transfers between devices  14.9 us (21%)
  local copies, waits for them, and re-layouts  1.12 us (2%)
  other arithmetic  0.88 us (1%)
    ppermute x2, waiting for transfers between devices, local(): parts.append(lax.ppermute(row_sums, 'blk', back(moves)))  16.3 us
    pallas_call x4, Pallas kernels, tile(): pl.pallas_call(functools.partial(tile_kernel, len(columns), turns, own_bl...  15.6 us
    all_to_all x1, waiting for transfers between devices, local(): lax.all_to_all(grams_of(image, 2 * blocks), ('blk', 'sub'), 0, 0, tiled=T...  5.54 us
    ppermute x2, starting transfers between devices, local(): sent = [lax.ppermute(mine, 'blk', moves) for moves, _ in plans]  4.97 us
    ppermute x1, waiting for transfers between devices, local(): beside_mine = lax.ppermute(mine, 'blk', beside)  4 us
    ppermute x2, waiting for transfers between devices, local(): sent = [lax.ppermute(mine, 'blk', moves) for moves, _ in plans]  3.79 us
    all_to_all x1, starting transfers between devices, local(): lax.all_to_all(grams_of(image, 2 * blocks), ('blk', 'sub'), 0, 0, tiled=T...  3.5 us
    ppermute x1, starting transfers between devices, local(): beside_mine = lax.ppermute(mine, 'blk', beside)  3.03 us
  transfers between devices with their start and end apart: 13, of which 8 were waited for; matrix products, arithmetic and copies ran while one was open for 3% of the time, Pallas kernels for 22%

profile of v10, /device:TPU:0, one launch (start us, length us, event | category | flops | bytes accessed | tf_op | source)
XLA Modules:
  0.0 69.3 jit_solution(13768690159451234289)
XLA Ops:
  0.0 0.5 collective-permute-start
  0.5 0.1 collective-permute-start.1
  0.5 1.1 %constant_dynamic-slice_fusion = (bf16[512,256]{1,0:T(8,128)(2,1)S(1)}, bf16[512,256]{1,0:T(8,128)(2,1)S(1)}) fusion(bf16[1024,256]{1,0:T(8,128)(2,1)} %param.5, s32[]{:T(128)S(6)} %select_n.7, s32[]{:T(128)S(6)} %select_n.6), kind=kLoop, calls=%fused_computation.4 | loop fusion | bytes 1048584 | tf_op jit(solution)/shard_map/dynamic_slice | solution.py:397
  1.6 0.8 %pad_add_fusion.meta_ref = s32[7,1024]{1,0:T(8,128)S(1)} fusion(s32[1,1024]{1,0:T(1,128)} %bitcast.1, s32[2,1024]{1,0:T(2,128)} %param.8, s32[4,1024]{1,0:T(4,128)} %param.7), kind=kLoop, calls=%fused_computation.3 | loop fusion | flops 14336 | bytes 57344 | tf_op jit(solution)/shard_map/concatenate | solution.py:395
  2.4 0.0 collective-permute-done.emb_other_ref
  2.4 0.7 pack.1
  3.1 3.0 %collective-permute-start.2 = (bf16[560,512]{1,0:T(8,128)(2,1)S(1)}, bf16[560,512]{1,0:T(8,128)(2,1)S(1)}, u32[]{:S(2)}, u32[]{:S(2)}) collective-permute-start(bf16[560,512]{1,0:T(8,128)(2,1)S(1)} %get-tuple-element.22.refs_0_.refs_1_), channel_id=1, source_target_pairs={{0,2},{2,0},{4,6},{6,4},{8,10},{10,8},{12,14},{14,12},{1,3},{3,1},... | collective-permute-start | bytes 1720328 | tf_op jit(solution)/shard_map/ppermute | solution.py:400
  6.1 3.6 %collective-permute-start.3 = (bf16[560,512]{1,0:T(8,128)(2,1)S(1)}, bf16[560,512]{1,0:T(8,128)(2,1)S(1)}, u32[]{:S(2)}, u32[]{:S(2)}) collective-permute-start(bf16[560,512]{1,0:T(8,128)(2,1)S(1)} %get-tuple-element.22.refs_0_.refs_1_), channel_id=1, source_target_pairs={{4,0},{6,2},{8,4},{10,6},{12,8},{14,10},{0,12},{2,14},{5,1},{7,3},... | collective-permute-start | bytes 1720328 | tf_op jit(solution)/shard_map/ppermute | solution.py:399
  9.7 1.4 %collective-permute-start.6 = (bf16[560,512]{1,0:T(8,128)(2,1)S(1)}, bf16[560,512]{1,0:T(8,128)(2,1)S(1)}, u32[]{:S(2)}, u32[]{:S(2)}) collective-permute-start(bf16[560,512]{1,0:T(8,128)(2,1)S(1)} %get-tuple-element.22.refs_0_.refs_1_), channel_id=1, source_target_pairs={{0,8},{2,10},{12,4},{14,6},{1,9},{3,11},{13,5},{15,7},{16,24},{18,... | collective-permute-start | bytes 1720328 | tf_op jit(solution)/shard_map/ppermute | solution.py:399
  11.1 4.2 %tile.4 = (f32[40,512]{1,0:T(8,128)S(1)}, bf16[560,1024]{1,0:T(8,128)(2,1)S(1)}) custom-call(bf16[560,512]{1,0:T(8,128)(2,1)S(1)} %get-tuple-element.22.refs_0_.refs_1_, bf16[560,512]{1,0:T(8,128)(2,1)S(1)} %get-tuple-element.22.refs_0_.refs_1_, bf16[560,512]{1,0:T(8,128)(2,1)S(1)} %get-tuple-element.23.refs_2_), custom_call_target="tpu_custom_call" | custom-call | flops 1 | bytes 1 | tf_op jit(solution)/shard_map/tile/pallas_call | solution.py:249
  15.3 4.0 %collective-permute-done.2.refs_1_ = bf16[560,512]{1,0:T(8,128)(2,1)S(1)} collective-permute-done((bf16[560,512]{1,0:T(8,128)(2,1)S(1)}, bf16[560,512]{1,0:T(8,128)(2,1)S(1)}, u32[]{:S(2)}, u32[]{:S(2)}) %collective-permute-start.2) | collective-permute-done | bytes 573472 | tf_op jit(solution)/shard_map/ppermute | solution.py:400
  19.3 3.8 %collective-permute-done.3.refs_0_ = bf16[560,512]{1,0:T(8,128)(2,1)S(1)} collective-permute-done((bf16[560,512]{1,0:T(8,128)(2,1)S(1)}, bf16[560,512]{1,0:T(8,128)(2,1)S(1)}, u32[]{:S(2)}, u32[]{:S(2)}) %collective-permute-start.3) | collective-permute-done | bytes 573472 | tf_op jit(solution)/shard_map/ppermute | solution.py:399
  23.1 0.1 collective-permute-start.5
  23.2 0.6 collective-permute-start.4
  23.8 1.4 %collective-permute-done.4 = bf16[272,512]{1,0:T(8,128)(2,1)S(1)} collective-permute-done((bf16[272,512]{1,0:T(8,128)(2,1)S(1)}, bf16[272,512]{1,0:T(8,128)(2,1)S(1)}, u32[]{:S(2)}, u32[]{:S(2)}) %collective-permute-start.4) | collective-permute-done | bytes 278560 | tf_op jit(solution)/shard_map/ppermute | solution.py:406
  25.2 4.0 %tile.5 = (f32[40,512]{1,0:T(8,128)S(1)}, bf16[560,1024]{1,0:T(8,128)(2,1)S(1)}) custom-call(bf16[560,512]{1,0:T(8,128)(2,1)S(1)} %get-tuple-element.22.refs_0_.refs_1_, bf16[560,512]{1,0:T(8,128)(2,1)S(1)} %collective-permute-done.2.refs_1_, bf16[560,512]{1,0:T(8,128)(2,1)S(1)} %pad_maximum_fusion.refs_2_), custom_call_target="tpu_custom_call" | custom-call | flops 1 | bytes 1 | tf_op jit(solution)/shard_map/tile/pallas_call | solution.py:249
  29.2 7.2 %tile.6 = (f32[40,512]{1,0:T(8,128)S(1)}, f32[40,2048]{1,0:T(8,128)S(1)}) custom-call(bf16[560,512]{1,0:T(8,128)(2,1)S(1)} %collective-permute-done.3.refs_0_, bf16[560,1024]{1,0:T(8,128)(2,1)S(1)} %get-tuple-element.30.refs_1_, bf16[560,1024]{1,0:T(8,128)(2,1)S(1)} %get-tuple-element.31.refs_2_), custom_call_target="tpu_custom_call" | custom-call | flops 1 | bytes 1 | tf_op jit(solution)/shard_map/tile/pallas_call | solution.py:249
  36.4 0.0 collective-permute-start.7
  36.4 7.0 %collective-permute-done.7.refs_2_ = f32[40,512]{1,0:T(8,128)S(1)} collective-permute-done((f32[40,512]{1,0:T(8,128)S(1)}, f32[40,512]{1,0:T(8,128)S(1)}, u32[]{:S(2)}, u32[]{:S(2)}) %collective-permute-start.7) | collective-permute-done | bytes 81952 | tf_op jit(solution)/shard_map/ppermute | solution.py:414
  43.5 0.2 tile.7
  43.8 0.1 collective-permute-start.9
  43.9 1.3 %collective-permute-start.8 = (f32[40,512]{1,0:T(8,128)S(1)}, f32[40,512]{1,0:T(8,128)S(1)}, u32[]{:S(2)}, u32[]{:S(2)}) collective-permute-start(f32[40,512]{1,0:T(8,128)S(1)} %get-tuple-element.36), channel_id=1, source_target_pairs={{8,0},{10,2},{4,12},{6,14},{9,1},{11,3},{5,13},{7,15},{24,16},{26,... | collective-permute-start | bytes 245768 | tf_op jit(solution)/shard_map/ppermute | solution.py:414
  45.2 0.1 collective-permute-done.9
  45.3 0.6 collective-permute-start.10
  45.8 9.3 %collective-permute-done.8.refs_3_ = f32[40,512]{1,0:T(8,128)S(1)} collective-permute-done((f32[40,512]{1,0:T(8,128)S(1)}, f32[40,512]{1,0:T(8,128)S(1)}, u32[]{:S(2)}, u32[]{:S(2)}) %collective-permute-start.8) | collective-permute-done | bytes 81952 | tf_op jit(solution)/shard_map/ppermute | solution.py:414
  55.1 0.0 collective-permute-done.10.refs_6_
  55.2 0.9 %gram.1 = f32[16,8,128]{2,1,0:T(8,128)} custom-call(f32[32,512]{1,0:T(8,128)S(1)} %image.1.image_ref.mine_ref), custom_call_target="tpu_custom_call" | custom-call | tf_op jit(solution)/shard_map/gram/pallas_call | solution.py:304
  56.1 3.5 %all-to-all-start = ((f32[16,8,128]{2,1,0:T(8,128)}), f32[16,8,128]{2,1,0:T(8,128)S(1)}, u32[]{:S(2)}, u32[]{:S(2)}) async-start(f32[16,8,128]{2,1,0:T(8,128)} %gram.1), calls=%async_computation | async-start | bytes 131072 | tf_op jit(solution)/shard_map/all_to_all | solution.py:424
  59.6 0.3 collective-permute-start.11
  59.9 1.0 %collective-permute-done.11.other_ref = f32[32,512]{1,0:T(8,128)S(1)} collective-permute-done((f32[32,512]{1,0:T(8,128)S(1)}, f32[32,512]{1,0:T(8,128)S(1)}, u32[]{:S(2)}, u32[]{:S(2)}) %collective-permute-start.11) | collective-permute-done | bytes 65568 | tf_op jit(solution)/shard_map/ppermute | solution.py:423
  60.9 5.5 %all-to-all-done.grams_ref = f32[16,8,128]{2,1,0:T(8,128)S(1)} async-done(((f32[16,8,128]{2,1,0:T(8,128)}), f32[16,8,128]{2,1,0:T(8,128)S(1)}, u32[]{:S(2)}, u32[]{:S(2)}) %all-to-all-start) | async-done | bytes 65568 | tf_op jit(solution)/shard_map/all_to_all | solution.py:424
  66.4 2.9 %basis.1 = f32[16,1024]{1,0:T(8,128)} custom-call(f32[16,8,128]{2,1,0:T(8,128)S(1)} %all-to-all-done.grams_ref, f32[32,512]{1,0:T(8,128)S(1)} %image.1.image_ref.mine_ref, f32[32,512]{1,0:T(8,128)S(1)} %collective-permute-done.11.other_ref), custom_call_target="tpu_custom_call" | custom-call | tf_op jit(solution)/shard_map/basis/pallas_call | solution.py:354
  (13 shorter events, 0.2 us)
Async XLA Ops:
  0.0 2.4 %copy-start = (bf16[16,1024]{1,0:T(8,128)(2,1)S(1)}, bf16[16,1024]{1,0:T(8,128)(2,1)}, u32[]{:S(2)}) copy-start(bf16[16,1024]{1,0:T(8,128)(2,1)} %vec_ref.1) | copy-start | bytes 98308
  0.0 2.4 %collective-permute-start = (bf16[1024,256]{1,0:T(8,128)(2,1)}, bf16[1024,256]{1,0:T(8,128)(2,1)S(1)}, u32[]{:S(2)}, u32[]{:S(2)}) collective-permute-start(bf16[1024,256]{1,0:T(8,128)(2,1)} %param.5), channel_id=1, source_target_pairs={{0,1},{1,0},{2,3},{3,2},{4,5},{5,4},{6,7},{7,6},{8,9},{9,8},{10,11... | collective-permute-start | bytes 1572872 | tf_op jit(solution)/shard_map/ppermute | solution.py:393
  0.5 1.9 %collective-permute-start.1 = (bf16[16,1024]{1,0:T(8,128)(2,1)}, bf16[16,1024]{1,0:T(8,128)(2,1)S(1)}, u32[]{:S(2)}, u32[]{:S(2)}) collective-permute-start(bf16[16,1024]{1,0:T(8,128)(2,1)} %vec_ref.1), channel_id=1, source_target_pairs={{0,1},{1,0},{2,3},{3,2},{4,5},{5,4},{6,7},{7,6},{8,9},{9,8},{10,11... | collective-permute-start | bytes 98312 | tf_op jit(solution)/shard_map/ppermute | solution.py:394
  3.1 16.2 %collective-permute-start.2 = (bf16[560,512]{1,0:T(8,128)(2,1)S(1)}, bf16[560,512]{1,0:T(8,128)(2,1)S(1)}, u32[]{:S(2)}, u32[]{:S(2)}) collective-permute-start(bf16[560,512]{1,0:T(8,128)(2,1)S(1)} %get-tuple-element.22.refs_0_.refs_1_), channel_id=1, source_target_pairs={{0,2},{2,0},{4,6},{6,4},{8,10},{10,8},{12,14},{14,12},{1,3},{3,1},... | collective-permute-start | bytes 1720328 | tf_op jit(solution)/shard_map/ppermute | solution.py:400
  6.1 17.0 %collective-permute-start.3 = (bf16[560,512]{1,0:T(8,128)(2,1)S(1)}, bf16[560,512]{1,0:T(8,128)(2,1)S(1)}, u32[]{:S(2)}, u32[]{:S(2)}) collective-permute-start(bf16[560,512]{1,0:T(8,128)(2,1)S(1)} %get-tuple-element.22.refs_0_.refs_1_), channel_id=1, source_target_pairs={{4,0},{6,2},{8,4},{10,6},{12,8},{14,10},{0,12},{2,14},{5,1},{7,3},... | collective-permute-start | bytes 1720328 | tf_op jit(solution)/shard_map/ppermute | solution.py:399
  9.7 26.7 %collective-permute-start.6 = (bf16[560,512]{1,0:T(8,128)(2,1)S(1)}, bf16[560,512]{1,0:T(8,128)(2,1)S(1)}, u32[]{:S(2)}, u32[]{:S(2)}) collective-permute-start(bf16[560,512]{1,0:T(8,128)(2,1)S(1)} %get-tuple-element.22.refs_0_.refs_1_), channel_id=1, source_target_pairs={{0,8},{2,10},{12,4},{14,6},{1,9},{3,11},{13,5},{15,7},{16,24},{18,... | collective-permute-start | bytes 1720328 | tf_op jit(solution)/shard_map/ppermute | solution.py:399
  23.1 2.0 %collective-permute-start.5 = (bf16[288,512]{1,0:T(8,128)(2,1)S(1)}, bf16[288,512]{1,0:T(8,128)(2,1)S(1)}, u32[]{:S(2)}, u32[]{:S(2)}) collective-permute-start(bf16[288,512]{1,0:T(8,128)(2,1)S(1)} %slice.25), channel_id=1, source_target_pairs={{0,1},{1,0},{2,3},{3,2},{4,5},{5,4},{6,7},{7,6},{8,9},{9,8},{10,11... | collective-permute-start | bytes 884744 | tf_op jit(solution)/shard_map/ppermute | solution.py:406
  23.2 1.9 %collective-permute-start.4 = (bf16[272,512]{1,0:T(8,128)(2,1)S(1)}, bf16[272,512]{1,0:T(8,128)(2,1)S(1)}, u32[]{:S(2)}, u32[]{:S(2)}) collective-permute-start(bf16[272,512]{1,0:T(8,128)(2,1)S(1)} %slice.24), channel_id=1, source_target_pairs={{0,1},{1,0},{2,3},{3,2},{4,5},{5,4},{6,7},{7,6},{8,9},{9,8},{10,11... | collective-permute-start | bytes 835592 | tf_op jit(solution)/shard_map/ppermute | solution.py:406
  36.4 7.1 %collective-permute-start.7 = (f32[40,512]{1,0:T(8,128)S(1)}, f32[40,512]{1,0:T(8,128)S(1)}, u32[]{:S(2)}, u32[]{:S(2)}) collective-permute-start(f32[40,512]{1,0:T(8,128)S(1)} %get-tuple-element.33), channel_id=1, source_target_pairs={{0,4},{2,6},{4,8},{6,10},{8,12},{10,14},{12,0},{14,2},{1,5},{3,7},... | collective-permute-start | bytes 245768 | tf_op jit(solution)/shard_map/ppermute | solution.py:414
  43.8 1.5 %collective-permute-start.9 = (f32[40,1024]{1,0:T(8,128)S(1)}, f32[40,1024]{1,0:T(8,128)S(1)}, u32[]{:S(2)}, u32[]{:S(2)}) collective-permute-start(f32[40,1024]{1,0:T(8,128)S(1)} %pad_maximum_fusion.1), channel_id=1, source_target_pairs={{0,1},{1,0},{2,3},{3,2},{4,5},{5,4},{6,7},{7,6},{8,9},{9,8},{10,11... | collective-permute-start | bytes 491528 | tf_op jit(solution)/shard_map/ppermute | solution.py:418
  43.9 11.3 %collective-permute-start.8 = (f32[40,512]{1,0:T(8,128)S(1)}, f32[40,512]{1,0:T(8,128)S(1)}, u32[]{:S(2)}, u32[]{:S(2)}) collective-permute-start(f32[40,512]{1,0:T(8,128)S(1)} %get-tuple-element.36), channel_id=1, source_target_pairs={{8,0},{10,2},{4,12},{6,14},{9,1},{11,3},{5,13},{7,15},{24,16},{26,... | collective-permute-start | bytes 245768 | tf_op jit(solution)/shard_map/ppermute | solution.py:414
  45.3 9.9 %collective-permute-start.10 = (f32[40,512]{1,0:T(8,128)S(1)}, f32[40,512]{1,0:T(8,128)S(1)}, u32[]{:S(2)}, u32[]{:S(2)}) collective-permute-start(f32[40,512]{1,0:T(8,128)S(1)} %get-tuple-element.41), channel_id=1, source_target_pairs={{0,2},{2,0},{4,6},{6,4},{8,10},{10,8},{12,14},{14,12},{1,3},{3,1},... | collective-permute-start | bytes 245768 | tf_op jit(solution)/shard_map/ppermute | solution.py:421
  56.1 10.4 %all-to-all-start = ((f32[16,8,128]{2,1,0:T(8,128)}), f32[16,8,128]{2,1,0:T(8,128)S(1)}, u32[]{:S(2)}, u32[]{:S(2)}) async-start(f32[16,8,128]{2,1,0:T(8,128)} %gram.1), calls=%async_computation | async-start | bytes 131072 | tf_op jit(solution)/shard_map/all_to_all | solution.py:424
  59.6 1.3 %collective-permute-start.11 = (f32[32,512]{1,0:T(8,128)S(1)}, f32[32,512]{1,0:T(8,128)S(1)}, u32[]{:S(2)}, u32[]{:S(2)}) collective-permute-start(f32[32,512]{1,0:T(8,128)S(1)} %image.1.image_ref.mine_ref), channel_id=1, source_target_pairs={{0,1},{1,0},{2,3},{3,2},{4,5},{5,4},{6,7},{7,6},{8,9},{9,8},{10,11... | collective-permute-start | bytes 196616 | tf_op jit(solution)/shard_map/ppermute | solution.py:423

commit v11 on v9

--- a/solution.py
+++ b/solution.py
@@ -132,7 +132,7 @@
     height = jnp.maximum(jnp.minimum(row(TOP), col(TOP)) - jnp.maximum(row(BOTTOM), col(BOTTOM)), 0.0)
     inter = width * height
     both = row(AREA) + col(AREA)
-    share = (both + inter) * pl.reciprocal(both - inter, approx=True)
+    share = (both + inter) * pltpu.reciprocal(both - inter, approx=True, full_range=False)
     gap = jnp.maximum(col(FIRST) - row(LAST), row(FIRST) - col(LAST))
     logit = products * row(NORM) * col(NORM)
     value = jnp.exp2(logit - jnp.maximum(gap, BASE)) * share
@@ -142,31 +142,30 @@
     return jnp.where(barred, 0.0, value)
 
 
-def tile_kernel(blocks, turns, own_block, receivers, vecs, *refs):
+def tile_kernel(blocks, turns, own_block, receivers, vecs, lines, *refs):
     row_ref, col_refs = refs[0], refs[1 : 1 + blocks]
     row_out_ref, col_out_ref, field_ref, spread_ref, sum_ref = refs[1 + blocks : 6 + blocks]
-    products, weights, col_spreads = [refs[at : at + 2] for at in range(6 + blocks, 12 + blocks, 2)]
+    products, weights = [refs[at : at + 2] for at in (6 + blocks, 8 + blocks)]
+    col_spread_ref, row_vec_ref, col_vec_ref = refs[10 + blocks :]
     size, rows = row_ref.shape
     features = size - vecs - CODE_ROWS
     vec_rows, code_rows = slice(features, features + vecs), slice(features + vecs, size)
     sum_ref[...] = jnp.zeros_like(sum_ref)
 
-    def block(col_ref, done, row_vecs):
+    def block(col_ref, done):
         chunks = col_ref.shape[1] // CHUNK
 
         def place(step, base=0):
             return pl.ds(pl.multiple_of(base + step * CHUNK, CHUNK), CHUNK)
 
-        def multiply(step, product_ref):
-            product_ref[...] = jnp.dot(
-                row_ref[0:rows, :], col_ref[0:features, place(step)], preferred_element_type=jnp.float32
+        def multiply(step, part, product_ref):
+            product_ref[part, :] = jnp.dot(
+                row_ref[part, :], col_ref[0:features, place(step)], preferred_element_type=jnp.float32
             )
 
-        def weigh(step, product_ref, weight_ref, col_spread_ref):
-            for field, values in enumerate(decode(col_ref[code_rows, place(step)])):
-                col_spread_ref[field] = jnp.broadcast_to(values, (8, CHUNK))
-            for first_row in range(0, rows, GROUP):
-                row_part = slice(first_row, first_row + GROUP)
+        def weigh(step, first, product_ref, weight_ref):
+            for start in range(0, lines, GROUP):
+                row_part = pl.ds(pl.multiple_of(first + start, GROUP), GROUP)
 
                 def row(field):
                     return jnp.concatenate([spread_ref[field, row_part, :]] * (CHUNK // LANES), axis=1)
@@ -176,29 +175,46 @@
 
                 same = None
                 if own_block:
-                    row_ids = lax.broadcasted_iota(jnp.int32, (GROUP, CHUNK), 0) + (first_row - step * CHUNK)
+                    row_ids = lax.broadcasted_iota(jnp.int32, (GROUP, CHUNK), 0) + (first + start - step * CHUNK)
                     same = row_ids == lax.broadcasted_iota(jnp.int32, (GROUP, CHUNK), 1)
                 weight_ref[row_part, :] = weights_of(product_ref[row_part, :], row, col, same).astype(jnp.bfloat16)
 
-        def total(step, weight_ref):
-            sum_ref[:, 0 : vecs + CODE_ROWS] += dot_nt(weight_ref[...], with_ones(col_ref[vec_rows, place(step)]))
+        def prepare_total(step):
+            col_vec_ref[...] = with_ones(col_ref[vec_rows, place(step)])
             if not turns:
-                col_out_ref[:, place(step, done)] = jnp.dot(
-                    row_vecs, weight_ref[...], preferred_element_type=jnp.float32
+                col_out_ref[:, place(step, done)] = jnp.zeros((OUT_ROWS, CHUNK), jnp.float32)
+
+        def total(step, part, weight_ref):
+            sum_ref[part, 0 : vecs + CODE_ROWS] += dot_nt(weight_ref[part, :], col_vec_ref[...])
+            if not turns:
+                col_out_ref[:, place(step, done)] += jnp.dot(
+                    row_vec_ref[:, part], weight_ref[part, :], preferred_element_type=jnp.float32
                 )[0:OUT_ROWS]
 
         def steps(index, carry):
             for parity in range(2):
                 step = 2 * index + parity
-                multiply(lax.rem(step + 1, chunks), products[1 - parity])
-                weigh(step, products[parity], weights[parity], col_spreads[parity])
-                total(lax.rem(step + chunks - 1, chunks), weights[1 - parity])
+                ahead, behind = lax.rem(step + 1, chunks), lax.rem(step + chunks - 1, chunks)
+                for field, values in enumerate(decode(col_ref[code_rows, place(step)])):
+                    col_spread_ref[field] = jnp.broadcast_to(values, (8, CHUNK))
+                prepare_total(behind)
+
+                def some_lines(number, inner, parity=parity, step=step, ahead=ahead, behind=behind):
+                    first = pl.multiple_of(number * lines, lines)
+                    part = pl.ds(first, lines)
+                    multiply(ahead, part, products[1 - parity])
+                    weigh(step, first, products[parity], weights[parity])
+                    total(behind, part, weights[1 - parity])
+                    return inner
+
+                lax.fori_loop(0, rows // lines, some_lines, 0)
             return carry
 
-        multiply(0, products[0])
+        multiply(0, pl.ds(0, rows), products[0])
         weights[1][...] = jnp.zeros_like(weights[1])
         lax.fori_loop(0, chunks // 2, steps, 0)
-        total(chunks - 1, weights[1])
+        prepare_total(chunks - 1)
+        total(chunks - 1, pl.ds(0, rows), weights[1])
 
     def compute():
         for field, values in enumerate(decode(row_ref[code_rows, :])):
@@ -206,17 +222,17 @@
         turned = field_ref[...].T
         for field in range(FIELDS):
             spread_ref[field] = jnp.broadcast_to(turned[:, field : field + 1], (rows, LANES))
-        row_vecs = with_ones(row_ref[vec_rows, :])
+        row_vec_ref[...] = with_ones(row_ref[vec_rows, :])
         if turns:
             for number, pack_ref in enumerate(col_refs):
                 part = pl.ds(number * rows, rows)
                 col_out_ref[0:features, part] = pack_ref[0:rows, :].T
                 col_out_ref[features:size, part] = pack_ref[features:size, :]
-            block(col_out_ref, 0, row_vecs)
+            block(col_out_ref, 0)
         else:
             done = 0
             for col_ref in col_refs:
-                block(col_ref, done, row_vecs)
+                block(col_ref, done)
                 done += col_ref.shape[1]
 
     def finish():
@@ -240,14 +256,14 @@
         col_out_ref[...] = jnp.zeros_like(col_out_ref)
 
 
-def tile(row, columns, vecs, turns=False, own_block=False, receivers=None):
+def tile(row, columns, vecs, lines, turns=False, own_block=False, receivers=None):
     size, rows = row.shape
     cols = len(columns) * rows if turns else sum(part.shape[1] for part in columns)
     second = jax.ShapeDtypeStruct((size, cols), jnp.bfloat16)
     if not turns:
         second = jax.ShapeDtypeStruct((OUT_ROWS, cols), jnp.float32)
     return pl.pallas_call(
-        functools.partial(tile_kernel, len(columns), turns, own_block, receivers, vecs),
+        functools.partial(tile_kernel, len(columns), turns, own_block, receivers, vecs, lines),
         out_shape=[jax.ShapeDtypeStruct((OUT_ROWS, rows), jnp.float32), second],
         in_specs=[VMEM_SPEC] * (1 + len(columns)),
         out_specs=[VMEM_SPEC] * 2,
@@ -260,7 +276,8 @@
             pltpu.VMEM((rows, CHUNK), jnp.bfloat16),
             pltpu.VMEM((rows, CHUNK), jnp.bfloat16),
             pltpu.VMEM((FIELDS, 8, CHUNK), jnp.float32),
-            pltpu.VMEM((FIELDS, 8, CHUNK), jnp.float32),
+            pltpu.VMEM((vecs + CODE_ROWS, rows), jnp.bfloat16),
+            pltpu.VMEM((vecs + CODE_ROWS, CHUNK), jnp.bfloat16),
         ],
         cost_estimate=pl.CostEstimate(flops=COST, bytes_accessed=COST, transcendentals=0),
         compiler_params=params(),
@@ -312,7 +329,7 @@
 
 
 def inverse_of(number):
-    guess = pl.reciprocal(number, approx=True)
+    guess = pltpu.reciprocal(number, approx=True)
     guess = guess * (2.0 - number * guess)
     return guess * (2.0 - number * guess)
 
@@ -399,19 +416,19 @@
     sent = [lax.ppermute(mine, "blk", moves) for moves, _ in plans]
     beside_mine = lax.ppermute(mine, "blk", beside)
     weigh = functools.partial(tile, vecs=vecs)
-    own_sums, own = weigh(mine, [mine, rest], turns=True, own_block=True)
+    own_sums, own = weigh(mine, [mine, rest], lines=128, turns=True, own_block=True)
     own_sums, own, beside_mine, sent[:1] = lax.optimization_barrier((own_sums, own, beside_mine, sent[:1]))
     cut = beside_mine.shape[0] // SWAPS // 16 * 16
     shares = [beside_mine[at * cut : (at + 1) * cut if at < SWAPS - 1 else None] for at in range(SWAPS)]
     beside_rest = jnp.concatenate([lax.ppermute(share, "sub", swap) for share in shares], axis=0)
-    beside_sums, next_to = weigh(mine, [beside_mine, beside_rest], turns=True)
+    beside_sums, next_to = weigh(mine, [beside_mine, beside_rest], lines=256, turns=True)
     parts = [own_sums, beside_sums]
     col_sums = None
     returns = []
-    for (moves, takers), pack in zip(plans, sent):
+    for number, ((moves, takers), pack) in enumerate(zip(plans, sent)):
         if col_sums is not None:
             pack, col_sums = lax.optimization_barrier((pack, col_sums))
-        row_sums, sums = weigh(pack, [own, next_to], receivers=takers)
+        row_sums, sums = weigh(pack, [own, next_to], lines=128 if number == 0 else 256, receivers=takers)
         returns.append((row_sums, back(moves)))
         col_sums = sums if col_sums is None else col_sums + sums
     if col_sums is not None:

time: 64.3 us -> 72.1 us (1.12)
  Pallas kernels: 20.1 us -> 27.6 us
  starting transfers between devices: 21.7 us -> 23.4 us
  waiting for transfers between devices: 20 us -> 18.6 us
    pallas_call x4, Pallas kernels: 15.6 us -> 23.1 us  [tile(): pl.pallas_call(functools.partial(tile_kernel, len(columns), turns, own_bl...]
    ppermute x1, starting transfers between devices: 6.59 us -> 8.3 us  [local(): parts.append(lax.ppermute(row_sums, 'blk', moves))]
    ppermute x1, waiting for transfers between devices: 4 us -> 2.56 us  [local(): beside_mine = lax.ppermute(mine, 'blk', beside)]
  transfers between devices with their start and end apart: 13 -> 13, of which waited for: 6 -> 6; matrix products, arithmetic and copies ran while one was open for 3% -> 3% of each run, Pallas kernels for 24% -> 32%
where the time goes in v11:
time: 72.1 us; the launch traced here: 71.7 us
  Pallas kernels  27.6 us (38%)
  starting transfers between devices  23.4 us (32%)
  waiting for transfers between devices  18.6 us (26%)
  local copies, waits for them, and re-layouts  1.12 us (2%)
  other arithmetic  0.88 us (1%)
    pallas_call x4, Pallas kernels, tile(): pl.pallas_call(functools.partial(tile_kernel, len(columns), turns, own_bl...  23.1 us
    ppermute x1, starting transfers between devices, local(): parts.append(lax.ppermute(row_sums, 'blk', moves))  8.3 us
    all_to_all x1, waiting for transfers between devices, local(): lax.all_to_all(grams_of(image, 2 * blocks), ('blk', 'sub'), 0, 0, tiled=T...  5.58 us
    ppermute x2, starting transfers between devices, local(): sent = [lax.ppermute(mine, 'blk', moves) for moves, _ in plans]  4.97 us
    ppermute x1, waiting for transfers between devices, local(): parts.append(lax.ppermute(last_sums, 'blk', last_moves))  4.34 us
    ppermute x2, waiting for transfers between devices, local(): sent = [lax.ppermute(mine, 'blk', moves) for moves, _ in plans]  3.79 us
    all_to_all x1, starting transfers between devices, local(): lax.all_to_all(grams_of(image, 2 * blocks), ('blk', 'sub'), 0, 0, tiled=T...  3.56 us
    ppermute x1, starting transfers between devices, local(): beside_mine = lax.ppermute(mine, 'blk', beside)  3.03 us
  transfers between devices with their start and end apart: 13, of which 6 were waited for; matrix products, arithmetic and copies ran while one was open for 3% of the time, Pallas kernels for 32%

profile of v11, /device:TPU:0, one launch (start us, length us, event | category | flops | bytes accessed | tf_op | source)
XLA Modules:
  0.0 71.7 jit_solution(12457063532033265550)
XLA Ops:
  0.0 0.5 collective-permute-start
  0.5 0.1 collective-permute-start.1
  0.5 1.1 %constant_dynamic-slice_fusion = (bf16[512,256]{1,0:T(8,128)(2,1)S(1)}, bf16[512,256]{1,0:T(8,128)(2,1)S(1)}) fusion(bf16[1024,256]{1,0:T(8,128)(2,1)} %param.5, s32[]{:T(128)S(6)} %select_n.7, s32[]{:T(128)S(6)} %select_n.6), kind=kLoop, calls=%fused_computation.4 | loop fusion | bytes 1048584 | tf_op jit(solution)/shard_map/dynamic_slice | solution.py:414
  1.6 0.8 %pad_add_fusion.meta_ref = s32[7,1024]{1,0:T(8,128)S(1)} fusion(s32[1,1024]{1,0:T(1,128)} %bitcast.1, s32[2,1024]{1,0:T(2,128)} %param.8, s32[4,1024]{1,0:T(4,128)} %param.7), kind=kLoop, calls=%fused_computation.3 | loop fusion | flops 14336 | bytes 57344 | tf_op jit(solution)/shard_map/concatenate | solution.py:412
  2.4 0.0 collective-permute-done.1.vec_other_ref
  2.4 0.0 collective-permute-done.emb_other_ref
  2.4 0.7 pack.1
  3.1 3.0 %collective-permute-start.2 = (bf16[560,512]{1,0:T(8,128)(2,1)S(1)}, bf16[560,512]{1,0:T(8,128)(2,1)S(1)}, u32[]{:S(2)}, u32[]{:S(2)}) collective-permute-start(bf16[560,512]{1,0:T(8,128)(2,1)S(1)} %get-tuple-element.22.refs_0_.refs_1_), channel_id=1, source_target_pairs={{0,2},{2,0},{4,6},{6,4},{8,10},{10,8},{12,14},{14,12},{1,3},{3,1},... | collective-permute-start | bytes 1720328 | tf_op jit(solution)/shard_map/ppermute | solution.py:417
  6.1 3.6 %collective-permute-start.3 = (bf16[560,512]{1,0:T(8,128)(2,1)S(1)}, bf16[560,512]{1,0:T(8,128)(2,1)S(1)}, u32[]{:S(2)}, u32[]{:S(2)}) collective-permute-start(bf16[560,512]{1,0:T(8,128)(2,1)S(1)} %get-tuple-element.22.refs_0_.refs_1_), channel_id=1, source_target_pairs={{4,0},{6,2},{8,4},{10,6},{12,8},{14,10},{0,12},{2,14},{5,1},{7,3},... | collective-permute-start | bytes 1720328 | tf_op jit(solution)/shard_map/ppermute | solution.py:416
  9.7 1.4 %collective-permute-start.6 = (bf16[560,512]{1,0:T(8,128)(2,1)S(1)}, bf16[560,512]{1,0:T(8,128)(2,1)S(1)}, u32[]{:S(2)}, u32[]{:S(2)}) collective-permute-start(bf16[560,512]{1,0:T(8,128)(2,1)S(1)} %get-tuple-element.22.refs_0_.refs_1_), channel_id=1, source_target_pairs={{0,8},{2,10},{12,4},{14,6},{1,9},{3,11},{13,5},{15,7},{16,24},{18,... | collective-permute-start | bytes 1720328 | tf_op jit(solution)/shard_map/ppermute | solution.py:416
  11.1 5.7 %tile.4 = (f32[40,512]{1,0:T(8,128)S(1)}, bf16[560,1024]{1,0:T(8,128)(2,1)S(1)}) custom-call(bf16[560,512]{1,0:T(8,128)(2,1)S(1)} %get-tuple-element.22.refs_0_.refs_1_, bf16[560,512]{1,0:T(8,128)(2,1)S(1)} %get-tuple-element.22.refs_0_.refs_1_, bf16[560,512]{1,0:T(8,128)(2,1)S(1)} %get-tuple-element.23.refs_2_), custom_call_target="tpu_custom_call" | custom-call | flops 1 | bytes 1 | tf_op jit(solution)/shard_map/tile/pallas_call | solution.py:265
  16.8 2.6 %collective-permute-done.2.refs_1_ = bf16[560,512]{1,0:T(8,128)(2,1)S(1)} collective-permute-done((bf16[560,512]{1,0:T(8,128)(2,1)S(1)}, bf16[560,512]{1,0:T(8,128)(2,1)S(1)}, u32[]{:S(2)}, u32[]{:S(2)}) %collective-permute-start.2) | collective-permute-done | bytes 573472 | tf_op jit(solution)/shard_map/ppermute | solution.py:417
  19.3 3.8 %collective-permute-done.3.refs_0_ = bf16[560,512]{1,0:T(8,128)(2,1)S(1)} collective-permute-done((bf16[560,512]{1,0:T(8,128)(2,1)S(1)}, bf16[560,512]{1,0:T(8,128)(2,1)S(1)}, u32[]{:S(2)}, u32[]{:S(2)}) %collective-permute-start.3) | collective-permute-done | bytes 573472 | tf_op jit(solution)/shard_map/ppermute | solution.py:416
  23.1 0.1 collective-permute-start.5
  23.2 0.6 collective-permute-start.4
  23.8 1.4 %collective-permute-done.4 = bf16[272,512]{1,0:T(8,128)(2,1)S(1)} collective-permute-done((bf16[272,512]{1,0:T(8,128)(2,1)S(1)}, bf16[272,512]{1,0:T(8,128)(2,1)S(1)}, u32[]{:S(2)}, u32[]{:S(2)}) %collective-permute-start.4) | collective-permute-done | bytes 278560 | tf_op jit(solution)/shard_map/ppermute | solution.py:423
  25.2 0.0 collective-permute-done.5
  25.2 5.3 %tile.5 = (f32[40,512]{1,0:T(8,128)S(1)}, bf16[560,1024]{1,0:T(8,128)(2,1)S(1)}) custom-call(bf16[560,512]{1,0:T(8,128)(2,1)S(1)} %get-tuple-element.22.refs_0_.refs_1_, bf16[560,512]{1,0:T(8,128)(2,1)S(1)} %collective-permute-done.2.refs_1_, bf16[560,512]{1,0:T(8,128)(2,1)S(1)} %pad_maximum_fusion.refs_2_), custom_call_target="tpu_custom_call" | custom-call | flops 1 | bytes 1 | tf_op jit(solution)/shard_map/tile/pallas_call | solution.py:265
  30.6 12.0 %tile.6 = (f32[40,512]{1,0:T(8,128)S(1)}, f32[40,2048]{1,0:T(8,128)S(1)}) custom-call(bf16[560,512]{1,0:T(8,128)(2,1)S(1)} %collective-permute-done.3.refs_0_, bf16[560,1024]{1,0:T(8,128)(2,1)S(1)} %get-tuple-element.30.refs_1_, bf16[560,1024]{1,0:T(8,128)(2,1)S(1)} %get-tuple-element.31.refs_2_), custom_call_target="tpu_custom_call" | custom-call | flops 1 | bytes 1 | tf_op jit(solution)/shard_map/tile/pallas_call | solution.py:265
  42.6 0.0 collective-permute-done.6.refs_0_
  42.6 0.1 tile.7
  42.7 0.2 collective-permute-start.8
  43.0 1.3 %collective-permute-start.7 = (f32[40,512]{1,0:T(8,128)S(1)}, f32[40,512]{1,0:T(8,128)S(1)}, u32[]{:S(2)}, u32[]{:S(2)}) collective-permute-start(f32[40,512]{1,0:T(8,128)S(1)} %get-tuple-element.34), channel_id=1, source_target_pairs={{8,0},{10,2},{4,12},{6,14},{9,1},{11,3},{5,13},{7,15},{24,16},{26,... | collective-permute-start | bytes 245768 | tf_op jit(solution)/shard_map/ppermute | solution.py:438
  44.3 8.3 %collective-permute-start.9 = (f32[40,512]{1,0:T(8,128)S(1)}, f32[40,512]{1,0:T(8,128)S(1)}, u32[]{:S(2)}, u32[]{:S(2)}) collective-permute-start(f32[40,512]{1,0:T(8,128)S(1)} %get-tuple-element.38), channel_id=1, source_target_pairs={{0,4},{2,6},{4,8},{6,10},{8,12},{10,14},{12,0},{14,2},{1,5},{3,7},... | collective-permute-start | bytes 245768 | tf_op jit(solution)/shard_map/ppermute | solution.py:444
  52.6 0.5 collective-permute-start.10
  53.1 4.3 %collective-permute-done.7.refs_2_ = f32[40,512]{1,0:T(8,128)S(1)} collective-permute-done((f32[40,512]{1,0:T(8,128)S(1)}, f32[40,512]{1,0:T(8,128)S(1)}, u32[]{:S(2)}, u32[]{:S(2)}) %collective-permute-start.7) | collective-permute-done | bytes 81952 | tf_op jit(solution)/shard_map/ppermute | solution.py:438
  57.5 0.9 %gram.1 = f32[16,8,128]{2,1,0:T(8,128)} custom-call(f32[32,512]{1,0:T(8,128)S(1)} %image.1.image_ref.mine_ref), custom_call_target="tpu_custom_call" | custom-call | tf_op jit(solution)/shard_map/gram/pallas_call | solution.py:321
  58.4 3.6 %all-to-all-start = ((f32[16,8,128]{2,1,0:T(8,128)}), f32[16,8,128]{2,1,0:T(8,128)S(1)}, u32[]{:S(2)}, u32[]{:S(2)}) async-start(f32[16,8,128]{2,1,0:T(8,128)} %gram.1), calls=%async_computation | async-start | bytes 131072 | tf_op jit(solution)/shard_map/all_to_all | solution.py:448
  61.9 0.4 collective-permute-start.11
  62.4 0.9 %collective-permute-done.11.other_ref = f32[32,512]{1,0:T(8,128)S(1)} collective-permute-done((f32[32,512]{1,0:T(8,128)S(1)}, f32[32,512]{1,0:T(8,128)S(1)}, u32[]{:S(2)}, u32[]{:S(2)}) %collective-permute-start.11) | collective-permute-done | bytes 65568 | tf_op jit(solution)/shard_map/ppermute | solution.py:447
  63.3 5.6 %all-to-all-done.grams_ref = f32[16,8,128]{2,1,0:T(8,128)S(1)} async-done(((f32[16,8,128]{2,1,0:T(8,128)}), f32[16,8,128]{2,1,0:T(8,128)S(1)}, u32[]{:S(2)}, u32[]{:S(2)}) %all-to-all-start) | async-done | bytes 65568 | tf_op jit(solution)/shard_map/all_to_all | solution.py:448
  68.8 2.9 %basis.1 = f32[16,1024]{1,0:T(8,128)} custom-call(f32[16,8,128]{2,1,0:T(8,128)S(1)} %all-to-all-done.grams_ref, f32[32,512]{1,0:T(8,128)S(1)} %image.1.image_ref.mine_ref, f32[32,512]{1,0:T(8,128)S(1)} %collective-permute-done.11.other_ref), custom_call_target="tpu_custom_call" | custom-call | tf_op jit(solution)/shard_map/basis/pallas_call | solution.py:371
  (13 shorter events, 0.2 us)
Async XLA Ops:
  0.0 2.4 %copy-start = (bf16[16,1024]{1,0:T(8,128)(2,1)S(1)}, bf16[16,1024]{1,0:T(8,128)(2,1)}, u32[]{:S(2)}) copy-start(bf16[16,1024]{1,0:T(8,128)(2,1)} %vec_ref.1) | copy-start | bytes 98308
  0.0 2.4 %collective-permute-start = (bf16[1024,256]{1,0:T(8,128)(2,1)}, bf16[1024,256]{1,0:T(8,128)(2,1)S(1)}, u32[]{:S(2)}, u32[]{:S(2)}) collective-permute-start(bf16[1024,256]{1,0:T(8,128)(2,1)} %param.5), channel_id=1, source_target_pairs={{0,1},{1,0},{2,3},{3,2},{4,5},{5,4},{6,7},{7,6},{8,9},{9,8},{10,11... | collective-permute-start | bytes 1572872 | tf_op jit(solution)/shard_map/ppermute | solution.py:410
  0.5 1.9 %collective-permute-start.1 = (bf16[16,1024]{1,0:T(8,128)(2,1)}, bf16[16,1024]{1,0:T(8,128)(2,1)S(1)}, u32[]{:S(2)}, u32[]{:S(2)}) collective-permute-start(bf16[16,1024]{1,0:T(8,128)(2,1)} %vec_ref.1), channel_id=1, source_target_pairs={{0,1},{1,0},{2,3},{3,2},{4,5},{5,4},{6,7},{7,6},{8,9},{9,8},{10,11... | collective-permute-start | bytes 98312 | tf_op jit(solution)/shard_map/ppermute | solution.py:411
  3.1 16.2 %collective-permute-start.2 = (bf16[560,512]{1,0:T(8,128)(2,1)S(1)}, bf16[560,512]{1,0:T(8,128)(2,1)S(1)}, u32[]{:S(2)}, u32[]{:S(2)}) collective-permute-start(bf16[560,512]{1,0:T(8,128)(2,1)S(1)} %get-tuple-element.22.refs_0_.refs_1_), channel_id=1, source_target_pairs={{0,2},{2,0},{4,6},{6,4},{8,10},{10,8},{12,14},{14,12},{1,3},{3,1},... | collective-permute-start | bytes 1720328 | tf_op jit(solution)/shard_map/ppermute | solution.py:417
  6.1 17.0 %collective-permute-start.3 = (bf16[560,512]{1,0:T(8,128)(2,1)S(1)}, bf16[560,512]{1,0:T(8,128)(2,1)S(1)}, u32[]{:S(2)}, u32[]{:S(2)}) collective-permute-start(bf16[560,512]{1,0:T(8,128)(2,1)S(1)} %get-tuple-element.22.refs_0_.refs_1_), channel_id=1, source_target_pairs={{4,0},{6,2},{8,4},{10,6},{12,8},{14,10},{0,12},{2,14},{5,1},{7,3},... | collective-permute-start | bytes 1720328 | tf_op jit(solution)/shard_map/ppermute | solution.py:416
  9.7 32.9 %collective-permute-start.6 = (bf16[560,512]{1,0:T(8,128)(2,1)S(1)}, bf16[560,512]{1,0:T(8,128)(2,1)S(1)}, u32[]{:S(2)}, u32[]{:S(2)}) collective-permute-start(bf16[560,512]{1,0:T(8,128)(2,1)S(1)} %get-tuple-element.22.refs_0_.refs_1_), channel_id=1, source_target_pairs={{0,8},{2,10},{12,4},{14,6},{1,9},{3,11},{13,5},{15,7},{16,24},{18,... | collective-permute-start | bytes 1720328 | tf_op jit(solution)/shard_map/ppermute | solution.py:416
  23.1 2.0 %collective-permute-start.5 = (bf16[288,512]{1,0:T(8,128)(2,1)S(1)}, bf16[288,512]{1,0:T(8,128)(2,1)S(1)}, u32[]{:S(2)}, u32[]{:S(2)}) collective-permute-start(bf16[288,512]{1,0:T(8,128)(2,1)S(1)} %slice.25), channel_id=1, source_target_pairs={{0,1},{1,0},{2,3},{3,2},{4,5},{5,4},{6,7},{7,6},{8,9},{9,8},{10,11... | collective-permute-start | bytes 884744 | tf_op jit(solution)/shard_map/ppermute | solution.py:423
  23.2 1.9 %collective-permute-start.4 = (bf16[272,512]{1,0:T(8,128)(2,1)S(1)}, bf16[272,512]{1,0:T(8,128)(2,1)S(1)}, u32[]{:S(2)}, u32[]{:S(2)}) collective-permute-start(bf16[272,512]{1,0:T(8,128)(2,1)S(1)} %slice.24), channel_id=1, source_target_pairs={{0,1},{1,0},{2,3},{3,2},{4,5},{5,4},{6,7},{7,6},{8,9},{9,8},{10,11... | collective-permute-start | bytes 835592 | tf_op jit(solution)/shard_map/ppermute | solution.py:423
  42.7 1.5 %collective-permute-start.8 = (f32[40,1024]{1,0:T(8,128)S(1)}, f32[40,1024]{1,0:T(8,128)S(1)}, u32[]{:S(2)}, u32[]{:S(2)}) collective-permute-start(f32[40,1024]{1,0:T(8,128)S(1)} %pad_maximum_fusion.1), channel_id=1, source_target_pairs={{0,1},{1,0},{2,3},{3,2},{4,5},{5,4},{6,7},{7,6},{8,9},{9,8},{10,11... | collective-permute-start | bytes 491528 | tf_op jit(solution)/shard_map/ppermute | solution.py:436
  43.0 14.5 %collective-permute-start.7 = (f32[40,512]{1,0:T(8,128)S(1)}, f32[40,512]{1,0:T(8,128)S(1)}, u32[]{:S(2)}, u32[]{:S(2)}) collective-permute-start(f32[40,512]{1,0:T(8,128)S(1)} %get-tuple-element.34), channel_id=1, source_target_pairs={{8,0},{10,2},{4,12},{6,14},{9,1},{11,3},{5,13},{7,15},{24,16},{26,... | collective-permute-start | bytes 245768 | tf_op jit(solution)/shard_map/ppermute | solution.py:438
  44.3 13.1 %collective-permute-start.9 = (f32[40,512]{1,0:T(8,128)S(1)}, f32[40,512]{1,0:T(8,128)S(1)}, u32[]{:S(2)}, u32[]{:S(2)}) collective-permute-start(f32[40,512]{1,0:T(8,128)S(1)} %get-tuple-element.38), channel_id=1, source_target_pairs={{0,4},{2,6},{4,8},{6,10},{8,12},{10,14},{12,0},{14,2},{1,5},{3,7},... | collective-permute-start | bytes 245768 | tf_op jit(solution)/shard_map/ppermute | solution.py:444
  52.6 4.9 %collective-permute-start.10 = (f32[40,512]{1,0:T(8,128)S(1)}, f32[40,512]{1,0:T(8,128)S(1)}, u32[]{:S(2)}, u32[]{:S(2)}) collective-permute-start(f32[40,512]{1,0:T(8,128)S(1)} %get-tuple-element.41), channel_id=1, source_target_pairs={{0,2},{2,0},{4,6},{6,4},{8,10},{10,8},{12,14},{14,12},{1,3},{3,1},... | collective-permute-start | bytes 245768 | tf_op jit(solution)/shard_map/ppermute | solution.py:445
  58.4 10.5 %all-to-all-start = ((f32[16,8,128]{2,1,0:T(8,128)}), f32[16,8,128]{2,1,0:T(8,128)S(1)}, u32[]{:S(2)}, u32[]{:S(2)}) async-start(f32[16,8,128]{2,1,0:T(8,128)} %gram.1), calls=%async_computation | async-start | bytes 131072 | tf_op jit(solution)/shard_map/all_to_all | solution.py:448
  61.9 1.3 %collective-permute-start.11 = (f32[32,512]{1,0:T(8,128)S(1)}, f32[32,512]{1,0:T(8,128)S(1)}, u32[]{:S(2)}, u32[]{:S(2)}) collective-permute-start(f32[32,512]{1,0:T(8,128)S(1)} %image.1.image_ref.mine_ref), channel_id=1, source_target_pairs={{0,1},{1,0},{2,3},{3,2},{4,5},{5,4},{6,7},{7,6},{8,9},{9,8},{10,11... | collective-permute-start | bytes 196616 | tf_op jit(solution)/shard_map/ppermute | solution.py:447

commit v12 on v11

--- a/solution.py
+++ b/solution.py
@@ -26,7 +26,8 @@
 CHUNK = 256
 OUT_ROWS = 40
 COST = 1
-GROUP = 32
+WIDE = 512
+GROUP = 16
 SWAPS = 2
 VMEM_LIMIT = 48 * 1024 * 1024
 
@@ -144,19 +145,19 @@
 
 def tile_kernel(blocks, turns, own_block, receivers, vecs, lines, *refs):
     row_ref, col_refs = refs[0], refs[1 : 1 + blocks]
-    row_out_ref, col_out_ref, field_ref, spread_ref, sum_ref = refs[1 + blocks : 6 + blocks]
-    products, weights = [refs[at : at + 2] for at in (6 + blocks, 8 + blocks)]
-    col_spread_ref, row_vec_ref, col_vec_ref = refs[10 + blocks :]
+    row_out_ref, col_out_ref, field_ref, spread_ref = refs[1 + blocks : 5 + blocks]
+    products, weights = [refs[at : at + 2] for at in (5 + blocks, 7 + blocks)]
+    col_spread_ref, row_vec_ref, col_vec_ref = refs[9 + blocks :]
     size, rows = row_ref.shape
     features = size - vecs - CODE_ROWS
     vec_rows, code_rows = slice(features, features + vecs), slice(features + vecs, size)
-    sum_ref[...] = jnp.zeros_like(sum_ref)
+    row_out_ref[...] = jnp.zeros_like(row_out_ref)
 
     def block(col_ref, done):
-        chunks = col_ref.shape[1] // CHUNK
+        chunks = col_ref.shape[1] // WIDE
 
         def place(step, base=0):
-            return pl.ds(pl.multiple_of(base + step * CHUNK, CHUNK), CHUNK)
+            return pl.ds(pl.multiple_of(base + step * WIDE, WIDE), WIDE)
 
         def multiply(step, part, product_ref):
             product_ref[part, :] = jnp.dot(
@@ -168,24 +169,24 @@
                 row_part = pl.ds(pl.multiple_of(first + start, GROUP), GROUP)
 
                 def row(field):
-                    return jnp.concatenate([spread_ref[field, row_part, :]] * (CHUNK // LANES), axis=1)
+                    return jnp.concatenate([spread_ref[field, row_part, :]] * (WIDE // LANES), axis=1)
 
                 def col(field):
                     return jnp.concatenate([col_spread_ref[field]] * (GROUP // 8), axis=0)
 
                 same = None
                 if own_block:
-                    row_ids = lax.broadcasted_iota(jnp.int32, (GROUP, CHUNK), 0) + (first + start - step * CHUNK)
-                    same = row_ids == lax.broadcasted_iota(jnp.int32, (GROUP, CHUNK), 1)
+                    row_ids = lax.broadcasted_iota(jnp.int32, (GROUP, WIDE), 0) + (first + start - step * WIDE)
+                    same = row_ids == lax.broadcasted_iota(jnp.int32, (GROUP, WIDE), 1)
                 weight_ref[row_part, :] = weights_of(product_ref[row_part, :], row, col, same).astype(jnp.bfloat16)
 
         def prepare_total(step):
             col_vec_ref[...] = with_ones(col_ref[vec_rows, place(step)])
             if not turns:
-                col_out_ref[:, place(step, done)] = jnp.zeros((OUT_ROWS, CHUNK), jnp.float32)
+                col_out_ref[:, place(step, done)] = jnp.zeros((OUT_ROWS, WIDE), jnp.float32)
 
         def total(step, part, weight_ref):
-            sum_ref[part, 0 : vecs + CODE_ROWS] += dot_nt(weight_ref[part, :], col_vec_ref[...])
+            row_out_ref[:, part] += dot_nt(col_vec_ref[...], weight_ref[part, :])[0:OUT_ROWS]
             if not turns:
                 col_out_ref[:, place(step, done)] += jnp.dot(
                     row_vec_ref[:, part], weight_ref[part, :], preferred_element_type=jnp.float32
@@ -196,7 +197,7 @@
                 step = 2 * index + parity
                 ahead, behind = lax.rem(step + 1, chunks), lax.rem(step + chunks - 1, chunks)
                 for field, values in enumerate(decode(col_ref[code_rows, place(step)])):
-                    col_spread_ref[field] = jnp.broadcast_to(values, (8, CHUNK))
+                    col_spread_ref[field] = jnp.broadcast_to(values, (8, WIDE))
                 prepare_total(behind)
 
                 def some_lines(number, inner, parity=parity, step=step, ahead=ahead, behind=behind):
@@ -235,12 +236,8 @@
                 block(col_ref, done)
                 done += col_ref.shape[1]
 
-    def finish():
-        row_out_ref[...] = sum_ref[...].T[0:OUT_ROWS]
-
     if receivers is None:
         compute()
-        finish()
         return
     pair = lax.axis_index("blk") // 2
     takes_part = functools.reduce(jnp.logical_or, [pair == one for one in receivers])
@@ -248,11 +245,9 @@
     @pl.when(takes_part)
     def _():
         compute()
-        finish()
 
     @pl.when(jnp.logical_not(takes_part))
     def _():
-        row_out_ref[...] = jnp.zeros_like(row_out_ref)
         col_out_ref[...] = jnp.zeros_like(col_out_ref)
 
 
@@ -270,14 +265,13 @@
         scratch_shapes=[
             pltpu.VMEM((LANES, rows), jnp.float32),
             pltpu.VMEM((FIELDS, rows, LANES), jnp.float32),
-            pltpu.VMEM((rows, LANES), jnp.float32),
-            pltpu.VMEM((rows, CHUNK), jnp.float32),
-            pltpu.VMEM((rows, CHUNK), jnp.float32),
-            pltpu.VMEM((rows, CHUNK), jnp.bfloat16),
-            pltpu.VMEM((rows, CHUNK), jnp.bfloat16),
-            pltpu.VMEM((FIELDS, 8, CHUNK), jnp.float32),
+            pltpu.VMEM((rows, WIDE), jnp.float32),
+            pltpu.VMEM((rows, WIDE), jnp.float32),
+            pltpu.VMEM((rows, WIDE), jnp.bfloat16),
+            pltpu.VMEM((rows, WIDE), jnp.bfloat16),
+            pltpu.VMEM((FIELDS, 8, WIDE), jnp.float32),
             pltpu.VMEM((vecs + CODE_ROWS, rows), jnp.bfloat16),
-            pltpu.VMEM((vecs + CODE_ROWS, CHUNK), jnp.bfloat16),
+            pltpu.VMEM((vecs + CODE_ROWS, WIDE), jnp.bfloat16),
         ],
         cost_estimate=pl.CostEstimate(flops=COST, bytes_accessed=COST, transcendentals=0),
         compiler_params=params(),
@@ -416,7 +410,7 @@
     sent = [lax.ppermute(mine, "blk", moves) for moves, _ in plans]
     beside_mine = lax.ppermute(mine, "blk", beside)
     weigh = functools.partial(tile, vecs=vecs)
-    own_sums, own = weigh(mine, [mine, rest], lines=128, turns=True, own_block=True)
+    own_sums, own = weigh(mine, [mine, rest], lines=256, turns=True, own_block=True)
     own_sums, own, beside_mine, sent[:1] = lax.optimization_barrier((own_sums, own, beside_mine, sent[:1]))
     cut = beside_mine.shape[0] // SWAPS // 16 * 16
     shares = [beside_mine[at * cut : (at + 1) * cut if at < SWAPS - 1 else None] for at in range(SWAPS)]
@@ -428,7 +422,7 @@
     for number, ((moves, takers), pack) in enumerate(zip(plans, sent)):
         if col_sums is not None:
             pack, col_sums = lax.optimization_barrier((pack, col_sums))
-        row_sums, sums = weigh(pack, [own, next_to], lines=128 if number == 0 else 256, receivers=takers)
+        row_sums, sums = weigh(pack, [own, next_to], lines=256 if number == 0 else 512, receivers=takers)
         returns.append((row_sums, back(moves)))
         col_sums = sums if col_sums is None else col_sums + sums
     if col_sums is not None:

time: 72.1 us -> 64.9 us (0.900)
  Pallas kernels: 27.6 us -> 22.6 us
  starting transfers between devices: 23.4 us -> 20.7 us
    pallas_call x4, Pallas kernels: 23.1 us -> 18.1 us  [tile(): pl.pallas_call(functools.partial(tile_kernel, len(columns), turns, own_bl...]
    ppermute x1, starting transfers between devices: 8.3 us -> 5.5 us  [local(): parts.append(lax.ppermute(row_sums, 'blk', moves))]
    ppermute x1, waiting for transfers between devices: 2.56 us -> 3.45 us  [local(): beside_mine = lax.ppermute(mine, 'blk', beside)]
  transfers between devices with their start and end apart: 13 -> 13, of which waited for: 6 -> 7; matrix products, arithmetic and copies ran while one was open for 3% -> 3% of each run, Pallas kernels for 32% -> 28%
where the time goes in v12:
time: 64.9 us; the launch traced here: 64.5 us
  Pallas kernels  22.6 us (35%)
  starting transfers between devices  20.7 us (32%)
  waiting for transfers between devices  19 us (29%)
  local copies, waits for them, and re-layouts  1.12 us (2%)
  other arithmetic  0.88 us (1%)
    pallas_call x4, Pallas kernels, tile(): pl.pallas_call(functools.partial(tile_kernel, len(columns), turns, own_bl...  18.1 us
    all_to_all x1, waiting for transfers between devices, local(): lax.all_to_all(grams_of(image, 2 * blocks), ('blk', 'sub'), 0, 0, tiled=T...  5.58 us
    ppermute x1, starting transfers between devices, local(): parts.append(lax.ppermute(row_sums, 'blk', moves))  5.5 us
    ppermute x2, starting transfers between devices, local(): sent = [lax.ppermute(mine, 'blk', moves) for moves, _ in plans]  4.97 us
    ppermute x2, waiting for transfers between devices, local(): sent = [lax.ppermute(mine, 'blk', moves) for moves, _ in plans]  3.79 us
    ppermute x1, waiting for transfers between devices, local(): parts.append(lax.ppermute(last_sums, 'blk', last_moves))  3.71 us
    all_to_all x1, starting transfers between devices, local(): lax.all_to_all(grams_of(image, 2 * blocks), ('blk', 'sub'), 0, 0, tiled=T...  3.61 us
    ppermute x1, waiting for transfers between devices, local(): beside_mine = lax.ppermute(mine, 'blk', beside)  3.45 us
  transfers between devices with their start and end apart: 13, of which 7 were waited for; matrix products, arithmetic and copies ran while one was open for 3% of the time, Pallas kernels for 28%

profile of v12, /device:TPU:0, one launch (start us, length us, event | category | flops | bytes accessed | tf_op | source)
XLA Modules:
  0.0 64.5 jit_solution(4637135335627009301)
XLA Ops:
  0.0 0.5 collective-permute-start
  0.5 0.1 collective-permute-start.1
  0.5 1.1 %constant_dynamic-slice_fusion = (bf16[512,256]{1,0:T(8,128)(2,1)S(1)}, bf16[512,256]{1,0:T(8,128)(2,1)S(1)}) fusion(bf16[1024,256]{1,0:T(8,128)(2,1)} %param.5, s32[]{:T(128)S(6)} %select_n.7, s32[]{:T(128)S(6)} %select_n.6), kind=kLoop, calls=%fused_computation.4 | loop fusion | bytes 1048584 | tf_op jit(solution)/shard_map/dynamic_slice | solution.py:408
  1.6 0.8 %pad_add_fusion.meta_ref = s32[7,1024]{1,0:T(8,128)S(1)} fusion(s32[1,1024]{1,0:T(1,128)} %bitcast.1, s32[2,1024]{1,0:T(2,128)} %param.8, s32[4,1024]{1,0:T(4,128)} %param.7), kind=kLoop, calls=%fused_computation.3 | loop fusion | flops 14336 | bytes 57344 | tf_op jit(solution)/shard_map/concatenate | solution.py:406
  2.4 0.0 collective-permute-done.emb_other_ref
  2.4 0.7 %pack.1 = (bf16[560,512]{1,0:T(8,128)(2,1)S(1)}, bf16[560,512]{1,0:T(8,128)(2,1)S(1)}) custom-call(bf16[512,256]{1,0:T(8,128)(2,1)S(1)} %get-tuple-element.40.emb_mine_ref, bf16[512,256]{1,0:T(8,128)(2,1)S(1)} %get-tuple-element.39.emb_rest_ref, bf16[1024,256]{1,0:T(8,128)(2,1)S(1)} %collective-permute-done.emb_other_ref, bf16[16,1024]{1,0:T(8,128)(2,1)S(1)} %copy-done, ...), custom_call_target="tpu_custom_call" | custom-call | tf_op jit(solution)/shard_map/pack/pallas_call | solution.py:103
  3.1 3.0 %collective-permute-start.2 = (bf16[560,512]{1,0:T(8,128)(2,1)S(1)}, bf16[560,512]{1,0:T(8,128)(2,1)S(1)}, u32[]{:S(2)}, u32[]{:S(2)}) collective-permute-start(bf16[560,512]{1,0:T(8,128)(2,1)S(1)} %get-tuple-element.22.refs_0_.refs_1_), channel_id=1, source_target_pairs={{0,2},{2,0},{4,6},{6,4},{8,10},{10,8},{12,14},{14,12},{1,3},{3,1},... | collective-permute-start | bytes 1720328 | tf_op jit(solution)/shard_map/ppermute | solution.py:411
  6.1 3.6 %collective-permute-start.3 = (bf16[560,512]{1,0:T(8,128)(2,1)S(1)}, bf16[560,512]{1,0:T(8,128)(2,1)S(1)}, u32[]{:S(2)}, u32[]{:S(2)}) collective-permute-start(bf16[560,512]{1,0:T(8,128)(2,1)S(1)} %get-tuple-element.22.refs_0_.refs_1_), channel_id=1, source_target_pairs={{4,0},{6,2},{8,4},{10,6},{12,8},{14,10},{0,12},{2,14},{5,1},{7,3},... | collective-permute-start | bytes 1720328 | tf_op jit(solution)/shard_map/ppermute | solution.py:410
  9.7 1.4 %collective-permute-start.6 = (bf16[560,512]{1,0:T(8,128)(2,1)S(1)}, bf16[560,512]{1,0:T(8,128)(2,1)S(1)}, u32[]{:S(2)}, u32[]{:S(2)}) collective-permute-start(bf16[560,512]{1,0:T(8,128)(2,1)S(1)} %get-tuple-element.22.refs_0_.refs_1_), channel_id=1, source_target_pairs={{0,8},{2,10},{12,4},{14,6},{1,9},{3,11},{13,5},{15,7},{16,24},{18,... | collective-permute-start | bytes 1720328 | tf_op jit(solution)/shard_map/ppermute | solution.py:410
  11.1 4.8 %tile.4 = (f32[40,512]{1,0:T(8,128)S(1)}, bf16[560,1024]{1,0:T(8,128)(2,1)S(1)}) custom-call(bf16[560,512]{1,0:T(8,128)(2,1)S(1)} %get-tuple-element.22.refs_0_.refs_1_, bf16[560,512]{1,0:T(8,128)(2,1)S(1)} %get-tuple-element.22.refs_0_.refs_1_, bf16[560,512]{1,0:T(8,128)(2,1)S(1)} %get-tuple-element.23.refs_2_), custom_call_target="tpu_custom_call" | custom-call | flops 1 | bytes 1 | tf_op jit(solution)/shard_map/tile/pallas_call | solution.py:260
  15.9 3.4 %collective-permute-done.2.refs_1_ = bf16[560,512]{1,0:T(8,128)(2,1)S(1)} collective-permute-done((bf16[560,512]{1,0:T(8,128)(2,1)S(1)}, bf16[560,512]{1,0:T(8,128)(2,1)S(1)}, u32[]{:S(2)}, u32[]{:S(2)}) %collective-permute-start.2) | collective-permute-done | bytes 573472 | tf_op jit(solution)/shard_map/ppermute | solution.py:411
  19.3 3.8 %collective-permute-done.3.refs_0_ = bf16[560,512]{1,0:T(8,128)(2,1)S(1)} collective-permute-done((bf16[560,512]{1,0:T(8,128)(2,1)S(1)}, bf16[560,512]{1,0:T(8,128)(2,1)S(1)}, u32[]{:S(2)}, u32[]{:S(2)}) %collective-permute-start.3) | collective-permute-done | bytes 573472 | tf_op jit(solution)/shard_map/ppermute | solution.py:410
  23.1 0.1 collective-permute-start.5
  23.2 0.6 collective-permute-start.4
  23.8 1.4 %collective-permute-done.4 = bf16[272,512]{1,0:T(8,128)(2,1)S(1)} collective-permute-done((bf16[272,512]{1,0:T(8,128)(2,1)S(1)}, bf16[272,512]{1,0:T(8,128)(2,1)S(1)}, u32[]{:S(2)}, u32[]{:S(2)}) %collective-permute-start.4) | collective-permute-done | bytes 278560 | tf_op jit(solution)/shard_map/ppermute | solution.py:417
  25.2 0.0 collective-permute-done.5
  25.2 4.5 %tile.5 = (f32[40,512]{1,0:T(8,128)S(1)}, bf16[560,1024]{1,0:T(8,128)(2,1)S(1)}) custom-call(bf16[560,512]{1,0:T(8,128)(2,1)S(1)} %get-tuple-element.22.refs_0_.refs_1_, bf16[560,512]{1,0:T(8,128)(2,1)S(1)} %collective-permute-done.2.refs_1_, bf16[560,512]{1,0:T(8,128)(2,1)S(1)} %pad_maximum_fusion.refs_2_), custom_call_target="tpu_custom_call" | custom-call | flops 1 | bytes 1 | tf_op jit(solution)/shard_map/tile/pallas_call | solution.py:260
  29.7 8.6 %tile.6 = (f32[40,512]{1,0:T(8,128)S(1)}, f32[40,2048]{1,0:T(8,128)S(1)}) custom-call(bf16[560,512]{1,0:T(8,128)(2,1)S(1)} %collective-permute-done.3.refs_0_, bf16[560,1024]{1,0:T(8,128)(2,1)S(1)} %get-tuple-element.30.refs_1_, bf16[560,1024]{1,0:T(8,128)(2,1)S(1)} %get-tuple-element.31.refs_2_), custom_call_target="tpu_custom_call" | custom-call | flops 1 | bytes 1 | tf_op jit(solution)/shard_map/tile/pallas_call | solution.py:260
  38.4 0.0 collective-permute-done.6.refs_0_
  38.4 0.2 tile.7
  38.7 0.2 collective-permute-start.8
  38.9 1.3 %collective-permute-start.7 = (f32[40,512]{1,0:T(8,128)S(1)}, f32[40,512]{1,0:T(8,128)S(1)}, u32[]{:S(2)}, u32[]{:S(2)}) collective-permute-start(f32[40,512]{1,0:T(8,128)S(1)} %get-tuple-element.34), channel_id=1, source_target_pairs={{8,0},{10,2},{4,12},{6,14},{9,1},{11,3},{5,13},{7,15},{24,16},{26,... | collective-permute-start | bytes 245768 | tf_op jit(solution)/shard_map/ppermute | solution.py:432
  40.3 5.5 %collective-permute-start.9 = (f32[40,512]{1,0:T(8,128)S(1)}, f32[40,512]{1,0:T(8,128)S(1)}, u32[]{:S(2)}, u32[]{:S(2)}) collective-permute-start(f32[40,512]{1,0:T(8,128)S(1)} %get-tuple-element.38), channel_id=1, source_target_pairs={{0,4},{2,6},{4,8},{6,10},{8,12},{10,14},{12,0},{14,2},{1,5},{3,7},... | collective-permute-start | bytes 245768 | tf_op jit(solution)/shard_map/ppermute | solution.py:438
  45.8 0.5 collective-permute-start.10
  46.3 3.7 %collective-permute-done.7.refs_2_ = f32[40,512]{1,0:T(8,128)S(1)} collective-permute-done((f32[40,512]{1,0:T(8,128)S(1)}, f32[40,512]{1,0:T(8,128)S(1)}, u32[]{:S(2)}, u32[]{:S(2)}) %collective-permute-start.7) | collective-permute-done | bytes 81952 | tf_op jit(solution)/shard_map/ppermute | solution.py:432
  50.0 0.2 collective-permute-done.10.refs_6_
  50.2 0.9 %gram.1 = f32[16,8,128]{2,1,0:T(8,128)} custom-call(f32[32,512]{1,0:T(8,128)S(1)} %image.1.image_ref.mine_ref), custom_call_target="tpu_custom_call" | custom-call | tf_op jit(solution)/shard_map/gram/pallas_call | solution.py:315
  51.1 3.6 %all-to-all-start = ((f32[16,8,128]{2,1,0:T(8,128)}), f32[16,8,128]{2,1,0:T(8,128)S(1)}, u32[]{:S(2)}, u32[]{:S(2)}) async-start(f32[16,8,128]{2,1,0:T(8,128)} %gram.1), calls=%async_computation | async-start | bytes 131072 | tf_op jit(solution)/shard_map/all_to_all | solution.py:442
  54.8 0.4 collective-permute-start.11
  55.2 0.9 %collective-permute-done.11.other_ref = f32[32,512]{1,0:T(8,128)S(1)} collective-permute-done((f32[32,512]{1,0:T(8,128)S(1)}, f32[32,512]{1,0:T(8,128)S(1)}, u32[]{:S(2)}, u32[]{:S(2)}) %collective-permute-start.11) | collective-permute-done | bytes 65568 | tf_op jit(solution)/shard_map/ppermute | solution.py:441
  56.1 5.6 %all-to-all-done.grams_ref = f32[16,8,128]{2,1,0:T(8,128)S(1)} async-done(((f32[16,8,128]{2,1,0:T(8,128)}), f32[16,8,128]{2,1,0:T(8,128)S(1)}, u32[]{:S(2)}, u32[]{:S(2)}) %all-to-all-start) | async-done | bytes 65568 | tf_op jit(solution)/shard_map/all_to_all | solution.py:442
  61.7 2.9 %basis.1 = f32[16,1024]{1,0:T(8,128)} custom-call(f32[16,8,128]{2,1,0:T(8,128)S(1)} %all-to-all-done.grams_ref, f32[32,512]{1,0:T(8,128)S(1)} %image.1.image_ref.mine_ref, f32[32,512]{1,0:T(8,128)S(1)} %collective-permute-done.11.other_ref), custom_call_target="tpu_custom_call" | custom-call | tf_op jit(solution)/shard_map/basis/pallas_call | solution.py:365
  (13 shorter events, 0.2 us)
Async XLA Ops:
  0.0 2.4 %copy-start = (bf16[16,1024]{1,0:T(8,128)(2,1)S(1)}, bf16[16,1024]{1,0:T(8,128)(2,1)}, u32[]{:S(2)}) copy-start(bf16[16,1024]{1,0:T(8,128)(2,1)} %vec_ref.1) | copy-start | bytes 98308
  0.0 2.4 %collective-permute-start = (bf16[1024,256]{1,0:T(8,128)(2,1)}, bf16[1024,256]{1,0:T(8,128)(2,1)S(1)}, u32[]{:S(2)}, u32[]{:S(2)}) collective-permute-start(bf16[1024,256]{1,0:T(8,128)(2,1)} %param.5), channel_id=1, source_target_pairs={{0,1},{1,0},{2,3},{3,2},{4,5},{5,4},{6,7},{7,6},{8,9},{9,8},{10,11... | collective-permute-start | bytes 1572872 | tf_op jit(solution)/shard_map/ppermute | solution.py:404
  0.5 1.9 %collective-permute-start.1 = (bf16[16,1024]{1,0:T(8,128)(2,1)}, bf16[16,1024]{1,0:T(8,128)(2,1)S(1)}, u32[]{:S(2)}, u32[]{:S(2)}) collective-permute-start(bf16[16,1024]{1,0:T(8,128)(2,1)} %vec_ref.1), channel_id=1, source_target_pairs={{0,1},{1,0},{2,3},{3,2},{4,5},{5,4},{6,7},{7,6},{8,9},{9,8},{10,11... | collective-permute-start | bytes 98312 | tf_op jit(solution)/shard_map/ppermute | solution.py:405
  3.1 16.2 %collective-permute-start.2 = (bf16[560,512]{1,0:T(8,128)(2,1)S(1)}, bf16[560,512]{1,0:T(8,128)(2,1)S(1)}, u32[]{:S(2)}, u32[]{:S(2)}) collective-permute-start(bf16[560,512]{1,0:T(8,128)(2,1)S(1)} %get-tuple-element.22.refs_0_.refs_1_), channel_id=1, source_target_pairs={{0,2},{2,0},{4,6},{6,4},{8,10},{10,8},{12,14},{14,12},{1,3},{3,1},... | collective-permute-start | bytes 1720328 | tf_op jit(solution)/shard_map/ppermute | solution.py:411
  6.1 17.0 %collective-permute-start.3 = (bf16[560,512]{1,0:T(8,128)(2,1)S(1)}, bf16[560,512]{1,0:T(8,128)(2,1)S(1)}, u32[]{:S(2)}, u32[]{:S(2)}) collective-permute-start(bf16[560,512]{1,0:T(8,128)(2,1)S(1)} %get-tuple-element.22.refs_0_.refs_1_), channel_id=1, source_target_pairs={{4,0},{6,2},{8,4},{10,6},{12,8},{14,10},{0,12},{2,14},{5,1},{7,3},... | collective-permute-start | bytes 1720328 | tf_op jit(solution)/shard_map/ppermute | solution.py:410
  9.7 28.6 %collective-permute-start.6 = (bf16[560,512]{1,0:T(8,128)(2,1)S(1)}, bf16[560,512]{1,0:T(8,128)(2,1)S(1)}, u32[]{:S(2)}, u32[]{:S(2)}) collective-permute-start(bf16[560,512]{1,0:T(8,128)(2,1)S(1)} %get-tuple-element.22.refs_0_.refs_1_), channel_id=1, source_target_pairs={{0,8},{2,10},{12,4},{14,6},{1,9},{3,11},{13,5},{15,7},{16,24},{18,... | collective-permute-start | bytes 1720328 | tf_op jit(solution)/shard_map/ppermute | solution.py:410
  23.1 2.0 %collective-permute-start.5 = (bf16[288,512]{1,0:T(8,128)(2,1)S(1)}, bf16[288,512]{1,0:T(8,128)(2,1)S(1)}, u32[]{:S(2)}, u32[]{:S(2)}) collective-permute-start(bf16[288,512]{1,0:T(8,128)(2,1)S(1)} %slice.25), channel_id=1, source_target_pairs={{0,1},{1,0},{2,3},{3,2},{4,5},{5,4},{6,7},{7,6},{8,9},{9,8},{10,11... | collective-permute-start | bytes 884744 | tf_op jit(solution)/shard_map/ppermute | solution.py:417
  23.2 1.9 %collective-permute-start.4 = (bf16[272,512]{1,0:T(8,128)(2,1)S(1)}, bf16[272,512]{1,0:T(8,128)(2,1)S(1)}, u32[]{:S(2)}, u32[]{:S(2)}) collective-permute-start(bf16[272,512]{1,0:T(8,128)(2,1)S(1)} %slice.24), channel_id=1, source_target_pairs={{0,1},{1,0},{2,3},{3,2},{4,5},{5,4},{6,7},{7,6},{8,9},{9,8},{10,11... | collective-permute-start | bytes 835592 | tf_op jit(solution)/shard_map/ppermute | solution.py:417
  38.7 1.5 %collective-permute-start.8 = (f32[40,1024]{1,0:T(8,128)S(1)}, f32[40,1024]{1,0:T(8,128)S(1)}, u32[]{:S(2)}, u32[]{:S(2)}) collective-permute-start(f32[40,1024]{1,0:T(8,128)S(1)} %pad_maximum_fusion.1), channel_id=1, source_target_pairs={{0,1},{1,0},{2,3},{3,2},{4,5},{5,4},{6,7},{7,6},{8,9},{9,8},{10,11... | collective-permute-start | bytes 491528 | tf_op jit(solution)/shard_map/ppermute | solution.py:430
  38.9 11.1 %collective-permute-start.7 = (f32[40,512]{1,0:T(8,128)S(1)}, f32[40,512]{1,0:T(8,128)S(1)}, u32[]{:S(2)}, u32[]{:S(2)}) collective-permute-start(f32[40,512]{1,0:T(8,128)S(1)} %get-tuple-element.34), channel_id=1, source_target_pairs={{8,0},{10,2},{4,12},{6,14},{9,1},{11,3},{5,13},{7,15},{24,16},{26,... | collective-permute-start | bytes 245768 | tf_op jit(solution)/shard_map/ppermute | solution.py:432
  40.3 9.7 %collective-permute-start.9 = (f32[40,512]{1,0:T(8,128)S(1)}, f32[40,512]{1,0:T(8,128)S(1)}, u32[]{:S(2)}, u32[]{:S(2)}) collective-permute-start(f32[40,512]{1,0:T(8,128)S(1)} %get-tuple-element.38), channel_id=1, source_target_pairs={{0,4},{2,6},{4,8},{6,10},{8,12},{10,14},{12,0},{14,2},{1,5},{3,7},... | collective-permute-start | bytes 245768 | tf_op jit(solution)/shard_map/ppermute | solution.py:438
  45.8 4.4 %collective-permute-start.10 = (f32[40,512]{1,0:T(8,128)S(1)}, f32[40,512]{1,0:T(8,128)S(1)}, u32[]{:S(2)}, u32[]{:S(2)}) collective-permute-start(f32[40,512]{1,0:T(8,128)S(1)} %get-tuple-element.41), channel_id=1, source_target_pairs={{0,2},{2,0},{4,6},{6,4},{8,10},{10,8},{12,14},{14,12},{1,3},{3,1},... | collective-permute-start | bytes 245768 | tf_op jit(solution)/shard_map/ppermute | solution.py:439
  51.1 10.5 %all-to-all-start = ((f32[16,8,128]{2,1,0:T(8,128)}), f32[16,8,128]{2,1,0:T(8,128)S(1)}, u32[]{:S(2)}, u32[]{:S(2)}) async-start(f32[16,8,128]{2,1,0:T(8,128)} %gram.1), calls=%async_computation | async-start | bytes 131072 | tf_op jit(solution)/shard_map/all_to_all | solution.py:442
  54.8 1.3 %collective-permute-start.11 = (f32[32,512]{1,0:T(8,128)S(1)}, f32[32,512]{1,0:T(8,128)S(1)}, u32[]{:S(2)}, u32[]{:S(2)}) collective-permute-start(f32[32,512]{1,0:T(8,128)S(1)} %image.1.image_ref.mine_ref), channel_id=1, source_target_pairs={{0,1},{1,0},{2,3},{3,2},{4,5},{5,4},{6,7},{7,6},{8,9},{9,8},{10,11... | collective-permute-start | bytes 196616 | tf_op jit(solution)/shard_map/ppermute | solution.py:441

commit v13 on v10

--- a/solution.py
+++ b/solution.py
@@ -26,7 +26,8 @@
 CHUNK = 256
 OUT_ROWS = 40
 COST = 1
-GROUP = 32
+WIDE = 512
+GROUP = 16
 SWAPS = 2
 VMEM_LIMIT = 48 * 1024 * 1024
 
@@ -144,54 +145,56 @@
 
 def tile_kernel(blocks, turns, own_block, receivers, vecs, *refs):
     row_ref, col_refs = refs[0], refs[1 : 1 + blocks]
-    row_out_ref, col_out_ref, field_ref, spread_ref, sum_ref = refs[1 + blocks : 6 + blocks]
-    products, weights, col_spreads = [refs[at : at + 2] for at in range(6 + blocks, 12 + blocks, 2)]
+    row_out_ref, col_out_ref, field_ref, spread_ref = refs[1 + blocks : 5 + blocks]
+    products, weights = [refs[at : at + 2] for at in (5 + blocks, 7 + blocks)]
+    col_spread_ref, row_vec_ref = refs[9 + blocks :]
     size, rows = row_ref.shape
     features = size - vecs - CODE_ROWS
     vec_rows, code_rows = slice(features, features + vecs), slice(features + vecs, size)
-    sum_ref[...] = jnp.zeros_like(sum_ref)
-
-    def block(col_ref, done, row_vecs):
-        chunks = col_ref.shape[1] // CHUNK
+    row_out_ref[...] = jnp.zeros_like(row_out_ref)
+
+    def block(col_ref, done):
+        chunks = col_ref.shape[1] // WIDE
 
         def place(step, base=0):
-            return pl.ds(pl.multiple_of(base + step * CHUNK, CHUNK), CHUNK)
+            return pl.ds(pl.multiple_of(base + step * WIDE, WIDE), WIDE)
 
         def multiply(step, product_ref):
             product_ref[...] = jnp.dot(
                 row_ref[0:rows, :], col_ref[0:features, place(step)], preferred_element_type=jnp.float32
             )
 
-        def weigh(step, product_ref, weight_ref, col_spread_ref):
+        def weigh(step, product_ref, weight_ref):
             for field, values in enumerate(decode(col_ref[code_rows, place(step)])):
-                col_spread_ref[field] = jnp.broadcast_to(values, (8, CHUNK))
-            for first_row in range(0, rows, GROUP):
-                row_part = slice(first_row, first_row + GROUP)
+                col_spread_ref[field] = jnp.broadcast_to(values, (8, WIDE))
+            for start in range(0, rows, GROUP):
+                row_part = slice(start, start + GROUP)
 
                 def row(field):
-                    return jnp.concatenate([spread_ref[field, row_part, :]] * (CHUNK // LANES), axis=1)
+                    return jnp.concatenate([spread_ref[field, row_part, :]] * (WIDE // LANES), axis=1)
 
                 def col(field):
                     return jnp.concatenate([col_spread_ref[field]] * (GROUP // 8), axis=0)
 
                 same = None
                 if own_block:
-                    row_ids = lax.broadcasted_iota(jnp.int32, (GROUP, CHUNK), 0) + (first_row - step * CHUNK)
-                    same = row_ids == lax.broadcasted_iota(jnp.int32, (GROUP, CHUNK), 1)
+                    row_ids = lax.broadcasted_iota(jnp.int32, (GROUP, WIDE), 0) + (start - step * WIDE)
+                    same = row_ids == lax.broadcasted_iota(jnp.int32, (GROUP, WIDE), 1)
                 weight_ref[row_part, :] = weights_of(product_ref[row_part, :], row, col, same).astype(jnp.bfloat16)
 
         def total(step, weight_ref):
-            sum_ref[:, 0 : vecs + CODE_ROWS] += dot_nt(weight_ref[...], with_ones(col_ref[vec_rows, place(step)]))
+            col_vecs = with_ones(col_ref[vec_rows, place(step)])
+            row_out_ref[...] += dot_nt(col_vecs, weight_ref[...])[0:OUT_ROWS]
             if not turns:
                 col_out_ref[:, place(step, done)] = jnp.dot(
-                    row_vecs, weight_ref[...], preferred_element_type=jnp.float32
+                    row_vec_ref[...], weight_ref[...], preferred_element_type=jnp.float32
                 )[0:OUT_ROWS]
 
         def steps(index, carry):
             for parity in range(2):
                 step = 2 * index + parity
                 multiply(lax.rem(step + 1, chunks), products[1 - parity])
-                weigh(step, products[parity], weights[parity], col_spreads[parity])
+                weigh(step, products[parity], weights[parity])
                 total(lax.rem(step + chunks - 1, chunks), weights[1 - parity])
             return carry
 
@@ -206,25 +209,21 @@
         turned = field_ref[...].T
         for field in range(FIELDS):
             spread_ref[field] = jnp.broadcast_to(turned[:, field : field + 1], (rows, LANES))
-        row_vecs = with_ones(row_ref[vec_rows, :])
+        row_vec_ref[...] = with_ones(row_ref[vec_rows, :])
         if turns:
             for number, pack_ref in enumerate(col_refs):
                 part = pl.ds(number * rows, rows)
                 col_out_ref[0:features, part] = pack_ref[0:rows, :].T
                 col_out_ref[features:size, part] = pack_ref[features:size, :]
-            block(col_out_ref, 0, row_vecs)
+            block(col_out_ref, 0)
         else:
             done = 0
             for col_ref in col_refs:
-                block(col_ref, done, row_vecs)
+                block(col_ref, done)
                 done += col_ref.shape[1]
-
-    def finish():
-        row_out_ref[...] = sum_ref[...].T[0:OUT_ROWS]
 
     if receivers is None:
         compute()
-        finish()
         return
     pair = lax.axis_index("blk") // 2
     takes_part = functools.reduce(jnp.logical_or, [pair == one for one in receivers])
@@ -232,11 +231,9 @@
     @pl.when(takes_part)
     def _():
         compute()
-        finish()
 
     @pl.when(jnp.logical_not(takes_part))
     def _():
-        row_out_ref[...] = jnp.zeros_like(row_out_ref)
         col_out_ref[...] = jnp.zeros_like(col_out_ref)
 
 
@@ -254,13 +251,12 @@
         scratch_shapes=[
             pltpu.VMEM((LANES, rows), jnp.float32),
             pltpu.VMEM((FIELDS, rows, LANES), jnp.float32),
-            pltpu.VMEM((rows, LANES), jnp.float32),
-            pltpu.VMEM((rows, CHUNK), jnp.float32),
-            pltpu.VMEM((rows, CHUNK), jnp.float32),
-            pltpu.VMEM((rows, CHUNK), jnp.bfloat16),
-            pltpu.VMEM((rows, CHUNK), jnp.bfloat16),
-            pltpu.VMEM((FIELDS, 8, CHUNK), jnp.float32),
-            pltpu.VMEM((FIELDS, 8, CHUNK), jnp.float32),
+            pltpu.VMEM((rows, WIDE), jnp.float32),
+            pltpu.VMEM((rows, WIDE), jnp.float32),
+            pltpu.VMEM((rows, WIDE), jnp.bfloat16),
+            pltpu.VMEM((rows, WIDE), jnp.bfloat16),
+            pltpu.VMEM((FIELDS, 8, WIDE), jnp.float32),
+            pltpu.VMEM((vecs + CODE_ROWS, rows), jnp.bfloat16),
         ],
         cost_estimate=pl.CostEstimate(flops=COST, bytes_accessed=COST, transcendentals=0),
         compiler_params=params(),
@@ -404,15 +400,22 @@
     cut = beside_mine.shape[0] // SWAPS // 16 * 16
     shares = [beside_mine[at * cut : (at + 1) * cut if at < SWAPS - 1 else None] for at in range(SWAPS)]
     beside_rest = jnp.concatenate([lax.ppermute(share, "sub", swap) for share in shares], axis=0)
+    first_sums = [weigh(pack, [own], receivers=takers) for (_, takers), pack in zip(plans[:1], sent[:1])]
+    if first_sums:
+        first_sums, beside_rest = lax.optimization_barrier((first_sums, beside_rest))
     beside_sums, next_to = weigh(mine, [beside_mine, beside_rest], turns=True)
     parts = [own_sums, beside_sums]
     col_sums = None
-    for (moves, takers), pack in zip(plans, sent):
-        if col_sums is not None:
+    for number, ((moves, takers), pack) in enumerate(zip(plans, sent)):
+        if number == 0:
+            row_sums, sums = weigh(pack, [next_to], receivers=takers)
+            row_sums = row_sums + first_sums[0][0]
+            col_sums = jnp.concatenate([first_sums[0][1], sums], axis=1)
+        else:
             pack, col_sums, parts[-1] = lax.optimization_barrier((pack, col_sums, parts[-1]))
-        row_sums, sums = weigh(pack, [own, next_to], receivers=takers)
+            row_sums, sums = weigh(pack, [own, next_to], receivers=takers)
+            col_sums = col_sums + sums
         parts.append(lax.ppermute(row_sums, "blk", back(moves)))
-        col_sums = sums if col_sums is None else col_sums + sums
     if col_sums is not None:
         own_mine, own_rest, next_mine, next_rest = [col_sums[:, place * half : (place + 1) * half] for place in range(4)]
         sides = lax.ppermute(jnp.concatenate([own_rest, next_rest], axis=1), "sub", swap)

time: 69.7 us -> 68.1 us (0.977)
  Pallas kernels: 20.1 us -> 16.1 us
  starting transfers between devices: 14.9 us -> 17.1 us
    ppermute x2, waiting for transfers between devices: 16.3 us -> 12 us  [local(): parts.append(lax.ppermute(row_sums, 'blk', back(moves)))]
    pallas_call x4 -> x5, Pallas kernels: 15.6 us -> 11.6 us  [tile(): pl.pallas_call(functools.partial(tile_kernel, len(columns), turns, own_bl...]
    ppermute x2, waiting for transfers between devices: 3.79 us -> 6.88 us  [local(): sent = [lax.ppermute(mine, 'blk', moves) for moves, _ in plans]]
    ppermute x1, waiting for transfers between devices: 4 us -> 6.63 us  [local(): beside_mine = lax.ppermute(mine, 'blk', beside)]
    ppermute x2, starting transfers between devices: 4.97 us -> 7.18 us  [local(): sent = [lax.ppermute(mine, 'blk', moves) for moves, _ in plans]]
    ppermute x2, waiting for transfers between devices: 1.39 us -> 0.01 us  [local(): lax.ppermute(share, 'sub', swap)]
  transfers between devices with their start and end apart: 13 -> 13, of which waited for: 8 -> 8; matrix products, arithmetic and copies ran while one was open for 3% -> 3% of each run, Pallas kernels for 22% -> 17%
where the time goes in v13:
time: 68.1 us; the launch traced here: 67.7 us
  waiting for transfers between devices  32.2 us (47%)
  starting transfers between devices  17.1 us (25%)
  Pallas kernels  16.1 us (24%)
  local copies, waits for them, and re-layouts  1.12 us (2%)
  other arithmetic  0.92 us (1%)
    ppermute x2, waiting for transfers between devices, local(): parts.append(lax.ppermute(row_sums, 'blk', back(moves)))  12 us
    pallas_call x5, Pallas kernels, tile(): pl.pallas_call(functools.partial(tile_kernel, len(columns), turns, own_bl...  11.6 us
    ppermute x2, starting transfers between devices, local(): sent = [lax.ppermute(mine, 'blk', moves) for moves, _ in plans]  7.18 us
    ppermute x2, waiting for transfers between devices, local(): sent = [lax.ppermute(mine, 'blk', moves) for moves, _ in plans]  6.88 us
    ppermute x1, waiting for transfers between devices, local(): beside_mine = lax.ppermute(mine, 'blk', beside)  6.63 us
    all_to_all x1, waiting for transfers between devices, local(): lax.all_to_all(grams_of(image, 2 * blocks), ('blk', 'sub'), 0, 0, tiled=T...  5.54 us
    all_to_all x1, starting transfers between devices, local(): lax.all_to_all(grams_of(image, 2 * blocks), ('blk', 'sub'), 0, 0, tiled=T...  3.5 us
    ppermute x1, starting transfers between devices, local(): beside_mine = lax.ppermute(mine, 'blk', beside)  3.03 us
  transfers between devices with their start and end apart: 13, of which 8 were waited for; matrix products, arithmetic and copies ran while one was open for 3% of the time, Pallas kernels for 17%

profile of v13, /device:TPU:0, one launch (start us, length us, event | category | flops | bytes accessed | tf_op | source)
XLA Modules:
  0.0 67.7 jit_solution(13708422285483627135)
XLA Ops:
  0.0 0.5 collective-permute-start
  0.5 0.1 collective-permute-start.1
  0.5 1.1 %constant_dynamic-slice_fusion = (bf16[512,256]{1,0:T(8,128)(2,1)S(1)}, bf16[512,256]{1,0:T(8,128)(2,1)S(1)}) fusion(bf16[1024,256]{1,0:T(8,128)(2,1)} %param.5, s32[]{:T(128)S(6)} %select_n.7, s32[]{:T(128)S(6)} %select_n.6), kind=kLoop, calls=%fused_computation.5 | loop fusion | bytes 1048584 | tf_op jit(solution)/shard_map/dynamic_slice | solution.py:393
  1.6 0.8 %pad_add_fusion.meta_ref = s32[7,1024]{1,0:T(8,128)S(1)} fusion(s32[1,1024]{1,0:T(1,128)} %bitcast.1, s32[2,1024]{1,0:T(2,128)} %param.8, s32[4,1024]{1,0:T(4,128)} %param.7), kind=kLoop, calls=%fused_computation.4 | loop fusion | flops 14336 | bytes 57344 | tf_op jit(solution)/shard_map/concatenate | solution.py:391
  2.4 0.0 collective-permute-done.1.vec_other_ref
  2.4 0.0 collective-permute-done.emb_other_ref
  2.4 0.7 %pack.1 = (bf16[560,512]{1,0:T(8,128)(2,1)S(1)}, bf16[560,512]{1,0:T(8,128)(2,1)S(1)}) custom-call(bf16[512,256]{1,0:T(8,128)(2,1)S(1)} %get-tuple-element.50.emb_mine_ref, bf16[512,256]{1,0:T(8,128)(2,1)S(1)} %get-tuple-element.49.emb_rest_ref, bf16[1024,256]{1,0:T(8,128)(2,1)S(1)} %collective-permute-done.emb_other_ref, bf16[16,1024]{1,0:T(8,128)(2,1)S(1)} %copy-done, ...), custom_call_target="tpu_custom_call" | custom-call | tf_op jit(solution)/shard_map/pack/pallas_call | solution.py:103
  3.1 3.0 %collective-permute-start.2 = (bf16[560,512]{1,0:T(8,128)(2,1)S(1)}, bf16[560,512]{1,0:T(8,128)(2,1)S(1)}, u32[]{:S(2)}, u32[]{:S(2)}) collective-permute-start(bf16[560,512]{1,0:T(8,128)(2,1)S(1)} %get-tuple-element.27.refs_0_.refs_1_), channel_id=1, source_target_pairs={{0,2},{2,0},{4,6},{6,4},{8,10},{10,8},{12,14},{14,12},{1,3},{3,1},... | collective-permute-start | bytes 1720328 | tf_op jit(solution)/shard_map/ppermute | solution.py:396
  6.1 3.6 %collective-permute-start.3 = (bf16[560,512]{1,0:T(8,128)(2,1)S(1)}, bf16[560,512]{1,0:T(8,128)(2,1)S(1)}, u32[]{:S(2)}, u32[]{:S(2)}) collective-permute-start(bf16[560,512]{1,0:T(8,128)(2,1)S(1)} %get-tuple-element.27.refs_0_.refs_1_), channel_id=1, source_target_pairs={{4,0},{6,2},{8,4},{10,6},{12,8},{14,10},{0,12},{2,14},{5,1},{7,3},... | collective-permute-start | bytes 1720328 | tf_op jit(solution)/shard_map/ppermute | solution.py:395
  9.7 3.0 %tile.5 = (f32[40,512]{1,0:T(8,128)S(1)}, bf16[560,1024]{1,0:T(8,128)(2,1)S(1)}) custom-call(bf16[560,512]{1,0:T(8,128)(2,1)S(1)} %get-tuple-element.27.refs_0_.refs_1_, bf16[560,512]{1,0:T(8,128)(2,1)S(1)} %get-tuple-element.27.refs_0_.refs_1_, bf16[560,512]{1,0:T(8,128)(2,1)S(1)} %get-tuple-element.28.refs_2_), custom_call_target="tpu_custom_call" | custom-call | flops 1 | bytes 1 | tf_op jit(solution)/shard_map/tile/pallas_call | solution.py:246
  12.7 6.6 %collective-permute-done.2.refs_1_ = bf16[560,512]{1,0:T(8,128)(2,1)S(1)} collective-permute-done((bf16[560,512]{1,0:T(8,128)(2,1)S(1)}, bf16[560,512]{1,0:T(8,128)(2,1)S(1)}, u32[]{:S(2)}, u32[]{:S(2)}) %collective-permute-start.2) | collective-permute-done | bytes 573472 | tf_op jit(solution)/shard_map/ppermute | solution.py:396
  19.3 2.6 %collective-permute-done.3.refs_0_ = bf16[560,512]{1,0:T(8,128)(2,1)S(1)} collective-permute-done((bf16[560,512]{1,0:T(8,128)(2,1)S(1)}, bf16[560,512]{1,0:T(8,128)(2,1)S(1)}, u32[]{:S(2)}, u32[]{:S(2)}) %collective-permute-start.3) | collective-permute-done | bytes 573472 | tf_op jit(solution)/shard_map/ppermute | solution.py:395
  21.9 0.1 collective-permute-start.5
  22.0 0.6 collective-permute-start.4
  22.6 3.6 %collective-permute-start.6 = (bf16[560,512]{1,0:T(8,128)(2,1)S(1)}, bf16[560,512]{1,0:T(8,128)(2,1)S(1)}, u32[]{:S(2)}, u32[]{:S(2)}) collective-permute-start(bf16[560,512]{1,0:T(8,128)(2,1)S(1)} %get-tuple-element.27.refs_0_.refs_1_), channel_id=1, source_target_pairs={{0,8},{2,10},{12,4},{14,6},{1,9},{3,11},{13,5},{15,7},{16,24},{18,... | collective-permute-start | bytes 1720328 | tf_op jit(solution)/shard_map/ppermute | solution.py:395
  26.2 2.9 %tile.6 = (f32[40,512]{1,0:T(8,128)S(1)}, f32[40,1024]{1,0:T(8,128)S(1)}) custom-call(bf16[560,512]{1,0:T(8,128)(2,1)S(1)} %collective-permute-done.3.refs_0_, bf16[560,1024]{1,0:T(8,128)(2,1)S(1)} %get-tuple-element.34.refs_1_), custom_call_target="tpu_custom_call" | custom-call | flops 1 | bytes 1 | tf_op jit(solution)/shard_map/tile/pallas_call | solution.py:246
  29.1 2.9 %tile.7 = (f32[40,512]{1,0:T(8,128)S(1)}, bf16[560,1024]{1,0:T(8,128)(2,1)S(1)}) custom-call(bf16[560,512]{1,0:T(8,128)(2,1)S(1)} %get-tuple-element.27.refs_0_.refs_1_, bf16[560,512]{1,0:T(8,128)(2,1)S(1)} %collective-permute-done.2.refs_1_, bf16[560,512]{1,0:T(8,128)(2,1)S(1)} %pad_maximum_fusion.refs_2_), custom_call_target="tpu_custom_call" | custom-call | flops 1 | bytes 1 | tf_op jit(solution)/shard_map/tile/pallas_call | solution.py:246
  32.0 2.9 %tile.8 = (f32[40,512]{1,0:T(8,128)S(1)}, f32[40,1024]{1,0:T(8,128)S(1)}) custom-call(bf16[560,512]{1,0:T(8,128)(2,1)S(1)} %collective-permute-done.3.refs_0_, bf16[560,1024]{1,0:T(8,128)(2,1)S(1)} %get-tuple-element.40.refs_1_.refs_2_), custom_call_target="tpu_custom_call" | custom-call | flops 1 | bytes 1 | tf_op jit(solution)/shard_map/tile/pallas_call | solution.py:246
  34.9 0.1 collective-permute-start.7
  35.0 4.3 %collective-permute-done.6.refs_0_ = bf16[560,512]{1,0:T(8,128)(2,1)S(1)} collective-permute-done((bf16[560,512]{1,0:T(8,128)(2,1)S(1)}, bf16[560,512]{1,0:T(8,128)(2,1)S(1)}, u32[]{:S(2)}, u32[]{:S(2)}) %collective-permute-start.6) | collective-permute-done | bytes 573472 | tf_op jit(solution)/shard_map/ppermute | solution.py:395
  39.3 3.7 %collective-permute-done.7.refs_2_ = f32[40,512]{1,0:T(8,128)S(1)} collective-permute-done((f32[40,512]{1,0:T(8,128)S(1)}, f32[40,512]{1,0:T(8,128)S(1)}, u32[]{:S(2)}, u32[]{:S(2)}) %collective-permute-start.7) | collective-permute-done | bytes 81952 | tf_op jit(solution)/shard_map/ppermute | solution.py:418
  43.2 0.1 collective-permute-start.9
  43.2 1.3 %collective-permute-start.8 = (f32[40,512]{1,0:T(8,128)S(1)}, f32[40,512]{1,0:T(8,128)S(1)}, u32[]{:S(2)}, u32[]{:S(2)}) collective-permute-start(f32[40,512]{1,0:T(8,128)S(1)} %get-tuple-element.46), channel_id=1, source_target_pairs={{8,0},{10,2},{4,12},{6,14},{9,1},{11,3},{5,13},{7,15},{24,16},{26,... | collective-permute-start | bytes 245768 | tf_op jit(solution)/shard_map/ppermute | solution.py:418
  44.5 0.1 collective-permute-done.9
  44.7 0.6 collective-permute-start.10
  45.2 8.2 %collective-permute-done.8.refs_3_ = f32[40,512]{1,0:T(8,128)S(1)} collective-permute-done((f32[40,512]{1,0:T(8,128)S(1)}, f32[40,512]{1,0:T(8,128)S(1)}, u32[]{:S(2)}, u32[]{:S(2)}) %collective-permute-start.8) | collective-permute-done | bytes 81952 | tf_op jit(solution)/shard_map/ppermute | solution.py:418
  53.5 0.9 %gram.1 = f32[16,8,128]{2,1,0:T(8,128)} custom-call(f32[32,512]{1,0:T(8,128)S(1)} %image.1.image_ref.mine_ref), custom_call_target="tpu_custom_call" | custom-call | tf_op jit(solution)/shard_map/gram/pallas_call | solution.py:300
  54.4 3.5 %all-to-all-start = ((f32[16,8,128]{2,1,0:T(8,128)}), f32[16,8,128]{2,1,0:T(8,128)S(1)}, u32[]{:S(2)}, u32[]{:S(2)}) async-start(f32[16,8,128]{2,1,0:T(8,128)} %gram.1), calls=%async_computation | async-start | bytes 131072 | tf_op jit(solution)/shard_map/all_to_all | solution.py:427
  57.9 0.3 collective-permute-start.11
  58.2 1.0 %collective-permute-done.11.other_ref = f32[32,512]{1,0:T(8,128)S(1)} collective-permute-done((f32[32,512]{1,0:T(8,128)S(1)}, f32[32,512]{1,0:T(8,128)S(1)}, u32[]{:S(2)}, u32[]{:S(2)}) %collective-permute-start.11) | collective-permute-done | bytes 65568 | tf_op jit(solution)/shard_map/ppermute | solution.py:426
  59.2 5.5 %all-to-all-done.grams_ref = f32[16,8,128]{2,1,0:T(8,128)S(1)} async-done(((f32[16,8,128]{2,1,0:T(8,128)}), f32[16,8,128]{2,1,0:T(8,128)S(1)}, u32[]{:S(2)}, u32[]{:S(2)}) %all-to-all-start) | async-done | bytes 65568 | tf_op jit(solution)/shard_map/all_to_all | solution.py:427
  64.8 2.9 %basis.1 = f32[16,1024]{1,0:T(8,128)} custom-call(f32[16,8,128]{2,1,0:T(8,128)S(1)} %all-to-all-done.grams_ref, f32[32,512]{1,0:T(8,128)S(1)} %image.1.image_ref.mine_ref, f32[32,512]{1,0:T(8,128)S(1)} %collective-permute-done.11.other_ref), custom_call_target="tpu_custom_call" | custom-call | tf_op jit(solution)/shard_map/basis/pallas_call | solution.py:350
  (16 shorter events, 0.3 us)
Async XLA Ops:
  0.0 2.4 %copy-start = (bf16[16,1024]{1,0:T(8,128)(2,1)S(1)}, bf16[16,1024]{1,0:T(8,128)(2,1)}, u32[]{:S(2)}) copy-start(bf16[16,1024]{1,0:T(8,128)(2,1)} %vec_ref.1) | copy-start | bytes 98308
  0.0 2.4 %collective-permute-start = (bf16[1024,256]{1,0:T(8,128)(2,1)}, bf16[1024,256]{1,0:T(8,128)(2,1)S(1)}, u32[]{:S(2)}, u32[]{:S(2)}) collective-permute-start(bf16[1024,256]{1,0:T(8,128)(2,1)} %param.5), channel_id=1, source_target_pairs={{0,1},{1,0},{2,3},{3,2},{4,5},{5,4},{6,7},{7,6},{8,9},{9,8},{10,11... | collective-permute-start | bytes 1572872 | tf_op jit(solution)/shard_map/ppermute | solution.py:389
  0.5 1.9 %collective-permute-start.1 = (bf16[16,1024]{1,0:T(8,128)(2,1)}, bf16[16,1024]{1,0:T(8,128)(2,1)S(1)}, u32[]{:S(2)}, u32[]{:S(2)}) collective-permute-start(bf16[16,1024]{1,0:T(8,128)(2,1)} %vec_ref.1), channel_id=1, source_target_pairs={{0,1},{1,0},{2,3},{3,2},{4,5},{5,4},{6,7},{7,6},{8,9},{9,8},{10,11... | collective-permute-start | bytes 98312 | tf_op jit(solution)/shard_map/ppermute | solution.py:390
  3.1 16.2 %collective-permute-start.2 = (bf16[560,512]{1,0:T(8,128)(2,1)S(1)}, bf16[560,512]{1,0:T(8,128)(2,1)S(1)}, u32[]{:S(2)}, u32[]{:S(2)}) collective-permute-start(bf16[560,512]{1,0:T(8,128)(2,1)S(1)} %get-tuple-element.27.refs_0_.refs_1_), channel_id=1, source_target_pairs={{0,2},{2,0},{4,6},{6,4},{8,10},{10,8},{12,14},{14,12},{1,3},{3,1},... | collective-permute-start | bytes 1720328 | tf_op jit(solution)/shard_map/ppermute | solution.py:396
  6.1 15.8 %collective-permute-start.3 = (bf16[560,512]{1,0:T(8,128)(2,1)S(1)}, bf16[560,512]{1,0:T(8,128)(2,1)S(1)}, u32[]{:S(2)}, u32[]{:S(2)}) collective-permute-start(bf16[560,512]{1,0:T(8,128)(2,1)S(1)} %get-tuple-element.27.refs_0_.refs_1_), channel_id=1, source_target_pairs={{4,0},{6,2},{8,4},{10,6},{12,8},{14,10},{0,12},{2,14},{5,1},{7,3},... | collective-permute-start | bytes 1720328 | tf_op jit(solution)/shard_map/ppermute | solution.py:395
  21.9 7.1 %collective-permute-start.5 = (bf16[288,512]{1,0:T(8,128)(2,1)S(1)}, bf16[288,512]{1,0:T(8,128)(2,1)S(1)}, u32[]{:S(2)}, u32[]{:S(2)}) collective-permute-start(bf16[288,512]{1,0:T(8,128)(2,1)S(1)} %slice.25), channel_id=1, source_target_pairs={{0,1},{1,0},{2,3},{3,2},{4,5},{5,4},{6,7},{7,6},{8,9},{9,8},{10,11... | collective-permute-start | bytes 884744 | tf_op jit(solution)/shard_map/ppermute | solution.py:402
  22.0 7.0 %collective-permute-start.4 = (bf16[272,512]{1,0:T(8,128)(2,1)S(1)}, bf16[272,512]{1,0:T(8,128)(2,1)S(1)}, u32[]{:S(2)}, u32[]{:S(2)}) collective-permute-start(bf16[272,512]{1,0:T(8,128)(2,1)S(1)} %slice.24), channel_id=1, source_target_pairs={{0,1},{1,0},{2,3},{3,2},{4,5},{5,4},{6,7},{7,6},{8,9},{9,8},{10,11... | collective-permute-start | bytes 835592 | tf_op jit(solution)/shard_map/ppermute | solution.py:402
  22.6 16.7 %collective-permute-start.6 = (bf16[560,512]{1,0:T(8,128)(2,1)S(1)}, bf16[560,512]{1,0:T(8,128)(2,1)S(1)}, u32[]{:S(2)}, u32[]{:S(2)}) collective-permute-start(bf16[560,512]{1,0:T(8,128)(2,1)S(1)} %get-tuple-element.27.refs_0_.refs_1_), channel_id=1, source_target_pairs={{0,8},{2,10},{12,4},{14,6},{1,9},{3,11},{13,5},{15,7},{16,24},{18,... | collective-permute-start | bytes 1720328 | tf_op jit(solution)/shard_map/ppermute | solution.py:395
  34.9 8.1 %collective-permute-start.7 = (f32[40,512]{1,0:T(8,128)S(1)}, f32[40,512]{1,0:T(8,128)S(1)}, u32[]{:S(2)}, u32[]{:S(2)}) collective-permute-start(f32[40,512]{1,0:T(8,128)S(1)} %add.17), channel_id=1, source_target_pairs={{0,4},{2,6},{4,8},{6,10},{8,12},{10,14},{12,0},{14,2},{1,5},{3,7},... | collective-permute-start | bytes 245768 | tf_op jit(solution)/shard_map/ppermute | solution.py:418
  43.2 1.5 %collective-permute-start.9 = (f32[40,1024]{1,0:T(8,128)S(1)}, f32[40,1024]{1,0:T(8,128)S(1)}, u32[]{:S(2)}, u32[]{:S(2)}) collective-permute-start(f32[40,1024]{1,0:T(8,128)S(1)} %pad_maximum_fusion.2), channel_id=1, source_target_pairs={{0,1},{1,0},{2,3},{3,2},{4,5},{5,4},{6,7},{7,6},{8,9},{9,8},{10,11... | collective-permute-start | bytes 491528 | tf_op jit(solution)/shard_map/ppermute | solution.py:421
  43.2 10.2 %collective-permute-start.8 = (f32[40,512]{1,0:T(8,128)S(1)}, f32[40,512]{1,0:T(8,128)S(1)}, u32[]{:S(2)}, u32[]{:S(2)}) collective-permute-start(f32[40,512]{1,0:T(8,128)S(1)} %get-tuple-element.46), channel_id=1, source_target_pairs={{8,0},{10,2},{4,12},{6,14},{9,1},{11,3},{5,13},{7,15},{24,16},{26,... | collective-permute-start | bytes 245768 | tf_op jit(solution)/shard_map/ppermute | solution.py:418
  44.7 8.8 %collective-permute-start.10 = (f32[40,512]{1,0:T(8,128)S(1)}, f32[40,512]{1,0:T(8,128)S(1)}, u32[]{:S(2)}, u32[]{:S(2)}) collective-permute-start(f32[40,512]{1,0:T(8,128)S(1)} %get-tuple-element.51), channel_id=1, source_target_pairs={{0,2},{2,0},{4,6},{6,4},{8,10},{10,8},{12,14},{14,12},{1,3},{3,1},... | collective-permute-start | bytes 245768 | tf_op jit(solution)/shard_map/ppermute | solution.py:424
  54.4 10.4 %all-to-all-start = ((f32[16,8,128]{2,1,0:T(8,128)}), f32[16,8,128]{2,1,0:T(8,128)S(1)}, u32[]{:S(2)}, u32[]{:S(2)}) async-start(f32[16,8,128]{2,1,0:T(8,128)} %gram.1), calls=%async_computation | async-start | bytes 131072 | tf_op jit(solution)/shard_map/all_to_all | solution.py:427
  57.9 1.3 %collective-permute-start.11 = (f32[32,512]{1,0:T(8,128)S(1)}, f32[32,512]{1,0:T(8,128)S(1)}, u32[]{:S(2)}, u32[]{:S(2)}) collective-permute-start(f32[32,512]{1,0:T(8,128)S(1)} %image.1.image_ref.mine_ref), channel_id=1, source_target_pairs={{0,1},{1,0},{2,3},{3,2},{4,5},{5,4},{6,7},{7,6},{8,9},{9,8},{10,11... | collective-permute-start | bytes 196616 | tf_op jit(solution)/shard_map/ppermute | solution.py:426

commit v14 on v13

--- a/solution.py
+++ b/solution.py
@@ -28,7 +28,7 @@
 COST = 1
 WIDE = 512
 GROUP = 16
-SWAPS = 2
+SWAPS = 3
 VMEM_LIMIT = 48 * 1024 * 1024
 
 NT = (((1,), (1,)), ((), ()))
@@ -143,14 +143,16 @@
     return jnp.where(barred, 0.0, value)
 
 
-def tile_kernel(blocks, turns, own_block, receivers, vecs, *refs):
+def tile_kernel(blocks, turns, own_block, streams, receivers, vecs, *refs):
     row_ref, col_refs = refs[0], refs[1 : 1 + blocks]
     row_out_ref, col_out_ref, field_ref, spread_ref = refs[1 + blocks : 5 + blocks]
     products, weights = [refs[at : at + 2] for at in (5 + blocks, 7 + blocks)]
-    col_spread_ref, row_vec_ref = refs[9 + blocks :]
+    col_spread_ref, row_vec_ref, sum_ref = refs[9 + blocks :]
     size, rows = row_ref.shape
     features = size - vecs - CODE_ROWS
     vec_rows, code_rows = slice(features, features + vecs), slice(features + vecs, size)
+    if streams:
+        sum_ref[...] = jnp.zeros_like(sum_ref)
     row_out_ref[...] = jnp.zeros_like(row_out_ref)
 
     def block(col_ref, done):
@@ -184,7 +186,10 @@
 
         def total(step, weight_ref):
             col_vecs = with_ones(col_ref[vec_rows, place(step)])
-            row_out_ref[...] += dot_nt(col_vecs, weight_ref[...])[0:OUT_ROWS]
+            if streams:
+                sum_ref[:, 0 : vecs + CODE_ROWS] += dot_nt(weight_ref[...], col_vecs)
+            else:
+                row_out_ref[...] += dot_nt(col_vecs, weight_ref[...])[0:OUT_ROWS]
             if not turns:
                 col_out_ref[:, place(step, done)] = jnp.dot(
                     row_vec_ref[...], weight_ref[...], preferred_element_type=jnp.float32
@@ -221,6 +226,8 @@
             for col_ref in col_refs:
                 block(col_ref, done)
                 done += col_ref.shape[1]
+        if streams:
+            row_out_ref[...] = sum_ref[...].T[0:OUT_ROWS]
 
     if receivers is None:
         compute()
@@ -237,14 +244,14 @@
         col_out_ref[...] = jnp.zeros_like(col_out_ref)
 
 
-def tile(row, columns, vecs, turns=False, own_block=False, receivers=None):
+def tile(row, columns, vecs, turns=False, own_block=False, streams=False, receivers=None):
     size, rows = row.shape
     cols = len(columns) * rows if turns else sum(part.shape[1] for part in columns)
     second = jax.ShapeDtypeStruct((size, cols), jnp.bfloat16)
     if not turns:
         second = jax.ShapeDtypeStruct((OUT_ROWS, cols), jnp.float32)
     return pl.pallas_call(
-        functools.partial(tile_kernel, len(columns), turns, own_block, receivers, vecs),
+        functools.partial(tile_kernel, len(columns), turns, own_block, streams, receivers, vecs),
         out_shape=[jax.ShapeDtypeStruct((OUT_ROWS, rows), jnp.float32), second],
         in_specs=[VMEM_SPEC] * (1 + len(columns)),
         out_specs=[VMEM_SPEC] * 2,
@@ -257,6 +264,7 @@
             pltpu.VMEM((rows, WIDE), jnp.bfloat16),
             pltpu.VMEM((FIELDS, 8, WIDE), jnp.float32),
             pltpu.VMEM((vecs + CODE_ROWS, rows), jnp.bfloat16),
+            pltpu.VMEM((rows, LANES), jnp.float32),
         ],
         cost_estimate=pl.CostEstimate(flops=COST, bytes_accessed=COST, transcendentals=0),
         compiler_params=params(),
@@ -413,7 +421,7 @@
             col_sums = jnp.concatenate([first_sums[0][1], sums], axis=1)
         else:
             pack, col_sums, parts[-1] = lax.optimization_barrier((pack, col_sums, parts[-1]))
-            row_sums, sums = weigh(pack, [own, next_to], receivers=takers)
+            row_sums, sums = weigh(pack, [own, next_to], streams=True, receivers=takers)
             col_sums = col_sums + sums
         parts.append(lax.ppermute(row_sums, "blk", back(moves)))
     if col_sums is not None:

time: 68.1 us -> 64.4 us (0.946)
  starting transfers between devices: 17.1 us -> 15 us
  waiting for transfers between devices: 32.2 us -> 30.4 us
    ppermute x2, starting transfers between devices: 7.18 us -> 4.97 us  [local(): sent = [lax.ppermute(mine, 'blk', moves) for moves, _ in plans]]
    ppermute x1, waiting for transfers between devices: 6.63 us -> 5.25 us  [local(): beside_mine = lax.ppermute(mine, 'blk', beside)]
    ppermute x2, waiting for transfers between devices: 6.88 us -> 5.88 us  [local(): sent = [lax.ppermute(mine, 'blk', moves) for moves, _ in plans]]
  transfers between devices with their start and end apart: 13 -> 14, of which waited for: 8 -> 8; matrix products, arithmetic and copies ran while one was open for 3% -> 3% of each run, Pallas kernels for 17% -> 18%
where the time goes in v14:
time: 64.4 us; the launch traced here: 64 us
  waiting for transfers between devices  30.4 us (47%)
  Pallas kernels  16.3 us (25%)
  starting transfers between devices  15 us (23%)
  local copies, waits for them, and re-layouts  1.12 us (2%)
  other arithmetic  0.92 us (1%)
    ppermute x2, waiting for transfers between devices, local(): parts.append(lax.ppermute(row_sums, 'blk', back(moves)))  12.6 us
    pallas_call x5, Pallas kernels, tile(): pl.pallas_call(functools.partial(tile_kernel, len(columns), turns, own_bl...  11.8 us
    ppermute x2, waiting for transfers between devices, local(): sent = [lax.ppermute(mine, 'blk', moves) for moves, _ in plans]  5.88 us
    all_to_all x1, waiting for transfers between devices, local(): lax.all_to_all(grams_of(image, 2 * blocks), ('blk', 'sub'), 0, 0, tiled=T...  5.54 us
    ppermute x1, waiting for transfers between devices, local(): beside_mine = lax.ppermute(mine, 'blk', beside)  5.25 us
    ppermute x2, starting transfers between devices, local(): sent = [lax.ppermute(mine, 'blk', moves) for moves, _ in plans]  4.97 us
    all_to_all x1, starting transfers between devices, local(): lax.all_to_all(grams_of(image, 2 * blocks), ('blk', 'sub'), 0, 0, tiled=T...  3.5 us
    ppermute x1, starting transfers between devices, local(): beside_mine = lax.ppermute(mine, 'blk', beside)  3.03 us
  transfers between devices with their start and end apart: 14, of which 8 were waited for; matrix products, arithmetic and copies ran while one was open for 3% of the time, Pallas kernels for 18%

profile of v14, /device:TPU:0, one launch (start us, length us, event | category | flops | bytes accessed | tf_op | source)
XLA Modules:
  0.0 64.0 jit_solution(16999760240297359044)
XLA Ops:
  0.0 0.5 collective-permute-start
  0.5 0.1 collective-permute-start.1
  0.5 1.1 %constant_dynamic-slice_fusion = (bf16[512,256]{1,0:T(8,128)(2,1)S(1)}, bf16[512,256]{1,0:T(8,128)(2,1)S(1)}) fusion(bf16[1024,256]{1,0:T(8,128)(2,1)} %param.5, s32[]{:T(128)S(6)} %select_n.7, s32[]{:T(128)S(6)} %select_n.6), kind=kLoop, calls=%fused_computation.5 | loop fusion | bytes 1048584 | tf_op jit(solution)/shard_map/dynamic_slice | solution.py:401
  1.6 0.8 %pad_add_fusion.meta_ref = s32[7,1024]{1,0:T(8,128)S(1)} fusion(s32[1,1024]{1,0:T(1,128)} %bitcast.1, s32[2,1024]{1,0:T(2,128)} %param.8, s32[4,1024]{1,0:T(4,128)} %param.7), kind=kLoop, calls=%fused_computation.4 | loop fusion | flops 14336 | bytes 57344 | tf_op jit(solution)/shard_map/concatenate | solution.py:399
  2.4 0.7 %pack.1 = (bf16[560,512]{1,0:T(8,128)(2,1)S(1)}, bf16[560,512]{1,0:T(8,128)(2,1)S(1)}) custom-call(bf16[512,256]{1,0:T(8,128)(2,1)S(1)} %get-tuple-element.52.emb_mine_ref, bf16[512,256]{1,0:T(8,128)(2,1)S(1)} %get-tuple-element.51.emb_rest_ref, bf16[1024,256]{1,0:T(8,128)(2,1)S(1)} %collective-permute-done.emb_other_ref, bf16[16,1024]{1,0:T(8,128)(2,1)S(1)} %copy-done, ...), custom_call_target="tpu_custom_call" | custom-call | tf_op jit(solution)/shard_map/pack/pallas_call | solution.py:103
  3.1 3.0 %collective-permute-start.2 = (bf16[560,512]{1,0:T(8,128)(2,1)S(1)}, bf16[560,512]{1,0:T(8,128)(2,1)S(1)}, u32[]{:S(2)}, u32[]{:S(2)}) collective-permute-start(bf16[560,512]{1,0:T(8,128)(2,1)S(1)} %get-tuple-element.27.refs_0_.refs_1_), channel_id=1, source_target_pairs={{0,2},{2,0},{4,6},{6,4},{8,10},{10,8},{12,14},{14,12},{1,3},{3,1},... | collective-permute-start | bytes 1720328 | tf_op jit(solution)/shard_map/ppermute | solution.py:404
  6.1 3.6 %collective-permute-start.3 = (bf16[560,512]{1,0:T(8,128)(2,1)S(1)}, bf16[560,512]{1,0:T(8,128)(2,1)S(1)}, u32[]{:S(2)}, u32[]{:S(2)}) collective-permute-start(bf16[560,512]{1,0:T(8,128)(2,1)S(1)} %get-tuple-element.27.refs_0_.refs_1_), channel_id=1, source_target_pairs={{4,0},{6,2},{8,4},{10,6},{12,8},{14,10},{0,12},{2,14},{5,1},{7,3},... | collective-permute-start | bytes 1720328 | tf_op jit(solution)/shard_map/ppermute | solution.py:403
  9.7 1.4 %collective-permute-start.7 = (bf16[560,512]{1,0:T(8,128)(2,1)S(1)}, bf16[560,512]{1,0:T(8,128)(2,1)S(1)}, u32[]{:S(2)}, u32[]{:S(2)}) collective-permute-start(bf16[560,512]{1,0:T(8,128)(2,1)S(1)} %get-tuple-element.27.refs_0_.refs_1_), channel_id=1, source_target_pairs={{0,8},{2,10},{12,4},{14,6},{1,9},{3,11},{13,5},{15,7},{16,24},{18,... | collective-permute-start | bytes 1720328 | tf_op jit(solution)/shard_map/ppermute | solution.py:403
  11.1 3.0 %tile.5 = (f32[40,512]{1,0:T(8,128)S(1)}, bf16[560,1024]{1,0:T(8,128)(2,1)S(1)}) custom-call(bf16[560,512]{1,0:T(8,128)(2,1)S(1)} %get-tuple-element.27.refs_0_.refs_1_, bf16[560,512]{1,0:T(8,128)(2,1)S(1)} %get-tuple-element.27.refs_0_.refs_1_, bf16[560,512]{1,0:T(8,128)(2,1)S(1)} %get-tuple-element.28.refs_2_), custom_call_target="tpu_custom_call" | custom-call | flops 1 | bytes 1 | tf_op jit(solution)/shard_map/tile/pallas_call | solution.py:253
  14.1 5.2 %collective-permute-done.2.refs_1_ = bf16[560,512]{1,0:T(8,128)(2,1)S(1)} collective-permute-done((bf16[560,512]{1,0:T(8,128)(2,1)S(1)}, bf16[560,512]{1,0:T(8,128)(2,1)S(1)}, u32[]{:S(2)}, u32[]{:S(2)}) %collective-permute-start.2) | collective-permute-done | bytes 573472 | tf_op jit(solution)/shard_map/ppermute | solution.py:404
  19.3 3.8 %collective-permute-done.3.refs_0_ = bf16[560,512]{1,0:T(8,128)(2,1)S(1)} collective-permute-done((bf16[560,512]{1,0:T(8,128)(2,1)S(1)}, bf16[560,512]{1,0:T(8,128)(2,1)S(1)}, u32[]{:S(2)}, u32[]{:S(2)}) %collective-permute-start.3) | collective-permute-done | bytes 573472 | tf_op jit(solution)/shard_map/ppermute | solution.py:403
  23.1 0.1 collective-permute-start.6
  23.2 0.6 collective-permute-start.5
  23.8 0.1 collective-permute-start.4
  23.9 2.9 %tile.6 = (f32[40,512]{1,0:T(8,128)S(1)}, f32[40,1024]{1,0:T(8,128)S(1)}) custom-call(bf16[560,512]{1,0:T(8,128)(2,1)S(1)} %collective-permute-done.3.refs_0_, bf16[560,1024]{1,0:T(8,128)(2,1)S(1)} %get-tuple-element.34.refs_1_), custom_call_target="tpu_custom_call" | custom-call | flops 1 | bytes 1 | tf_op jit(solution)/shard_map/tile/pallas_call | solution.py:253
  26.8 2.9 %tile.7 = (f32[40,512]{1,0:T(8,128)S(1)}, bf16[560,1024]{1,0:T(8,128)(2,1)S(1)}) custom-call(bf16[560,512]{1,0:T(8,128)(2,1)S(1)} %get-tuple-element.27.refs_0_.refs_1_, bf16[560,512]{1,0:T(8,128)(2,1)S(1)} %collective-permute-done.2.refs_1_, bf16[560,512]{1,0:T(8,128)(2,1)S(1)} %pad_maximum_fusion.refs_2_), custom_call_target="tpu_custom_call" | custom-call | flops 1 | bytes 1 | tf_op jit(solution)/shard_map/tile/pallas_call | solution.py:253
  29.7 2.9 %tile.8 = (f32[40,512]{1,0:T(8,128)S(1)}, f32[40,1024]{1,0:T(8,128)S(1)}) custom-call(bf16[560,512]{1,0:T(8,128)(2,1)S(1)} %collective-permute-done.3.refs_0_, bf16[560,1024]{1,0:T(8,128)(2,1)S(1)} %get-tuple-element.40.refs_1_.refs_2_), custom_call_target="tpu_custom_call" | custom-call | flops 1 | bytes 1 | tf_op jit(solution)/shard_map/tile/pallas_call | solution.py:253
  32.6 0.1 collective-permute-start.8
  32.7 2.1 %collective-permute-done.7.refs_0_ = bf16[560,512]{1,0:T(8,128)(2,1)S(1)} collective-permute-done((bf16[560,512]{1,0:T(8,128)(2,1)S(1)}, bf16[560,512]{1,0:T(8,128)(2,1)S(1)}, u32[]{:S(2)}, u32[]{:S(2)}) %collective-permute-start.7) | collective-permute-done | bytes 573472 | tf_op jit(solution)/shard_map/ppermute | solution.py:403
  34.8 5.2 %collective-permute-done.8.refs_2_ = f32[40,512]{1,0:T(8,128)S(1)} collective-permute-done((f32[40,512]{1,0:T(8,128)S(1)}, f32[40,512]{1,0:T(8,128)S(1)}, u32[]{:S(2)}, u32[]{:S(2)}) %collective-permute-start.8) | collective-permute-done | bytes 81952 | tf_op jit(solution)/shard_map/ppermute | solution.py:426
  40.0 0.2 tile.9
  40.3 0.1 collective-permute-start.10
  40.4 1.3 %collective-permute-start.9 = (f32[40,512]{1,0:T(8,128)S(1)}, f32[40,512]{1,0:T(8,128)S(1)}, u32[]{:S(2)}, u32[]{:S(2)}) collective-permute-start(f32[40,512]{1,0:T(8,128)S(1)} %get-tuple-element.46), channel_id=1, source_target_pairs={{8,0},{10,2},{4,12},{6,14},{9,1},{11,3},{5,13},{7,15},{24,16},{26,... | collective-permute-start | bytes 245768 | tf_op jit(solution)/shard_map/ppermute | solution.py:426
  41.7 0.1 collective-permute-done.10
  41.8 0.6 collective-permute-start.11
  42.4 7.5 %collective-permute-done.9.refs_3_ = f32[40,512]{1,0:T(8,128)S(1)} collective-permute-done((f32[40,512]{1,0:T(8,128)S(1)}, f32[40,512]{1,0:T(8,128)S(1)}, u32[]{:S(2)}, u32[]{:S(2)}) %collective-permute-start.9) | collective-permute-done | bytes 81952 | tf_op jit(solution)/shard_map/ppermute | solution.py:426
  49.9 0.9 %gram.1 = f32[16,8,128]{2,1,0:T(8,128)} custom-call(f32[32,512]{1,0:T(8,128)S(1)} %image.1.image_ref.mine_ref), custom_call_target="tpu_custom_call" | custom-call | tf_op jit(solution)/shard_map/gram/pallas_call | solution.py:308
  50.8 3.5 %all-to-all-start = ((f32[16,8,128]{2,1,0:T(8,128)}), f32[16,8,128]{2,1,0:T(8,128)S(1)}, u32[]{:S(2)}, u32[]{:S(2)}) async-start(f32[16,8,128]{2,1,0:T(8,128)} %gram.1), calls=%async_computation | async-start | bytes 131072 | tf_op jit(solution)/shard_map/all_to_all | solution.py:435
  54.3 0.3 collective-permute-start.12
  54.6 1.0 %collective-permute-done.12.other_ref = f32[32,512]{1,0:T(8,128)S(1)} collective-permute-done((f32[32,512]{1,0:T(8,128)S(1)}, f32[32,512]{1,0:T(8,128)S(1)}, u32[]{:S(2)}, u32[]{:S(2)}) %collective-permute-start.12) | collective-permute-done | bytes 65568 | tf_op jit(solution)/shard_map/ppermute | solution.py:434
  55.6 5.5 %all-to-all-done.grams_ref = f32[16,8,128]{2,1,0:T(8,128)S(1)} async-done(((f32[16,8,128]{2,1,0:T(8,128)}), f32[16,8,128]{2,1,0:T(8,128)S(1)}, u32[]{:S(2)}, u32[]{:S(2)}) %all-to-all-start) | async-done | bytes 65568 | tf_op jit(solution)/shard_map/all_to_all | solution.py:435
  61.1 2.9 %basis.1 = f32[16,1024]{1,0:T(8,128)} custom-call(f32[16,8,128]{2,1,0:T(8,128)S(1)} %all-to-all-done.grams_ref, f32[32,512]{1,0:T(8,128)S(1)} %image.1.image_ref.mine_ref, f32[32,512]{1,0:T(8,128)S(1)} %collective-permute-done.12.other_ref), custom_call_target="tpu_custom_call" | custom-call | tf_op jit(solution)/shard_map/basis/pallas_call | solution.py:358
  (18 shorter events, 0.3 us)
Async XLA Ops:
  0.0 2.4 %copy-start = (bf16[16,1024]{1,0:T(8,128)(2,1)S(1)}, bf16[16,1024]{1,0:T(8,128)(2,1)}, u32[]{:S(2)}) copy-start(bf16[16,1024]{1,0:T(8,128)(2,1)} %vec_ref.1) | copy-start | bytes 98308
  0.0 2.4 %collective-permute-start = (bf16[1024,256]{1,0:T(8,128)(2,1)}, bf16[1024,256]{1,0:T(8,128)(2,1)S(1)}, u32[]{:S(2)}, u32[]{:S(2)}) collective-permute-start(bf16[1024,256]{1,0:T(8,128)(2,1)} %param.5), channel_id=1, source_target_pairs={{0,1},{1,0},{2,3},{3,2},{4,5},{5,4},{6,7},{7,6},{8,9},{9,8},{10,11... | collective-permute-start | bytes 1572872 | tf_op jit(solution)/shard_map/ppermute | solution.py:397
  0.5 1.9 %collective-permute-start.1 = (bf16[16,1024]{1,0:T(8,128)(2,1)}, bf16[16,1024]{1,0:T(8,128)(2,1)S(1)}, u32[]{:S(2)}, u32[]{:S(2)}) collective-permute-start(bf16[16,1024]{1,0:T(8,128)(2,1)} %vec_ref.1), channel_id=1, source_target_pairs={{0,1},{1,0},{2,3},{3,2},{4,5},{5,4},{6,7},{7,6},{8,9},{9,8},{10,11... | collective-permute-start | bytes 98312 | tf_op jit(solution)/shard_map/ppermute | solution.py:398
  3.1 16.2 %collective-permute-start.2 = (bf16[560,512]{1,0:T(8,128)(2,1)S(1)}, bf16[560,512]{1,0:T(8,128)(2,1)S(1)}, u32[]{:S(2)}, u32[]{:S(2)}) collective-permute-start(bf16[560,512]{1,0:T(8,128)(2,1)S(1)} %get-tuple-element.27.refs_0_.refs_1_), channel_id=1, source_target_pairs={{0,2},{2,0},{4,6},{6,4},{8,10},{10,8},{12,14},{14,12},{1,3},{3,1},... | collective-permute-start | bytes 1720328 | tf_op jit(solution)/shard_map/ppermute | solution.py:404
  6.1 17.0 %collective-permute-start.3 = (bf16[560,512]{1,0:T(8,128)(2,1)S(1)}, bf16[560,512]{1,0:T(8,128)(2,1)S(1)}, u32[]{:S(2)}, u32[]{:S(2)}) collective-permute-start(bf16[560,512]{1,0:T(8,128)(2,1)S(1)} %get-tuple-element.27.refs_0_.refs_1_), channel_id=1, source_target_pairs={{4,0},{6,2},{8,4},{10,6},{12,8},{14,10},{0,12},{2,14},{5,1},{7,3},... | collective-permute-start | bytes 1720328 | tf_op jit(solution)/shard_map/ppermute | solution.py:403
  9.7 25.1 %collective-permute-start.7 = (bf16[560,512]{1,0:T(8,128)(2,1)S(1)}, bf16[560,512]{1,0:T(8,128)(2,1)S(1)}, u32[]{:S(2)}, u32[]{:S(2)}) collective-permute-start(bf16[560,512]{1,0:T(8,128)(2,1)S(1)} %get-tuple-element.27.refs_0_.refs_1_), channel_id=1, source_target_pairs={{0,8},{2,10},{12,4},{14,6},{1,9},{3,11},{13,5},{15,7},{16,24},{18,... | collective-permute-start | bytes 1720328 | tf_op jit(solution)/shard_map/ppermute | solution.py:403
  23.1 3.6 %collective-permute-start.6 = (bf16[208,512]{1,0:T(8,128)(2,1)S(1)}, bf16[208,512]{1,0:T(8,128)(2,1)S(1)}, u32[]{:S(2)}, u32[]{:S(2)}) collective-permute-start(bf16[208,512]{1,0:T(8,128)(2,1)S(1)} %slice.29), channel_id=1, source_target_pairs={{0,1},{1,0},{2,3},{3,2},{4,5},{5,4},{6,7},{7,6},{8,9},{9,8},{10,11... | collective-permute-start | bytes 638984 | tf_op jit(solution)/shard_map/ppermute | solution.py:410
  23.2 3.5 %collective-permute-start.5 = (bf16[176,512]{1,0:T(8,128)(2,1)S(1)}, bf16[176,512]{1,0:T(8,128)(2,1)S(1)}, u32[]{:S(2)}, u32[]{:S(2)}) collective-permute-start(bf16[176,512]{1,0:T(8,128)(2,1)S(1)} %get-tuple-element.50), channel_id=1, source_target_pairs={{0,1},{1,0},{2,3},{3,2},{4,5},{5,4},{6,7},{7,6},{8,9},{9,8},{10,11... | collective-permute-start | bytes 540680 | tf_op jit(solution)/shard_map/ppermute | solution.py:410
  23.8 3.0 %collective-permute-start.4 = (bf16[176,512]{1,0:T(8,128)(2,1)S(1)}, bf16[176,512]{1,0:T(8,128)(2,1)S(1)}, u32[]{:S(2)}, u32[]{:S(2)}) collective-permute-start(bf16[176,512]{1,0:T(8,128)(2,1)S(1)} %get-tuple-element.49), channel_id=1, source_target_pairs={{0,1},{1,0},{2,3},{3,2},{4,5},{5,4},{6,7},{7,6},{8,9},{9,8},{10,11... | collective-permute-start | bytes 540680 | tf_op jit(solution)/shard_map/ppermute | solution.py:410
  32.6 7.4 %collective-permute-start.8 = (f32[40,512]{1,0:T(8,128)S(1)}, f32[40,512]{1,0:T(8,128)S(1)}, u32[]{:S(2)}, u32[]{:S(2)}) collective-permute-start(f32[40,512]{1,0:T(8,128)S(1)} %add.17), channel_id=1, source_target_pairs={{0,4},{2,6},{4,8},{6,10},{8,12},{10,14},{12,0},{14,2},{1,5},{3,7},... | collective-permute-start | bytes 245768 | tf_op jit(solution)/shard_map/ppermute | solution.py:426
  40.3 1.5 %collective-permute-start.10 = (f32[40,1024]{1,0:T(8,128)S(1)}, f32[40,1024]{1,0:T(8,128)S(1)}, u32[]{:S(2)}, u32[]{:S(2)}) collective-permute-start(f32[40,1024]{1,0:T(8,128)S(1)} %pad_maximum_fusion.2), channel_id=1, source_target_pairs={{0,1},{1,0},{2,3},{3,2},{4,5},{5,4},{6,7},{7,6},{8,9},{9,8},{10,11... | collective-permute-start | bytes 491528 | tf_op jit(solution)/shard_map/ppermute | solution.py:429
  40.4 9.4 %collective-permute-start.9 = (f32[40,512]{1,0:T(8,128)S(1)}, f32[40,512]{1,0:T(8,128)S(1)}, u32[]{:S(2)}, u32[]{:S(2)}) collective-permute-start(f32[40,512]{1,0:T(8,128)S(1)} %get-tuple-element.46), channel_id=1, source_target_pairs={{8,0},{10,2},{4,12},{6,14},{9,1},{11,3},{5,13},{7,15},{24,16},{26,... | collective-permute-start | bytes 245768 | tf_op jit(solution)/shard_map/ppermute | solution.py:426
  41.8 8.0 %collective-permute-start.11 = (f32[40,512]{1,0:T(8,128)S(1)}, f32[40,512]{1,0:T(8,128)S(1)}, u32[]{:S(2)}, u32[]{:S(2)}) collective-permute-start(f32[40,512]{1,0:T(8,128)S(1)} %get-tuple-element.53), channel_id=1, source_target_pairs={{0,2},{2,0},{4,6},{6,4},{8,10},{10,8},{12,14},{14,12},{1,3},{3,1},... | collective-permute-start | bytes 245768 | tf_op jit(solution)/shard_map/ppermute | solution.py:432
  50.8 10.4 %all-to-all-start = ((f32[16,8,128]{2,1,0:T(8,128)}), f32[16,8,128]{2,1,0:T(8,128)S(1)}, u32[]{:S(2)}, u32[]{:S(2)}) async-start(f32[16,8,128]{2,1,0:T(8,128)} %gram.1), calls=%async_computation | async-start | bytes 131072 | tf_op jit(solution)/shard_map/all_to_all | solution.py:435
  54.3 1.3 %collective-permute-start.12 = (f32[32,512]{1,0:T(8,128)S(1)}, f32[32,512]{1,0:T(8,128)S(1)}, u32[]{:S(2)}, u32[]{:S(2)}) collective-permute-start(f32[32,512]{1,0:T(8,128)S(1)} %image.1.image_ref.mine_ref), channel_id=1, source_target_pairs={{0,1},{1,0},{2,3},{3,2},{4,5},{5,4},{6,7},{7,6},{8,9},{9,8},{10,11... | collective-permute-start | bytes 196616 | tf_op jit(solution)/shard_map/ppermute | solution.py:434

commit v15 on v13

--- a/solution.py
+++ b/solution.py
@@ -26,9 +26,10 @@
 CHUNK = 256
 OUT_ROWS = 40
 COST = 1
+LAST_COST = 4 * 1024 * 1024 * 1024
 WIDE = 512
 GROUP = 16
-SWAPS = 2
+SWAPS = 3
 VMEM_LIMIT = 48 * 1024 * 1024
 
 NT = (((1,), (1,)), ((), ()))
@@ -237,7 +238,7 @@
         col_out_ref[...] = jnp.zeros_like(col_out_ref)
 
 
-def tile(row, columns, vecs, turns=False, own_block=False, receivers=None):
+def tile(row, columns, vecs, turns=False, own_block=False, receivers=None, last=False):
     size, rows = row.shape
     cols = len(columns) * rows if turns else sum(part.shape[1] for part in columns)
     second = jax.ShapeDtypeStruct((size, cols), jnp.bfloat16)
@@ -258,7 +259,7 @@
             pltpu.VMEM((FIELDS, 8, WIDE), jnp.float32),
             pltpu.VMEM((vecs + CODE_ROWS, rows), jnp.bfloat16),
         ],
-        cost_estimate=pl.CostEstimate(flops=COST, bytes_accessed=COST, transcendentals=0),
+        cost_estimate=pl.CostEstimate(flops=LAST_COST if last else COST, bytes_accessed=COST, transcendentals=0),
         compiler_params=params(),
         name="tile",
     )(row, *columns)
@@ -400,28 +401,31 @@
     cut = beside_mine.shape[0] // SWAPS // 16 * 16
     shares = [beside_mine[at * cut : (at + 1) * cut if at < SWAPS - 1 else None] for at in range(SWAPS)]
     beside_rest = jnp.concatenate([lax.ppermute(share, "sub", swap) for share in shares], axis=0)
-    first_sums = [weigh(pack, [own], receivers=takers) for (_, takers), pack in zip(plans[:1], sent[:1])]
-    if first_sums:
-        first_sums, beside_rest = lax.optimization_barrier((first_sums, beside_rest))
-    beside_sums, next_to = weigh(mine, [beside_mine, beside_rest], turns=True)
-    parts = [own_sums, beside_sums]
-    col_sums = None
+    parts = [own_sums]
+    if not plans:
+        parts.append(weigh(mine, [beside_mine, beside_rest], turns=True)[0])
     for number, ((moves, takers), pack) in enumerate(zip(plans, sent)):
+        last = number == len(plans) - 1
         if number == 0:
-            row_sums, sums = weigh(pack, [next_to], receivers=takers)
-            row_sums = row_sums + first_sums[0][0]
-            col_sums = jnp.concatenate([first_sums[0][1], sums], axis=1)
+            own_lines, own_cols = weigh(pack, [own], receivers=takers)
+            own_lines, own_cols, beside_rest = lax.optimization_barrier((own_lines, own_cols, beside_rest))
+            beside_sums, next_to = weigh(mine, [beside_mine, beside_rest], turns=True)
+            parts.append(beside_sums)
+            next_lines, next_cols = weigh(pack, [next_to], receivers=takers)
         else:
-            pack, col_sums, parts[-1] = lax.optimization_barrier((pack, col_sums, parts[-1]))
-            row_sums, sums = weigh(pack, [own, next_to], receivers=takers)
-            col_sums = col_sums + sums
-        parts.append(lax.ppermute(row_sums, "blk", back(moves)))
-    if col_sums is not None:
-        own_mine, own_rest, next_mine, next_rest = [col_sums[:, place * half : (place + 1) * half] for place in range(4)]
-        sides = lax.ppermute(jnp.concatenate([own_rest, next_rest], axis=1), "sub", swap)
-        parts.append(own_mine)
-        parts.append(sides[:, :half])
-        parts.append(lax.ppermute(next_mine + sides[:, half:], "blk", beside))
+            pack, own_cols, next_cols = lax.optimization_barrier((pack, own_cols, next_cols))
+            next_lines, cols = weigh(pack, [next_to], receivers=takers)
+            next_cols = next_cols + cols
+            pack, next_cols, parts[-1] = lax.optimization_barrier((pack, next_cols, parts[-1]))
+            own_lines, cols = weigh(pack, [own], receivers=takers, last=last)
+            own_cols = own_cols + cols
+        if last:
+            next_rest = lax.ppermute(next_cols[:, half:], "sub", swap)
+            crossing = next_cols[:, :half] + next_rest
+            crossed = lax.ppermute(crossing, "blk", beside)
+            own_lines, _ = lax.optimization_barrier((own_lines, crossing))
+            parts += [crossed, own_cols[:, :half], lax.ppermute(own_cols[:, half:], "sub", swap)]
+        parts.append(lax.ppermute(own_lines + next_lines, "blk", back(moves)))
     image = image_of(parts, vecs)
     image_other = lax.ppermute(image, "sub", swap)
     grams = lax.all_to_all(grams_of(image, 2 * blocks), ("blk", "sub"), 0, 0, tiled=True)

time: 68.1 us -> 64.3 us (0.944)
  waiting for transfers between devices: 32.2 us -> 29.3 us
  starting transfers between devices: 17.1 us -> 16.2 us
    ppermute x2, starting transfers between devices: 7.18 us -> 4.97 us  [local(): sent = [lax.ppermute(mine, 'blk', moves) for moves, _ in plans]]
    ppermute x1, waiting for transfers between devices: 6.63 us -> 5.25 us  [local(): beside_mine = lax.ppermute(mine, 'blk', beside)]
    ppermute x2, waiting for transfers between devices: 6.88 us -> 5.9 us  [local(): sent = [lax.ppermute(mine, 'blk', moves) for moves, _ in plans]]
    ppermute x4 -> x5, starting transfers between devices: 1.99 us -> 2.47 us  [the longest x2 1.35 us: local(): parts.append(lax.ppermute(own_lines + next_lines, 'blk', back(moves)))]
    ppermute x4 -> x5, waiting for transfers between devices: 12.1 us -> 11.7 us  [the longest x2 8.39 us: local(): parts.append(lax.ppermute(own_lines + next_lines, 'blk', back(moves)))]
    pallas_call x5 -> x6, Pallas kernels: 11.6 us -> 11.7 us  [tile(): pl.pallas_call(functools.partial(tile_kernel, len(columns), turns, own_bl...]
  transfers between devices with their start and end apart: 13 -> 15, of which waited for: 8 -> 9; matrix products, arithmetic and copies ran while one was open for 3% -> 3% of each run, Pallas kernels for 17% -> 18%
where the time goes in v15:
time: 64.3 us; the launch traced here: 63.9 us
  waiting for transfers between devices  29.3 us (46%)
  starting transfers between devices  16.2 us (25%)
  Pallas kernels  16.2 us (25%)
  local copies, waits for them, and re-layouts  1.13 us (2%)
  other arithmetic  0.89 us (1%)
    pallas_call x6, Pallas kernels, tile(): pl.pallas_call(functools.partial(tile_kernel, len(columns), turns, own_bl...  11.7 us
    ppermute x2, waiting for transfers between devices, local(): parts.append(lax.ppermute(own_lines + next_lines, 'blk', back(moves)))  8.39 us
    ppermute x2, waiting for transfers between devices, local(): sent = [lax.ppermute(mine, 'blk', moves) for moves, _ in plans]  5.9 us
    all_to_all x1, waiting for transfers between devices, local(): lax.all_to_all(grams_of(image, 2 * blocks), ('blk', 'sub'), 0, 0, tiled=T...  5.58 us
    ppermute x1, waiting for transfers between devices, local(): beside_mine = lax.ppermute(mine, 'blk', beside)  5.25 us
    ppermute x2, starting transfers between devices, local(): sent = [lax.ppermute(mine, 'blk', moves) for moves, _ in plans]  4.97 us
    all_to_all x1, starting transfers between devices, local(): lax.all_to_all(grams_of(image, 2 * blocks), ('blk', 'sub'), 0, 0, tiled=T...  4.09 us
    ppermute x1, starting transfers between devices, local(): beside_mine = lax.ppermute(mine, 'blk', beside)  3.03 us
  transfers between devices with their start and end apart: 15, of which 9 were waited for; matrix products, arithmetic and copies ran while one was open for 3% of the time, Pallas kernels for 18%

profile of v15, /device:TPU:0, one launch (start us, length us, event | category | flops | bytes accessed | tf_op | source)
XLA Modules:
  0.0 63.9 jit_solution(12855356674241930534)
XLA Ops:
  0.0 0.5 collective-permute-start
  0.5 0.1 collective-permute-start.1
  0.5 1.1 %constant_dynamic-slice_fusion = (bf16[512,256]{1,0:T(8,128)(2,1)S(1)}, bf16[512,256]{1,0:T(8,128)(2,1)S(1)}) fusion(bf16[1024,256]{1,0:T(8,128)(2,1)} %param.5, s32[]{:T(128)S(6)} %select_n.7, s32[]{:T(128)S(6)} %select_n.6), kind=kLoop, calls=%fused_computation.3 | loop fusion | bytes 1048584 | tf_op jit(solution)/shard_map/dynamic_slice | solution.py:394
  1.6 0.8 %pad_add_fusion.meta_ref = s32[7,1024]{1,0:T(8,128)S(1)} fusion(s32[1,1024]{1,0:T(1,128)} %bitcast.1, s32[2,1024]{1,0:T(2,128)} %param.8, s32[4,1024]{1,0:T(4,128)} %param.7), kind=kLoop, calls=%fused_computation.2 | loop fusion | flops 14336 | bytes 57344 | tf_op jit(solution)/shard_map/concatenate | solution.py:392
  2.4 0.7 %pack.1 = (bf16[560,512]{1,0:T(8,128)(2,1)S(1)}, bf16[560,512]{1,0:T(8,128)(2,1)S(1)}) custom-call(bf16[512,256]{1,0:T(8,128)(2,1)S(1)} %get-tuple-element.64.emb_mine_ref, bf16[512,256]{1,0:T(8,128)(2,1)S(1)} %get-tuple-element.63.emb_rest_ref, bf16[1024,256]{1,0:T(8,128)(2,1)S(1)} %collective-permute-done.emb_other_ref, bf16[16,1024]{1,0:T(8,128)(2,1)S(1)} %copy-done, ...), custom_call_target="tpu_custom_call" | custom-call | tf_op jit(solution)/shard_map/pack/pallas_call | solution.py:104
  3.1 3.0 %collective-permute-start.2 = (bf16[560,512]{1,0:T(8,128)(2,1)S(1)}, bf16[560,512]{1,0:T(8,128)(2,1)S(1)}, u32[]{:S(2)}, u32[]{:S(2)}) collective-permute-start(bf16[560,512]{1,0:T(8,128)(2,1)S(1)} %get-tuple-element.33.refs_0_.refs_1_), channel_id=1, source_target_pairs={{0,2},{2,0},{4,6},{6,4},{8,10},{10,8},{12,14},{14,12},{1,3},{3,1},... | collective-permute-start | bytes 1720328 | tf_op jit(solution)/shard_map/ppermute | solution.py:397
  6.1 3.6 %collective-permute-start.3 = (bf16[560,512]{1,0:T(8,128)(2,1)S(1)}, bf16[560,512]{1,0:T(8,128)(2,1)S(1)}, u32[]{:S(2)}, u32[]{:S(2)}) collective-permute-start(bf16[560,512]{1,0:T(8,128)(2,1)S(1)} %get-tuple-element.33.refs_0_.refs_1_), channel_id=1, source_target_pairs={{4,0},{6,2},{8,4},{10,6},{12,8},{14,10},{0,12},{2,14},{5,1},{7,3},... | collective-permute-start | bytes 1720328 | tf_op jit(solution)/shard_map/ppermute | solution.py:396
  9.7 1.4 %collective-permute-start.7 = (bf16[560,512]{1,0:T(8,128)(2,1)S(1)}, bf16[560,512]{1,0:T(8,128)(2,1)S(1)}, u32[]{:S(2)}, u32[]{:S(2)}) collective-permute-start(bf16[560,512]{1,0:T(8,128)(2,1)S(1)} %get-tuple-element.33.refs_0_.refs_1_), channel_id=1, source_target_pairs={{0,8},{2,10},{12,4},{14,6},{1,9},{3,11},{13,5},{15,7},{16,24},{18,... | collective-permute-start | bytes 1720328 | tf_op jit(solution)/shard_map/ppermute | solution.py:396
  11.1 3.0 %tile.6 = (f32[40,512]{1,0:T(8,128)S(1)}, bf16[560,1024]{1,0:T(8,128)(2,1)S(1)}) custom-call(bf16[560,512]{1,0:T(8,128)(2,1)S(1)} %get-tuple-element.33.refs_0_.refs_1_, bf16[560,512]{1,0:T(8,128)(2,1)S(1)} %get-tuple-element.33.refs_0_.refs_1_, bf16[560,512]{1,0:T(8,128)(2,1)S(1)} %get-tuple-element.34.refs_2_), custom_call_target="tpu_custom_call" | custom-call | flops 1 | bytes 1 | tf_op jit(solution)/shard_map/tile/pallas_call | solution.py:247
  14.1 5.2 %collective-permute-done.2.refs_1_ = bf16[560,512]{1,0:T(8,128)(2,1)S(1)} collective-permute-done((bf16[560,512]{1,0:T(8,128)(2,1)S(1)}, bf16[560,512]{1,0:T(8,128)(2,1)S(1)}, u32[]{:S(2)}, u32[]{:S(2)}) %collective-permute-start.2) | collective-permute-done | bytes 573472 | tf_op jit(solution)/shard_map/ppermute | solution.py:397
  19.3 3.8 %collective-permute-done.3.refs_0_ = bf16[560,512]{1,0:T(8,128)(2,1)S(1)} collective-permute-done((bf16[560,512]{1,0:T(8,128)(2,1)S(1)}, bf16[560,512]{1,0:T(8,128)(2,1)S(1)}, u32[]{:S(2)}, u32[]{:S(2)}) %collective-permute-start.3) | collective-permute-done | bytes 573472 | tf_op jit(solution)/shard_map/ppermute | solution.py:396
  23.1 0.1 collective-permute-start.6
  23.2 0.6 collective-permute-start.5
  23.8 0.1 collective-permute-start.4
  23.9 2.9 %tile.7 = (f32[40,512]{1,0:T(8,128)S(1)}, f32[40,1024]{1,0:T(8,128)S(1)}) custom-call(bf16[560,512]{1,0:T(8,128)(2,1)S(1)} %collective-permute-done.3.refs_0_, bf16[560,1024]{1,0:T(8,128)(2,1)S(1)} %get-tuple-element.40.refs_1_), custom_call_target="tpu_custom_call" | custom-call | flops 1 | bytes 1 | tf_op jit(solution)/shard_map/tile/pallas_call | solution.py:247
  26.8 2.9 %tile.8 = (f32[40,512]{1,0:T(8,128)S(1)}, bf16[560,1024]{1,0:T(8,128)(2,1)S(1)}) custom-call(bf16[560,512]{1,0:T(8,128)(2,1)S(1)} %get-tuple-element.33.refs_0_.refs_1_, bf16[560,512]{1,0:T(8,128)(2,1)S(1)} %collective-permute-done.2.refs_1_, bf16[560,512]{1,0:T(8,128)(2,1)S(1)} %pad_maximum_fusion.refs_2_), custom_call_target="tpu_custom_call" | custom-call | flops 1 | bytes 1 | tf_op jit(solution)/shard_map/tile/pallas_call | solution.py:247
  29.7 2.9 %tile.9 = (f32[40,512]{1,0:T(8,128)S(1)}, f32[40,1024]{1,0:T(8,128)S(1)}) custom-call(bf16[560,512]{1,0:T(8,128)(2,1)S(1)} %collective-permute-done.3.refs_0_, bf16[560,1024]{1,0:T(8,128)(2,1)S(1)} %get-tuple-element.46.refs_1_), custom_call_target="tpu_custom_call" | custom-call | flops 1 | bytes 1 | tf_op jit(solution)/shard_map/tile/pallas_call | solution.py:247
  32.6 0.1 collective-permute-start.8
  32.7 2.1 %collective-permute-done.7.refs_0_ = bf16[560,512]{1,0:T(8,128)(2,1)S(1)} collective-permute-done((bf16[560,512]{1,0:T(8,128)(2,1)S(1)}, bf16[560,512]{1,0:T(8,128)(2,1)S(1)}, u32[]{:S(2)}, u32[]{:S(2)}) %collective-permute-start.7) | collective-permute-done | bytes 573472 | tf_op jit(solution)/shard_map/ppermute | solution.py:396
  34.9 5.1 %collective-permute-done.8.refs_2_ = f32[40,512]{1,0:T(8,128)S(1)} collective-permute-done((f32[40,512]{1,0:T(8,128)S(1)}, f32[40,512]{1,0:T(8,128)S(1)}, u32[]{:S(2)}, u32[]{:S(2)}) %collective-permute-start.8) | collective-permute-done | bytes 81952 | tf_op jit(solution)/shard_map/ppermute | solution.py:428
  40.1 0.5 collective-permute-start.11
  40.6 0.6 collective-permute-done.9
  41.3 0.6 collective-permute-start.10
  41.9 1.3 %collective-permute-start.12 = (f32[40,512]{1,0:T(8,128)S(1)}, f32[40,512]{1,0:T(8,128)S(1)}, u32[]{:S(2)}, u32[]{:S(2)}) collective-permute-start(f32[40,512]{1,0:T(8,128)S(1)} %add.27), channel_id=1, source_target_pairs={{8,0},{10,2},{4,12},{6,14},{9,1},{11,3},{5,13},{7,15},{24,16},{26,... | collective-permute-start | bytes 245768 | tf_op jit(solution)/shard_map/ppermute | solution.py:428
  43.2 2.7 %collective-permute-done.10.refs_3_ = f32[40,512]{1,0:T(8,128)S(1)} collective-permute-done((f32[40,512]{1,0:T(8,128)S(1)}, f32[40,512]{1,0:T(8,128)S(1)}, u32[]{:S(2)}, u32[]{:S(2)}) %collective-permute-start.10) | collective-permute-done | bytes 81952 | tf_op jit(solution)/shard_map/ppermute | solution.py:425
  45.9 3.3 %collective-permute-done.12.refs_6_ = f32[40,512]{1,0:T(8,128)S(1)} collective-permute-done((f32[40,512]{1,0:T(8,128)S(1)}, f32[40,512]{1,0:T(8,128)S(1)}, u32[]{:S(2)}, u32[]{:S(2)}) %collective-permute-start.12) | collective-permute-done | bytes 81952 | tf_op jit(solution)/shard_map/ppermute | solution.py:428
  49.2 0.9 %gram.1 = f32[16,8,128]{2,1,0:T(8,128)} custom-call(f32[32,512]{1,0:T(8,128)S(1)} %image.1.image_ref.mine_ref), custom_call_target="tpu_custom_call" | custom-call | tf_op jit(solution)/shard_map/gram/pallas_call | solution.py:301
  50.0 4.1 %all-to-all-start = ((f32[16,8,128]{2,1,0:T(8,128)}), f32[16,8,128]{2,1,0:T(8,128)S(1)}, u32[]{:S(2)}, u32[]{:S(2)}) async-start(f32[16,8,128]{2,1,0:T(8,128)} %gram.1), calls=%async_computation | async-start | bytes 131072 | tf_op jit(solution)/shard_map/all_to_all | solution.py:431
  54.1 0.4 collective-permute-start.13
  54.6 0.9 %collective-permute-done.13.other_ref = f32[32,512]{1,0:T(8,128)S(1)} collective-permute-done((f32[32,512]{1,0:T(8,128)S(1)}, f32[32,512]{1,0:T(8,128)S(1)}, u32[]{:S(2)}, u32[]{:S(2)}) %collective-permute-start.13) | collective-permute-done | bytes 65568 | tf_op jit(solution)/shard_map/ppermute | solution.py:430
  55.5 5.6 %all-to-all-done.grams_ref = f32[16,8,128]{2,1,0:T(8,128)S(1)} async-done(((f32[16,8,128]{2,1,0:T(8,128)}), f32[16,8,128]{2,1,0:T(8,128)S(1)}, u32[]{:S(2)}, u32[]{:S(2)}) %all-to-all-start) | async-done | bytes 65568 | tf_op jit(solution)/shard_map/all_to_all | solution.py:431
  61.0 2.9 %basis.1 = f32[16,1024]{1,0:T(8,128)} custom-call(f32[16,8,128]{2,1,0:T(8,128)S(1)} %all-to-all-done.grams_ref, f32[32,512]{1,0:T(8,128)S(1)} %image.1.image_ref.mine_ref, f32[32,512]{1,0:T(8,128)S(1)} %collective-permute-done.13.other_ref), custom_call_target="tpu_custom_call" | custom-call | tf_op jit(solution)/shard_map/basis/pallas_call | solution.py:351
  (22 shorter events, 0.3 us)
Async XLA Ops:
  0.0 2.4 %copy-start = (bf16[16,1024]{1,0:T(8,128)(2,1)S(1)}, bf16[16,1024]{1,0:T(8,128)(2,1)}, u32[]{:S(2)}) copy-start(bf16[16,1024]{1,0:T(8,128)(2,1)} %vec_ref.1) | copy-start | bytes 98308
  0.0 2.4 %collective-permute-start = (bf16[1024,256]{1,0:T(8,128)(2,1)}, bf16[1024,256]{1,0:T(8,128)(2,1)S(1)}, u32[]{:S(2)}, u32[]{:S(2)}) collective-permute-start(bf16[1024,256]{1,0:T(8,128)(2,1)} %param.5), channel_id=1, source_target_pairs={{0,1},{1,0},{2,3},{3,2},{4,5},{5,4},{6,7},{7,6},{8,9},{9,8},{10,11... | collective-permute-start | bytes 1572872 | tf_op jit(solution)/shard_map/ppermute | solution.py:390
  0.5 1.9 %collective-permute-start.1 = (bf16[16,1024]{1,0:T(8,128)(2,1)}, bf16[16,1024]{1,0:T(8,128)(2,1)S(1)}, u32[]{:S(2)}, u32[]{:S(2)}) collective-permute-start(bf16[16,1024]{1,0:T(8,128)(2,1)} %vec_ref.1), channel_id=1, source_target_pairs={{0,1},{1,0},{2,3},{3,2},{4,5},{5,4},{6,7},{7,6},{8,9},{9,8},{10,11... | collective-permute-start | bytes 98312 | tf_op jit(solution)/shard_map/ppermute | solution.py:391
  3.1 16.2 %collective-permute-start.2 = (bf16[560,512]{1,0:T(8,128)(2,1)S(1)}, bf16[560,512]{1,0:T(8,128)(2,1)S(1)}, u32[]{:S(2)}, u32[]{:S(2)}) collective-permute-start(bf16[560,512]{1,0:T(8,128)(2,1)S(1)} %get-tuple-element.33.refs_0_.refs_1_), channel_id=1, source_target_pairs={{0,2},{2,0},{4,6},{6,4},{8,10},{10,8},{12,14},{14,12},{1,3},{3,1},... | collective-permute-start | bytes 1720328 | tf_op jit(solution)/shard_map/ppermute | solution.py:397
  6.1 17.0 %collective-permute-start.3 = (bf16[560,512]{1,0:T(8,128)(2,1)S(1)}, bf16[560,512]{1,0:T(8,128)(2,1)S(1)}, u32[]{:S(2)}, u32[]{:S(2)}) collective-permute-start(bf16[560,512]{1,0:T(8,128)(2,1)S(1)} %get-tuple-element.33.refs_0_.refs_1_), channel_id=1, source_target_pairs={{4,0},{6,2},{8,4},{10,6},{12,8},{14,10},{0,12},{2,14},{5,1},{7,3},... | collective-permute-start | bytes 1720328 | tf_op jit(solution)/shard_map/ppermute | solution.py:396
  9.7 25.1 %collective-permute-start.7 = (bf16[560,512]{1,0:T(8,128)(2,1)S(1)}, bf16[560,512]{1,0:T(8,128)(2,1)S(1)}, u32[]{:S(2)}, u32[]{:S(2)}) collective-permute-start(bf16[560,512]{1,0:T(8,128)(2,1)S(1)} %get-tuple-element.33.refs_0_.refs_1_), channel_id=1, source_target_pairs={{0,8},{2,10},{12,4},{14,6},{1,9},{3,11},{13,5},{15,7},{16,24},{18,... | collective-permute-start | bytes 1720328 | tf_op jit(solution)/shard_map/ppermute | solution.py:396
  23.1 3.6 %collective-permute-start.6 = (bf16[208,512]{1,0:T(8,128)(2,1)S(1)}, bf16[208,512]{1,0:T(8,128)(2,1)S(1)}, u32[]{:S(2)}, u32[]{:S(2)}) collective-permute-start(bf16[208,512]{1,0:T(8,128)(2,1)S(1)} %slice.23), channel_id=1, source_target_pairs={{0,1},{1,0},{2,3},{3,2},{4,5},{5,4},{6,7},{7,6},{8,9},{9,8},{10,11... | collective-permute-start | bytes 638984 | tf_op jit(solution)/shard_map/ppermute | solution.py:403
  23.2 3.5 %collective-permute-start.5 = (bf16[176,512]{1,0:T(8,128)(2,1)S(1)}, bf16[176,512]{1,0:T(8,128)(2,1)S(1)}, u32[]{:S(2)}, u32[]{:S(2)}) collective-permute-start(bf16[176,512]{1,0:T(8,128)(2,1)S(1)} %get-tuple-element.62), channel_id=1, source_target_pairs={{0,1},{1,0},{2,3},{3,2},{4,5},{5,4},{6,7},{7,6},{8,9},{9,8},{10,11... | collective-permute-start | bytes 540680 | tf_op jit(solution)/shard_map/ppermute | solution.py:403
  23.8 3.0 %collective-permute-start.4 = (bf16[176,512]{1,0:T(8,128)(2,1)S(1)}, bf16[176,512]{1,0:T(8,128)(2,1)S(1)}, u32[]{:S(2)}, u32[]{:S(2)}) collective-permute-start(bf16[176,512]{1,0:T(8,128)(2,1)S(1)} %get-tuple-element.61), channel_id=1, source_target_pairs={{0,1},{1,0},{2,3},{3,2},{4,5},{5,4},{6,7},{7,6},{8,9},{9,8},{10,11... | collective-permute-start | bytes 540680 | tf_op jit(solution)/shard_map/ppermute | solution.py:403
  32.6 7.4 %collective-permute-start.8 = (f32[40,512]{1,0:T(8,128)S(1)}, f32[40,512]{1,0:T(8,128)S(1)}, u32[]{:S(2)}, u32[]{:S(2)}) collective-permute-start(f32[40,512]{1,0:T(8,128)S(1)} %add.24), channel_id=1, source_target_pairs={{0,4},{2,6},{4,8},{6,10},{8,12},{10,14},{12,0},{14,2},{1,5},{3,7},... | collective-permute-start | bytes 245768 | tf_op jit(solution)/shard_map/ppermute | solution.py:428
  40.0 1.3 %collective-permute-start.9 = (f32[40,512]{1,0:T(8,128)S(1)}, f32[40,512]{1,0:T(8,128)S(1)}, u32[]{:S(2)}, u32[]{:S(2)}) collective-permute-start(f32[40,512]{1,0:T(8,128)S(1)} %slice.25), channel_id=1, source_target_pairs={{0,1},{1,0},{2,3},{3,2},{4,5},{5,4},{6,7},{7,6},{8,9},{9,8},{10,11... | collective-permute-start | bytes 245768 | tf_op jit(solution)/shard_map/ppermute | solution.py:423
  40.1 3.1 %collective-permute-start.11 = (f32[40,512]{1,0:T(8,128)S(1)}, f32[40,512]{1,0:T(8,128)S(1)}, u32[]{:S(2)}, u32[]{:S(2)}) collective-permute-start(f32[40,512]{1,0:T(8,128)S(1)} %get-tuple-element.65), channel_id=1, source_target_pairs={{0,1},{1,0},{2,3},{3,2},{4,5},{5,4},{6,7},{7,6},{8,9},{9,8},{10,11... | collective-permute-start | bytes 245768 | tf_op jit(solution)/shard_map/ppermute | solution.py:427
  41.3 4.6 %collective-permute-start.10 = (f32[40,512]{1,0:T(8,128)S(1)}, f32[40,512]{1,0:T(8,128)S(1)}, u32[]{:S(2)}, u32[]{:S(2)}) collective-permute-start(f32[40,512]{1,0:T(8,128)S(1)} %slice_add_fusion), channel_id=1, source_target_pairs={{0,2},{2,0},{4,6},{6,4},{8,10},{10,8},{12,14},{14,12},{1,3},{3,1},... | collective-permute-start | bytes 245768 | tf_op jit(solution)/shard_map/ppermute | solution.py:425
  41.9 7.2 %collective-permute-start.12 = (f32[40,512]{1,0:T(8,128)S(1)}, f32[40,512]{1,0:T(8,128)S(1)}, u32[]{:S(2)}, u32[]{:S(2)}) collective-permute-start(f32[40,512]{1,0:T(8,128)S(1)} %add.27), channel_id=1, source_target_pairs={{8,0},{10,2},{4,12},{6,14},{9,1},{11,3},{5,13},{7,15},{24,16},{26,... | collective-permute-start | bytes 245768 | tf_op jit(solution)/shard_map/ppermute | solution.py:428
  50.0 11.0 %all-to-all-start = ((f32[16,8,128]{2,1,0:T(8,128)}), f32[16,8,128]{2,1,0:T(8,128)S(1)}, u32[]{:S(2)}, u32[]{:S(2)}) async-start(f32[16,8,128]{2,1,0:T(8,128)} %gram.1), calls=%async_computation | async-start | bytes 131072 | tf_op jit(solution)/shard_map/all_to_all | solution.py:431
  54.1 1.3 %collective-permute-start.13 = (f32[32,512]{1,0:T(8,128)S(1)}, f32[32,512]{1,0:T(8,128)S(1)}, u32[]{:S(2)}, u32[]{:S(2)}) collective-permute-start(f32[32,512]{1,0:T(8,128)S(1)} %image.1.image_ref.mine_ref), channel_id=1, source_target_pairs={{0,1},{1,0},{2,3},{3,2},{4,5},{5,4},{6,7},{7,6},{8,9},{9,8},{10,11... | collective-permute-start | bytes 196616 | tf_op jit(solution)/shard_map/ppermute | solution.py:430

commit v16 on v15

--- a/solution.py
+++ b/solution.py
@@ -360,6 +360,8 @@
 
 
 def exchanges(pairs):
+    if pairs == 4:
+        return [([(0, 2), (3, 1), (1, 0), (2, 3)], None), ([(2, 1), (0, 3)], [1, 3])]
     plans = []
     for distance in range(1, pairs // 2):
         plans.append(([((p + distance) % pairs, p) for p in range(pairs)], None))

time: 64.3 us -> 62.8 us (0.977)
  waiting for transfers between devices: 29.3 us -> 26.4 us
  starting transfers between devices: 16.2 us -> 17.6 us
    ppermute x2, waiting for transfers between devices: 5.9 us -> 3.02 us  [local(): sent = [lax.ppermute(mine, 'blk', moves) for moves, _ in plans]]
    ppermute x2, starting transfers between devices: 1.35 us -> 2.61 us  [local(): parts.append(lax.ppermute(own_lines + next_lines, 'blk', back(moves)))]
    ppermute x2, starting transfers between devices: 4.97 us -> 5.87 us  [local(): sent = [lax.ppermute(mine, 'blk', moves) for moves, _ in plans]]
    ppermute x1, waiting for transfers between devices: 5.25 us -> 4.35 us  [local(): beside_mine = lax.ppermute(mine, 'blk', beside)]
    ppermute x2, waiting for transfers between devices: 8.39 us -> 9.16 us  [local(): parts.append(lax.ppermute(own_lines + next_lines, 'blk', back(moves)))]
  transfers between devices with their start and end apart: 15 -> 15, of which waited for: 9 -> 9; matrix products, arithmetic and copies ran while one was open for 3% -> 3% of each run, Pallas kernels for 18% -> 19%
where the time goes in v16:
time: 62.8 us; the launch traced here: 62.4 us
  waiting for transfers between devices  26.4 us (42%)
  starting transfers between devices  17.6 us (28%)
  Pallas kernels  16.2 us (26%)
  local copies, waits for them, and re-layouts  1.13 us (2%)
  other arithmetic  0.89 us (1%)
    pallas_call x6, Pallas kernels, tile(): pl.pallas_call(functools.partial(tile_kernel, len(columns), turns, own_bl...  11.7 us
    ppermute x2, waiting for transfers between devices, local(): parts.append(lax.ppermute(own_lines + next_lines, 'blk', back(moves)))  9.16 us
    ppermute x2, starting transfers between devices, local(): sent = [lax.ppermute(mine, 'blk', moves) for moves, _ in plans]  5.87 us
    all_to_all x1, waiting for transfers between devices, local(): lax.all_to_all(grams_of(image, 2 * blocks), ('blk', 'sub'), 0, 0, tiled=T...  5.54 us
    ppermute x1, waiting for transfers between devices, local(): beside_mine = lax.ppermute(mine, 'blk', beside)  4.35 us
    all_to_all x1, starting transfers between devices, local(): lax.all_to_all(grams_of(image, 2 * blocks), ('blk', 'sub'), 0, 0, tiled=T...  3.5 us
    ppermute x1, starting transfers between devices, local(): beside_mine = lax.ppermute(mine, 'blk', beside)  3.03 us
    ppermute x2, waiting for transfers between devices, local(): sent = [lax.ppermute(mine, 'blk', moves) for moves, _ in plans]  3.02 us
  transfers between devices with their start and end apart: 15, of which 9 were waited for; matrix products, arithmetic and copies ran while one was open for 3% of the time, Pallas kernels for 19%

profile of v16, /device:TPU:0, one launch (start us, length us, event | category | flops | bytes accessed | tf_op | source)
XLA Modules:
  0.0 62.4 jit_solution(2262640470593827845)
XLA Ops:
  0.0 0.5 collective-permute-start
  0.5 0.1 collective-permute-start.1
  0.5 1.1 %constant_dynamic-slice_fusion = (bf16[512,256]{1,0:T(8,128)(2,1)S(1)}, bf16[512,256]{1,0:T(8,128)(2,1)S(1)}) fusion(bf16[1024,256]{1,0:T(8,128)(2,1)} %param.5, s32[]{:T(128)S(6)} %select_n.7, s32[]{:T(128)S(6)} %select_n.6), kind=kLoop, calls=%fused_computation.3 | loop fusion | bytes 1048584 | tf_op jit(solution)/shard_map/dynamic_slice | solution.py:396
  1.6 0.8 %pad_add_fusion.meta_ref = s32[7,1024]{1,0:T(8,128)S(1)} fusion(s32[1,1024]{1,0:T(1,128)} %bitcast.1, s32[2,1024]{1,0:T(2,128)} %param.8, s32[4,1024]{1,0:T(4,128)} %param.7), kind=kLoop, calls=%fused_computation.2 | loop fusion | flops 14336 | bytes 57344 | tf_op jit(solution)/shard_map/concatenate | solution.py:394
  2.4 0.7 %pack.1 = (bf16[560,512]{1,0:T(8,128)(2,1)S(1)}, bf16[560,512]{1,0:T(8,128)(2,1)S(1)}) custom-call(bf16[512,256]{1,0:T(8,128)(2,1)S(1)} %get-tuple-element.64.emb_mine_ref, bf16[512,256]{1,0:T(8,128)(2,1)S(1)} %get-tuple-element.63.emb_rest_ref, bf16[1024,256]{1,0:T(8,128)(2,1)S(1)} %collective-permute-done.emb_other_ref, bf16[16,1024]{1,0:T(8,128)(2,1)S(1)} %copy-done, ...), custom_call_target="tpu_custom_call" | custom-call | tf_op jit(solution)/shard_map/pack/pallas_call | solution.py:104
  3.1 3.0 %collective-permute-start.2 = (bf16[560,512]{1,0:T(8,128)(2,1)S(1)}, bf16[560,512]{1,0:T(8,128)(2,1)S(1)}, u32[]{:S(2)}, u32[]{:S(2)}) collective-permute-start(bf16[560,512]{1,0:T(8,128)(2,1)S(1)} %get-tuple-element.33.refs_0_.refs_1_), channel_id=1, source_target_pairs={{0,2},{2,0},{4,6},{6,4},{8,10},{10,8},{12,14},{14,12},{1,3},{3,1},... | collective-permute-start | bytes 1720328 | tf_op jit(solution)/shard_map/ppermute | solution.py:399
  6.1 2.6 %collective-permute-start.3 = (bf16[560,512]{1,0:T(8,128)(2,1)S(1)}, bf16[560,512]{1,0:T(8,128)(2,1)S(1)}, u32[]{:S(2)}, u32[]{:S(2)}) collective-permute-start(bf16[560,512]{1,0:T(8,128)(2,1)S(1)} %get-tuple-element.33.refs_0_.refs_1_), channel_id=1, source_target_pairs={{0,8},{2,10},{12,4},{14,6},{4,0},{6,2},{8,12},{10,14},{1,9},{3,11}... | collective-permute-start | bytes 1720328 | tf_op jit(solution)/shard_map/ppermute | solution.py:398
  8.7 3.3 %collective-permute-start.7 = (bf16[560,512]{1,0:T(8,128)(2,1)S(1)}, bf16[560,512]{1,0:T(8,128)(2,1)S(1)}, u32[]{:S(2)}, u32[]{:S(2)}) collective-permute-start(bf16[560,512]{1,0:T(8,128)(2,1)S(1)} %get-tuple-element.33.refs_0_.refs_1_), channel_id=1, source_target_pairs={{8,4},{10,6},{0,12},{2,14},{9,5},{11,7},{1,13},{3,15},{24,20},{26,... | collective-permute-start | bytes 1720328 | tf_op jit(solution)/shard_map/ppermute | solution.py:398
  12.0 3.0 %tile.6 = (f32[40,512]{1,0:T(8,128)S(1)}, bf16[560,1024]{1,0:T(8,128)(2,1)S(1)}) custom-call(bf16[560,512]{1,0:T(8,128)(2,1)S(1)} %get-tuple-element.33.refs_0_.refs_1_, bf16[560,512]{1,0:T(8,128)(2,1)S(1)} %get-tuple-element.33.refs_0_.refs_1_, bf16[560,512]{1,0:T(8,128)(2,1)S(1)} %get-tuple-element.34.refs_2_), custom_call_target="tpu_custom_call" | custom-call | flops 1 | bytes 1 | tf_op jit(solution)/shard_map/tile/pallas_call | solution.py:247
  15.0 4.4 %collective-permute-done.2.refs_1_ = bf16[560,512]{1,0:T(8,128)(2,1)S(1)} collective-permute-done((bf16[560,512]{1,0:T(8,128)(2,1)S(1)}, bf16[560,512]{1,0:T(8,128)(2,1)S(1)}, u32[]{:S(2)}, u32[]{:S(2)}) %collective-permute-start.2) | collective-permute-done | bytes 573472 | tf_op jit(solution)/shard_map/ppermute | solution.py:399
  19.3 2.8 %collective-permute-done.3.refs_0_ = bf16[560,512]{1,0:T(8,128)(2,1)S(1)} collective-permute-done((bf16[560,512]{1,0:T(8,128)(2,1)S(1)}, bf16[560,512]{1,0:T(8,128)(2,1)S(1)}, u32[]{:S(2)}, u32[]{:S(2)}) %collective-permute-start.3) | collective-permute-done | bytes 573472 | tf_op jit(solution)/shard_map/ppermute | solution.py:398
  22.1 0.1 collective-permute-start.6
  22.2 0.6 collective-permute-start.5
  22.8 0.1 collective-permute-start.4
  22.9 2.9 %tile.7 = (f32[40,512]{1,0:T(8,128)S(1)}, f32[40,1024]{1,0:T(8,128)S(1)}) custom-call(bf16[560,512]{1,0:T(8,128)(2,1)S(1)} %collective-permute-done.3.refs_0_, bf16[560,1024]{1,0:T(8,128)(2,1)S(1)} %get-tuple-element.40.refs_1_), custom_call_target="tpu_custom_call" | custom-call | flops 1 | bytes 1 | tf_op jit(solution)/shard_map/tile/pallas_call | solution.py:247
  25.8 2.9 %tile.8 = (f32[40,512]{1,0:T(8,128)S(1)}, bf16[560,1024]{1,0:T(8,128)(2,1)S(1)}) custom-call(bf16[560,512]{1,0:T(8,128)(2,1)S(1)} %get-tuple-element.33.refs_0_.refs_1_, bf16[560,512]{1,0:T(8,128)(2,1)S(1)} %collective-permute-done.2.refs_1_, bf16[560,512]{1,0:T(8,128)(2,1)S(1)} %pad_maximum_fusion.refs_2_), custom_call_target="tpu_custom_call" | custom-call | flops 1 | bytes 1 | tf_op jit(solution)/shard_map/tile/pallas_call | solution.py:247
  28.7 2.9 %tile.9 = (f32[40,512]{1,0:T(8,128)S(1)}, f32[40,1024]{1,0:T(8,128)S(1)}) custom-call(bf16[560,512]{1,0:T(8,128)(2,1)S(1)} %collective-permute-done.3.refs_0_, bf16[560,1024]{1,0:T(8,128)(2,1)S(1)} %get-tuple-element.46.refs_1_), custom_call_target="tpu_custom_call" | custom-call | flops 1 | bytes 1 | tf_op jit(solution)/shard_map/tile/pallas_call | solution.py:247
  31.6 1.3 %collective-permute-start.8 = (f32[40,512]{1,0:T(8,128)S(1)}, f32[40,512]{1,0:T(8,128)S(1)}, u32[]{:S(2)}, u32[]{:S(2)}) collective-permute-start(f32[40,512]{1,0:T(8,128)S(1)} %add.24), channel_id=1, source_target_pairs={{8,0},{10,2},{4,12},{6,14},{0,4},{2,6},{12,8},{14,10},{9,1},{11,3}... | collective-permute-start | bytes 245768 | tf_op jit(solution)/shard_map/ppermute | solution.py:430
  32.9 0.2 collective-permute-done.7.refs_0_
  33.2 4.9 %collective-permute-done.8.refs_2_ = f32[40,512]{1,0:T(8,128)S(1)} collective-permute-done((f32[40,512]{1,0:T(8,128)S(1)}, f32[40,512]{1,0:T(8,128)S(1)}, u32[]{:S(2)}, u32[]{:S(2)}) %collective-permute-start.8) | collective-permute-done | bytes 81952 | tf_op jit(solution)/shard_map/ppermute | solution.py:430
  38.2 0.5 collective-permute-start.11
  38.7 0.6 %collective-permute-done.9 = f32[40,512]{1,0:T(8,128)S(1)} collective-permute-done((f32[40,512]{1,0:T(8,128)S(1)}, f32[40,512]{1,0:T(8,128)S(1)}, u32[]{:S(2)}, u32[]{:S(2)}) %collective-permute-start.9) | collective-permute-done | bytes 81952 | tf_op jit(solution)/shard_map/ppermute | solution.py:425
  39.4 0.6 collective-permute-start.10
  40.0 1.3 %collective-permute-start.12 = (f32[40,512]{1,0:T(8,128)S(1)}, f32[40,512]{1,0:T(8,128)S(1)}, u32[]{:S(2)}, u32[]{:S(2)}) collective-permute-start(f32[40,512]{1,0:T(8,128)S(1)} %add.27), channel_id=1, source_target_pairs={{4,8},{6,10},{12,0},{14,2},{5,9},{7,11},{13,1},{15,3},{20,24},{22,... | collective-permute-start | bytes 245768 | tf_op jit(solution)/shard_map/ppermute | solution.py:430
  41.3 2.7 %collective-permute-done.10.refs_3_ = f32[40,512]{1,0:T(8,128)S(1)} collective-permute-done((f32[40,512]{1,0:T(8,128)S(1)}, f32[40,512]{1,0:T(8,128)S(1)}, u32[]{:S(2)}, u32[]{:S(2)}) %collective-permute-start.10) | collective-permute-done | bytes 81952 | tf_op jit(solution)/shard_map/ppermute | solution.py:427
  44.0 4.3 %collective-permute-done.12.refs_6_ = f32[40,512]{1,0:T(8,128)S(1)} collective-permute-done((f32[40,512]{1,0:T(8,128)S(1)}, f32[40,512]{1,0:T(8,128)S(1)}, u32[]{:S(2)}, u32[]{:S(2)}) %collective-permute-start.12) | collective-permute-done | bytes 81952 | tf_op jit(solution)/shard_map/ppermute | solution.py:430
  48.3 0.9 %gram.1 = f32[16,8,128]{2,1,0:T(8,128)} custom-call(f32[32,512]{1,0:T(8,128)S(1)} %image.1.image_ref.mine_ref), custom_call_target="tpu_custom_call" | custom-call | tf_op jit(solution)/shard_map/gram/pallas_call | solution.py:301
  49.2 3.5 %all-to-all-start = ((f32[16,8,128]{2,1,0:T(8,128)}), f32[16,8,128]{2,1,0:T(8,128)S(1)}, u32[]{:S(2)}, u32[]{:S(2)}) async-start(f32[16,8,128]{2,1,0:T(8,128)} %gram.1), calls=%async_computation | async-start | bytes 131072 | tf_op jit(solution)/shard_map/all_to_all | solution.py:433
  52.7 0.3 collective-permute-start.13
  53.0 1.0 %collective-permute-done.13.other_ref = f32[32,512]{1,0:T(8,128)S(1)} collective-permute-done((f32[32,512]{1,0:T(8,128)S(1)}, f32[32,512]{1,0:T(8,128)S(1)}, u32[]{:S(2)}, u32[]{:S(2)}) %collective-permute-start.13) | collective-permute-done | bytes 65568 | tf_op jit(solution)/shard_map/ppermute | solution.py:432
  54.0 5.5 %all-to-all-done.grams_ref = f32[16,8,128]{2,1,0:T(8,128)S(1)} async-done(((f32[16,8,128]{2,1,0:T(8,128)}), f32[16,8,128]{2,1,0:T(8,128)S(1)}, u32[]{:S(2)}, u32[]{:S(2)}) %all-to-all-start) | async-done | bytes 65568 | tf_op jit(solution)/shard_map/all_to_all | solution.py:433
  59.6 2.9 %basis.1 = f32[16,1024]{1,0:T(8,128)} custom-call(f32[16,8,128]{2,1,0:T(8,128)S(1)} %all-to-all-done.grams_ref, f32[32,512]{1,0:T(8,128)S(1)} %image.1.image_ref.mine_ref, f32[32,512]{1,0:T(8,128)S(1)} %collective-permute-done.13.other_ref), custom_call_target="tpu_custom_call" | custom-call | tf_op jit(solution)/shard_map/basis/pallas_call | solution.py:351
  (22 shorter events, 0.3 us)
Async XLA Ops:
  0.0 2.4 %copy-start = (bf16[16,1024]{1,0:T(8,128)(2,1)S(1)}, bf16[16,1024]{1,0:T(8,128)(2,1)}, u32[]{:S(2)}) copy-start(bf16[16,1024]{1,0:T(8,128)(2,1)} %vec_ref.1) | copy-start | bytes 98308
  0.0 2.4 %collective-permute-start = (bf16[1024,256]{1,0:T(8,128)(2,1)}, bf16[1024,256]{1,0:T(8,128)(2,1)S(1)}, u32[]{:S(2)}, u32[]{:S(2)}) collective-permute-start(bf16[1024,256]{1,0:T(8,128)(2,1)} %param.5), channel_id=1, source_target_pairs={{0,1},{1,0},{2,3},{3,2},{4,5},{5,4},{6,7},{7,6},{8,9},{9,8},{10,11... | collective-permute-start | bytes 1572872 | tf_op jit(solution)/shard_map/ppermute | solution.py:392
  0.5 1.9 %collective-permute-start.1 = (bf16[16,1024]{1,0:T(8,128)(2,1)}, bf16[16,1024]{1,0:T(8,128)(2,1)S(1)}, u32[]{:S(2)}, u32[]{:S(2)}) collective-permute-start(bf16[16,1024]{1,0:T(8,128)(2,1)} %vec_ref.1), channel_id=1, source_target_pairs={{0,1},{1,0},{2,3},{3,2},{4,5},{5,4},{6,7},{7,6},{8,9},{9,8},{10,11... | collective-permute-start | bytes 98312 | tf_op jit(solution)/shard_map/ppermute | solution.py:393
  3.1 16.2 %collective-permute-start.2 = (bf16[560,512]{1,0:T(8,128)(2,1)S(1)}, bf16[560,512]{1,0:T(8,128)(2,1)S(1)}, u32[]{:S(2)}, u32[]{:S(2)}) collective-permute-start(bf16[560,512]{1,0:T(8,128)(2,1)S(1)} %get-tuple-element.33.refs_0_.refs_1_), channel_id=1, source_target_pairs={{0,2},{2,0},{4,6},{6,4},{8,10},{10,8},{12,14},{14,12},{1,3},{3,1},... | collective-permute-start | bytes 1720328 | tf_op jit(solution)/shard_map/ppermute | solution.py:399
  6.1 16.0 %collective-permute-start.3 = (bf16[560,512]{1,0:T(8,128)(2,1)S(1)}, bf16[560,512]{1,0:T(8,128)(2,1)S(1)}, u32[]{:S(2)}, u32[]{:S(2)}) collective-permute-start(bf16[560,512]{1,0:T(8,128)(2,1)S(1)} %get-tuple-element.33.refs_0_.refs_1_), channel_id=1, source_target_pairs={{0,8},{2,10},{12,4},{14,6},{4,0},{6,2},{8,12},{10,14},{1,9},{3,11}... | collective-permute-start | bytes 1720328 | tf_op jit(solution)/shard_map/ppermute | solution.py:398
  8.7 24.5 %collective-permute-start.7 = (bf16[560,512]{1,0:T(8,128)(2,1)S(1)}, bf16[560,512]{1,0:T(8,128)(2,1)S(1)}, u32[]{:S(2)}, u32[]{:S(2)}) collective-permute-start(bf16[560,512]{1,0:T(8,128)(2,1)S(1)} %get-tuple-element.33.refs_0_.refs_1_), channel_id=1, source_target_pairs={{8,4},{10,6},{0,12},{2,14},{9,5},{11,7},{1,13},{3,15},{24,20},{26,... | collective-permute-start | bytes 1720328 | tf_op jit(solution)/shard_map/ppermute | solution.py:398
  22.1 3.6 %collective-permute-start.6 = (bf16[208,512]{1,0:T(8,128)(2,1)S(1)}, bf16[208,512]{1,0:T(8,128)(2,1)S(1)}, u32[]{:S(2)}, u32[]{:S(2)}) collective-permute-start(bf16[208,512]{1,0:T(8,128)(2,1)S(1)} %slice.23), channel_id=1, source_target_pairs={{0,1},{1,0},{2,3},{3,2},{4,5},{5,4},{6,7},{7,6},{8,9},{9,8},{10,11... | collective-permute-start | bytes 638984 | tf_op jit(solution)/shard_map/ppermute | solution.py:405
  22.2 3.5 %collective-permute-start.5 = (bf16[176,512]{1,0:T(8,128)(2,1)S(1)}, bf16[176,512]{1,0:T(8,128)(2,1)S(1)}, u32[]{:S(2)}, u32[]{:S(2)}) collective-permute-start(bf16[176,512]{1,0:T(8,128)(2,1)S(1)} %get-tuple-element.62), channel_id=1, source_target_pairs={{0,1},{1,0},{2,3},{3,2},{4,5},{5,4},{6,7},{7,6},{8,9},{9,8},{10,11... | collective-permute-start | bytes 540680 | tf_op jit(solution)/shard_map/ppermute | solution.py:405
  22.8 3.0 %collective-permute-start.4 = (bf16[176,512]{1,0:T(8,128)(2,1)S(1)}, bf16[176,512]{1,0:T(8,128)(2,1)S(1)}, u32[]{:S(2)}, u32[]{:S(2)}) collective-permute-start(bf16[176,512]{1,0:T(8,128)(2,1)S(1)} %get-tuple-element.61), channel_id=1, source_target_pairs={{0,1},{1,0},{2,3},{3,2},{4,5},{5,4},{6,7},{7,6},{8,9},{9,8},{10,11... | collective-permute-start | bytes 540680 | tf_op jit(solution)/shard_map/ppermute | solution.py:405
  31.6 6.5 %collective-permute-start.8 = (f32[40,512]{1,0:T(8,128)S(1)}, f32[40,512]{1,0:T(8,128)S(1)}, u32[]{:S(2)}, u32[]{:S(2)}) collective-permute-start(f32[40,512]{1,0:T(8,128)S(1)} %add.24), channel_id=1, source_target_pairs={{8,0},{10,2},{4,12},{6,14},{0,4},{2,6},{12,8},{14,10},{9,1},{11,3}... | collective-permute-start | bytes 245768 | tf_op jit(solution)/shard_map/ppermute | solution.py:430
  38.1 1.3 %collective-permute-start.9 = (f32[40,512]{1,0:T(8,128)S(1)}, f32[40,512]{1,0:T(8,128)S(1)}, u32[]{:S(2)}, u32[]{:S(2)}) collective-permute-start(f32[40,512]{1,0:T(8,128)S(1)} %slice.25), channel_id=1, source_target_pairs={{0,1},{1,0},{2,3},{3,2},{4,5},{5,4},{6,7},{7,6},{8,9},{9,8},{10,11... | collective-permute-start | bytes 245768 | tf_op jit(solution)/shard_map/ppermute | solution.py:425
  38.2 3.1 %collective-permute-start.11 = (f32[40,512]{1,0:T(8,128)S(1)}, f32[40,512]{1,0:T(8,128)S(1)}, u32[]{:S(2)}, u32[]{:S(2)}) collective-permute-start(f32[40,512]{1,0:T(8,128)S(1)} %get-tuple-element.65), channel_id=1, source_target_pairs={{0,1},{1,0},{2,3},{3,2},{4,5},{5,4},{6,7},{7,6},{8,9},{9,8},{10,11... | collective-permute-start | bytes 245768 | tf_op jit(solution)/shard_map/ppermute | solution.py:429
  39.4 4.6 %collective-permute-start.10 = (f32[40,512]{1,0:T(8,128)S(1)}, f32[40,512]{1,0:T(8,128)S(1)}, u32[]{:S(2)}, u32[]{:S(2)}) collective-permute-start(f32[40,512]{1,0:T(8,128)S(1)} %slice_add_fusion), channel_id=1, source_target_pairs={{0,2},{2,0},{4,6},{6,4},{8,10},{10,8},{12,14},{14,12},{1,3},{3,1},... | collective-permute-start | bytes 245768 | tf_op jit(solution)/shard_map/ppermute | solution.py:427
  40.0 8.3 %collective-permute-start.12 = (f32[40,512]{1,0:T(8,128)S(1)}, f32[40,512]{1,0:T(8,128)S(1)}, u32[]{:S(2)}, u32[]{:S(2)}) collective-permute-start(f32[40,512]{1,0:T(8,128)S(1)} %add.27), channel_id=1, source_target_pairs={{4,8},{6,10},{12,0},{14,2},{5,9},{7,11},{13,1},{15,3},{20,24},{22,... | collective-permute-start | bytes 245768 | tf_op jit(solution)/shard_map/ppermute | solution.py:430
  49.2 10.4 %all-to-all-start = ((f32[16,8,128]{2,1,0:T(8,128)}), f32[16,8,128]{2,1,0:T(8,128)S(1)}, u32[]{:S(2)}, u32[]{:S(2)}) async-start(f32[16,8,128]{2,1,0:T(8,128)} %gram.1), calls=%async_computation | async-start | bytes 131072 | tf_op jit(solution)/shard_map/all_to_all | solution.py:433
  52.7 1.3 %collective-permute-start.13 = (f32[32,512]{1,0:T(8,128)S(1)}, f32[32,512]{1,0:T(8,128)S(1)}, u32[]{:S(2)}, u32[]{:S(2)}) collective-permute-start(f32[32,512]{1,0:T(8,128)S(1)} %image.1.image_ref.mine_ref), channel_id=1, source_target_pairs={{0,1},{1,0},{2,3},{3,2},{4,5},{5,4},{6,7},{7,6},{8,9},{9,8},{10,11... | collective-permute-start | bytes 196616 | tf_op jit(solution)/shard_map/ppermute | solution.py:432

commit v17 on v16

--- a/solution.py
+++ b/solution.py
@@ -399,7 +399,8 @@
     beside_mine = lax.ppermute(mine, "blk", beside)
     weigh = functools.partial(tile, vecs=vecs)
     own_sums, own = weigh(mine, [mine, rest], turns=True, own_block=True)
-    own_sums, own, beside_mine, sent[:1] = lax.optimization_barrier((own_sums, own, beside_mine, sent[:1]))
+    own_sums, own, sent[:1] = lax.optimization_barrier((own_sums, own, sent[:1]))
+    beside_mine, sent[:1] = lax.optimization_barrier((beside_mine, sent[:1]))
     cut = beside_mine.shape[0] // SWAPS // 16 * 16
     shares = [beside_mine[at * cut : (at + 1) * cut if at < SWAPS - 1 else None] for at in range(SWAPS)]
     beside_rest = jnp.concatenate([lax.ppermute(share, "sub", swap) for share in shares], axis=0)

time: 62.8 us -> 62.7 us (level)
    ppermute x1, waiting for transfers between devices: 4.35 us -> 1.31 us  [local(): beside_mine = lax.ppermute(mine, 'blk', beside)]
    ppermute x2, waiting for transfers between devices: 3.02 us -> 5.81 us  [local(): sent = [lax.ppermute(mine, 'blk', moves) for moves, _ in plans]]
    ppermute x1, starting transfers between devices: 3.03 us -> 1.52 us  [local(): beside_mine = lax.ppermute(mine, 'blk', beside)]
    ppermute x2, starting transfers between devices: 5.87 us -> 7.36 us  [local(): sent = [lax.ppermute(mine, 'blk', moves) for moves, _ in plans]]
    ppermute x2, waiting for transfers between devices: 9.16 us -> 10.3 us  [local(): parts.append(lax.ppermute(own_lines + next_lines, 'blk', back(moves)))]
    ppermute x1, starting transfers between devices: 0.56 us -> 1.58 us  [local(): crossed = lax.ppermute(crossing, 'blk', beside)]
    ppermute x1, waiting for transfers between devices: 2.68 us -> 1.66 us  [local(): crossed = lax.ppermute(crossing, 'blk', beside)]
    ppermute x2, starting transfers between devices: 2.61 us -> 1.62 us  [local(): parts.append(lax.ppermute(own_lines + next_lines, 'blk', back(moves)))]
where the time goes in v17:
time: 62.7 us; the launch traced here: 62.3 us
  waiting for transfers between devices  26.3 us (42%)
  starting transfers between devices  17.6 us (28%)
  Pallas kernels  16.2 us (26%)
  local copies, waits for them, and re-layouts  1.13 us (2%)
  other arithmetic  0.89 us (1%)
    pallas_call x6, Pallas kernels, tile(): pl.pallas_call(functools.partial(tile_kernel, len(columns), turns, own_bl...  11.7 us
    ppermute x2, waiting for transfers between devices, local(): parts.append(lax.ppermute(own_lines + next_lines, 'blk', back(moves)))  10.3 us
    ppermute x2, starting transfers between devices, local(): sent = [lax.ppermute(mine, 'blk', moves) for moves, _ in plans]  7.36 us
    ppermute x2, waiting for transfers between devices, local(): sent = [lax.ppermute(mine, 'blk', moves) for moves, _ in plans]  5.81 us
    all_to_all x1, waiting for transfers between devices, local(): lax.all_to_all(grams_of(image, 2 * blocks), ('blk', 'sub'), 0, 0, tiled=T...  5.54 us
    all_to_all x1, starting transfers between devices, local(): lax.all_to_all(grams_of(image, 2 * blocks), ('blk', 'sub'), 0, 0, tiled=T...  3.5 us
    pallas_call x1, Pallas kernels, basis_of(): pl.pallas_call(functools.partial(basis_kernel, total_rows), out_shape=jax...  2.88 us
    ppermute x1, waiting for transfers between devices, local(): crossed = lax.ppermute(crossing, 'blk', beside)  1.66 us
  transfers between devices with their start and end apart: 15, of which 9 were waited for; matrix products, arithmetic and copies ran while one was open for 3% of the time, Pallas kernels for 19%

profile of v17, /device:TPU:0, one launch (start us, length us, event | category | flops | bytes accessed | tf_op | source)
XLA Modules:
  0.0 62.3 jit_solution(18175424012983555612)
XLA Ops:
  0.0 0.5 collective-permute-start
  0.5 0.1 collective-permute-start.1
  0.5 1.1 %constant_dynamic-slice_fusion = (bf16[512,256]{1,0:T(8,128)(2,1)S(1)}, bf16[512,256]{1,0:T(8,128)(2,1)S(1)}) fusion(bf16[1024,256]{1,0:T(8,128)(2,1)} %param.5, s32[]{:T(128)S(6)} %select_n.7, s32[]{:T(128)S(6)} %select_n.6), kind=kLoop, calls=%fused_computation.3 | loop fusion | bytes 1048584 | tf_op jit(solution)/shard_map/dynamic_slice | solution.py:396
  1.6 0.8 %pad_add_fusion.meta_ref = s32[7,1024]{1,0:T(8,128)S(1)} fusion(s32[1,1024]{1,0:T(1,128)} %bitcast.1, s32[2,1024]{1,0:T(2,128)} %param.8, s32[4,1024]{1,0:T(4,128)} %param.7), kind=kLoop, calls=%fused_computation.2 | loop fusion | flops 14336 | bytes 57344 | tf_op jit(solution)/shard_map/concatenate | solution.py:394
  2.4 0.7 %pack.1 = (bf16[560,512]{1,0:T(8,128)(2,1)S(1)}, bf16[560,512]{1,0:T(8,128)(2,1)S(1)}) custom-call(bf16[512,256]{1,0:T(8,128)(2,1)S(1)} %get-tuple-element.66.emb_mine_ref, bf16[512,256]{1,0:T(8,128)(2,1)S(1)} %get-tuple-element.65.emb_rest_ref, bf16[1024,256]{1,0:T(8,128)(2,1)S(1)} %collective-permute-done.emb_other_ref, bf16[16,1024]{1,0:T(8,128)(2,1)S(1)} %copy-done, ...), custom_call_target="tpu_custom_call" | custom-call | tf_op jit(solution)/shard_map/pack/pallas_call | solution.py:104
  3.1 4.1 %collective-permute-start.2 = (bf16[560,512]{1,0:T(8,128)(2,1)S(1)}, bf16[560,512]{1,0:T(8,128)(2,1)S(1)}, u32[]{:S(2)}, u32[]{:S(2)}) collective-permute-start(bf16[560,512]{1,0:T(8,128)(2,1)S(1)} %get-tuple-element.34.refs_0_.refs_1_), channel_id=1, source_target_pairs={{0,8},{2,10},{12,4},{14,6},{4,0},{6,2},{8,12},{10,14},{1,9},{3,11}... | collective-permute-start | bytes 1720328 | tf_op jit(solution)/shard_map/ppermute | solution.py:398
  7.2 1.5 %collective-permute-start.3 = (bf16[560,512]{1,0:T(8,128)(2,1)S(1)}, bf16[560,512]{1,0:T(8,128)(2,1)S(1)}, u32[]{:S(2)}, u32[]{:S(2)}) collective-permute-start(bf16[560,512]{1,0:T(8,128)(2,1)S(1)} %get-tuple-element.34.refs_0_.refs_1_), channel_id=1, source_target_pairs={{0,2},{2,0},{4,6},{6,4},{8,10},{10,8},{12,14},{14,12},{1,3},{3,1},... | collective-permute-start | bytes 1720328 | tf_op jit(solution)/shard_map/ppermute | solution.py:399
  8.7 3.3 %collective-permute-start.7 = (bf16[560,512]{1,0:T(8,128)(2,1)S(1)}, bf16[560,512]{1,0:T(8,128)(2,1)S(1)}, u32[]{:S(2)}, u32[]{:S(2)}) collective-permute-start(bf16[560,512]{1,0:T(8,128)(2,1)S(1)} %get-tuple-element.34.refs_0_.refs_1_), channel_id=1, source_target_pairs={{8,4},{10,6},{0,12},{2,14},{9,5},{11,7},{1,13},{3,15},{24,20},{26,... | collective-permute-start | bytes 1720328 | tf_op jit(solution)/shard_map/ppermute | solution.py:398
  12.0 3.0 %tile.6 = (f32[40,512]{1,0:T(8,128)S(1)}, bf16[560,1024]{1,0:T(8,128)(2,1)S(1)}) custom-call(bf16[560,512]{1,0:T(8,128)(2,1)S(1)} %get-tuple-element.34.refs_0_.refs_1_, bf16[560,512]{1,0:T(8,128)(2,1)S(1)} %get-tuple-element.34.refs_0_.refs_1_, bf16[560,512]{1,0:T(8,128)(2,1)S(1)} %get-tuple-element.35.refs_2_), custom_call_target="tpu_custom_call" | custom-call | flops 1 | bytes 1 | tf_op jit(solution)/shard_map/tile/pallas_call | solution.py:247
  14.9 5.6 %collective-permute-done.2.refs_0_ = bf16[560,512]{1,0:T(8,128)(2,1)S(1)} collective-permute-done((bf16[560,512]{1,0:T(8,128)(2,1)S(1)}, bf16[560,512]{1,0:T(8,128)(2,1)S(1)}, u32[]{:S(2)}, u32[]{:S(2)}) %collective-permute-start.2) | collective-permute-done | bytes 573472 | tf_op jit(solution)/shard_map/ppermute | solution.py:398
  20.5 1.3 %collective-permute-done.3.refs_1_ = bf16[560,512]{1,0:T(8,128)(2,1)S(1)} collective-permute-done((bf16[560,512]{1,0:T(8,128)(2,1)S(1)}, bf16[560,512]{1,0:T(8,128)(2,1)S(1)}, u32[]{:S(2)}, u32[]{:S(2)}) %collective-permute-start.3) | collective-permute-done | bytes 573472 | tf_op jit(solution)/shard_map/ppermute | solution.py:399
  21.9 0.1 collective-permute-start.6
  22.0 0.6 collective-permute-start.5
  22.5 0.1 collective-permute-start.4
  22.6 2.9 %tile.7 = (f32[40,512]{1,0:T(8,128)S(1)}, f32[40,1024]{1,0:T(8,128)S(1)}) custom-call(bf16[560,512]{1,0:T(8,128)(2,1)S(1)} %collective-permute-done.2.refs_0_, bf16[560,1024]{1,0:T(8,128)(2,1)S(1)} %get-tuple-element.42.refs_1_), custom_call_target="tpu_custom_call" | custom-call | flops 1 | bytes 1 | tf_op jit(solution)/shard_map/tile/pallas_call | solution.py:247
  25.6 2.9 %tile.8 = (f32[40,512]{1,0:T(8,128)S(1)}, bf16[560,1024]{1,0:T(8,128)(2,1)S(1)}) custom-call(bf16[560,512]{1,0:T(8,128)(2,1)S(1)} %get-tuple-element.34.refs_0_.refs_1_, bf16[560,512]{1,0:T(8,128)(2,1)S(1)} %collective-permute-done.3.refs_1_, bf16[560,512]{1,0:T(8,128)(2,1)S(1)} %pad_maximum_fusion.refs_2_), custom_call_target="tpu_custom_call" | custom-call | flops 1 | bytes 1 | tf_op jit(solution)/shard_map/tile/pallas_call | solution.py:247
  28.5 2.9 %tile.9 = (f32[40,512]{1,0:T(8,128)S(1)}, f32[40,1024]{1,0:T(8,128)S(1)}) custom-call(bf16[560,512]{1,0:T(8,128)(2,1)S(1)} %collective-permute-done.2.refs_0_, bf16[560,1024]{1,0:T(8,128)(2,1)S(1)} %get-tuple-element.48.refs_1_), custom_call_target="tpu_custom_call" | custom-call | flops 1 | bytes 1 | tf_op jit(solution)/shard_map/tile/pallas_call | solution.py:247
  31.4 0.3 collective-permute-start.8
  31.7 0.2 collective-permute-done.7.refs_0_
  32.0 5.1 %collective-permute-done.8.refs_2_ = f32[40,512]{1,0:T(8,128)S(1)} collective-permute-done((f32[40,512]{1,0:T(8,128)S(1)}, f32[40,512]{1,0:T(8,128)S(1)}, u32[]{:S(2)}, u32[]{:S(2)}) %collective-permute-start.8) | collective-permute-done | bytes 81952 | tf_op jit(solution)/shard_map/ppermute | solution.py:431
  37.2 0.5 collective-permute-start.11
  37.8 0.6 %collective-permute-done.9 = f32[40,512]{1,0:T(8,128)S(1)} collective-permute-done((f32[40,512]{1,0:T(8,128)S(1)}, f32[40,512]{1,0:T(8,128)S(1)}, u32[]{:S(2)}, u32[]{:S(2)}) %collective-permute-start.9) | collective-permute-done | bytes 81952 | tf_op jit(solution)/shard_map/ppermute | solution.py:426
  38.4 1.6 %collective-permute-start.10 = (f32[40,512]{1,0:T(8,128)S(1)}, f32[40,512]{1,0:T(8,128)S(1)}, u32[]{:S(2)}, u32[]{:S(2)}) collective-permute-start(f32[40,512]{1,0:T(8,128)S(1)} %slice_add_fusion), channel_id=1, source_target_pairs={{0,2},{2,0},{4,6},{6,4},{8,10},{10,8},{12,14},{14,12},{1,3},{3,1},... | collective-permute-start | bytes 245768 | tf_op jit(solution)/shard_map/ppermute | solution.py:428
  40.0 1.3 %collective-permute-start.12 = (f32[40,512]{1,0:T(8,128)S(1)}, f32[40,512]{1,0:T(8,128)S(1)}, u32[]{:S(2)}, u32[]{:S(2)}) collective-permute-start(f32[40,512]{1,0:T(8,128)S(1)} %add.27), channel_id=1, source_target_pairs={{4,8},{6,10},{12,0},{14,2},{5,9},{7,11},{13,1},{15,3},{20,24},{22,... | collective-permute-start | bytes 245768 | tf_op jit(solution)/shard_map/ppermute | solution.py:431
  41.3 1.7 %collective-permute-done.10.refs_3_ = f32[40,512]{1,0:T(8,128)S(1)} collective-permute-done((f32[40,512]{1,0:T(8,128)S(1)}, f32[40,512]{1,0:T(8,128)S(1)}, u32[]{:S(2)}, u32[]{:S(2)}) %collective-permute-start.10) | collective-permute-done | bytes 81952 | tf_op jit(solution)/shard_map/ppermute | solution.py:428
  43.0 5.2 %collective-permute-done.12.refs_6_ = f32[40,512]{1,0:T(8,128)S(1)} collective-permute-done((f32[40,512]{1,0:T(8,128)S(1)}, f32[40,512]{1,0:T(8,128)S(1)}, u32[]{:S(2)}, u32[]{:S(2)}) %collective-permute-start.12) | collective-permute-done | bytes 81952 | tf_op jit(solution)/shard_map/ppermute | solution.py:431
  48.2 0.9 %gram.1 = f32[16,8,128]{2,1,0:T(8,128)} custom-call(f32[32,512]{1,0:T(8,128)S(1)} %image.1.image_ref.mine_ref), custom_call_target="tpu_custom_call" | custom-call | tf_op jit(solution)/shard_map/gram/pallas_call | solution.py:301
  49.1 3.5 %all-to-all-start = ((f32[16,8,128]{2,1,0:T(8,128)}), f32[16,8,128]{2,1,0:T(8,128)S(1)}, u32[]{:S(2)}, u32[]{:S(2)}) async-start(f32[16,8,128]{2,1,0:T(8,128)} %gram.1), calls=%async_computation | async-start | bytes 131072 | tf_op jit(solution)/shard_map/all_to_all | solution.py:434
  52.6 0.3 collective-permute-start.13
  52.9 1.0 %collective-permute-done.13.other_ref = f32[32,512]{1,0:T(8,128)S(1)} collective-permute-done((f32[32,512]{1,0:T(8,128)S(1)}, f32[32,512]{1,0:T(8,128)S(1)}, u32[]{:S(2)}, u32[]{:S(2)}) %collective-permute-start.13) | collective-permute-done | bytes 65568 | tf_op jit(solution)/shard_map/ppermute | solution.py:433
  53.9 5.5 %all-to-all-done.grams_ref = f32[16,8,128]{2,1,0:T(8,128)S(1)} async-done(((f32[16,8,128]{2,1,0:T(8,128)}), f32[16,8,128]{2,1,0:T(8,128)S(1)}, u32[]{:S(2)}, u32[]{:S(2)}) %all-to-all-start) | async-done | bytes 65568 | tf_op jit(solution)/shard_map/all_to_all | solution.py:434
  59.4 2.9 %basis.1 = f32[16,1024]{1,0:T(8,128)} custom-call(f32[16,8,128]{2,1,0:T(8,128)S(1)} %all-to-all-done.grams_ref, f32[32,512]{1,0:T(8,128)S(1)} %image.1.image_ref.mine_ref, f32[32,512]{1,0:T(8,128)S(1)} %collective-permute-done.13.other_ref), custom_call_target="tpu_custom_call" | custom-call | tf_op jit(solution)/shard_map/basis/pallas_call | solution.py:351
  (22 shorter events, 0.3 us)
Async XLA Ops:
  0.0 2.4 %copy-start = (bf16[16,1024]{1,0:T(8,128)(2,1)S(1)}, bf16[16,1024]{1,0:T(8,128)(2,1)}, u32[]{:S(2)}) copy-start(bf16[16,1024]{1,0:T(8,128)(2,1)} %vec_ref.1) | copy-start | bytes 98308
  0.0 2.4 %collective-permute-start = (bf16[1024,256]{1,0:T(8,128)(2,1)}, bf16[1024,256]{1,0:T(8,128)(2,1)S(1)}, u32[]{:S(2)}, u32[]{:S(2)}) collective-permute-start(bf16[1024,256]{1,0:T(8,128)(2,1)} %param.5), channel_id=1, source_target_pairs={{0,1},{1,0},{2,3},{3,2},{4,5},{5,4},{6,7},{7,6},{8,9},{9,8},{10,11... | collective-permute-start | bytes 1572872 | tf_op jit(solution)/shard_map/ppermute | solution.py:392
  0.5 1.9 %collective-permute-start.1 = (bf16[16,1024]{1,0:T(8,128)(2,1)}, bf16[16,1024]{1,0:T(8,128)(2,1)S(1)}, u32[]{:S(2)}, u32[]{:S(2)}) collective-permute-start(bf16[16,1024]{1,0:T(8,128)(2,1)} %vec_ref.1), channel_id=1, source_target_pairs={{0,1},{1,0},{2,3},{3,2},{4,5},{5,4},{6,7},{7,6},{8,9},{9,8},{10,11... | collective-permute-start | bytes 98312 | tf_op jit(solution)/shard_map/ppermute | solution.py:393
  3.1 17.4 %collective-permute-start.2 = (bf16[560,512]{1,0:T(8,128)(2,1)S(1)}, bf16[560,512]{1,0:T(8,128)(2,1)S(1)}, u32[]{:S(2)}, u32[]{:S(2)}) collective-permute-start(bf16[560,512]{1,0:T(8,128)(2,1)S(1)} %get-tuple-element.34.refs_0_.refs_1_), channel_id=1, source_target_pairs={{0,8},{2,10},{12,4},{14,6},{4,0},{6,2},{8,12},{10,14},{1,9},{3,11}... | collective-permute-start | bytes 1720328 | tf_op jit(solution)/shard_map/ppermute | solution.py:398
  7.2 14.7 %collective-permute-start.3 = (bf16[560,512]{1,0:T(8,128)(2,1)S(1)}, bf16[560,512]{1,0:T(8,128)(2,1)S(1)}, u32[]{:S(2)}, u32[]{:S(2)}) collective-permute-start(bf16[560,512]{1,0:T(8,128)(2,1)S(1)} %get-tuple-element.34.refs_0_.refs_1_), channel_id=1, source_target_pairs={{0,2},{2,0},{4,6},{6,4},{8,10},{10,8},{12,14},{14,12},{1,3},{3,1},... | collective-permute-start | bytes 1720328 | tf_op jit(solution)/shard_map/ppermute | solution.py:399
  8.7 23.2 %collective-permute-start.7 = (bf16[560,512]{1,0:T(8,128)(2,1)S(1)}, bf16[560,512]{1,0:T(8,128)(2,1)S(1)}, u32[]{:S(2)}, u32[]{:S(2)}) collective-permute-start(bf16[560,512]{1,0:T(8,128)(2,1)S(1)} %get-tuple-element.34.refs_0_.refs_1_), channel_id=1, source_target_pairs={{8,4},{10,6},{0,12},{2,14},{9,5},{11,7},{1,13},{3,15},{24,20},{26,... | collective-permute-start | bytes 1720328 | tf_op jit(solution)/shard_map/ppermute | solution.py:398
  21.9 3.6 %collective-permute-start.6 = (bf16[208,512]{1,0:T(8,128)(2,1)S(1)}, bf16[208,512]{1,0:T(8,128)(2,1)S(1)}, u32[]{:S(2)}, u32[]{:S(2)}) collective-permute-start(bf16[208,512]{1,0:T(8,128)(2,1)S(1)} %slice.23), channel_id=1, source_target_pairs={{0,1},{1,0},{2,3},{3,2},{4,5},{5,4},{6,7},{7,6},{8,9},{9,8},{10,11... | collective-permute-start | bytes 638984 | tf_op jit(solution)/shard_map/ppermute | solution.py:406
  22.0 3.5 %collective-permute-start.5 = (bf16[176,512]{1,0:T(8,128)(2,1)S(1)}, bf16[176,512]{1,0:T(8,128)(2,1)S(1)}, u32[]{:S(2)}, u32[]{:S(2)}) collective-permute-start(bf16[176,512]{1,0:T(8,128)(2,1)S(1)} %get-tuple-element.64), channel_id=1, source_target_pairs={{0,1},{1,0},{2,3},{3,2},{4,5},{5,4},{6,7},{7,6},{8,9},{9,8},{10,11... | collective-permute-start | bytes 540680 | tf_op jit(solution)/shard_map/ppermute | solution.py:406
  22.5 3.0 %collective-permute-start.4 = (bf16[176,512]{1,0:T(8,128)(2,1)S(1)}, bf16[176,512]{1,0:T(8,128)(2,1)S(1)}, u32[]{:S(2)}, u32[]{:S(2)}) collective-permute-start(bf16[176,512]{1,0:T(8,128)(2,1)S(1)} %get-tuple-element.63), channel_id=1, source_target_pairs={{0,1},{1,0},{2,3},{3,2},{4,5},{5,4},{6,7},{7,6},{8,9},{9,8},{10,11... | collective-permute-start | bytes 540680 | tf_op jit(solution)/shard_map/ppermute | solution.py:406
  31.4 5.7 %collective-permute-start.8 = (f32[40,512]{1,0:T(8,128)S(1)}, f32[40,512]{1,0:T(8,128)S(1)}, u32[]{:S(2)}, u32[]{:S(2)}) collective-permute-start(f32[40,512]{1,0:T(8,128)S(1)} %add.24), channel_id=1, source_target_pairs={{8,0},{10,2},{4,12},{6,14},{0,4},{2,6},{12,8},{14,10},{9,1},{11,3}... | collective-permute-start | bytes 245768 | tf_op jit(solution)/shard_map/ppermute | solution.py:431
  37.1 1.3 %collective-permute-start.9 = (f32[40,512]{1,0:T(8,128)S(1)}, f32[40,512]{1,0:T(8,128)S(1)}, u32[]{:S(2)}, u32[]{:S(2)}) collective-permute-start(f32[40,512]{1,0:T(8,128)S(1)} %slice.25), channel_id=1, source_target_pairs={{0,1},{1,0},{2,3},{3,2},{4,5},{5,4},{6,7},{7,6},{8,9},{9,8},{10,11... | collective-permute-start | bytes 245768 | tf_op jit(solution)/shard_map/ppermute | solution.py:426
  37.2 4.1 %collective-permute-start.11 = (f32[40,512]{1,0:T(8,128)S(1)}, f32[40,512]{1,0:T(8,128)S(1)}, u32[]{:S(2)}, u32[]{:S(2)}) collective-permute-start(f32[40,512]{1,0:T(8,128)S(1)} %get-tuple-element.67), channel_id=1, source_target_pairs={{0,1},{1,0},{2,3},{3,2},{4,5},{5,4},{6,7},{7,6},{8,9},{9,8},{10,11... | collective-permute-start | bytes 245768 | tf_op jit(solution)/shard_map/ppermute | solution.py:430
  38.4 4.6 %collective-permute-start.10 = (f32[40,512]{1,0:T(8,128)S(1)}, f32[40,512]{1,0:T(8,128)S(1)}, u32[]{:S(2)}, u32[]{:S(2)}) collective-permute-start(f32[40,512]{1,0:T(8,128)S(1)} %slice_add_fusion), channel_id=1, source_target_pairs={{0,2},{2,0},{4,6},{6,4},{8,10},{10,8},{12,14},{14,12},{1,3},{3,1},... | collective-permute-start | bytes 245768 | tf_op jit(solution)/shard_map/ppermute | solution.py:428
  40.0 8.1 %collective-permute-start.12 = (f32[40,512]{1,0:T(8,128)S(1)}, f32[40,512]{1,0:T(8,128)S(1)}, u32[]{:S(2)}, u32[]{:S(2)}) collective-permute-start(f32[40,512]{1,0:T(8,128)S(1)} %add.27), channel_id=1, source_target_pairs={{4,8},{6,10},{12,0},{14,2},{5,9},{7,11},{13,1},{15,3},{20,24},{22,... | collective-permute-start | bytes 245768 | tf_op jit(solution)/shard_map/ppermute | solution.py:431
  49.1 10.4 %all-to-all-start = ((f32[16,8,128]{2,1,0:T(8,128)}), f32[16,8,128]{2,1,0:T(8,128)S(1)}, u32[]{:S(2)}, u32[]{:S(2)}) async-start(f32[16,8,128]{2,1,0:T(8,128)} %gram.1), calls=%async_computation | async-start | bytes 131072 | tf_op jit(solution)/shard_map/all_to_all | solution.py:434
  52.6 1.3 %collective-permute-start.13 = (f32[32,512]{1,0:T(8,128)S(1)}, f32[32,512]{1,0:T(8,128)S(1)}, u32[]{:S(2)}, u32[]{:S(2)}) collective-permute-start(f32[32,512]{1,0:T(8,128)S(1)} %image.1.image_ref.mine_ref), channel_id=1, source_target_pairs={{0,1},{1,0},{2,3},{3,2},{4,5},{5,4},{6,7},{7,6},{8,9},{9,8},{10,11... | collective-permute-start | bytes 196616 | tf_op jit(solution)/shard_map/ppermute | solution.py:433

commit v18 on v17

--- a/solution.py
+++ b/solution.py
@@ -422,13 +422,13 @@
             pack, next_cols, parts[-1] = lax.optimization_barrier((pack, next_cols, parts[-1]))
             own_lines, cols = weigh(pack, [own], receivers=takers, last=last)
             own_cols = own_cols + cols
+        parts.append(lax.ppermute(own_lines + next_lines, "blk", back(moves)))
         if last:
             next_rest = lax.ppermute(next_cols[:, half:], "sub", swap)
             crossing = next_cols[:, :half] + next_rest
-            crossed = lax.ppermute(crossing, "blk", beside)
-            own_lines, _ = lax.optimization_barrier((own_lines, crossing))
-            parts += [crossed, own_cols[:, :half], lax.ppermute(own_cols[:, half:], "sub", swap)]
-        parts.append(lax.ppermute(own_lines + next_lines, "blk", back(moves)))
+            parts.append(lax.ppermute(crossing, "blk", beside))
+            own_cols, _ = lax.optimization_barrier((own_cols, crossing))
+            parts += [own_cols[:, :half], lax.ppermute(own_cols[:, half:], "sub", swap)]
     image = image_of(parts, vecs)
     image_other = lax.ppermute(image, "sub", swap)
     grams = lax.all_to_all(grams_of(image, 2 * blocks), ("blk", "sub"), 0, 0, tiled=True)

time: 62.7 us -> 61.8 us (0.986)
  waiting for transfers between devices: 26.3 us -> 24.8 us
    ppermute x2, waiting for transfers between devices: 1.66 us -> 0.01 us  [the longest x1 0.01 us: local(): parts.append(lax.ppermute(crossing, 'blk', beside))]
    ppermute x2, waiting for transfers between devices: 10.3 us -> 11.2 us  [local(): parts.append(lax.ppermute(own_lines + next_lines, 'blk', back(moves)))]
    all_to_all x1, starting transfers between devices: 3.5 us -> 4.23 us  [local(): lax.all_to_all(grams_of(image, 2 * blocks), ('blk', 'sub'), 0, 0, tiled=T...]
    ppermute x1, waiting for transfers between devices: 0.63 us -> 0.01 us  [local(): next_rest = lax.ppermute(next_cols[:, half:], 'sub', swap)]
  transfers between devices with their start and end apart: 15 -> 15, of which waited for: 9 -> 7; matrix products, arithmetic and copies ran while one was open for 3% -> 3% of each run, Pallas kernels for 19% -> 19%
where the time goes in v18:
time: 61.8 us; the launch traced here: 61.4 us
  waiting for transfers between devices  24.8 us (40%)
  starting transfers between devices  18.2 us (29%)
  Pallas kernels  16.2 us (26%)
  local copies, waits for them, and re-layouts  1.13 us (2%)
  other arithmetic  0.9 us (1%)
    pallas_call x6, Pallas kernels, tile(): pl.pallas_call(functools.partial(tile_kernel, len(columns), turns, own_bl...  11.7 us
    ppermute x2, waiting for transfers between devices, local(): parts.append(lax.ppermute(own_lines + next_lines, 'blk', back(moves)))  11.2 us
    ppermute x2, starting transfers between devices, local(): sent = [lax.ppermute(mine, 'blk', moves) for moves, _ in plans]  7.36 us
    ppermute x2, waiting for transfers between devices, local(): sent = [lax.ppermute(mine, 'blk', moves) for moves, _ in plans]  5.81 us
    all_to_all x1, waiting for transfers between devices, local(): lax.all_to_all(grams_of(image, 2 * blocks), ('blk', 'sub'), 0, 0, tiled=T...  5.58 us
    all_to_all x1, starting transfers between devices, local(): lax.all_to_all(grams_of(image, 2 * blocks), ('blk', 'sub'), 0, 0, tiled=T...  4.23 us
    pallas_call x1, Pallas kernels, basis_of(): pl.pallas_call(functools.partial(basis_kernel, total_rows), out_shape=jax...  2.89 us
    ppermute x2, starting transfers between devices, local(): parts.append(lax.ppermute(own_lines + next_lines, 'blk', back(moves)))  1.62 us
  transfers between devices with their start and end apart: 15, of which 7 were waited for; matrix products, arithmetic and copies ran while one was open for 3% of the time, Pallas kernels for 19%

profile of v18, /device:TPU:0, one launch (start us, length us, event | category | flops | bytes accessed | tf_op | source)
XLA Modules:
  0.0 61.4 jit_solution(15738062692905924505)
XLA Ops:
  0.0 0.5 collective-permute-start
  0.5 0.1 collective-permute-start.1
  0.5 1.1 %constant_dynamic-slice_fusion = (bf16[512,256]{1,0:T(8,128)(2,1)S(1)}, bf16[512,256]{1,0:T(8,128)(2,1)S(1)}) fusion(bf16[1024,256]{1,0:T(8,128)(2,1)} %param.5, s32[]{:T(128)S(6)} %select_n.7, s32[]{:T(128)S(6)} %select_n.6), kind=kLoop, calls=%fused_computation.3 | loop fusion | bytes 1048584 | tf_op jit(solution)/shard_map/dynamic_slice | solution.py:396
  1.6 0.8 %pad_add_fusion.meta_ref = s32[7,1024]{1,0:T(8,128)S(1)} fusion(s32[1,1024]{1,0:T(1,128)} %bitcast.1, s32[2,1024]{1,0:T(2,128)} %param.8, s32[4,1024]{1,0:T(4,128)} %param.7), kind=kLoop, calls=%fused_computation.2 | loop fusion | flops 14336 | bytes 57344 | tf_op jit(solution)/shard_map/concatenate | solution.py:394
  2.4 0.0 collective-permute-done.1.vec_other_ref
  2.4 0.0 collective-permute-done.emb_other_ref
  2.4 0.7 %pack.1 = (bf16[560,512]{1,0:T(8,128)(2,1)S(1)}, bf16[560,512]{1,0:T(8,128)(2,1)S(1)}) custom-call(bf16[512,256]{1,0:T(8,128)(2,1)S(1)} %get-tuple-element.66.emb_mine_ref, bf16[512,256]{1,0:T(8,128)(2,1)S(1)} %get-tuple-element.65.emb_rest_ref, bf16[1024,256]{1,0:T(8,128)(2,1)S(1)} %collective-permute-done.emb_other_ref, bf16[16,1024]{1,0:T(8,128)(2,1)S(1)} %copy-done, ...), custom_call_target="tpu_custom_call" | custom-call | tf_op jit(solution)/shard_map/pack/pallas_call | solution.py:104
  3.1 4.1 %collective-permute-start.2 = (bf16[560,512]{1,0:T(8,128)(2,1)S(1)}, bf16[560,512]{1,0:T(8,128)(2,1)S(1)}, u32[]{:S(2)}, u32[]{:S(2)}) collective-permute-start(bf16[560,512]{1,0:T(8,128)(2,1)S(1)} %get-tuple-element.34.refs_0_.refs_1_), channel_id=1, source_target_pairs={{0,8},{2,10},{12,4},{14,6},{4,0},{6,2},{8,12},{10,14},{1,9},{3,11}... | collective-permute-start | bytes 1720328 | tf_op jit(solution)/shard_map/ppermute | solution.py:398
  7.2 1.5 %collective-permute-start.3 = (bf16[560,512]{1,0:T(8,128)(2,1)S(1)}, bf16[560,512]{1,0:T(8,128)(2,1)S(1)}, u32[]{:S(2)}, u32[]{:S(2)}) collective-permute-start(bf16[560,512]{1,0:T(8,128)(2,1)S(1)} %get-tuple-element.34.refs_0_.refs_1_), channel_id=1, source_target_pairs={{0,2},{2,0},{4,6},{6,4},{8,10},{10,8},{12,14},{14,12},{1,3},{3,1},... | collective-permute-start | bytes 1720328 | tf_op jit(solution)/shard_map/ppermute | solution.py:399
  8.7 3.3 %collective-permute-start.7 = (bf16[560,512]{1,0:T(8,128)(2,1)S(1)}, bf16[560,512]{1,0:T(8,128)(2,1)S(1)}, u32[]{:S(2)}, u32[]{:S(2)}) collective-permute-start(bf16[560,512]{1,0:T(8,128)(2,1)S(1)} %get-tuple-element.34.refs_0_.refs_1_), channel_id=1, source_target_pairs={{8,4},{10,6},{0,12},{2,14},{9,5},{11,7},{1,13},{3,15},{24,20},{26,... | collective-permute-start | bytes 1720328 | tf_op jit(solution)/shard_map/ppermute | solution.py:398
  12.0 3.0 %tile.6 = (f32[40,512]{1,0:T(8,128)S(1)}, bf16[560,1024]{1,0:T(8,128)(2,1)S(1)}) custom-call(bf16[560,512]{1,0:T(8,128)(2,1)S(1)} %get-tuple-element.34.refs_0_.refs_1_, bf16[560,512]{1,0:T(8,128)(2,1)S(1)} %get-tuple-element.34.refs_0_.refs_1_, bf16[560,512]{1,0:T(8,128)(2,1)S(1)} %get-tuple-element.35.refs_2_), custom_call_target="tpu_custom_call" | custom-call | flops 1 | bytes 1 | tf_op jit(solution)/shard_map/tile/pallas_call | solution.py:247
  14.9 5.6 %collective-permute-done.2.refs_0_ = bf16[560,512]{1,0:T(8,128)(2,1)S(1)} collective-permute-done((bf16[560,512]{1,0:T(8,128)(2,1)S(1)}, bf16[560,512]{1,0:T(8,128)(2,1)S(1)}, u32[]{:S(2)}, u32[]{:S(2)}) %collective-permute-start.2) | collective-permute-done | bytes 573472 | tf_op jit(solution)/shard_map/ppermute | solution.py:398
  20.5 1.3 %collective-permute-done.3.refs_1_ = bf16[560,512]{1,0:T(8,128)(2,1)S(1)} collective-permute-done((bf16[560,512]{1,0:T(8,128)(2,1)S(1)}, bf16[560,512]{1,0:T(8,128)(2,1)S(1)}, u32[]{:S(2)}, u32[]{:S(2)}) %collective-permute-start.3) | collective-permute-done | bytes 573472 | tf_op jit(solution)/shard_map/ppermute | solution.py:399
  21.9 0.1 collective-permute-start.6
  22.0 0.6 collective-permute-start.5
  22.5 0.1 collective-permute-start.4
  22.6 2.9 %tile.7 = (f32[40,512]{1,0:T(8,128)S(1)}, f32[40,1024]{1,0:T(8,128)S(1)}) custom-call(bf16[560,512]{1,0:T(8,128)(2,1)S(1)} %collective-permute-done.2.refs_0_, bf16[560,1024]{1,0:T(8,128)(2,1)S(1)} %get-tuple-element.42.refs_1_), custom_call_target="tpu_custom_call" | custom-call | flops 1 | bytes 1 | tf_op jit(solution)/shard_map/tile/pallas_call | solution.py:247
  25.6 2.9 %tile.8 = (f32[40,512]{1,0:T(8,128)S(1)}, bf16[560,1024]{1,0:T(8,128)(2,1)S(1)}) custom-call(bf16[560,512]{1,0:T(8,128)(2,1)S(1)} %get-tuple-element.34.refs_0_.refs_1_, bf16[560,512]{1,0:T(8,128)(2,1)S(1)} %collective-permute-done.3.refs_1_, bf16[560,512]{1,0:T(8,128)(2,1)S(1)} %pad_maximum_fusion.refs_2_), custom_call_target="tpu_custom_call" | custom-call | flops 1 | bytes 1 | tf_op jit(solution)/shard_map/tile/pallas_call | solution.py:247
  28.5 2.9 %tile.9 = (f32[40,512]{1,0:T(8,128)S(1)}, f32[40,1024]{1,0:T(8,128)S(1)}) custom-call(bf16[560,512]{1,0:T(8,128)(2,1)S(1)} %collective-permute-done.2.refs_0_, bf16[560,1024]{1,0:T(8,128)(2,1)S(1)} %get-tuple-element.48.refs_1_), custom_call_target="tpu_custom_call" | custom-call | flops 1 | bytes 1 | tf_op jit(solution)/shard_map/tile/pallas_call | solution.py:247
  31.4 0.3 collective-permute-start.8
  31.7 0.2 collective-permute-done.7.refs_0_
  32.0 5.1 %collective-permute-done.8.refs_2_ = f32[40,512]{1,0:T(8,128)S(1)} collective-permute-done((f32[40,512]{1,0:T(8,128)S(1)}, f32[40,512]{1,0:T(8,128)S(1)}, u32[]{:S(2)}, u32[]{:S(2)}) %collective-permute-start.8) | collective-permute-done | bytes 81952 | tf_op jit(solution)/shard_map/ppermute | solution.py:425
  37.2 1.3 %collective-permute-start.9 = (f32[40,512]{1,0:T(8,128)S(1)}, f32[40,512]{1,0:T(8,128)S(1)}, u32[]{:S(2)}, u32[]{:S(2)}) collective-permute-start(f32[40,512]{1,0:T(8,128)S(1)} %add.25), channel_id=1, source_target_pairs={{4,8},{6,10},{12,0},{14,2},{5,9},{7,11},{13,1},{15,3},{20,24},{22,... | collective-permute-start | bytes 245768 | tf_op jit(solution)/shard_map/ppermute | solution.py:425
  38.5 1.6 %collective-permute-start.11 = (f32[40,512]{1,0:T(8,128)S(1)}, f32[40,512]{1,0:T(8,128)S(1)}, u32[]{:S(2)}, u32[]{:S(2)}) collective-permute-start(f32[40,512]{1,0:T(8,128)S(1)} %slice_add_fusion), channel_id=1, source_target_pairs={{0,2},{2,0},{4,6},{6,4},{8,10},{10,8},{12,14},{14,12},{1,3},{3,1},... | collective-permute-start | bytes 245768 | tf_op jit(solution)/shard_map/ppermute | solution.py:429
  40.1 0.3 collective-permute-start.12
  40.4 6.1 %collective-permute-done.9.refs_3_ = f32[40,512]{1,0:T(8,128)S(1)} collective-permute-done((f32[40,512]{1,0:T(8,128)S(1)}, f32[40,512]{1,0:T(8,128)S(1)}, u32[]{:S(2)}, u32[]{:S(2)}) %collective-permute-start.9) | collective-permute-done | bytes 81952 | tf_op jit(solution)/shard_map/ppermute | solution.py:425
  46.5 0.9 %gram.1 = f32[16,8,128]{2,1,0:T(8,128)} custom-call(f32[32,512]{1,0:T(8,128)S(1)} %image.1.image_ref.mine_ref), custom_call_target="tpu_custom_call" | custom-call | tf_op jit(solution)/shard_map/gram/pallas_call | solution.py:301
  47.4 4.2 %all-to-all-start = ((f32[16,8,128]{2,1,0:T(8,128)}), f32[16,8,128]{2,1,0:T(8,128)S(1)}, u32[]{:S(2)}, u32[]{:S(2)}) async-start(f32[16,8,128]{2,1,0:T(8,128)} %gram.1), calls=%async_computation | async-start | bytes 131072 | tf_op jit(solution)/shard_map/all_to_all | solution.py:434
  51.7 0.4 collective-permute-start.13
  52.1 0.9 %collective-permute-done.13.other_ref = f32[32,512]{1,0:T(8,128)S(1)} collective-permute-done((f32[32,512]{1,0:T(8,128)S(1)}, f32[32,512]{1,0:T(8,128)S(1)}, u32[]{:S(2)}, u32[]{:S(2)}) %collective-permute-start.13) | collective-permute-done | bytes 65568 | tf_op jit(solution)/shard_map/ppermute | solution.py:433
  53.0 5.6 %all-to-all-done.grams_ref = f32[16,8,128]{2,1,0:T(8,128)S(1)} async-done(((f32[16,8,128]{2,1,0:T(8,128)}), f32[16,8,128]{2,1,0:T(8,128)S(1)}, u32[]{:S(2)}, u32[]{:S(2)}) %all-to-all-start) | async-done | bytes 65568 | tf_op jit(solution)/shard_map/all_to_all | solution.py:434
  58.6 2.9 %basis.1 = f32[16,1024]{1,0:T(8,128)} custom-call(f32[16,8,128]{2,1,0:T(8,128)S(1)} %all-to-all-done.grams_ref, f32[32,512]{1,0:T(8,128)S(1)} %image.1.image_ref.mine_ref, f32[32,512]{1,0:T(8,128)S(1)} %collective-permute-done.13.other_ref), custom_call_target="tpu_custom_call" | custom-call | tf_op jit(solution)/shard_map/basis/pallas_call | solution.py:351
  (22 shorter events, 0.3 us)
Async XLA Ops:
  0.0 2.4 %copy-start = (bf16[16,1024]{1,0:T(8,128)(2,1)S(1)}, bf16[16,1024]{1,0:T(8,128)(2,1)}, u32[]{:S(2)}) copy-start(bf16[16,1024]{1,0:T(8,128)(2,1)} %vec_ref.1) | copy-start | bytes 98308
  0.0 2.4 %collective-permute-start = (bf16[1024,256]{1,0:T(8,128)(2,1)}, bf16[1024,256]{1,0:T(8,128)(2,1)S(1)}, u32[]{:S(2)}, u32[]{:S(2)}) collective-permute-start(bf16[1024,256]{1,0:T(8,128)(2,1)} %param.5), channel_id=1, source_target_pairs={{0,1},{1,0},{2,3},{3,2},{4,5},{5,4},{6,7},{7,6},{8,9},{9,8},{10,11... | collective-permute-start | bytes 1572872 | tf_op jit(solution)/shard_map/ppermute | solution.py:392
  0.5 1.9 %collective-permute-start.1 = (bf16[16,1024]{1,0:T(8,128)(2,1)}, bf16[16,1024]{1,0:T(8,128)(2,1)S(1)}, u32[]{:S(2)}, u32[]{:S(2)}) collective-permute-start(bf16[16,1024]{1,0:T(8,128)(2,1)} %vec_ref.1), channel_id=1, source_target_pairs={{0,1},{1,0},{2,3},{3,2},{4,5},{5,4},{6,7},{7,6},{8,9},{9,8},{10,11... | collective-permute-start | bytes 98312 | tf_op jit(solution)/shard_map/ppermute | solution.py:393
  3.1 17.4 %collective-permute-start.2 = (bf16[560,512]{1,0:T(8,128)(2,1)S(1)}, bf16[560,512]{1,0:T(8,128)(2,1)S(1)}, u32[]{:S(2)}, u32[]{:S(2)}) collective-permute-start(bf16[560,512]{1,0:T(8,128)(2,1)S(1)} %get-tuple-element.34.refs_0_.refs_1_), channel_id=1, source_target_pairs={{0,8},{2,10},{12,4},{14,6},{4,0},{6,2},{8,12},{10,14},{1,9},{3,11}... | collective-permute-start | bytes 1720328 | tf_op jit(solution)/shard_map/ppermute | solution.py:398
  7.2 14.7 %collective-permute-start.3 = (bf16[560,512]{1,0:T(8,128)(2,1)S(1)}, bf16[560,512]{1,0:T(8,128)(2,1)S(1)}, u32[]{:S(2)}, u32[]{:S(2)}) collective-permute-start(bf16[560,512]{1,0:T(8,128)(2,1)S(1)} %get-tuple-element.34.refs_0_.refs_1_), channel_id=1, source_target_pairs={{0,2},{2,0},{4,6},{6,4},{8,10},{10,8},{12,14},{14,12},{1,3},{3,1},... | collective-permute-start | bytes 1720328 | tf_op jit(solution)/shard_map/ppermute | solution.py:399
  8.7 23.2 %collective-permute-start.7 = (bf16[560,512]{1,0:T(8,128)(2,1)S(1)}, bf16[560,512]{1,0:T(8,128)(2,1)S(1)}, u32[]{:S(2)}, u32[]{:S(2)}) collective-permute-start(bf16[560,512]{1,0:T(8,128)(2,1)S(1)} %get-tuple-element.34.refs_0_.refs_1_), channel_id=1, source_target_pairs={{8,4},{10,6},{0,12},{2,14},{9,5},{11,7},{1,13},{3,15},{24,20},{26,... | collective-permute-start | bytes 1720328 | tf_op jit(solution)/shard_map/ppermute | solution.py:398
  21.9 3.6 %collective-permute-start.6 = (bf16[208,512]{1,0:T(8,128)(2,1)S(1)}, bf16[208,512]{1,0:T(8,128)(2,1)S(1)}, u32[]{:S(2)}, u32[]{:S(2)}) collective-permute-start(bf16[208,512]{1,0:T(8,128)(2,1)S(1)} %slice.23), channel_id=1, source_target_pairs={{0,1},{1,0},{2,3},{3,2},{4,5},{5,4},{6,7},{7,6},{8,9},{9,8},{10,11... | collective-permute-start | bytes 638984 | tf_op jit(solution)/shard_map/ppermute | solution.py:406
  22.0 3.5 %collective-permute-start.5 = (bf16[176,512]{1,0:T(8,128)(2,1)S(1)}, bf16[176,512]{1,0:T(8,128)(2,1)S(1)}, u32[]{:S(2)}, u32[]{:S(2)}) collective-permute-start(bf16[176,512]{1,0:T(8,128)(2,1)S(1)} %get-tuple-element.64), channel_id=1, source_target_pairs={{0,1},{1,0},{2,3},{3,2},{4,5},{5,4},{6,7},{7,6},{8,9},{9,8},{10,11... | collective-permute-start | bytes 540680 | tf_op jit(solution)/shard_map/ppermute | solution.py:406
  22.5 3.0 %collective-permute-start.4 = (bf16[176,512]{1,0:T(8,128)(2,1)S(1)}, bf16[176,512]{1,0:T(8,128)(2,1)S(1)}, u32[]{:S(2)}, u32[]{:S(2)}) collective-permute-start(bf16[176,512]{1,0:T(8,128)(2,1)S(1)} %get-tuple-element.63), channel_id=1, source_target_pairs={{0,1},{1,0},{2,3},{3,2},{4,5},{5,4},{6,7},{7,6},{8,9},{9,8},{10,11... | collective-permute-start | bytes 540680 | tf_op jit(solution)/shard_map/ppermute | solution.py:406
  31.4 5.7 %collective-permute-start.8 = (f32[40,512]{1,0:T(8,128)S(1)}, f32[40,512]{1,0:T(8,128)S(1)}, u32[]{:S(2)}, u32[]{:S(2)}) collective-permute-start(f32[40,512]{1,0:T(8,128)S(1)} %add.24), channel_id=1, source_target_pairs={{8,0},{10,2},{4,12},{6,14},{0,4},{2,6},{12,8},{14,10},{9,1},{11,3}... | collective-permute-start | bytes 245768 | tf_op jit(solution)/shard_map/ppermute | solution.py:425
  37.1 1.4 %collective-permute-start.10 = (f32[40,512]{1,0:T(8,128)S(1)}, f32[40,512]{1,0:T(8,128)S(1)}, u32[]{:S(2)}, u32[]{:S(2)}) collective-permute-start(f32[40,512]{1,0:T(8,128)S(1)} %slice.25), channel_id=1, source_target_pairs={{0,1},{1,0},{2,3},{3,2},{4,5},{5,4},{6,7},{7,6},{8,9},{9,8},{10,11... | collective-permute-start | bytes 245768 | tf_op jit(solution)/shard_map/ppermute | solution.py:427
  37.2 9.3 %collective-permute-start.9 = (f32[40,512]{1,0:T(8,128)S(1)}, f32[40,512]{1,0:T(8,128)S(1)}, u32[]{:S(2)}, u32[]{:S(2)}) collective-permute-start(f32[40,512]{1,0:T(8,128)S(1)} %add.25), channel_id=1, source_target_pairs={{4,8},{6,10},{12,0},{14,2},{5,9},{7,11},{13,1},{15,3},{20,24},{22,... | collective-permute-start | bytes 245768 | tf_op jit(solution)/shard_map/ppermute | solution.py:425
  38.5 8.0 %collective-permute-start.11 = (f32[40,512]{1,0:T(8,128)S(1)}, f32[40,512]{1,0:T(8,128)S(1)}, u32[]{:S(2)}, u32[]{:S(2)}) collective-permute-start(f32[40,512]{1,0:T(8,128)S(1)} %slice_add_fusion), channel_id=1, source_target_pairs={{0,2},{2,0},{4,6},{6,4},{8,10},{10,8},{12,14},{14,12},{1,3},{3,1},... | collective-permute-start | bytes 245768 | tf_op jit(solution)/shard_map/ppermute | solution.py:429
  40.1 6.4 %collective-permute-start.12 = (f32[40,512]{1,0:T(8,128)S(1)}, f32[40,512]{1,0:T(8,128)S(1)}, u32[]{:S(2)}, u32[]{:S(2)}) collective-permute-start(f32[40,512]{1,0:T(8,128)S(1)} %get-tuple-element.67), channel_id=1, source_target_pairs={{0,1},{1,0},{2,3},{3,2},{4,5},{5,4},{6,7},{7,6},{8,9},{9,8},{10,11... | collective-permute-start | bytes 245768 | tf_op jit(solution)/shard_map/ppermute | solution.py:431
  47.4 11.1 %all-to-all-start = ((f32[16,8,128]{2,1,0:T(8,128)}), f32[16,8,128]{2,1,0:T(8,128)S(1)}, u32[]{:S(2)}, u32[]{:S(2)}) async-start(f32[16,8,128]{2,1,0:T(8,128)} %gram.1), calls=%async_computation | async-start | bytes 131072 | tf_op jit(solution)/shard_map/all_to_all | solution.py:434
  51.7 1.3 %collective-permute-start.13 = (f32[32,512]{1,0:T(8,128)S(1)}, f32[32,512]{1,0:T(8,128)S(1)}, u32[]{:S(2)}, u32[]{:S(2)}) collective-permute-start(f32[32,512]{1,0:T(8,128)S(1)} %image.1.image_ref.mine_ref), channel_id=1, source_target_pairs={{0,1},{1,0},{2,3},{3,2},{4,5},{5,4},{6,7},{7,6},{8,9},{9,8},{10,11... | collective-permute-start | bytes 196616 | tf_op jit(solution)/shard_map/ppermute | solution.py:433

commit v19 on v18

--- a/solution.py
+++ b/solution.py
@@ -360,8 +360,6 @@
 
 
 def exchanges(pairs):
-    if pairs == 4:
-        return [([(0, 2), (3, 1), (1, 0), (2, 3)], None), ([(2, 1), (0, 3)], [1, 3])]
     plans = []
     for distance in range(1, pairs // 2):
         plans.append(([((p + distance) % pairs, p) for p in range(pairs)], None))

time: 61.8 us -> 62 us (level)
  waiting for transfers between devices: 24.8 us -> 26.2 us
  starting transfers between devices: 18.2 us -> 17 us
    ppermute x2, waiting for transfers between devices: 5.81 us -> 7.99 us  [local(): sent = [lax.ppermute(mine, 'blk', moves) for moves, _ in plans]]
    ppermute x2, starting transfers between devices: 7.36 us -> 6.46 us  [local(): sent = [lax.ppermute(mine, 'blk', moves) for moves, _ in plans]]
    ppermute x2, waiting for transfers between devices: 11.2 us -> 10.4 us  [local(): parts.append(lax.ppermute(own_lines + next_lines, 'blk', back(moves)))]
where the time goes in v19:
time: 62 us; the launch traced here: 61.7 us
  waiting for transfers between devices  26.2 us (42%)
  starting transfers between devices  17 us (27%)
  Pallas kernels  16.2 us (26%)
  local copies, waits for them, and re-layouts  1.13 us (2%)
  other arithmetic  0.9 us (1%)
    pallas_call x6, Pallas kernels, tile(): pl.pallas_call(functools.partial(tile_kernel, len(columns), turns, own_bl...  11.7 us
    ppermute x2, waiting for transfers between devices, local(): parts.append(lax.ppermute(own_lines + next_lines, 'blk', back(moves)))  10.4 us
    ppermute x2, waiting for transfers between devices, local(): sent = [lax.ppermute(mine, 'blk', moves) for moves, _ in plans]  7.99 us
    ppermute x2, starting transfers between devices, local(): sent = [lax.ppermute(mine, 'blk', moves) for moves, _ in plans]  6.46 us
    all_to_all x1, waiting for transfers between devices, local(): lax.all_to_all(grams_of(image, 2 * blocks), ('blk', 'sub'), 0, 0, tiled=T...  5.58 us
    all_to_all x1, starting transfers between devices, local(): lax.all_to_all(grams_of(image, 2 * blocks), ('blk', 'sub'), 0, 0, tiled=T...  4.22 us
    pallas_call x1, Pallas kernels, basis_of(): pl.pallas_call(functools.partial(basis_kernel, total_rows), out_shape=jax...  2.89 us
    ppermute x1, starting transfers between devices, local(): parts.append(lax.ppermute(crossing, 'blk', beside))  1.58 us
  transfers between devices with their start and end apart: 15, of which 7 were waited for; matrix products, arithmetic and copies ran while one was open for 3% of the time, Pallas kernels for 19%

profile of v19, /device:TPU:0, one launch (start us, length us, event | category | flops | bytes accessed | tf_op | source)
XLA Modules:
  0.0 61.7 jit_solution(17512850274116753095)
XLA Ops:
  0.0 0.5 collective-permute-start
  0.5 0.1 collective-permute-start.1
  0.5 1.1 %constant_dynamic-slice_fusion = (bf16[512,256]{1,0:T(8,128)(2,1)S(1)}, bf16[512,256]{1,0:T(8,128)(2,1)S(1)}) fusion(bf16[1024,256]{1,0:T(8,128)(2,1)} %param.5, s32[]{:T(128)S(6)} %select_n.7, s32[]{:T(128)S(6)} %select_n.6), kind=kLoop, calls=%fused_computation.3 | loop fusion | bytes 1048584 | tf_op jit(solution)/shard_map/dynamic_slice | solution.py:394
  1.6 0.8 %pad_add_fusion.meta_ref = s32[7,1024]{1,0:T(8,128)S(1)} fusion(s32[1,1024]{1,0:T(1,128)} %bitcast.1, s32[2,1024]{1,0:T(2,128)} %param.8, s32[4,1024]{1,0:T(4,128)} %param.7), kind=kLoop, calls=%fused_computation.2 | loop fusion | flops 14336 | bytes 57344 | tf_op jit(solution)/shard_map/concatenate | solution.py:392
  2.4 0.0 collective-permute-done.emb_other_ref
  2.4 0.7 %pack.1 = (bf16[560,512]{1,0:T(8,128)(2,1)S(1)}, bf16[560,512]{1,0:T(8,128)(2,1)S(1)}) custom-call(bf16[512,256]{1,0:T(8,128)(2,1)S(1)} %get-tuple-element.66.emb_mine_ref, bf16[512,256]{1,0:T(8,128)(2,1)S(1)} %get-tuple-element.65.emb_rest_ref, bf16[1024,256]{1,0:T(8,128)(2,1)S(1)} %collective-permute-done.emb_other_ref, bf16[16,1024]{1,0:T(8,128)(2,1)S(1)} %copy-done, ...), custom_call_target="tpu_custom_call" | custom-call | tf_op jit(solution)/shard_map/pack/pallas_call | solution.py:104
  3.1 5.1 %collective-permute-start.2 = (bf16[560,512]{1,0:T(8,128)(2,1)S(1)}, bf16[560,512]{1,0:T(8,128)(2,1)S(1)}, u32[]{:S(2)}, u32[]{:S(2)}) collective-permute-start(bf16[560,512]{1,0:T(8,128)(2,1)S(1)} %get-tuple-element.34.refs_0_.refs_1_), channel_id=1, source_target_pairs={{4,0},{6,2},{8,4},{10,6},{12,8},{14,10},{0,12},{2,14},{5,1},{7,3},... | collective-permute-start | bytes 1720328 | tf_op jit(solution)/shard_map/ppermute | solution.py:396
  8.2 1.5 %collective-permute-start.3 = (bf16[560,512]{1,0:T(8,128)(2,1)S(1)}, bf16[560,512]{1,0:T(8,128)(2,1)S(1)}, u32[]{:S(2)}, u32[]{:S(2)}) collective-permute-start(bf16[560,512]{1,0:T(8,128)(2,1)S(1)} %get-tuple-element.34.refs_0_.refs_1_), channel_id=1, source_target_pairs={{0,2},{2,0},{4,6},{6,4},{8,10},{10,8},{12,14},{14,12},{1,3},{3,1},... | collective-permute-start | bytes 1720328 | tf_op jit(solution)/shard_map/ppermute | solution.py:397
  9.7 1.4 %collective-permute-start.7 = (bf16[560,512]{1,0:T(8,128)(2,1)S(1)}, bf16[560,512]{1,0:T(8,128)(2,1)S(1)}, u32[]{:S(2)}, u32[]{:S(2)}) collective-permute-start(bf16[560,512]{1,0:T(8,128)(2,1)S(1)} %get-tuple-element.34.refs_0_.refs_1_), channel_id=1, source_target_pairs={{0,8},{2,10},{12,4},{14,6},{1,9},{3,11},{13,5},{15,7},{16,24},{18,... | collective-permute-start | bytes 1720328 | tf_op jit(solution)/shard_map/ppermute | solution.py:396
  11.1 3.0 %tile.6 = (f32[40,512]{1,0:T(8,128)S(1)}, bf16[560,1024]{1,0:T(8,128)(2,1)S(1)}) custom-call(bf16[560,512]{1,0:T(8,128)(2,1)S(1)} %get-tuple-element.34.refs_0_.refs_1_, bf16[560,512]{1,0:T(8,128)(2,1)S(1)} %get-tuple-element.34.refs_0_.refs_1_, bf16[560,512]{1,0:T(8,128)(2,1)S(1)} %get-tuple-element.35.refs_2_), custom_call_target="tpu_custom_call" | custom-call | flops 1 | bytes 1 | tf_op jit(solution)/shard_map/tile/pallas_call | solution.py:247
  14.0 7.5 %collective-permute-done.2.refs_0_ = bf16[560,512]{1,0:T(8,128)(2,1)S(1)} collective-permute-done((bf16[560,512]{1,0:T(8,128)(2,1)S(1)}, bf16[560,512]{1,0:T(8,128)(2,1)S(1)}, u32[]{:S(2)}, u32[]{:S(2)}) %collective-permute-start.2) | collective-permute-done | bytes 573472 | tf_op jit(solution)/shard_map/ppermute | solution.py:396
  21.5 1.3 %collective-permute-done.3.refs_1_ = bf16[560,512]{1,0:T(8,128)(2,1)S(1)} collective-permute-done((bf16[560,512]{1,0:T(8,128)(2,1)S(1)}, bf16[560,512]{1,0:T(8,128)(2,1)S(1)}, u32[]{:S(2)}, u32[]{:S(2)}) %collective-permute-start.3) | collective-permute-done | bytes 573472 | tf_op jit(solution)/shard_map/ppermute | solution.py:397
  22.9 0.1 collective-permute-start.6
  23.0 0.6 collective-permute-start.5
  23.5 0.1 collective-permute-start.4
  23.6 2.9 %tile.7 = (f32[40,512]{1,0:T(8,128)S(1)}, f32[40,1024]{1,0:T(8,128)S(1)}) custom-call(bf16[560,512]{1,0:T(8,128)(2,1)S(1)} %collective-permute-done.2.refs_0_, bf16[560,1024]{1,0:T(8,128)(2,1)S(1)} %get-tuple-element.42.refs_1_), custom_call_target="tpu_custom_call" | custom-call | flops 1 | bytes 1 | tf_op jit(solution)/shard_map/tile/pallas_call | solution.py:247
  26.5 0.0 collective-permute-done.4
  26.6 2.9 %tile.8 = (f32[40,512]{1,0:T(8,128)S(1)}, bf16[560,1024]{1,0:T(8,128)(2,1)S(1)}) custom-call(bf16[560,512]{1,0:T(8,128)(2,1)S(1)} %get-tuple-element.34.refs_0_.refs_1_, bf16[560,512]{1,0:T(8,128)(2,1)S(1)} %collective-permute-done.3.refs_1_, bf16[560,512]{1,0:T(8,128)(2,1)S(1)} %pad_maximum_fusion.refs_2_), custom_call_target="tpu_custom_call" | custom-call | flops 1 | bytes 1 | tf_op jit(solution)/shard_map/tile/pallas_call | solution.py:247
  29.5 2.9 %tile.9 = (f32[40,512]{1,0:T(8,128)S(1)}, f32[40,1024]{1,0:T(8,128)S(1)}) custom-call(bf16[560,512]{1,0:T(8,128)(2,1)S(1)} %collective-permute-done.2.refs_0_, bf16[560,1024]{1,0:T(8,128)(2,1)S(1)} %get-tuple-element.48.refs_1_), custom_call_target="tpu_custom_call" | custom-call | flops 1 | bytes 1 | tf_op jit(solution)/shard_map/tile/pallas_call | solution.py:247
  32.4 0.1 collective-permute-start.8
  32.4 0.5 collective-permute-done.7.refs_0_
  33.0 6.0 %collective-permute-done.8.refs_2_ = f32[40,512]{1,0:T(8,128)S(1)} collective-permute-done((f32[40,512]{1,0:T(8,128)S(1)}, f32[40,512]{1,0:T(8,128)S(1)}, u32[]{:S(2)}, u32[]{:S(2)}) %collective-permute-start.8) | collective-permute-done | bytes 81952 | tf_op jit(solution)/shard_map/ppermute | solution.py:423
  39.1 1.3 %collective-permute-start.9 = (f32[40,512]{1,0:T(8,128)S(1)}, f32[40,512]{1,0:T(8,128)S(1)}, u32[]{:S(2)}, u32[]{:S(2)}) collective-permute-start(f32[40,512]{1,0:T(8,128)S(1)} %add.25), channel_id=1, source_target_pairs={{8,0},{10,2},{4,12},{6,14},{9,1},{11,3},{5,13},{7,15},{24,16},{26,... | collective-permute-start | bytes 245768 | tf_op jit(solution)/shard_map/ppermute | solution.py:423
  40.5 1.6 %collective-permute-start.11 = (f32[40,512]{1,0:T(8,128)S(1)}, f32[40,512]{1,0:T(8,128)S(1)}, u32[]{:S(2)}, u32[]{:S(2)}) collective-permute-start(f32[40,512]{1,0:T(8,128)S(1)} %slice_add_fusion), channel_id=1, source_target_pairs={{0,2},{2,0},{4,6},{6,4},{8,10},{10,8},{12,14},{14,12},{1,3},{3,1},... | collective-permute-start | bytes 245768 | tf_op jit(solution)/shard_map/ppermute | solution.py:427
  42.1 0.3 collective-permute-start.12
  42.3 4.4 %collective-permute-done.9.refs_3_ = f32[40,512]{1,0:T(8,128)S(1)} collective-permute-done((f32[40,512]{1,0:T(8,128)S(1)}, f32[40,512]{1,0:T(8,128)S(1)}, u32[]{:S(2)}, u32[]{:S(2)}) %collective-permute-start.9) | collective-permute-done | bytes 81952 | tf_op jit(solution)/shard_map/ppermute | solution.py:423
  46.8 0.9 %gram.1 = f32[16,8,128]{2,1,0:T(8,128)} custom-call(f32[32,512]{1,0:T(8,128)S(1)} %image.1.image_ref.mine_ref), custom_call_target="tpu_custom_call" | custom-call | tf_op jit(solution)/shard_map/gram/pallas_call | solution.py:301
  47.7 4.2 %all-to-all-start = ((f32[16,8,128]{2,1,0:T(8,128)}), f32[16,8,128]{2,1,0:T(8,128)S(1)}, u32[]{:S(2)}, u32[]{:S(2)}) async-start(f32[16,8,128]{2,1,0:T(8,128)} %gram.1), calls=%async_computation | async-start | bytes 131072 | tf_op jit(solution)/shard_map/all_to_all | solution.py:432
  51.9 0.4 collective-permute-start.13
  52.3 0.9 %collective-permute-done.13.other_ref = f32[32,512]{1,0:T(8,128)S(1)} collective-permute-done((f32[32,512]{1,0:T(8,128)S(1)}, f32[32,512]{1,0:T(8,128)S(1)}, u32[]{:S(2)}, u32[]{:S(2)}) %collective-permute-start.13) | collective-permute-done | bytes 65568 | tf_op jit(solution)/shard_map/ppermute | solution.py:431
  53.2 5.6 %all-to-all-done.grams_ref = f32[16,8,128]{2,1,0:T(8,128)S(1)} async-done(((f32[16,8,128]{2,1,0:T(8,128)}), f32[16,8,128]{2,1,0:T(8,128)S(1)}, u32[]{:S(2)}, u32[]{:S(2)}) %all-to-all-start) | async-done | bytes 65568 | tf_op jit(solution)/shard_map/all_to_all | solution.py:432
  58.8 2.9 %basis.1 = f32[16,1024]{1,0:T(8,128)} custom-call(f32[16,8,128]{2,1,0:T(8,128)S(1)} %all-to-all-done.grams_ref, f32[32,512]{1,0:T(8,128)S(1)} %image.1.image_ref.mine_ref, f32[32,512]{1,0:T(8,128)S(1)} %collective-permute-done.13.other_ref), custom_call_target="tpu_custom_call" | custom-call | tf_op jit(solution)/shard_map/basis/pallas_call | solution.py:351
  (22 shorter events, 0.3 us)
Async XLA Ops:
  0.0 2.4 %copy-start = (bf16[16,1024]{1,0:T(8,128)(2,1)S(1)}, bf16[16,1024]{1,0:T(8,128)(2,1)}, u32[]{:S(2)}) copy-start(bf16[16,1024]{1,0:T(8,128)(2,1)} %vec_ref.1) | copy-start | bytes 98308
  0.0 2.4 %collective-permute-start = (bf16[1024,256]{1,0:T(8,128)(2,1)}, bf16[1024,256]{1,0:T(8,128)(2,1)S(1)}, u32[]{:S(2)}, u32[]{:S(2)}) collective-permute-start(bf16[1024,256]{1,0:T(8,128)(2,1)} %param.5), channel_id=1, source_target_pairs={{0,1},{1,0},{2,3},{3,2},{4,5},{5,4},{6,7},{7,6},{8,9},{9,8},{10,11... | collective-permute-start | bytes 1572872 | tf_op jit(solution)/shard_map/ppermute | solution.py:390
  0.5 1.9 %collective-permute-start.1 = (bf16[16,1024]{1,0:T(8,128)(2,1)}, bf16[16,1024]{1,0:T(8,128)(2,1)S(1)}, u32[]{:S(2)}, u32[]{:S(2)}) collective-permute-start(bf16[16,1024]{1,0:T(8,128)(2,1)} %vec_ref.1), channel_id=1, source_target_pairs={{0,1},{1,0},{2,3},{3,2},{4,5},{5,4},{6,7},{7,6},{8,9},{9,8},{10,11... | collective-permute-start | bytes 98312 | tf_op jit(solution)/shard_map/ppermute | solution.py:391
  3.1 18.4 %collective-permute-start.2 = (bf16[560,512]{1,0:T(8,128)(2,1)S(1)}, bf16[560,512]{1,0:T(8,128)(2,1)S(1)}, u32[]{:S(2)}, u32[]{:S(2)}) collective-permute-start(bf16[560,512]{1,0:T(8,128)(2,1)S(1)} %get-tuple-element.34.refs_0_.refs_1_), channel_id=1, source_target_pairs={{4,0},{6,2},{8,4},{10,6},{12,8},{14,10},{0,12},{2,14},{5,1},{7,3},... | collective-permute-start | bytes 1720328 | tf_op jit(solution)/shard_map/ppermute | solution.py:396
  8.2 14.7 %collective-permute-start.3 = (bf16[560,512]{1,0:T(8,128)(2,1)S(1)}, bf16[560,512]{1,0:T(8,128)(2,1)S(1)}, u32[]{:S(2)}, u32[]{:S(2)}) collective-permute-start(bf16[560,512]{1,0:T(8,128)(2,1)S(1)} %get-tuple-element.34.refs_0_.refs_1_), channel_id=1, source_target_pairs={{0,2},{2,0},{4,6},{6,4},{8,10},{10,8},{12,14},{14,12},{1,3},{3,1},... | collective-permute-start | bytes 1720328 | tf_op jit(solution)/shard_map/ppermute | solution.py:397
  9.7 23.2 %collective-permute-start.7 = (bf16[560,512]{1,0:T(8,128)(2,1)S(1)}, bf16[560,512]{1,0:T(8,128)(2,1)S(1)}, u32[]{:S(2)}, u32[]{:S(2)}) collective-permute-start(bf16[560,512]{1,0:T(8,128)(2,1)S(1)} %get-tuple-element.34.refs_0_.refs_1_), channel_id=1, source_target_pairs={{0,8},{2,10},{12,4},{14,6},{1,9},{3,11},{13,5},{15,7},{16,24},{18,... | collective-permute-start | bytes 1720328 | tf_op jit(solution)/shard_map/ppermute | solution.py:396
  22.9 3.6 %collective-permute-start.6 = (bf16[208,512]{1,0:T(8,128)(2,1)S(1)}, bf16[208,512]{1,0:T(8,128)(2,1)S(1)}, u32[]{:S(2)}, u32[]{:S(2)}) collective-permute-start(bf16[208,512]{1,0:T(8,128)(2,1)S(1)} %slice.23), channel_id=1, source_target_pairs={{0,1},{1,0},{2,3},{3,2},{4,5},{5,4},{6,7},{7,6},{8,9},{9,8},{10,11... | collective-permute-start | bytes 638984 | tf_op jit(solution)/shard_map/ppermute | solution.py:404
  23.0 3.5 %collective-permute-start.5 = (bf16[176,512]{1,0:T(8,128)(2,1)S(1)}, bf16[176,512]{1,0:T(8,128)(2,1)S(1)}, u32[]{:S(2)}, u32[]{:S(2)}) collective-permute-start(bf16[176,512]{1,0:T(8,128)(2,1)S(1)} %get-tuple-element.64), channel_id=1, source_target_pairs={{0,1},{1,0},{2,3},{3,2},{4,5},{5,4},{6,7},{7,6},{8,9},{9,8},{10,11... | collective-permute-start | bytes 540680 | tf_op jit(solution)/shard_map/ppermute | solution.py:404
  23.5 3.0 %collective-permute-start.4 = (bf16[176,512]{1,0:T(8,128)(2,1)S(1)}, bf16[176,512]{1,0:T(8,128)(2,1)S(1)}, u32[]{:S(2)}, u32[]{:S(2)}) collective-permute-start(bf16[176,512]{1,0:T(8,128)(2,1)S(1)} %get-tuple-element.63), channel_id=1, source_target_pairs={{0,1},{1,0},{2,3},{3,2},{4,5},{5,4},{6,7},{7,6},{8,9},{9,8},{10,11... | collective-permute-start | bytes 540680 | tf_op jit(solution)/shard_map/ppermute | solution.py:404
  32.4 6.6 %collective-permute-start.8 = (f32[40,512]{1,0:T(8,128)S(1)}, f32[40,512]{1,0:T(8,128)S(1)}, u32[]{:S(2)}, u32[]{:S(2)}) collective-permute-start(f32[40,512]{1,0:T(8,128)S(1)} %add.24), channel_id=1, source_target_pairs={{0,4},{2,6},{4,8},{6,10},{8,12},{10,14},{12,0},{14,2},{1,5},{3,7},... | collective-permute-start | bytes 245768 | tf_op jit(solution)/shard_map/ppermute | solution.py:423
  39.0 1.4 %collective-permute-start.10 = (f32[40,512]{1,0:T(8,128)S(1)}, f32[40,512]{1,0:T(8,128)S(1)}, u32[]{:S(2)}, u32[]{:S(2)}) collective-permute-start(f32[40,512]{1,0:T(8,128)S(1)} %slice.25), channel_id=1, source_target_pairs={{0,1},{1,0},{2,3},{3,2},{4,5},{5,4},{6,7},{7,6},{8,9},{9,8},{10,11... | collective-permute-start | bytes 245768 | tf_op jit(solution)/shard_map/ppermute | solution.py:425
  39.1 7.6 %collective-permute-start.9 = (f32[40,512]{1,0:T(8,128)S(1)}, f32[40,512]{1,0:T(8,128)S(1)}, u32[]{:S(2)}, u32[]{:S(2)}) collective-permute-start(f32[40,512]{1,0:T(8,128)S(1)} %add.25), channel_id=1, source_target_pairs={{8,0},{10,2},{4,12},{6,14},{9,1},{11,3},{5,13},{7,15},{24,16},{26,... | collective-permute-start | bytes 245768 | tf_op jit(solution)/shard_map/ppermute | solution.py:423
  40.5 6.3 %collective-permute-start.11 = (f32[40,512]{1,0:T(8,128)S(1)}, f32[40,512]{1,0:T(8,128)S(1)}, u32[]{:S(2)}, u32[]{:S(2)}) collective-permute-start(f32[40,512]{1,0:T(8,128)S(1)} %slice_add_fusion), channel_id=1, source_target_pairs={{0,2},{2,0},{4,6},{6,4},{8,10},{10,8},{12,14},{14,12},{1,3},{3,1},... | collective-permute-start | bytes 245768 | tf_op jit(solution)/shard_map/ppermute | solution.py:427
  42.1 4.7 %collective-permute-start.12 = (f32[40,512]{1,0:T(8,128)S(1)}, f32[40,512]{1,0:T(8,128)S(1)}, u32[]{:S(2)}, u32[]{:S(2)}) collective-permute-start(f32[40,512]{1,0:T(8,128)S(1)} %get-tuple-element.67), channel_id=1, source_target_pairs={{0,1},{1,0},{2,3},{3,2},{4,5},{5,4},{6,7},{7,6},{8,9},{9,8},{10,11... | collective-permute-start | bytes 245768 | tf_op jit(solution)/shard_map/ppermute | solution.py:429
  47.7 11.1 %all-to-all-start = ((f32[16,8,128]{2,1,0:T(8,128)}), f32[16,8,128]{2,1,0:T(8,128)S(1)}, u32[]{:S(2)}, u32[]{:S(2)}) async-start(f32[16,8,128]{2,1,0:T(8,128)} %gram.1), calls=%async_computation | async-start | bytes 131072 | tf_op jit(solution)/shard_map/all_to_all | solution.py:432
  51.9 1.3 %collective-permute-start.13 = (f32[32,512]{1,0:T(8,128)S(1)}, f32[32,512]{1,0:T(8,128)S(1)}, u32[]{:S(2)}, u32[]{:S(2)}) collective-permute-start(f32[32,512]{1,0:T(8,128)S(1)} %image.1.image_ref.mine_ref), channel_id=1, source_target_pairs={{0,1},{1,0},{2,3},{3,2},{4,5},{5,4},{6,7},{7,6},{8,9},{9,8},{10,11... | collective-permute-start | bytes 196616 | tf_op jit(solution)/shard_map/ppermute | solution.py:431

commit v20 on v18

--- a/solution.py
+++ b/solution.py
@@ -154,55 +154,47 @@
     vec_rows, code_rows = slice(features, features + vecs), slice(features + vecs, size)
     row_out_ref[...] = jnp.zeros_like(row_out_ref)
 
-    def block(col_ref, done):
-        chunks = col_ref.shape[1] // WIDE
-
-        def place(step, base=0):
-            return pl.ds(pl.multiple_of(base + step * WIDE, WIDE), WIDE)
-
-        def multiply(step, product_ref):
-            product_ref[...] = jnp.dot(
-                row_ref[0:rows, :], col_ref[0:features, place(step)], preferred_element_type=jnp.float32
-            )
-
-        def weigh(step, product_ref, weight_ref):
-            for field, values in enumerate(decode(col_ref[code_rows, place(step)])):
-                col_spread_ref[field] = jnp.broadcast_to(values, (8, WIDE))
-            for start in range(0, rows, GROUP):
-                row_part = slice(start, start + GROUP)
-
-                def row(field):
-                    return jnp.concatenate([spread_ref[field, row_part, :]] * (WIDE // LANES), axis=1)
-
-                def col(field):
-                    return jnp.concatenate([col_spread_ref[field]] * (GROUP // 8), axis=0)
-
-                same = None
-                if own_block:
-                    row_ids = lax.broadcasted_iota(jnp.int32, (GROUP, WIDE), 0) + (start - step * WIDE)
-                    same = row_ids == lax.broadcasted_iota(jnp.int32, (GROUP, WIDE), 1)
-                weight_ref[row_part, :] = weights_of(product_ref[row_part, :], row, col, same).astype(jnp.bfloat16)
-
-        def total(step, weight_ref):
-            col_vecs = with_ones(col_ref[vec_rows, place(step)])
-            row_out_ref[...] += dot_nt(col_vecs, weight_ref[...])[0:OUT_ROWS]
-            if not turns:
-                col_out_ref[:, place(step, done)] = jnp.dot(
-                    row_vec_ref[...], weight_ref[...], preferred_element_type=jnp.float32
-                )[0:OUT_ROWS]
-
-        def steps(index, carry):
-            for parity in range(2):
-                step = 2 * index + parity
-                multiply(lax.rem(step + 1, chunks), products[1 - parity])
-                weigh(step, products[parity], weights[parity])
-                total(lax.rem(step + chunks - 1, chunks), weights[1 - parity])
-            return carry
-
-        multiply(0, products[0])
-        weights[1][...] = jnp.zeros_like(weights[1])
-        lax.fori_loop(0, chunks // 2, steps, 0)
-        total(chunks - 1, weights[1])
+    def multiply(chunk, product_ref):
+        col_ref, part, _ = chunk
+        product_ref[...] = jnp.dot(row_ref[0:rows, :], col_ref[0:features, part], preferred_element_type=jnp.float32)
+
+    def weigh(chunk, product_ref, weight_ref):
+        col_ref, part, done = chunk
+        for field, values in enumerate(decode(col_ref[code_rows, part])):
+            col_spread_ref[field] = jnp.broadcast_to(values, (8, WIDE))
+        for start in range(0, rows, GROUP):
+            row_part = slice(start, start + GROUP)
+
+            def row(field):
+                return jnp.concatenate([spread_ref[field, row_part, :]] * (WIDE // LANES), axis=1)
+
+            def col(field):
+                return jnp.concatenate([col_spread_ref[field]] * (GROUP // 8), axis=0)
+
+            same = None
+            if own_block and done < rows:
+                row_ids = lax.broadcasted_iota(jnp.int32, (GROUP, WIDE), 0) + (start - done)
+                same = row_ids == lax.broadcasted_iota(jnp.int32, (GROUP, WIDE), 1)
+            weight_ref[row_part, :] = weights_of(product_ref[row_part, :], row, col, same).astype(jnp.bfloat16)
+
+    def total(chunk, weight_ref):
+        col_ref, part, done = chunk
+        row_out_ref[...] += dot_nt(with_ones(col_ref[vec_rows, part]), weight_ref[...])[0:OUT_ROWS]
+        if not turns:
+            col_out_ref[:, done : done + WIDE] = jnp.dot(
+                row_vec_ref[...], weight_ref[...], preferred_element_type=jnp.float32
+            )[0:OUT_ROWS]
+
+    def pipeline(chunks):
+        multiply(chunks[0], products[0])
+        for step, chunk in enumerate(chunks):
+            now, later = step % 2, (step + 1) % 2
+            if step + 1 < len(chunks):
+                multiply(chunks[step + 1], products[later])
+            weigh(chunk, products[now], weights[now])
+            if step > 0:
+                total(chunks[step - 1], weights[later])
+        total(chunks[-1], weights[(len(chunks) - 1) % 2])
 
     def compute():
         for field, values in enumerate(decode(row_ref[code_rows, :])):
@@ -216,12 +208,12 @@
                 part = pl.ds(number * rows, rows)
                 col_out_ref[0:features, part] = pack_ref[0:rows, :].T
                 col_out_ref[features:size, part] = pack_ref[features:size, :]
-            block(col_out_ref, 0)
-        else:
-            done = 0
-            for col_ref in col_refs:
-                block(col_ref, done)
-                done += col_ref.shape[1]
+        sources = [col_out_ref] if turns else col_refs
+        chunks = []
+        for source in sources:
+            for start in range(0, source.shape[1], WIDE):
+                chunks.append((source, slice(start, start + WIDE), len(chunks) * WIDE))
+        pipeline(chunks)
 
     if receivers is None:
         compute()

time: 61.8 us -> 61.5 us (level)
  transfers between devices with their start and end apart: 15 -> 15, of which waited for: 7 -> 7; matrix products, arithmetic and copies ran while one was open for 3% -> 3% of each run, Pallas kernels for 19% -> 18%
where the time goes in v20:
time: 61.5 us; the launch traced here: 61.1 us
  waiting for transfers between devices  24.9 us (40%)
  starting transfers between devices  18.2 us (30%)
  Pallas kernels  15.8 us (26%)
  local copies, waits for them, and re-layouts  1.13 us (2%)
  other arithmetic  0.89 us (1%)
    pallas_call x6, Pallas kernels, tile(): pl.pallas_call(functools.partial(tile_kernel, len(columns), turns, own_bl...  11.3 us
    ppermute x2, waiting for transfers between devices, local(): parts.append(lax.ppermute(own_lines + next_lines, 'blk', back(moves)))  10.9 us
    ppermute x2, starting transfers between devices, local(): sent = [lax.ppermute(mine, 'blk', moves) for moves, _ in plans]  7.36 us
    ppermute x2, waiting for transfers between devices, local(): sent = [lax.ppermute(mine, 'blk', moves) for moves, _ in plans]  6.22 us
    all_to_all x1, waiting for transfers between devices, local(): lax.all_to_all(grams_of(image, 2 * blocks), ('blk', 'sub'), 0, 0, tiled=T...  5.58 us
    all_to_all x1, starting transfers between devices, local(): lax.all_to_all(grams_of(image, 2 * blocks), ('blk', 'sub'), 0, 0, tiled=T...  4.24 us
    pallas_call x1, Pallas kernels, basis_of(): pl.pallas_call(functools.partial(basis_kernel, total_rows), out_shape=jax...  2.89 us
    ppermute x2, starting transfers between devices, local(): parts.append(lax.ppermute(own_lines + next_lines, 'blk', back(moves)))  1.62 us
  transfers between devices with their start and end apart: 15, of which 7 were waited for; matrix products, arithmetic and copies ran while one was open for 3% of the time, Pallas kernels for 18%

profile of v20, /device:TPU:0, one launch (start us, length us, event | category | flops | bytes accessed | tf_op | source)
XLA Modules:
  0.0 61.1 jit_solution(5747435122499457106)
XLA Ops:
  0.0 0.5 collective-permute-start
  0.5 0.1 collective-permute-start.1
  0.5 1.1 %constant_dynamic-slice_fusion = (bf16[512,256]{1,0:T(8,128)(2,1)S(1)}, bf16[512,256]{1,0:T(8,128)(2,1)S(1)}) fusion(bf16[1024,256]{1,0:T(8,128)(2,1)} %param.5, s32[]{:T(128)S(6)} %select_n.7, s32[]{:T(128)S(6)} %select_n.6), kind=kLoop, calls=%fused_computation.3 | loop fusion | bytes 1048584 | tf_op jit(solution)/shard_map/dynamic_slice | solution.py:388
  1.6 0.8 %pad_add_fusion.meta_ref = s32[7,1024]{1,0:T(8,128)S(1)} fusion(s32[1,1024]{1,0:T(1,128)} %bitcast.1, s32[2,1024]{1,0:T(2,128)} %param.8, s32[4,1024]{1,0:T(4,128)} %param.7), kind=kLoop, calls=%fused_computation.2 | loop fusion | flops 14336 | bytes 57344 | tf_op jit(solution)/shard_map/concatenate | solution.py:386
  2.4 0.0 collective-permute-done.emb_other_ref
  2.4 0.7 %pack.1 = (bf16[560,512]{1,0:T(8,128)(2,1)S(1)}, bf16[560,512]{1,0:T(8,128)(2,1)S(1)}) custom-call(bf16[512,256]{1,0:T(8,128)(2,1)S(1)} %get-tuple-element.66.emb_mine_ref, bf16[512,256]{1,0:T(8,128)(2,1)S(1)} %get-tuple-element.65.emb_rest_ref, bf16[1024,256]{1,0:T(8,128)(2,1)S(1)} %collective-permute-done.emb_other_ref, bf16[16,1024]{1,0:T(8,128)(2,1)S(1)} %copy-done, ...), custom_call_target="tpu_custom_call" | custom-call | tf_op jit(solution)/shard_map/pack/pallas_call | solution.py:104
  3.1 4.1 %collective-permute-start.2 = (bf16[560,512]{1,0:T(8,128)(2,1)S(1)}, bf16[560,512]{1,0:T(8,128)(2,1)S(1)}, u32[]{:S(2)}, u32[]{:S(2)}) collective-permute-start(bf16[560,512]{1,0:T(8,128)(2,1)S(1)} %get-tuple-element.34.refs_0_.refs_1_), channel_id=1, source_target_pairs={{0,8},{2,10},{12,4},{14,6},{4,0},{6,2},{8,12},{10,14},{1,9},{3,11}... | collective-permute-start | bytes 1720328 | tf_op jit(solution)/shard_map/ppermute | solution.py:390
  7.2 1.5 %collective-permute-start.3 = (bf16[560,512]{1,0:T(8,128)(2,1)S(1)}, bf16[560,512]{1,0:T(8,128)(2,1)S(1)}, u32[]{:S(2)}, u32[]{:S(2)}) collective-permute-start(bf16[560,512]{1,0:T(8,128)(2,1)S(1)} %get-tuple-element.34.refs_0_.refs_1_), channel_id=1, source_target_pairs={{0,2},{2,0},{4,6},{6,4},{8,10},{10,8},{12,14},{14,12},{1,3},{3,1},... | collective-permute-start | bytes 1720328 | tf_op jit(solution)/shard_map/ppermute | solution.py:391
  8.7 3.3 %collective-permute-start.7 = (bf16[560,512]{1,0:T(8,128)(2,1)S(1)}, bf16[560,512]{1,0:T(8,128)(2,1)S(1)}, u32[]{:S(2)}, u32[]{:S(2)}) collective-permute-start(bf16[560,512]{1,0:T(8,128)(2,1)S(1)} %get-tuple-element.34.refs_0_.refs_1_), channel_id=1, source_target_pairs={{8,4},{10,6},{0,12},{2,14},{9,5},{11,7},{1,13},{3,15},{24,20},{26,... | collective-permute-start | bytes 1720328 | tf_op jit(solution)/shard_map/ppermute | solution.py:390
  12.0 2.9 %tile.6 = (f32[40,512]{1,0:T(8,128)S(1)}, bf16[560,1024]{1,0:T(8,128)(2,1)S(1)}) custom-call(bf16[560,512]{1,0:T(8,128)(2,1)S(1)} %get-tuple-element.34.refs_0_.refs_1_, bf16[560,512]{1,0:T(8,128)(2,1)S(1)} %get-tuple-element.34.refs_0_.refs_1_, bf16[560,512]{1,0:T(8,128)(2,1)S(1)} %get-tuple-element.35.refs_2_), custom_call_target="tpu_custom_call" | custom-call | flops 1 | bytes 1 | tf_op jit(solution)/shard_map/tile/pallas_call | solution.py:239
  14.9 5.6 %collective-permute-done.2.refs_0_ = bf16[560,512]{1,0:T(8,128)(2,1)S(1)} collective-permute-done((bf16[560,512]{1,0:T(8,128)(2,1)S(1)}, bf16[560,512]{1,0:T(8,128)(2,1)S(1)}, u32[]{:S(2)}, u32[]{:S(2)}) %collective-permute-start.2) | collective-permute-done | bytes 573472 | tf_op jit(solution)/shard_map/ppermute | solution.py:390
  20.5 1.3 %collective-permute-done.3.refs_1_ = bf16[560,512]{1,0:T(8,128)(2,1)S(1)} collective-permute-done((bf16[560,512]{1,0:T(8,128)(2,1)S(1)}, bf16[560,512]{1,0:T(8,128)(2,1)S(1)}, u32[]{:S(2)}, u32[]{:S(2)}) %collective-permute-start.3) | collective-permute-done | bytes 573472 | tf_op jit(solution)/shard_map/ppermute | solution.py:391
  21.9 0.1 collective-permute-start.6
  22.0 0.6 collective-permute-start.5
  22.5 0.1 collective-permute-start.4
  22.6 2.7 %tile.7 = (f32[40,512]{1,0:T(8,128)S(1)}, f32[40,1024]{1,0:T(8,128)S(1)}) custom-call(bf16[560,512]{1,0:T(8,128)(2,1)S(1)} %collective-permute-done.2.refs_0_, bf16[560,1024]{1,0:T(8,128)(2,1)S(1)} %get-tuple-element.42.refs_1_), custom_call_target="tpu_custom_call" | custom-call | flops 1 | bytes 1 | tf_op jit(solution)/shard_map/tile/pallas_call | solution.py:239
  25.3 0.0 collective-permute-done.6
  25.4 2.9 %tile.8 = (f32[40,512]{1,0:T(8,128)S(1)}, bf16[560,1024]{1,0:T(8,128)(2,1)S(1)}) custom-call(bf16[560,512]{1,0:T(8,128)(2,1)S(1)} %get-tuple-element.34.refs_0_.refs_1_, bf16[560,512]{1,0:T(8,128)(2,1)S(1)} %collective-permute-done.3.refs_1_, bf16[560,512]{1,0:T(8,128)(2,1)S(1)} %pad_maximum_fusion.refs_2_), custom_call_target="tpu_custom_call" | custom-call | flops 1 | bytes 1 | tf_op jit(solution)/shard_map/tile/pallas_call | solution.py:239
  28.3 2.7 %tile.9 = (f32[40,512]{1,0:T(8,128)S(1)}, f32[40,1024]{1,0:T(8,128)S(1)}) custom-call(bf16[560,512]{1,0:T(8,128)(2,1)S(1)} %collective-permute-done.2.refs_0_, bf16[560,1024]{1,0:T(8,128)(2,1)S(1)} %get-tuple-element.48.refs_1_), custom_call_target="tpu_custom_call" | custom-call | flops 1 | bytes 1 | tf_op jit(solution)/shard_map/tile/pallas_call | solution.py:239
  31.0 0.3 collective-permute-start.8
  31.3 0.6 collective-permute-done.7.refs_0_
  32.0 4.8 %collective-permute-done.8.refs_2_ = f32[40,512]{1,0:T(8,128)S(1)} collective-permute-done((f32[40,512]{1,0:T(8,128)S(1)}, f32[40,512]{1,0:T(8,128)S(1)}, u32[]{:S(2)}, u32[]{:S(2)}) %collective-permute-start.8) | collective-permute-done | bytes 81952 | tf_op jit(solution)/shard_map/ppermute | solution.py:417
  36.8 1.3 %collective-permute-start.9 = (f32[40,512]{1,0:T(8,128)S(1)}, f32[40,512]{1,0:T(8,128)S(1)}, u32[]{:S(2)}, u32[]{:S(2)}) collective-permute-start(f32[40,512]{1,0:T(8,128)S(1)} %add.25), channel_id=1, source_target_pairs={{4,8},{6,10},{12,0},{14,2},{5,9},{7,11},{13,1},{15,3},{20,24},{22,... | collective-permute-start | bytes 245768 | tf_op jit(solution)/shard_map/ppermute | solution.py:417
  38.2 1.6 %collective-permute-start.11 = (f32[40,512]{1,0:T(8,128)S(1)}, f32[40,512]{1,0:T(8,128)S(1)}, u32[]{:S(2)}, u32[]{:S(2)}) collective-permute-start(f32[40,512]{1,0:T(8,128)S(1)} %slice_add_fusion), channel_id=1, source_target_pairs={{0,2},{2,0},{4,6},{6,4},{8,10},{10,8},{12,14},{14,12},{1,3},{3,1},... | collective-permute-start | bytes 245768 | tf_op jit(solution)/shard_map/ppermute | solution.py:421
  39.8 0.3 collective-permute-start.12
  40.1 6.1 %collective-permute-done.9.refs_3_ = f32[40,512]{1,0:T(8,128)S(1)} collective-permute-done((f32[40,512]{1,0:T(8,128)S(1)}, f32[40,512]{1,0:T(8,128)S(1)}, u32[]{:S(2)}, u32[]{:S(2)}) %collective-permute-start.9) | collective-permute-done | bytes 81952 | tf_op jit(solution)/shard_map/ppermute | solution.py:417
  46.2 0.9 %gram.1 = f32[16,8,128]{2,1,0:T(8,128)} custom-call(f32[32,512]{1,0:T(8,128)S(1)} %image.1.image_ref.mine_ref), custom_call_target="tpu_custom_call" | custom-call | tf_op jit(solution)/shard_map/gram/pallas_call | solution.py:293
  47.1 4.2 %all-to-all-start = ((f32[16,8,128]{2,1,0:T(8,128)}), f32[16,8,128]{2,1,0:T(8,128)S(1)}, u32[]{:S(2)}, u32[]{:S(2)}) async-start(f32[16,8,128]{2,1,0:T(8,128)} %gram.1), calls=%async_computation | async-start | bytes 131072 | tf_op jit(solution)/shard_map/all_to_all | solution.py:426
  51.4 0.4 collective-permute-start.13
  51.8 0.9 %collective-permute-done.13.other_ref = f32[32,512]{1,0:T(8,128)S(1)} collective-permute-done((f32[32,512]{1,0:T(8,128)S(1)}, f32[32,512]{1,0:T(8,128)S(1)}, u32[]{:S(2)}, u32[]{:S(2)}) %collective-permute-start.13) | collective-permute-done | bytes 65568 | tf_op jit(solution)/shard_map/ppermute | solution.py:425
  52.7 5.6 %all-to-all-done.grams_ref = f32[16,8,128]{2,1,0:T(8,128)S(1)} async-done(((f32[16,8,128]{2,1,0:T(8,128)}), f32[16,8,128]{2,1,0:T(8,128)S(1)}, u32[]{:S(2)}, u32[]{:S(2)}) %all-to-all-start) | async-done | bytes 65568 | tf_op jit(solution)/shard_map/all_to_all | solution.py:426
  58.3 2.9 %basis.1 = f32[16,1024]{1,0:T(8,128)} custom-call(f32[16,8,128]{2,1,0:T(8,128)S(1)} %all-to-all-done.grams_ref, f32[32,512]{1,0:T(8,128)S(1)} %image.1.image_ref.mine_ref, f32[32,512]{1,0:T(8,128)S(1)} %collective-permute-done.13.other_ref), custom_call_target="tpu_custom_call" | custom-call | tf_op jit(solution)/shard_map/basis/pallas_call | solution.py:343
  (22 shorter events, 0.3 us)
Async XLA Ops:
  0.0 2.4 %copy-start = (bf16[16,1024]{1,0:T(8,128)(2,1)S(1)}, bf16[16,1024]{1,0:T(8,128)(2,1)}, u32[]{:S(2)}) copy-start(bf16[16,1024]{1,0:T(8,128)(2,1)} %vec_ref.1) | copy-start | bytes 98308
  0.0 2.4 %collective-permute-start = (bf16[1024,256]{1,0:T(8,128)(2,1)}, bf16[1024,256]{1,0:T(8,128)(2,1)S(1)}, u32[]{:S(2)}, u32[]{:S(2)}) collective-permute-start(bf16[1024,256]{1,0:T(8,128)(2,1)} %param.5), channel_id=1, source_target_pairs={{0,1},{1,0},{2,3},{3,2},{4,5},{5,4},{6,7},{7,6},{8,9},{9,8},{10,11... | collective-permute-start | bytes 1572872 | tf_op jit(solution)/shard_map/ppermute | solution.py:384
  0.5 1.9 %collective-permute-start.1 = (bf16[16,1024]{1,0:T(8,128)(2,1)}, bf16[16,1024]{1,0:T(8,128)(2,1)S(1)}, u32[]{:S(2)}, u32[]{:S(2)}) collective-permute-start(bf16[16,1024]{1,0:T(8,128)(2,1)} %vec_ref.1), channel_id=1, source_target_pairs={{0,1},{1,0},{2,3},{3,2},{4,5},{5,4},{6,7},{7,6},{8,9},{9,8},{10,11... | collective-permute-start | bytes 98312 | tf_op jit(solution)/shard_map/ppermute | solution.py:385
  3.1 17.4 %collective-permute-start.2 = (bf16[560,512]{1,0:T(8,128)(2,1)S(1)}, bf16[560,512]{1,0:T(8,128)(2,1)S(1)}, u32[]{:S(2)}, u32[]{:S(2)}) collective-permute-start(bf16[560,512]{1,0:T(8,128)(2,1)S(1)} %get-tuple-element.34.refs_0_.refs_1_), channel_id=1, source_target_pairs={{0,8},{2,10},{12,4},{14,6},{4,0},{6,2},{8,12},{10,14},{1,9},{3,11}... | collective-permute-start | bytes 1720328 | tf_op jit(solution)/shard_map/ppermute | solution.py:390
  7.2 14.7 %collective-permute-start.3 = (bf16[560,512]{1,0:T(8,128)(2,1)S(1)}, bf16[560,512]{1,0:T(8,128)(2,1)S(1)}, u32[]{:S(2)}, u32[]{:S(2)}) collective-permute-start(bf16[560,512]{1,0:T(8,128)(2,1)S(1)} %get-tuple-element.34.refs_0_.refs_1_), channel_id=1, source_target_pairs={{0,2},{2,0},{4,6},{6,4},{8,10},{10,8},{12,14},{14,12},{1,3},{3,1},... | collective-permute-start | bytes 1720328 | tf_op jit(solution)/shard_map/ppermute | solution.py:391
  8.7 23.2 %collective-permute-start.7 = (bf16[560,512]{1,0:T(8,128)(2,1)S(1)}, bf16[560,512]{1,0:T(8,128)(2,1)S(1)}, u32[]{:S(2)}, u32[]{:S(2)}) collective-permute-start(bf16[560,512]{1,0:T(8,128)(2,1)S(1)} %get-tuple-element.34.refs_0_.refs_1_), channel_id=1, source_target_pairs={{8,4},{10,6},{0,12},{2,14},{9,5},{11,7},{1,13},{3,15},{24,20},{26,... | collective-permute-start | bytes 1720328 | tf_op jit(solution)/shard_map/ppermute | solution.py:390
  21.9 3.5 %collective-permute-start.6 = (bf16[208,512]{1,0:T(8,128)(2,1)S(1)}, bf16[208,512]{1,0:T(8,128)(2,1)S(1)}, u32[]{:S(2)}, u32[]{:S(2)}) collective-permute-start(bf16[208,512]{1,0:T(8,128)(2,1)S(1)} %slice.23), channel_id=1, source_target_pairs={{0,1},{1,0},{2,3},{3,2},{4,5},{5,4},{6,7},{7,6},{8,9},{9,8},{10,11... | collective-permute-start | bytes 638984 | tf_op jit(solution)/shard_map/ppermute | solution.py:398
  22.0 3.4 %collective-permute-start.5 = (bf16[176,512]{1,0:T(8,128)(2,1)S(1)}, bf16[176,512]{1,0:T(8,128)(2,1)S(1)}, u32[]{:S(2)}, u32[]{:S(2)}) collective-permute-start(bf16[176,512]{1,0:T(8,128)(2,1)S(1)} %get-tuple-element.64), channel_id=1, source_target_pairs={{0,1},{1,0},{2,3},{3,2},{4,5},{5,4},{6,7},{7,6},{8,9},{9,8},{10,11... | collective-permute-start | bytes 540680 | tf_op jit(solution)/shard_map/ppermute | solution.py:398
  22.5 2.8 %collective-permute-start.4 = (bf16[176,512]{1,0:T(8,128)(2,1)S(1)}, bf16[176,512]{1,0:T(8,128)(2,1)S(1)}, u32[]{:S(2)}, u32[]{:S(2)}) collective-permute-start(bf16[176,512]{1,0:T(8,128)(2,1)S(1)} %get-tuple-element.63), channel_id=1, source_target_pairs={{0,1},{1,0},{2,3},{3,2},{4,5},{5,4},{6,7},{7,6},{8,9},{9,8},{10,11... | collective-permute-start | bytes 540680 | tf_op jit(solution)/shard_map/ppermute | solution.py:398
  31.0 5.7 %collective-permute-start.8 = (f32[40,512]{1,0:T(8,128)S(1)}, f32[40,512]{1,0:T(8,128)S(1)}, u32[]{:S(2)}, u32[]{:S(2)}) collective-permute-start(f32[40,512]{1,0:T(8,128)S(1)} %add.24), channel_id=1, source_target_pairs={{8,0},{10,2},{4,12},{6,14},{0,4},{2,6},{12,8},{14,10},{9,1},{11,3}... | collective-permute-start | bytes 245768 | tf_op jit(solution)/shard_map/ppermute | solution.py:417
  36.8 1.4 %collective-permute-start.10 = (f32[40,512]{1,0:T(8,128)S(1)}, f32[40,512]{1,0:T(8,128)S(1)}, u32[]{:S(2)}, u32[]{:S(2)}) collective-permute-start(f32[40,512]{1,0:T(8,128)S(1)} %slice.25), channel_id=1, source_target_pairs={{0,1},{1,0},{2,3},{3,2},{4,5},{5,4},{6,7},{7,6},{8,9},{9,8},{10,11... | collective-permute-start | bytes 245768 | tf_op jit(solution)/shard_map/ppermute | solution.py:419
  36.8 9.4 %collective-permute-start.9 = (f32[40,512]{1,0:T(8,128)S(1)}, f32[40,512]{1,0:T(8,128)S(1)}, u32[]{:S(2)}, u32[]{:S(2)}) collective-permute-start(f32[40,512]{1,0:T(8,128)S(1)} %add.25), channel_id=1, source_target_pairs={{4,8},{6,10},{12,0},{14,2},{5,9},{7,11},{13,1},{15,3},{20,24},{22,... | collective-permute-start | bytes 245768 | tf_op jit(solution)/shard_map/ppermute | solution.py:417
  38.2 8.0 %collective-permute-start.11 = (f32[40,512]{1,0:T(8,128)S(1)}, f32[40,512]{1,0:T(8,128)S(1)}, u32[]{:S(2)}, u32[]{:S(2)}) collective-permute-start(f32[40,512]{1,0:T(8,128)S(1)} %slice_add_fusion), channel_id=1, source_target_pairs={{0,2},{2,0},{4,6},{6,4},{8,10},{10,8},{12,14},{14,12},{1,3},{3,1},... | collective-permute-start | bytes 245768 | tf_op jit(solution)/shard_map/ppermute | solution.py:421
  39.8 6.4 %collective-permute-start.12 = (f32[40,512]{1,0:T(8,128)S(1)}, f32[40,512]{1,0:T(8,128)S(1)}, u32[]{:S(2)}, u32[]{:S(2)}) collective-permute-start(f32[40,512]{1,0:T(8,128)S(1)} %get-tuple-element.67), channel_id=1, source_target_pairs={{0,1},{1,0},{2,3},{3,2},{4,5},{5,4},{6,7},{7,6},{8,9},{9,8},{10,11... | collective-permute-start | bytes 245768 | tf_op jit(solution)/shard_map/ppermute | solution.py:423
  47.1 11.1 %all-to-all-start = ((f32[16,8,128]{2,1,0:T(8,128)}), f32[16,8,128]{2,1,0:T(8,128)S(1)}, u32[]{:S(2)}, u32[]{:S(2)}) async-start(f32[16,8,128]{2,1,0:T(8,128)} %gram.1), calls=%async_computation | async-start | bytes 131072 | tf_op jit(solution)/shard_map/all_to_all | solution.py:426
  51.4 1.3 %collective-permute-start.13 = (f32[32,512]{1,0:T(8,128)S(1)}, f32[32,512]{1,0:T(8,128)S(1)}, u32[]{:S(2)}, u32[]{:S(2)}) collective-permute-start(f32[32,512]{1,0:T(8,128)S(1)} %image.1.image_ref.mine_ref), channel_id=1, source_target_pairs={{0,1},{1,0},{2,3},{3,2},{4,5},{5,4},{6,7},{7,6},{8,9},{9,8},{10,11... | collective-permute-start | bytes 196616 | tf_op jit(solution)/shard_map/ppermute | solution.py:425

commit v21 on v20

--- a/solution.py
+++ b/solution.py
@@ -186,7 +186,6 @@
             )[0:OUT_ROWS]
 
     def pipeline(chunks):
-        multiply(chunks[0], products[0])
         for step, chunk in enumerate(chunks):
             now, later = step % 2, (step + 1) % 2
             if step + 1 < len(chunks):
@@ -197,12 +196,6 @@
         total(chunks[-1], weights[(len(chunks) - 1) % 2])
 
     def compute():
-        for field, values in enumerate(decode(row_ref[code_rows, :])):
-            field_ref[field : field + 1, :] = values
-        turned = field_ref[...].T
-        for field in range(FIELDS):
-            spread_ref[field] = jnp.broadcast_to(turned[:, field : field + 1], (rows, LANES))
-        row_vec_ref[...] = with_ones(row_ref[vec_rows, :])
         if turns:
             for number, pack_ref in enumerate(col_refs):
                 part = pl.ds(number * rows, rows)
@@ -213,6 +206,13 @@
         for source in sources:
             for start in range(0, source.shape[1], WIDE):
                 chunks.append((source, slice(start, start + WIDE), len(chunks) * WIDE))
+        multiply(chunks[0], products[0])
+        for field, values in enumerate(decode(row_ref[code_rows, :])):
+            field_ref[field : field + 1, :] = values
+        turned = field_ref[...].T
+        for field in range(FIELDS):
+            spread_ref[field] = jnp.broadcast_to(turned[:, field : field + 1], (rows, LANES))
+        row_vec_ref[...] = with_ones(row_ref[vec_rows, :])
         pipeline(chunks)
 
     if receivers is None:

time: 61.5 us -> 61.5 us (level)
  no operation moved by 1% of the time
where the time goes in v21:
time: 61.5 us; the launch traced here: 61.1 us
  waiting for transfers between devices  24.9 us (40%)
  starting transfers between devices  18.2 us (30%)
  Pallas kernels  15.8 us (26%)
  local copies, waits for them, and re-layouts  1.13 us (2%)
  other arithmetic  0.89 us (1%)
    pallas_call x6, Pallas kernels, tile(): pl.pallas_call(functools.partial(tile_kernel, len(columns), turns, own_bl...  11.3 us
    ppermute x2, waiting for transfers between devices, local(): parts.append(lax.ppermute(own_lines + next_lines, 'blk', back(moves)))  10.9 us
    ppermute x2, starting transfers between devices, local(): sent = [lax.ppermute(mine, 'blk', moves) for moves, _ in plans]  7.36 us
    ppermute x2, waiting for transfers between devices, local(): sent = [lax.ppermute(mine, 'blk', moves) for moves, _ in plans]  6.19 us
    all_to_all x1, waiting for transfers between devices, local(): lax.all_to_all(grams_of(image, 2 * blocks), ('blk', 'sub'), 0, 0, tiled=T...  5.58 us
    all_to_all x1, starting transfers between devices, local(): lax.all_to_all(grams_of(image, 2 * blocks), ('blk', 'sub'), 0, 0, tiled=T...  4.23 us
    pallas_call x1, Pallas kernels, basis_of(): pl.pallas_call(functools.partial(basis_kernel, total_rows), out_shape=jax...  2.89 us
    ppermute x2, starting transfers between devices, local(): parts.append(lax.ppermute(own_lines + next_lines, 'blk', back(moves)))  1.62 us
  transfers between devices with their start and end apart: 15, of which 7 were waited for; matrix products, arithmetic and copies ran while one was open for 3% of the time, Pallas kernels for 18%

profile of v21, /device:TPU:0, one launch (start us, length us, event | category | flops | bytes accessed | tf_op | source)
XLA Modules:
  0.0 61.1 jit_solution(9294966022230155624)
XLA Ops:
  0.0 0.5 collective-permute-start
  0.5 0.1 collective-permute-start.1
  0.5 1.1 %constant_dynamic-slice_fusion = (bf16[512,256]{1,0:T(8,128)(2,1)S(1)}, bf16[512,256]{1,0:T(8,128)(2,1)S(1)}) fusion(bf16[1024,256]{1,0:T(8,128)(2,1)} %param.5, s32[]{:T(128)S(6)} %select_n.7, s32[]{:T(128)S(6)} %select_n.6), kind=kLoop, calls=%fused_computation.3 | loop fusion | bytes 1048584 | tf_op jit(solution)/shard_map/dynamic_slice | solution.py:388
  1.6 0.8 %pad_add_fusion.meta_ref = s32[7,1024]{1,0:T(8,128)S(1)} fusion(s32[1,1024]{1,0:T(1,128)} %bitcast.1, s32[2,1024]{1,0:T(2,128)} %param.8, s32[4,1024]{1,0:T(4,128)} %param.7), kind=kLoop, calls=%fused_computation.2 | loop fusion | flops 14336 | bytes 57344 | tf_op jit(solution)/shard_map/concatenate | solution.py:386
  2.4 0.0 collective-permute-done.emb_other_ref
  2.4 0.7 %pack.1 = (bf16[560,512]{1,0:T(8,128)(2,1)S(1)}, bf16[560,512]{1,0:T(8,128)(2,1)S(1)}) custom-call(bf16[512,256]{1,0:T(8,128)(2,1)S(1)} %get-tuple-element.66.emb_mine_ref, bf16[512,256]{1,0:T(8,128)(2,1)S(1)} %get-tuple-element.65.emb_rest_ref, bf16[1024,256]{1,0:T(8,128)(2,1)S(1)} %collective-permute-done.emb_other_ref, bf16[16,1024]{1,0:T(8,128)(2,1)S(1)} %copy-done, ...), custom_call_target="tpu_custom_call" | custom-call | tf_op jit(solution)/shard_map/pack/pallas_call | solution.py:104
  3.1 4.1 %collective-permute-start.2 = (bf16[560,512]{1,0:T(8,128)(2,1)S(1)}, bf16[560,512]{1,0:T(8,128)(2,1)S(1)}, u32[]{:S(2)}, u32[]{:S(2)}) collective-permute-start(bf16[560,512]{1,0:T(8,128)(2,1)S(1)} %get-tuple-element.34.refs_0_.refs_1_), channel_id=1, source_target_pairs={{0,8},{2,10},{12,4},{14,6},{4,0},{6,2},{8,12},{10,14},{1,9},{3,11}... | collective-permute-start | bytes 1720328 | tf_op jit(solution)/shard_map/ppermute | solution.py:390
  7.2 1.5 %collective-permute-start.3 = (bf16[560,512]{1,0:T(8,128)(2,1)S(1)}, bf16[560,512]{1,0:T(8,128)(2,1)S(1)}, u32[]{:S(2)}, u32[]{:S(2)}) collective-permute-start(bf16[560,512]{1,0:T(8,128)(2,1)S(1)} %get-tuple-element.34.refs_0_.refs_1_), channel_id=1, source_target_pairs={{0,2},{2,0},{4,6},{6,4},{8,10},{10,8},{12,14},{14,12},{1,3},{3,1},... | collective-permute-start | bytes 1720328 | tf_op jit(solution)/shard_map/ppermute | solution.py:391
  8.7 3.3 %collective-permute-start.7 = (bf16[560,512]{1,0:T(8,128)(2,1)S(1)}, bf16[560,512]{1,0:T(8,128)(2,1)S(1)}, u32[]{:S(2)}, u32[]{:S(2)}) collective-permute-start(bf16[560,512]{1,0:T(8,128)(2,1)S(1)} %get-tuple-element.34.refs_0_.refs_1_), channel_id=1, source_target_pairs={{8,4},{10,6},{0,12},{2,14},{9,5},{11,7},{1,13},{3,15},{24,20},{26,... | collective-permute-start | bytes 1720328 | tf_op jit(solution)/shard_map/ppermute | solution.py:390
  12.0 2.9 %tile.6 = (f32[40,512]{1,0:T(8,128)S(1)}, bf16[560,1024]{1,0:T(8,128)(2,1)S(1)}) custom-call(bf16[560,512]{1,0:T(8,128)(2,1)S(1)} %get-tuple-element.34.refs_0_.refs_1_, bf16[560,512]{1,0:T(8,128)(2,1)S(1)} %get-tuple-element.34.refs_0_.refs_1_, bf16[560,512]{1,0:T(8,128)(2,1)S(1)} %get-tuple-element.35.refs_2_), custom_call_target="tpu_custom_call" | custom-call | flops 1 | bytes 1 | tf_op jit(solution)/shard_map/tile/pallas_call | solution.py:239
  14.9 5.6 %collective-permute-done.2.refs_0_ = bf16[560,512]{1,0:T(8,128)(2,1)S(1)} collective-permute-done((bf16[560,512]{1,0:T(8,128)(2,1)S(1)}, bf16[560,512]{1,0:T(8,128)(2,1)S(1)}, u32[]{:S(2)}, u32[]{:S(2)}) %collective-permute-start.2) | collective-permute-done | bytes 573472 | tf_op jit(solution)/shard_map/ppermute | solution.py:390
  20.5 1.3 %collective-permute-done.3.refs_1_ = bf16[560,512]{1,0:T(8,128)(2,1)S(1)} collective-permute-done((bf16[560,512]{1,0:T(8,128)(2,1)S(1)}, bf16[560,512]{1,0:T(8,128)(2,1)S(1)}, u32[]{:S(2)}, u32[]{:S(2)}) %collective-permute-start.3) | collective-permute-done | bytes 573472 | tf_op jit(solution)/shard_map/ppermute | solution.py:391
  21.9 0.1 collective-permute-start.6
  22.0 0.6 collective-permute-start.5
  22.5 0.1 collective-permute-start.4
  22.6 2.7 %tile.7 = (f32[40,512]{1,0:T(8,128)S(1)}, f32[40,1024]{1,0:T(8,128)S(1)}) custom-call(bf16[560,512]{1,0:T(8,128)(2,1)S(1)} %collective-permute-done.2.refs_0_, bf16[560,1024]{1,0:T(8,128)(2,1)S(1)} %get-tuple-element.42.refs_1_), custom_call_target="tpu_custom_call" | custom-call | flops 1 | bytes 1 | tf_op jit(solution)/shard_map/tile/pallas_call | solution.py:239
  25.3 0.0 collective-permute-done.5
  25.4 2.9 %tile.8 = (f32[40,512]{1,0:T(8,128)S(1)}, bf16[560,1024]{1,0:T(8,128)(2,1)S(1)}) custom-call(bf16[560,512]{1,0:T(8,128)(2,1)S(1)} %get-tuple-element.34.refs_0_.refs_1_, bf16[560,512]{1,0:T(8,128)(2,1)S(1)} %collective-permute-done.3.refs_1_, bf16[560,512]{1,0:T(8,128)(2,1)S(1)} %pad_maximum_fusion.refs_2_), custom_call_target="tpu_custom_call" | custom-call | flops 1 | bytes 1 | tf_op jit(solution)/shard_map/tile/pallas_call | solution.py:239
  28.3 2.7 %tile.9 = (f32[40,512]{1,0:T(8,128)S(1)}, f32[40,1024]{1,0:T(8,128)S(1)}) custom-call(bf16[560,512]{1,0:T(8,128)(2,1)S(1)} %collective-permute-done.2.refs_0_, bf16[560,1024]{1,0:T(8,128)(2,1)S(1)} %get-tuple-element.48.refs_1_), custom_call_target="tpu_custom_call" | custom-call | flops 1 | bytes 1 | tf_op jit(solution)/shard_map/tile/pallas_call | solution.py:239
  31.0 0.3 collective-permute-start.8
  31.3 0.6 collective-permute-done.7.refs_0_
  32.0 4.8 %collective-permute-done.8.refs_2_ = f32[40,512]{1,0:T(8,128)S(1)} collective-permute-done((f32[40,512]{1,0:T(8,128)S(1)}, f32[40,512]{1,0:T(8,128)S(1)}, u32[]{:S(2)}, u32[]{:S(2)}) %collective-permute-start.8) | collective-permute-done | bytes 81952 | tf_op jit(solution)/shard_map/ppermute | solution.py:417
  36.8 1.3 %collective-permute-start.9 = (f32[40,512]{1,0:T(8,128)S(1)}, f32[40,512]{1,0:T(8,128)S(1)}, u32[]{:S(2)}, u32[]{:S(2)}) collective-permute-start(f32[40,512]{1,0:T(8,128)S(1)} %add.25), channel_id=1, source_target_pairs={{4,8},{6,10},{12,0},{14,2},{5,9},{7,11},{13,1},{15,3},{20,24},{22,... | collective-permute-start | bytes 245768 | tf_op jit(solution)/shard_map/ppermute | solution.py:417
  38.2 1.6 %collective-permute-start.11 = (f32[40,512]{1,0:T(8,128)S(1)}, f32[40,512]{1,0:T(8,128)S(1)}, u32[]{:S(2)}, u32[]{:S(2)}) collective-permute-start(f32[40,512]{1,0:T(8,128)S(1)} %slice_add_fusion), channel_id=1, source_target_pairs={{0,2},{2,0},{4,6},{6,4},{8,10},{10,8},{12,14},{14,12},{1,3},{3,1},... | collective-permute-start | bytes 245768 | tf_op jit(solution)/shard_map/ppermute | solution.py:421
  39.8 0.3 collective-permute-start.12
  40.1 6.1 %collective-permute-done.9.refs_3_ = f32[40,512]{1,0:T(8,128)S(1)} collective-permute-done((f32[40,512]{1,0:T(8,128)S(1)}, f32[40,512]{1,0:T(8,128)S(1)}, u32[]{:S(2)}, u32[]{:S(2)}) %collective-permute-start.9) | collective-permute-done | bytes 81952 | tf_op jit(solution)/shard_map/ppermute | solution.py:417
  46.2 0.9 %gram.1 = f32[16,8,128]{2,1,0:T(8,128)} custom-call(f32[32,512]{1,0:T(8,128)S(1)} %image.1.image_ref.mine_ref), custom_call_target="tpu_custom_call" | custom-call | tf_op jit(solution)/shard_map/gram/pallas_call | solution.py:293
  47.1 4.2 %all-to-all-start = ((f32[16,8,128]{2,1,0:T(8,128)}), f32[16,8,128]{2,1,0:T(8,128)S(1)}, u32[]{:S(2)}, u32[]{:S(2)}) async-start(f32[16,8,128]{2,1,0:T(8,128)} %gram.1), calls=%async_computation | async-start | bytes 131072 | tf_op jit(solution)/shard_map/all_to_all | solution.py:426
  51.4 0.4 collective-permute-start.13
  51.8 0.9 %collective-permute-done.13.other_ref = f32[32,512]{1,0:T(8,128)S(1)} collective-permute-done((f32[32,512]{1,0:T(8,128)S(1)}, f32[32,512]{1,0:T(8,128)S(1)}, u32[]{:S(2)}, u32[]{:S(2)}) %collective-permute-start.13) | collective-permute-done | bytes 65568 | tf_op jit(solution)/shard_map/ppermute | solution.py:425
  52.7 5.6 %all-to-all-done.grams_ref = f32[16,8,128]{2,1,0:T(8,128)S(1)} async-done(((f32[16,8,128]{2,1,0:T(8,128)}), f32[16,8,128]{2,1,0:T(8,128)S(1)}, u32[]{:S(2)}, u32[]{:S(2)}) %all-to-all-start) | async-done | bytes 65568 | tf_op jit(solution)/shard_map/all_to_all | solution.py:426
  58.3 2.9 %basis.1 = f32[16,1024]{1,0:T(8,128)} custom-call(f32[16,8,128]{2,1,0:T(8,128)S(1)} %all-to-all-done.grams_ref, f32[32,512]{1,0:T(8,128)S(1)} %image.1.image_ref.mine_ref, f32[32,512]{1,0:T(8,128)S(1)} %collective-permute-done.13.other_ref), custom_call_target="tpu_custom_call" | custom-call | tf_op jit(solution)/shard_map/basis/pallas_call | solution.py:343
  (22 shorter events, 0.3 us)
Async XLA Ops:
  0.0 2.4 %copy-start = (bf16[16,1024]{1,0:T(8,128)(2,1)S(1)}, bf16[16,1024]{1,0:T(8,128)(2,1)}, u32[]{:S(2)}) copy-start(bf16[16,1024]{1,0:T(8,128)(2,1)} %vec_ref.1) | copy-start | bytes 98308
  0.0 2.4 %collective-permute-start = (bf16[1024,256]{1,0:T(8,128)(2,1)}, bf16[1024,256]{1,0:T(8,128)(2,1)S(1)}, u32[]{:S(2)}, u32[]{:S(2)}) collective-permute-start(bf16[1024,256]{1,0:T(8,128)(2,1)} %param.5), channel_id=1, source_target_pairs={{0,1},{1,0},{2,3},{3,2},{4,5},{5,4},{6,7},{7,6},{8,9},{9,8},{10,11... | collective-permute-start | bytes 1572872 | tf_op jit(solution)/shard_map/ppermute | solution.py:384
  0.5 1.9 %collective-permute-start.1 = (bf16[16,1024]{1,0:T(8,128)(2,1)}, bf16[16,1024]{1,0:T(8,128)(2,1)S(1)}, u32[]{:S(2)}, u32[]{:S(2)}) collective-permute-start(bf16[16,1024]{1,0:T(8,128)(2,1)} %vec_ref.1), channel_id=1, source_target_pairs={{0,1},{1,0},{2,3},{3,2},{4,5},{5,4},{6,7},{7,6},{8,9},{9,8},{10,11... | collective-permute-start | bytes 98312 | tf_op jit(solution)/shard_map/ppermute | solution.py:385
  3.1 17.4 %collective-permute-start.2 = (bf16[560,512]{1,0:T(8,128)(2,1)S(1)}, bf16[560,512]{1,0:T(8,128)(2,1)S(1)}, u32[]{:S(2)}, u32[]{:S(2)}) collective-permute-start(bf16[560,512]{1,0:T(8,128)(2,1)S(1)} %get-tuple-element.34.refs_0_.refs_1_), channel_id=1, source_target_pairs={{0,8},{2,10},{12,4},{14,6},{4,0},{6,2},{8,12},{10,14},{1,9},{3,11}... | collective-permute-start | bytes 1720328 | tf_op jit(solution)/shard_map/ppermute | solution.py:390
  7.2 14.7 %collective-permute-start.3 = (bf16[560,512]{1,0:T(8,128)(2,1)S(1)}, bf16[560,512]{1,0:T(8,128)(2,1)S(1)}, u32[]{:S(2)}, u32[]{:S(2)}) collective-permute-start(bf16[560,512]{1,0:T(8,128)(2,1)S(1)} %get-tuple-element.34.refs_0_.refs_1_), channel_id=1, source_target_pairs={{0,2},{2,0},{4,6},{6,4},{8,10},{10,8},{12,14},{14,12},{1,3},{3,1},... | collective-permute-start | bytes 1720328 | tf_op jit(solution)/shard_map/ppermute | solution.py:391
  8.7 23.2 %collective-permute-start.7 = (bf16[560,512]{1,0:T(8,128)(2,1)S(1)}, bf16[560,512]{1,0:T(8,128)(2,1)S(1)}, u32[]{:S(2)}, u32[]{:S(2)}) collective-permute-start(bf16[560,512]{1,0:T(8,128)(2,1)S(1)} %get-tuple-element.34.refs_0_.refs_1_), channel_id=1, source_target_pairs={{8,4},{10,6},{0,12},{2,14},{9,5},{11,7},{1,13},{3,15},{24,20},{26,... | collective-permute-start | bytes 1720328 | tf_op jit(solution)/shard_map/ppermute | solution.py:390
  21.9 3.5 %collective-permute-start.6 = (bf16[208,512]{1,0:T(8,128)(2,1)S(1)}, bf16[208,512]{1,0:T(8,128)(2,1)S(1)}, u32[]{:S(2)}, u32[]{:S(2)}) collective-permute-start(bf16[208,512]{1,0:T(8,128)(2,1)S(1)} %slice.23), channel_id=1, source_target_pairs={{0,1},{1,0},{2,3},{3,2},{4,5},{5,4},{6,7},{7,6},{8,9},{9,8},{10,11... | collective-permute-start | bytes 638984 | tf_op jit(solution)/shard_map/ppermute | solution.py:398
  22.0 3.4 %collective-permute-start.5 = (bf16[176,512]{1,0:T(8,128)(2,1)S(1)}, bf16[176,512]{1,0:T(8,128)(2,1)S(1)}, u32[]{:S(2)}, u32[]{:S(2)}) collective-permute-start(bf16[176,512]{1,0:T(8,128)(2,1)S(1)} %get-tuple-element.64), channel_id=1, source_target_pairs={{0,1},{1,0},{2,3},{3,2},{4,5},{5,4},{6,7},{7,6},{8,9},{9,8},{10,11... | collective-permute-start | bytes 540680 | tf_op jit(solution)/shard_map/ppermute | solution.py:398
  22.5 2.8 %collective-permute-start.4 = (bf16[176,512]{1,0:T(8,128)(2,1)S(1)}, bf16[176,512]{1,0:T(8,128)(2,1)S(1)}, u32[]{:S(2)}, u32[]{:S(2)}) collective-permute-start(bf16[176,512]{1,0:T(8,128)(2,1)S(1)} %get-tuple-element.63), channel_id=1, source_target_pairs={{0,1},{1,0},{2,3},{3,2},{4,5},{5,4},{6,7},{7,6},{8,9},{9,8},{10,11... | collective-permute-start | bytes 540680 | tf_op jit(solution)/shard_map/ppermute | solution.py:398
  31.0 5.7 %collective-permute-start.8 = (f32[40,512]{1,0:T(8,128)S(1)}, f32[40,512]{1,0:T(8,128)S(1)}, u32[]{:S(2)}, u32[]{:S(2)}) collective-permute-start(f32[40,512]{1,0:T(8,128)S(1)} %add.24), channel_id=1, source_target_pairs={{8,0},{10,2},{4,12},{6,14},{0,4},{2,6},{12,8},{14,10},{9,1},{11,3}... | collective-permute-start | bytes 245768 | tf_op jit(solution)/shard_map/ppermute | solution.py:417
  36.8 1.4 %collective-permute-start.10 = (f32[40,512]{1,0:T(8,128)S(1)}, f32[40,512]{1,0:T(8,128)S(1)}, u32[]{:S(2)}, u32[]{:S(2)}) collective-permute-start(f32[40,512]{1,0:T(8,128)S(1)} %slice.25), channel_id=1, source_target_pairs={{0,1},{1,0},{2,3},{3,2},{4,5},{5,4},{6,7},{7,6},{8,9},{9,8},{10,11... | collective-permute-start | bytes 245768 | tf_op jit(solution)/shard_map/ppermute | solution.py:419
  36.8 9.4 %collective-permute-start.9 = (f32[40,512]{1,0:T(8,128)S(1)}, f32[40,512]{1,0:T(8,128)S(1)}, u32[]{:S(2)}, u32[]{:S(2)}) collective-permute-start(f32[40,512]{1,0:T(8,128)S(1)} %add.25), channel_id=1, source_target_pairs={{4,8},{6,10},{12,0},{14,2},{5,9},{7,11},{13,1},{15,3},{20,24},{22,... | collective-permute-start | bytes 245768 | tf_op jit(solution)/shard_map/ppermute | solution.py:417
  38.2 8.0 %collective-permute-start.11 = (f32[40,512]{1,0:T(8,128)S(1)}, f32[40,512]{1,0:T(8,128)S(1)}, u32[]{:S(2)}, u32[]{:S(2)}) collective-permute-start(f32[40,512]{1,0:T(8,128)S(1)} %slice_add_fusion), channel_id=1, source_target_pairs={{0,2},{2,0},{4,6},{6,4},{8,10},{10,8},{12,14},{14,12},{1,3},{3,1},... | collective-permute-start | bytes 245768 | tf_op jit(solution)/shard_map/ppermute | solution.py:421
  39.8 6.4 %collective-permute-start.12 = (f32[40,512]{1,0:T(8,128)S(1)}, f32[40,512]{1,0:T(8,128)S(1)}, u32[]{:S(2)}, u32[]{:S(2)}) collective-permute-start(f32[40,512]{1,0:T(8,128)S(1)} %get-tuple-element.67), channel_id=1, source_target_pairs={{0,1},{1,0},{2,3},{3,2},{4,5},{5,4},{6,7},{7,6},{8,9},{9,8},{10,11... | collective-permute-start | bytes 245768 | tf_op jit(solution)/shard_map/ppermute | solution.py:423
  47.1 11.1 %all-to-all-start = ((f32[16,8,128]{2,1,0:T(8,128)}), f32[16,8,128]{2,1,0:T(8,128)S(1)}, u32[]{:S(2)}, u32[]{:S(2)}) async-start(f32[16,8,128]{2,1,0:T(8,128)} %gram.1), calls=%async_computation | async-start | bytes 131072 | tf_op jit(solution)/shard_map/all_to_all | solution.py:426
  51.4 1.3 %collective-permute-start.13 = (f32[32,512]{1,0:T(8,128)S(1)}, f32[32,512]{1,0:T(8,128)S(1)}, u32[]{:S(2)}, u32[]{:S(2)}) collective-permute-start(f32[32,512]{1,0:T(8,128)S(1)} %image.1.image_ref.mine_ref), channel_id=1, source_target_pairs={{0,1},{1,0},{2,3},{3,2},{4,5},{5,4},{6,7},{7,6},{8,9},{9,8},{10,11... | collective-permute-start | bytes 196616 | tf_op jit(solution)/shard_map/ppermute | solution.py:425

commit v22 on v20

--- a/solution.py
+++ b/solution.py
@@ -258,28 +258,13 @@
 
 
 def image_kernel(*refs):
-    parts, image_ref = refs[:-1], refs[-1]
+    parts, image_ref, grams_ref = refs[:-2], refs[-2], refs[-1]
     total = parts[0][...]
     for part in parts[1:]:
         total = total + part[...]
-    vecs = image_ref.shape[0]
-    image_ref[...] = total[0:vecs] / total[vecs : vecs + 1]
-
-
-def image_of(parts, vecs):
-    return pl.pallas_call(
-        image_kernel,
-        out_shape=jax.ShapeDtypeStruct((vecs, parts[0].shape[1]), jnp.float32),
-        in_specs=[VMEM_SPEC] * len(parts),
-        out_specs=VMEM_SPEC,
-        compiler_params=params(),
-        name="image",
-    )(*parts)
-
-
-def gram_kernel(image_ref, grams_ref):
     vecs, cols = image_ref.shape
-    image = image_ref[...]
+    image = total[0:vecs] / total[vecs : vecs + 1]
+    image_ref[...] = image
     padded = jnp.concatenate([image, jnp.zeros((LANES - vecs, cols), jnp.float32)], axis=0)
     gram = dot_nt(image, padded, lax.Precision.HIGHEST)
     packed = gram[0:8]
@@ -289,15 +274,18 @@
         grams_ref[copy] = packed
 
 
-def grams_of(image, copies):
+def image_of(parts, vecs, copies):
     return pl.pallas_call(
-        gram_kernel,
-        out_shape=jax.ShapeDtypeStruct((copies, 8, LANES), jnp.float32),
-        in_specs=[VMEM_SPEC],
-        out_specs=VMEM_SPEC,
+        image_kernel,
+        out_shape=[
+            jax.ShapeDtypeStruct((vecs, parts[0].shape[1]), jnp.float32),
+            jax.ShapeDtypeStruct((copies, 8, LANES), jnp.float32),
+        ],
+        in_specs=[VMEM_SPEC] * len(parts),
+        out_specs=[VMEM_SPEC] * 2,
         compiler_params=params(),
-        name="gram",
-    )(image)
+        name="image",
+    )(*parts)
 
 
 def inverse_of(number):
@@ -421,9 +409,9 @@
             parts.append(lax.ppermute(crossing, "blk", beside))
             own_cols, _ = lax.optimization_barrier((own_cols, crossing))
             parts += [own_cols[:, :half], lax.ppermute(own_cols[:, half:], "sub", swap)]
-    image = image_of(parts, vecs)
+    image, copies = image_of(parts, vecs, 2 * blocks)
     image_other = lax.ppermute(image, "sub", swap)
-    grams = lax.all_to_all(grams_of(image, 2 * blocks), ("blk", "sub"), 0, 0, tiled=True)
+    grams = lax.all_to_all(copies, ("blk", "sub"), 0, 0, tiled=True)
     return basis_of(grams, image, image_other, blocks * rows)
 
 

time: 61.5 us -> 61.5 us (level)
  no operation moved by 1% of the time
where the time goes in v22:
time: 61.5 us; the launch traced here: 61.1 us
  waiting for transfers between devices  24.9 us (40%)
  starting transfers between devices  18.2 us (30%)
  Pallas kernels  15.8 us (26%)
  local copies, waits for them, and re-layouts  1.13 us (2%)
  other arithmetic  0.89 us (1%)
    pallas_call x6, Pallas kernels, tile(): pl.pallas_call(functools.partial(tile_kernel, len(columns), turns, own_bl...  11.3 us
    ppermute x2, waiting for transfers between devices, local(): parts.append(lax.ppermute(own_lines + next_lines, 'blk', back(moves)))  10.9 us
    ppermute x2, starting transfers between devices, local(): sent = [lax.ppermute(mine, 'blk', moves) for moves, _ in plans]  7.36 us
    ppermute x2, waiting for transfers between devices, local(): sent = [lax.ppermute(mine, 'blk', moves) for moves, _ in plans]  6.22 us
    all_to_all x1, waiting for transfers between devices, local(): grams = lax.all_to_all(copies, ('blk', 'sub'), 0, 0, tiled=True)  5.58 us
    all_to_all x1, starting transfers between devices, local(): grams = lax.all_to_all(copies, ('blk', 'sub'), 0, 0, tiled=True)  4.24 us
    pallas_call x1, Pallas kernels, basis_of(): pl.pallas_call(functools.partial(basis_kernel, total_rows), out_shape=jax...  2.88 us
    ppermute x2, starting transfers between devices, local(): parts.append(lax.ppermute(own_lines + next_lines, 'blk', back(moves)))  1.62 us
  transfers between devices with their start and end apart: 15, of which 7 were waited for; matrix products, arithmetic and copies ran while one was open for 3% of the time, Pallas kernels for 18%

profile of v22, /device:TPU:0, one launch (start us, length us, event | category | flops | bytes accessed | tf_op | source)
XLA Modules:
  0.0 61.1 jit_solution(1060166090065986272)
XLA Ops:
  0.0 0.5 collective-permute-start
  0.5 0.1 collective-permute-start.1
  0.5 1.1 %constant_dynamic-slice_fusion = (bf16[512,256]{1,0:T(8,128)(2,1)S(1)}, bf16[512,256]{1,0:T(8,128)(2,1)S(1)}) fusion(bf16[1024,256]{1,0:T(8,128)(2,1)} %param.5, s32[]{:T(128)S(6)} %select_n.7, s32[]{:T(128)S(6)} %select_n.6), kind=kLoop, calls=%fused_computation.3 | loop fusion | bytes 1048584 | tf_op jit(solution)/shard_map/dynamic_slice | solution.py:376
  1.6 0.8 %pad_add_fusion.meta_ref = s32[7,1024]{1,0:T(8,128)S(1)} fusion(s32[1,1024]{1,0:T(1,128)} %bitcast.1, s32[2,1024]{1,0:T(2,128)} %param.8, s32[4,1024]{1,0:T(4,128)} %param.7), kind=kLoop, calls=%fused_computation.2 | loop fusion | flops 14336 | bytes 57344 | tf_op jit(solution)/shard_map/concatenate | solution.py:374
  2.4 0.0 collective-permute-done.1.vec_other_ref
  2.4 0.0 collective-permute-done.emb_other_ref
  2.4 0.7 %pack.1 = (bf16[560,512]{1,0:T(8,128)(2,1)S(1)}, bf16[560,512]{1,0:T(8,128)(2,1)S(1)}) custom-call(bf16[512,256]{1,0:T(8,128)(2,1)S(1)} %get-tuple-element.70.emb_mine_ref, bf16[512,256]{1,0:T(8,128)(2,1)S(1)} %get-tuple-element.69.emb_rest_ref, bf16[1024,256]{1,0:T(8,128)(2,1)S(1)} %collective-permute-done.emb_other_ref, bf16[16,1024]{1,0:T(8,128)(2,1)S(1)} %copy-done, ...), custom_call_target="tpu_custom_call" | custom-call | tf_op jit(solution)/shard_map/pack/pallas_call | solution.py:104
  3.1 4.1 %collective-permute-start.2 = (bf16[560,512]{1,0:T(8,128)(2,1)S(1)}, bf16[560,512]{1,0:T(8,128)(2,1)S(1)}, u32[]{:S(2)}, u32[]{:S(2)}) collective-permute-start(bf16[560,512]{1,0:T(8,128)(2,1)S(1)} %get-tuple-element.36.refs_0_.refs_1_), channel_id=1, source_target_pairs={{0,8},{2,10},{12,4},{14,6},{4,0},{6,2},{8,12},{10,14},{1,9},{3,11}... | collective-permute-start | bytes 1720328 | tf_op jit(solution)/shard_map/ppermute | solution.py:378
  7.2 1.5 %collective-permute-start.3 = (bf16[560,512]{1,0:T(8,128)(2,1)S(1)}, bf16[560,512]{1,0:T(8,128)(2,1)S(1)}, u32[]{:S(2)}, u32[]{:S(2)}) collective-permute-start(bf16[560,512]{1,0:T(8,128)(2,1)S(1)} %get-tuple-element.36.refs_0_.refs_1_), channel_id=1, source_target_pairs={{0,2},{2,0},{4,6},{6,4},{8,10},{10,8},{12,14},{14,12},{1,3},{3,1},... | collective-permute-start | bytes 1720328 | tf_op jit(solution)/shard_map/ppermute | solution.py:379
  8.7 3.3 %collective-permute-start.7 = (bf16[560,512]{1,0:T(8,128)(2,1)S(1)}, bf16[560,512]{1,0:T(8,128)(2,1)S(1)}, u32[]{:S(2)}, u32[]{:S(2)}) collective-permute-start(bf16[560,512]{1,0:T(8,128)(2,1)S(1)} %get-tuple-element.36.refs_0_.refs_1_), channel_id=1, source_target_pairs={{8,4},{10,6},{0,12},{2,14},{9,5},{11,7},{1,13},{3,15},{24,20},{26,... | collective-permute-start | bytes 1720328 | tf_op jit(solution)/shard_map/ppermute | solution.py:378
  12.0 2.9 %tile.6 = (f32[40,512]{1,0:T(8,128)S(1)}, bf16[560,1024]{1,0:T(8,128)(2,1)S(1)}) custom-call(bf16[560,512]{1,0:T(8,128)(2,1)S(1)} %get-tuple-element.36.refs_0_.refs_1_, bf16[560,512]{1,0:T(8,128)(2,1)S(1)} %get-tuple-element.36.refs_0_.refs_1_, bf16[560,512]{1,0:T(8,128)(2,1)S(1)} %get-tuple-element.37.refs_2_), custom_call_target="tpu_custom_call" | custom-call | flops 1 | bytes 1 | tf_op jit(solution)/shard_map/tile/pallas_call | solution.py:239
  14.9 5.6 %collective-permute-done.2.refs_0_ = bf16[560,512]{1,0:T(8,128)(2,1)S(1)} collective-permute-done((bf16[560,512]{1,0:T(8,128)(2,1)S(1)}, bf16[560,512]{1,0:T(8,128)(2,1)S(1)}, u32[]{:S(2)}, u32[]{:S(2)}) %collective-permute-start.2) | collective-permute-done | bytes 573472 | tf_op jit(solution)/shard_map/ppermute | solution.py:378
  20.5 1.3 %collective-permute-done.3.refs_1_ = bf16[560,512]{1,0:T(8,128)(2,1)S(1)} collective-permute-done((bf16[560,512]{1,0:T(8,128)(2,1)S(1)}, bf16[560,512]{1,0:T(8,128)(2,1)S(1)}, u32[]{:S(2)}, u32[]{:S(2)}) %collective-permute-start.3) | collective-permute-done | bytes 573472 | tf_op jit(solution)/shard_map/ppermute | solution.py:379
  21.9 0.1 collective-permute-start.6
  22.0 0.6 collective-permute-start.5
  22.5 0.1 collective-permute-start.4
  22.6 2.7 %tile.7 = (f32[40,512]{1,0:T(8,128)S(1)}, f32[40,1024]{1,0:T(8,128)S(1)}) custom-call(bf16[560,512]{1,0:T(8,128)(2,1)S(1)} %collective-permute-done.2.refs_0_, bf16[560,1024]{1,0:T(8,128)(2,1)S(1)} %get-tuple-element.44.refs_1_), custom_call_target="tpu_custom_call" | custom-call | flops 1 | bytes 1 | tf_op jit(solution)/shard_map/tile/pallas_call | solution.py:239
  25.4 2.9 %tile.8 = (f32[40,512]{1,0:T(8,128)S(1)}, bf16[560,1024]{1,0:T(8,128)(2,1)S(1)}) custom-call(bf16[560,512]{1,0:T(8,128)(2,1)S(1)} %get-tuple-element.36.refs_0_.refs_1_, bf16[560,512]{1,0:T(8,128)(2,1)S(1)} %collective-permute-done.3.refs_1_, bf16[560,512]{1,0:T(8,128)(2,1)S(1)} %pad_maximum_fusion.refs_2_), custom_call_target="tpu_custom_call" | custom-call | flops 1 | bytes 1 | tf_op jit(solution)/shard_map/tile/pallas_call | solution.py:239
  28.3 2.7 %tile.9 = (f32[40,512]{1,0:T(8,128)S(1)}, f32[40,1024]{1,0:T(8,128)S(1)}) custom-call(bf16[560,512]{1,0:T(8,128)(2,1)S(1)} %collective-permute-done.2.refs_0_, bf16[560,1024]{1,0:T(8,128)(2,1)S(1)} %get-tuple-element.50.refs_1_), custom_call_target="tpu_custom_call" | custom-call | flops 1 | bytes 1 | tf_op jit(solution)/shard_map/tile/pallas_call | solution.py:239
  31.0 0.3 collective-permute-start.8
  31.3 0.6 collective-permute-done.7.refs_0_
  32.0 4.8 %collective-permute-done.8.refs_2_ = f32[40,512]{1,0:T(8,128)S(1)} collective-permute-done((f32[40,512]{1,0:T(8,128)S(1)}, f32[40,512]{1,0:T(8,128)S(1)}, u32[]{:S(2)}, u32[]{:S(2)}) %collective-permute-start.8) | collective-permute-done | bytes 81952 | tf_op jit(solution)/shard_map/ppermute | solution.py:405
  36.8 1.3 %collective-permute-start.9 = (f32[40,512]{1,0:T(8,128)S(1)}, f32[40,512]{1,0:T(8,128)S(1)}, u32[]{:S(2)}, u32[]{:S(2)}) collective-permute-start(f32[40,512]{1,0:T(8,128)S(1)} %add.25), channel_id=1, source_target_pairs={{4,8},{6,10},{12,0},{14,2},{5,9},{7,11},{13,1},{15,3},{20,24},{22,... | collective-permute-start | bytes 245768 | tf_op jit(solution)/shard_map/ppermute | solution.py:405
  38.2 1.6 %collective-permute-start.11 = (f32[40,512]{1,0:T(8,128)S(1)}, f32[40,512]{1,0:T(8,128)S(1)}, u32[]{:S(2)}, u32[]{:S(2)}) collective-permute-start(f32[40,512]{1,0:T(8,128)S(1)} %slice_add_fusion), channel_id=1, source_target_pairs={{0,2},{2,0},{4,6},{6,4},{8,10},{10,8},{12,14},{14,12},{1,3},{3,1},... | collective-permute-start | bytes 245768 | tf_op jit(solution)/shard_map/ppermute | solution.py:409
  39.8 0.3 collective-permute-start.12
  40.1 6.1 %collective-permute-done.9.refs_3_ = f32[40,512]{1,0:T(8,128)S(1)} collective-permute-done((f32[40,512]{1,0:T(8,128)S(1)}, f32[40,512]{1,0:T(8,128)S(1)}, u32[]{:S(2)}, u32[]{:S(2)}) %collective-permute-start.9) | collective-permute-done | bytes 81952 | tf_op jit(solution)/shard_map/ppermute | solution.py:405
  46.2 0.9 %image.1 = (f32[32,512]{1,0:T(8,128)S(1)}, f32[16,8,128]{2,1,0:T(8,128)}) custom-call(f32[40,512]{1,0:T(8,128)S(1)} %get-tuple-element.40.refs_0_, f32[40,512]{1,0:T(8,128)S(1)} %get-tuple-element.48.refs_1_, f32[40,512]{1,0:T(8,128)S(1)} %collective-permute-done.8.refs_2_, f32[40,512]{1,0:T(8,128)S(1)} %collective-permute-done.9.refs_3_, ...), custom_call_target="tpu_custom_call" | custom-call | tf_op jit(solution)/shard_map/image/pallas_call | solution.py:278
  47.1 4.2 %all-to-all-start = ((f32[16,8,128]{2,1,0:T(8,128)}), f32[16,8,128]{2,1,0:T(8,128)S(1)}, u32[]{:S(2)}, u32[]{:S(2)}) async-start(f32[16,8,128]{2,1,0:T(8,128)} %get-tuple-element.65), calls=%async_computation | async-start | bytes 131072 | tf_op jit(solution)/shard_map/all_to_all | solution.py:414
  51.4 0.4 collective-permute-start.13
  51.8 0.9 %collective-permute-done.13.other_ref = f32[32,512]{1,0:T(8,128)S(1)} collective-permute-done((f32[32,512]{1,0:T(8,128)S(1)}, f32[32,512]{1,0:T(8,128)S(1)}, u32[]{:S(2)}, u32[]{:S(2)}) %collective-permute-start.13) | collective-permute-done | bytes 65568 | tf_op jit(solution)/shard_map/ppermute | solution.py:413
  52.7 5.6 %all-to-all-done.grams_ref = f32[16,8,128]{2,1,0:T(8,128)S(1)} async-done(((f32[16,8,128]{2,1,0:T(8,128)}), f32[16,8,128]{2,1,0:T(8,128)S(1)}, u32[]{:S(2)}, u32[]{:S(2)}) %all-to-all-start) | async-done | bytes 65568 | tf_op jit(solution)/shard_map/all_to_all | solution.py:414
  58.3 2.9 %basis.1 = f32[16,1024]{1,0:T(8,128)} custom-call(f32[16,8,128]{2,1,0:T(8,128)S(1)} %all-to-all-done.grams_ref, f32[32,512]{1,0:T(8,128)S(1)} %get-tuple-element.66.mine_ref, f32[32,512]{1,0:T(8,128)S(1)} %collective-permute-done.13.other_ref), custom_call_target="tpu_custom_call" | custom-call | tf_op jit(solution)/shard_map/basis/pallas_call | solution.py:331
  (21 shorter events, 0.3 us)
Async XLA Ops:
  0.0 2.4 %copy-start = (bf16[16,1024]{1,0:T(8,128)(2,1)S(1)}, bf16[16,1024]{1,0:T(8,128)(2,1)}, u32[]{:S(2)}) copy-start(bf16[16,1024]{1,0:T(8,128)(2,1)} %vec_ref.1) | copy-start | bytes 98308
  0.0 2.4 %collective-permute-start = (bf16[1024,256]{1,0:T(8,128)(2,1)}, bf16[1024,256]{1,0:T(8,128)(2,1)S(1)}, u32[]{:S(2)}, u32[]{:S(2)}) collective-permute-start(bf16[1024,256]{1,0:T(8,128)(2,1)} %param.5), channel_id=1, source_target_pairs={{0,1},{1,0},{2,3},{3,2},{4,5},{5,4},{6,7},{7,6},{8,9},{9,8},{10,11... | collective-permute-start | bytes 1572872 | tf_op jit(solution)/shard_map/ppermute | solution.py:372
  0.5 1.9 %collective-permute-start.1 = (bf16[16,1024]{1,0:T(8,128)(2,1)}, bf16[16,1024]{1,0:T(8,128)(2,1)S(1)}, u32[]{:S(2)}, u32[]{:S(2)}) collective-permute-start(bf16[16,1024]{1,0:T(8,128)(2,1)} %vec_ref.1), channel_id=1, source_target_pairs={{0,1},{1,0},{2,3},{3,2},{4,5},{5,4},{6,7},{7,6},{8,9},{9,8},{10,11... | collective-permute-start | bytes 98312 | tf_op jit(solution)/shard_map/ppermute | solution.py:373
  3.1 17.4 %collective-permute-start.2 = (bf16[560,512]{1,0:T(8,128)(2,1)S(1)}, bf16[560,512]{1,0:T(8,128)(2,1)S(1)}, u32[]{:S(2)}, u32[]{:S(2)}) collective-permute-start(bf16[560,512]{1,0:T(8,128)(2,1)S(1)} %get-tuple-element.36.refs_0_.refs_1_), channel_id=1, source_target_pairs={{0,8},{2,10},{12,4},{14,6},{4,0},{6,2},{8,12},{10,14},{1,9},{3,11}... | collective-permute-start | bytes 1720328 | tf_op jit(solution)/shard_map/ppermute | solution.py:378
  7.2 14.7 %collective-permute-start.3 = (bf16[560,512]{1,0:T(8,128)(2,1)S(1)}, bf16[560,512]{1,0:T(8,128)(2,1)S(1)}, u32[]{:S(2)}, u32[]{:S(2)}) collective-permute-start(bf16[560,512]{1,0:T(8,128)(2,1)S(1)} %get-tuple-element.36.refs_0_.refs_1_), channel_id=1, source_target_pairs={{0,2},{2,0},{4,6},{6,4},{8,10},{10,8},{12,14},{14,12},{1,3},{3,1},... | collective-permute-start | bytes 1720328 | tf_op jit(solution)/shard_map/ppermute | solution.py:379
  8.7 23.2 %collective-permute-start.7 = (bf16[560,512]{1,0:T(8,128)(2,1)S(1)}, bf16[560,512]{1,0:T(8,128)(2,1)S(1)}, u32[]{:S(2)}, u32[]{:S(2)}) collective-permute-start(bf16[560,512]{1,0:T(8,128)(2,1)S(1)} %get-tuple-element.36.refs_0_.refs_1_), channel_id=1, source_target_pairs={{8,4},{10,6},{0,12},{2,14},{9,5},{11,7},{1,13},{3,15},{24,20},{26,... | collective-permute-start | bytes 1720328 | tf_op jit(solution)/shard_map/ppermute | solution.py:378
  21.9 3.5 %collective-permute-start.6 = (bf16[208,512]{1,0:T(8,128)(2,1)S(1)}, bf16[208,512]{1,0:T(8,128)(2,1)S(1)}, u32[]{:S(2)}, u32[]{:S(2)}) collective-permute-start(bf16[208,512]{1,0:T(8,128)(2,1)S(1)} %slice.23), channel_id=1, source_target_pairs={{0,1},{1,0},{2,3},{3,2},{4,5},{5,4},{6,7},{7,6},{8,9},{9,8},{10,11... | collective-permute-start | bytes 638984 | tf_op jit(solution)/shard_map/ppermute | solution.py:386
  22.0 3.4 %collective-permute-start.5 = (bf16[176,512]{1,0:T(8,128)(2,1)S(1)}, bf16[176,512]{1,0:T(8,128)(2,1)S(1)}, u32[]{:S(2)}, u32[]{:S(2)}) collective-permute-start(bf16[176,512]{1,0:T(8,128)(2,1)S(1)} %get-tuple-element.68), channel_id=1, source_target_pairs={{0,1},{1,0},{2,3},{3,2},{4,5},{5,4},{6,7},{7,6},{8,9},{9,8},{10,11... | collective-permute-start | bytes 540680 | tf_op jit(solution)/shard_map/ppermute | solution.py:386
  22.5 2.8 %collective-permute-start.4 = (bf16[176,512]{1,0:T(8,128)(2,1)S(1)}, bf16[176,512]{1,0:T(8,128)(2,1)S(1)}, u32[]{:S(2)}, u32[]{:S(2)}) collective-permute-start(bf16[176,512]{1,0:T(8,128)(2,1)S(1)} %get-tuple-element.67), channel_id=1, source_target_pairs={{0,1},{1,0},{2,3},{3,2},{4,5},{5,4},{6,7},{7,6},{8,9},{9,8},{10,11... | collective-permute-start | bytes 540680 | tf_op jit(solution)/shard_map/ppermute | solution.py:386
  31.0 5.7 %collective-permute-start.8 = (f32[40,512]{1,0:T(8,128)S(1)}, f32[40,512]{1,0:T(8,128)S(1)}, u32[]{:S(2)}, u32[]{:S(2)}) collective-permute-start(f32[40,512]{1,0:T(8,128)S(1)} %add.24), channel_id=1, source_target_pairs={{8,0},{10,2},{4,12},{6,14},{0,4},{2,6},{12,8},{14,10},{9,1},{11,3}... | collective-permute-start | bytes 245768 | tf_op jit(solution)/shard_map/ppermute | solution.py:405
  36.8 1.4 %collective-permute-start.10 = (f32[40,512]{1,0:T(8,128)S(1)}, f32[40,512]{1,0:T(8,128)S(1)}, u32[]{:S(2)}, u32[]{:S(2)}) collective-permute-start(f32[40,512]{1,0:T(8,128)S(1)} %slice.25), channel_id=1, source_target_pairs={{0,1},{1,0},{2,3},{3,2},{4,5},{5,4},{6,7},{7,6},{8,9},{9,8},{10,11... | collective-permute-start | bytes 245768 | tf_op jit(solution)/shard_map/ppermute | solution.py:407
  36.8 9.4 %collective-permute-start.9 = (f32[40,512]{1,0:T(8,128)S(1)}, f32[40,512]{1,0:T(8,128)S(1)}, u32[]{:S(2)}, u32[]{:S(2)}) collective-permute-start(f32[40,512]{1,0:T(8,128)S(1)} %add.25), channel_id=1, source_target_pairs={{4,8},{6,10},{12,0},{14,2},{5,9},{7,11},{13,1},{15,3},{20,24},{22,... | collective-permute-start | bytes 245768 | tf_op jit(solution)/shard_map/ppermute | solution.py:405
  38.2 8.0 %collective-permute-start.11 = (f32[40,512]{1,0:T(8,128)S(1)}, f32[40,512]{1,0:T(8,128)S(1)}, u32[]{:S(2)}, u32[]{:S(2)}) collective-permute-start(f32[40,512]{1,0:T(8,128)S(1)} %slice_add_fusion), channel_id=1, source_target_pairs={{0,2},{2,0},{4,6},{6,4},{8,10},{10,8},{12,14},{14,12},{1,3},{3,1},... | collective-permute-start | bytes 245768 | tf_op jit(solution)/shard_map/ppermute | solution.py:409
  39.8 6.4 %collective-permute-start.12 = (f32[40,512]{1,0:T(8,128)S(1)}, f32[40,512]{1,0:T(8,128)S(1)}, u32[]{:S(2)}, u32[]{:S(2)}) collective-permute-start(f32[40,512]{1,0:T(8,128)S(1)} %get-tuple-element.71), channel_id=1, source_target_pairs={{0,1},{1,0},{2,3},{3,2},{4,5},{5,4},{6,7},{7,6},{8,9},{9,8},{10,11... | collective-permute-start | bytes 245768 | tf_op jit(solution)/shard_map/ppermute | solution.py:411
  47.1 11.1 %all-to-all-start = ((f32[16,8,128]{2,1,0:T(8,128)}), f32[16,8,128]{2,1,0:T(8,128)S(1)}, u32[]{:S(2)}, u32[]{:S(2)}) async-start(f32[16,8,128]{2,1,0:T(8,128)} %get-tuple-element.65), calls=%async_computation | async-start | bytes 131072 | tf_op jit(solution)/shard_map/all_to_all | solution.py:414
  51.4 1.3 %collective-permute-start.13 = (f32[32,512]{1,0:T(8,128)S(1)}, f32[32,512]{1,0:T(8,128)S(1)}, u32[]{:S(2)}, u32[]{:S(2)}) collective-permute-start(f32[32,512]{1,0:T(8,128)S(1)} %get-tuple-element.66.mine_ref), channel_id=1, source_target_pairs={{0,1},{1,0},{2,3},{3,2},{4,5},{5,4},{6,7},{7,6},{8,9},{9,8},{10,11... | collective-permute-start | bytes 196616 | tf_op jit(solution)/shard_map/ppermute | solution.py:413
